TPU v7x, 128 devices: a whole 4x4x4 slice. The times are simulated.
128 devices in a mesh: agent: 16 (over x, y_hi, core), mode: 8 (over z, y_lo).
Axes of the slice: x: 4, y: 4 (y_hi: 2, y_lo: 2; y = y_hi * 2 + y_lo), z: 4, core: 2. Of those that a mesh axis runs over, the one named last changes fastest.
Arguments:
- tokens: bfloat16 [128, 64, 4, 1024], P('agent', 'mode'), may hold values from -8 to 8
- cotangent: bfloat16 [128, 64, 4, 1024], P('agent', 'mode'), may hold values from -6 to 6
- weights: bfloat16 [8, 1024, 1024], replicated, may hold values from -2 to 2
- agent_mask: int32 [128], replicated, may hold values from 0 to 1, as said below
Outputs:
- token_grads: bfloat16 [128, 64, 4, 1024], P('agent', 'mode')
- agent_weight_grads: float32 [4096, 1024], P(('agent', 'mode'))
- mode_weight_grads: float32 [4096, 1024], P(('agent', 'mode'))
Inputs may be any that keep to these rules, and one draw needn't show every extreme that they name: `agent_mask`: 1 marks a valid agent; at least one agent is valid.
All inputs are finite; a program needn't handle non-finite values.
Results may differ from a plain program's by a relative error of at most 0.034.
The roundings to bfloat16 on the way count: a program that leaves them out, or rounds other values in their place, can miss the bound.
Values may be sent and summed in bfloat16 or wider, within the bound.
No kernel may reach another device: no remote copies, remote signals or barrier semaphores. Data moves between devices by JAX's collectives and lax.ppermute only.
A program may use at most 192 MiB of HBM per device.

v0:
```python
import jax
import jax.numpy as jnp
from jax import lax
from jax.sharding import PartitionSpec as P

HEADS = 16


epsilon = 1e-06
masked_score = -1000000000.0


def normalize(values):
    wide = values.astype(jnp.float32)
    factor = lax.rsqrt(jnp.mean(wide * wide, -1, keepdims=True) + epsilon)
    return (wide * factor, factor)


def normalize_back(values, factor, upstream):
    normed = values.astype(jnp.float32) * factor
    return factor * (upstream - normed * jnp.mean(upstream * normed, -1, keepdims=True))


def probabilities(query_in, keys_in, offset_add, forms):
    query_form, keys_form, score_form = forms
    scaling = query_in.shape[-1] ** (-0.5)
    scores = (
        jnp.einsum(
            query_form + "," + keys_form + "->" + score_form,
            query_in,
            keys_in,
            preferred_element_type=jnp.float32,
        )
        * scaling
        + offset_add
    )
    largest = jnp.max(scores, -1, keepdims=True)
    raised = jnp.exp(scores - largest)
    return raised / jnp.sum(raised, -1, keepdims=True)


def attend(table, values_in, forms):
    query_form, keys_form, score_form = forms
    return jnp.einsum(
        score_form + "," + keys_form + "->" + query_form,
        table.astype(jnp.bfloat16),
        values_in,
        preferred_element_type=jnp.float32,
    ).astype(jnp.bfloat16)


def attention_back(table, query_in, keys_in, values_in, upstream, forms):
    query_form, keys_form, score_form = forms
    scaling = query_in.shape[-1] ** (-0.5)
    rounded = table.astype(jnp.bfloat16)
    through = jnp.einsum(
        query_form + "," + keys_form + "->" + score_form,
        upstream,
        values_in,
        preferred_element_type=jnp.float32,
    )
    value_grad = jnp.einsum(
        score_form + "," + query_form + "->" + keys_form,
        rounded,
        upstream,
        preferred_element_type=jnp.float32,
    ).astype(jnp.bfloat16)
    centre = jnp.sum(through * table, -1, keepdims=True)
    score_grad = (table * (through - centre) * scaling).astype(jnp.bfloat16)
    query_grad = jnp.einsum(
        score_form + "," + keys_form + "->" + query_form,
        score_grad,
        keys_in,
        preferred_element_type=jnp.float32,
    ).astype(jnp.bfloat16)
    keys_grad = jnp.einsum(
        score_form + "," + query_form + "->" + keys_form,
        score_grad,
        query_in,
        preferred_element_type=jnp.float32,
    ).astype(jnp.bfloat16)
    return (query_grad, keys_grad, value_grad)


def spread_agents(stacked):
    return lax.all_to_all(stacked, "agent", split_axis=4, concat_axis=1, tiled=True)


def collect_agents(stacked):
    return lax.all_to_all(stacked, "agent", split_axis=1, concat_axis=4, tiled=True)


def weight_terms(lefts, rights, model_width):

    def compute(start_row, row_count):
        products = jnp.einsum("ktr,ktc->krc", lefts, rights, preferred_element_type=jnp.float32)
        return products.reshape(row_count, model_width)

    return compute


def reduce_grads(lefts, rights):
    model_width = lefts.shape[2]
    compute = weight_terms(lefts, rights, model_width)
    share_rows = 4 * model_width // lax.axis_size("agent")
    partial_rows = lax.psum_scatter(
        compute(jnp.int32(0), share_rows * lax.axis_size("agent")).astype(jnp.bfloat16),
        "agent",
        scatter_dimension=0,
        tiled=True,
    )
    return lax.psum_scatter(partial_rows, "mode", scatter_dimension=0, tiled=True).astype(
        jnp.float32
    )


def local(tokens, cotangent, weights, agent_mask):
    agents_here, modes_here, step_count, model_width = tokens.shape
    head_count = HEADS
    head_width = model_width // head_count
    split_shape = (agents_here, modes_here, step_count, head_count, head_width)
    token_rows = tokens.reshape(-1, model_width)
    grad_rows = cotangent.reshape(-1, model_width)
    key_offset = jnp.where(agent_mask == 1, 0.0, masked_score).astype(jnp.float32)
    agent_forms = ("amshe", "bmshe", "mshab")
    mode_forms = ("amshe", "anshe", "ashmn")

    def project_three(inputs, first_slot):
        products = jnp.einsum(
            "td,kdf->ktf",
            inputs,
            weights[first_slot : first_slot + 3],
            preferred_element_type=jnp.float32,
        )
        return products.astype(jnp.bfloat16).reshape((3,) + split_shape)

    def project_back(grads, matrix_slot):
        return lax.dot_general(
            grads,
            weights[matrix_slot],
            (((1,), (1,)), ((), ())),
            preferred_element_type=jnp.float32,
        )

    def project_back_three(stacked_grads, first_slot):
        return jnp.einsum(
            "ktf,kdf->td",
            stacked_grads,
            weights[first_slot : first_slot + 3],
            preferred_element_type=jnp.float32,
        )

    normed_one, factor_one = normalize(token_rows)
    hidden_one = normed_one.astype(jnp.bfloat16)
    spread_one = spread_agents(project_three(hidden_one, 0))
    query_one, keys_one, values_one = (spread_one[0], spread_one[1], spread_one[2])
    table_one = probabilities(query_one, keys_one, key_offset, agent_forms)
    collected_one = collect_agents(attend(table_one, values_one, agent_forms)[None])
    mixed_rows = collected_one[0].reshape(-1, model_width)
    after_agents = (
        token_rows.astype(jnp.float32)
        + jnp.dot(mixed_rows, weights[3], preferred_element_type=jnp.float32)
    ).astype(jnp.bfloat16)
    normed_two, factor_two = normalize(after_agents)
    hidden_two = normed_two.astype(jnp.bfloat16)
    upstream_two = project_back(grad_rows, 7).astype(jnp.bfloat16).reshape(split_shape)
    outgoing_two = jnp.concatenate([project_three(hidden_two, 4), upstream_two[None]], 0)
    spread_two = lax.all_to_all(outgoing_two, "mode", split_axis=4, concat_axis=2, tiled=True)
    query_two, keys_two, values_two, arriving_two = (
        spread_two[0],
        spread_two[1],
        spread_two[2],
        spread_two[3],
    )
    table_two = probabilities(query_two, keys_two, 0.0, mode_forms)
    mixed_two = attend(table_two, values_two, mode_forms)
    query_grad_two, keys_grad_two, value_grad_two = attention_back(
        table_two, query_two, keys_two, values_two, arriving_two, mode_forms
    )
    returning_two = jnp.stack([mixed_two, query_grad_two, keys_grad_two, value_grad_two])
    returned_two = lax.all_to_all(
        returning_two, "mode", split_axis=2, concat_axis=4, tiled=True
    ).reshape(4, -1, model_width)
    mixed_rows_two = returned_two[0]
    grads_rows_two = returned_two[1:4]
    hidden_grad_two = project_back_three(grads_rows_two, 4)
    grad_after = (
        grad_rows.astype(jnp.float32) + normalize_back(after_agents, factor_two, hidden_grad_two)
    ).astype(jnp.bfloat16)
    upstream_one = project_back(grad_after, 3).astype(jnp.bfloat16).reshape((1,) + split_shape)
    arriving_one = spread_agents(upstream_one)[0]
    query_grad_one, keys_grad_one, value_grad_one = attention_back(
        table_one, query_one, keys_one, values_one, arriving_one, agent_forms
    )
    grads_rows_one = collect_agents(
        jnp.stack([query_grad_one, keys_grad_one, value_grad_one])
    ).reshape(3, -1, model_width)
    hidden_grad_one = project_back_three(grads_rows_one, 0)
    token_grads = (
        grad_after.astype(jnp.float32) + normalize_back(token_rows, factor_one, hidden_grad_one)
    ).astype(jnp.bfloat16)
    mode_lefts = jnp.stack([hidden_two, hidden_two, hidden_two, mixed_rows_two])
    mode_rights = jnp.concatenate([grads_rows_two, grad_rows[None]], 0)
    mode_weight_grads = reduce_grads(mode_lefts, mode_rights)
    agent_lefts = jnp.stack([hidden_one, hidden_one, hidden_one, mixed_rows])
    agent_rights = jnp.concatenate([grads_rows_one, grad_after[None]], 0)
    agent_weight_grads = reduce_grads(agent_lefts, agent_rights)
    return (token_grads.reshape(tokens.shape), agent_weight_grads, mode_weight_grads)


def solution(mesh):
    placed = (P("agent", "mode", None, None), P("agent", "mode", None, None), P(), P())
    return jax.shard_map(
        local,
        mesh=mesh,
        in_specs=placed,
        out_specs=(
            P("agent", "mode", None, None),
            P(("agent", "mode"), None),
            P(("agent", "mode"), None),
        ),
        check_vma=False,
    )
```

profile of v0, /device:TPU:0, one launch (start us, length us, event | category | flops | bytes accessed | tf_op | source)
XLA Modules:
  0.0 579.5 jit_solution(7559284074271990758)
XLA Ops:
  10.6 5.8 fusion.76
  16.4 4.1 reshape.198
  20.5 3.7 copy.210
  24.2 4.9 reshape.213
  29.1 7.5 %all-to-all-start = ((bf16[16,2,24576]{2,1,0:T(2,128)(2,1)}), bf16[16,2,24576]{2,1,0:T(2,128)(2,1)}, u32[]{:S(2)}, u32[]{:S(2)}) async-start(bf16[16,2,24576]{2,1,0:T(2,128)(2,1)} %reshape.213), calls=%async_computation | async-start | bytes 3145728 | tf_op jit(solution)/shard_map/all_to_all | solution.py:86
  36.7 23.6 %all-to-all-done = bf16[16,2,24576]{2,1,0:T(2,128)(2,1)} async-done(((bf16[16,2,24576]{2,1,0:T(2,128)(2,1)}), bf16[16,2,24576]{2,1,0:T(2,128)(2,1)}, u32[]{:S(2)}, u32[]{:S(2)}) %all-to-all-start) | async-done | bytes 1572896 | tf_op jit(solution)/shard_map/all_to_all | solution.py:86
  60.3 3.8 reshape.214
  76.0 4.3 all-to-all-start.1
  85.9 6.8 %all-to-all-done.1 = bf16[16,2,8192]{2,1,0:T(2,128)(2,1)S(1)} async-done(((bf16[16,2,8192]{2,1,0:T(2,128)(2,1)}), bf16[16,2,8192]{2,1,0:T(2,128)(2,1)S(1)}, u32[]{:S(2)}, u32[]{:S(2)}) %all-to-all-start.1) | async-done | bytes 524320 | tf_op jit(solution)/shard_map/all_to_all | solution.py:90
  98.1 5.8 %fusion.73 = bf16[3,256,1024]{2,1,0:T(8,128)(2,1)} fusion(bf16[8,1024,1024]{2,1,0:T(8,128)(2,1)} %param.6, bf16[256,1024]{1,0:T(8,128)(2,1)S(1)} %get-tuple-element.15, f32[256]{0:T(256)S(1)} %add_rsqrt_fusion.1), kind=kOutput, calls=%fused_computation.67 | convolution fusion | flops 1612185600 | bytes 8389632 | tf_op jit(solution)/shard_map/td,kdf->ktf/dot_general | solution.py:129
  103.9 4.1 reshape.202
  110.1 2.8 fusion.197
  112.9 6.4 %reshape.217 = bf16[8,2,65536]{2,1,0:T(2,128)(2,1)S(1)} reshape(bf16[16,4,8,4,8,64]{5,4,3,2,1,0:T(8,128)(2,1)} %fusion.197) | data formatting | bytes 4194304
  119.3 32.1 %all_to_all.90 = bf16[8,2,65536]{2,1,0:T(2,128)(2,1)} all-to-all(bf16[8,2,65536]{2,1,0:T(2,128)(2,1)S(1)} %reshape.217), channel_id=1, replica_groups=mesh['agent'=16,'mode'=8] {'mode'}, dimensions={0} | all-to-all | bytes 4194304 | tf_op jit(solution)/shard_map/all_to_all | solution.py:168
  151.3 7.4 %reshape.218 = bf16[16,4,8,4,8,64]{5,4,3,2,1,0:T(8,128)(2,1)} reshape(bf16[8,2,65536]{2,1,0:T(2,128)(2,1)} %all_to_all.90) | data formatting | bytes 4194304
  158.7 3.4 copy.112
  165.9 3.4 fusion.192
  169.2 5.7 fusion.84
  175.0 5.5 fusion.81
  180.4 2.5 fusion.80
  184.4 2.5 pad_maximum_fusion.1
  187.0 11.8 %copy.125 = bf16[4,8,64,4,2,64]{5,4,3,1,0,2:T(2,128)(2,1)} copy(bf16[4,8,64,4,2,64]{2,5,4,3,1,0:T(8,128)(2,1)} %pad_maximum_fusion.1) | data formatting | bytes 4194304 | tf_op jit(solution)/shard_map/stack | solution.py:180
  198.7 7.6 %reshape.219 = bf16[8,2,65536]{2,1,0:T(2,128)(2,1)} reshape(bf16[64,4,8,4,2,64]{5,4,3,2,1,0:T(2,128)(2,1)} %bitcast.186) | data formatting | bytes 4194304
  206.3 3.7 all-to-all-start.3
  211.2 24.1 %all-to-all-done.3 = bf16[8,2,65536]{2,1,0:T(2,128)(2,1)S(1)} async-done(((bf16[8,2,65536]{2,1,0:T(2,128)(2,1)}), bf16[8,2,65536]{2,1,0:T(2,128)(2,1)S(1)}, u32[]{:S(2)}, u32[]{:S(2)}) %all-to-all-start.3) | async-done | bytes 2097184 | tf_op jit(solution)/shard_map/all_to_all | solution.py:181
  235.3 5.0 reshape.220
  240.3 7.0 %copy.209 = bf16[4,8,64,4,2,64]{5,2,4,3,1,0:T(8,128)(2,1)S(1)} copy(bf16[4,8,64,4,2,64]{5,4,3,1,0,2:T(2,128)(2,1)} %bitcast.187) | data formatting | bytes 4194304 | tf_op jit(solution)/shard_map/all_to_all | solution.py:181
  249.1 3.2 copy.127
  252.4 3.4 slice.67
  255.8 2.4 copy.143
  258.9 4.9 fusion.122
  264.8 6.0 %convolution_convert_fusion = bf16[4,1024,1024]{2,1,0:T(8,128)(2,1)} fusion(bf16[1,256,1024]{2,1,0:T(8,128)(2,1)S(1)} %slice.69, bf16[1,256,1024]{2,1,0:T(8,128)(2,1)S(1)} %get-tuple-element.10, bf16[1,256,1024]{2,1,0:T(8,128)(2,1)S(1)} %copy-done.22, bf16[3,256,1024]{2,1,0:T(8,128)(2,1)S(1)} %copy-done.16), kind=kOutput, calls=%fused_computation.4 | convolution fusion | flops 2155872256 | bytes 11534336 | tf_op jit(solution)/shard_map/ktr,ktc->krc/dot_general | solution.py:96
  275.3 17.5 %all_to_all.91 = bf16[16,2,8192]{2,1,0:T(2,128)(2,1)S(1)} all-to-all(bf16[16,2,8192]{2,1,0:T(2,128)(2,1)S(1)} %reshape.221), channel_id=1, replica_groups=mesh['agent'=16,'mode'=8] {'agent'}, dimensions={0} | all-to-all | bytes 1048576 | tf_op jit(solution)/shard_map/all_to_all | solution.py:86
  295.1 4.0 fusion.119
  299.1 3.8 fusion.116
  302.9 2.5 fusion.115
  306.8 4.6 copy.137
  311.5 3.2 reshape.223
  314.7 4.5 all-to-all-start.5
  322.3 25.4 %all-to-all-done.5 = bf16[16,2,24576]{2,1,0:T(2,128)(2,1)} async-done(((bf16[16,2,24576]{2,1,0:T(2,128)(2,1)}), bf16[16,2,24576]{2,1,0:T(2,128)(2,1)}, u32[]{:S(2)}, u32[]{:S(2)}) %all-to-all-start.5) | async-done | bytes 1572896 | tf_op jit(solution)/shard_map/all_to_all | solution.py:90
  347.7 4.0 reshape.224
  354.5 3.2 reshape.205
  357.6 7.8 %convolution_convert_fusion.1 = bf16[4,1024,1024]{2,1,0:T(8,128)(2,1)} fusion(bf16[1,256,1024]{1,2,0:T(8,128)(2,1)} %copy.142, bf16[1,256,1024]{1,2,0:T(8,128)(2,1)} %multiply_convert_fusion.2, bf16[1,256,1024]{2,1,0:T(8,128)(2,1)} %bitcast.202, bf16[3,256,1024]{2,1,0:T(8,128)(2,1)} %reshape.205), kind=kOutput, calls=%fused_computation.5 | convolution fusion | flops 2155872256 | bytes 11534336 | tf_op jit(solution)/shard_map/ktr,ktc->krc/dot_general | solution.py:96
  365.5 20.8 %reduce-scatter.9.cloned.1.call-done = bf16[256,1024]{1,0:T(8,128)(2,1)} async-done(((bf16[4096,1024]{1,0:T(8,128)(2,1)}), bf16[256,1024]{1,0:T(8,128)(2,1)}) %reduce-scatter.9.cloned.1.call-update) | async-done | bytes 524304 | tf_op jit(solution)/shard_map/reduce_scatter | solution.py:106
  386.4 105.6 %reduce-scatter.5.cloned.1.call-done = bf16[256,1024]{1,0:T(8,128)(2,1)} async-done(((bf16[4096,1024]{1,0:T(8,128)(2,1)}), bf16[256,1024]{1,0:T(8,128)(2,1)}) %reduce-scatter.5.cloned.1.call-update) | async-done | bytes 524304 | tf_op jit(solution)/shard_map/reduce_scatter | solution.py:106
  492.0 4.7 multiply_reduce_fusion.3
  498.1 33.6 %reduce-scatter.11.cloned.1.call-done = bf16[32,1024]{1,0:T(8,128)(2,1)} async-done(((bf16[256,1024]{1,0:T(8,128)(2,1)}), bf16[32,1024]{1,0:T(8,128)(2,1)}) %reduce-scatter.11.cloned.1.call-update) | async-done | bytes 65552 | tf_op jit(solution)/shard_map/reduce_scatter | solution.py:112
  533.2 37.8 %reduce-scatter.7.cloned.1.call-done = bf16[32,1024]{1,0:T(8,128)(2,1)} async-done(((bf16[256,1024]{1,0:T(8,128)(2,1)}), bf16[32,1024]{1,0:T(8,128)(2,1)}) %reduce-scatter.7.cloned.1.call-update) | async-done | bytes 65552 | tf_op jit(solution)/shard_map/reduce_scatter | solution.py:112
  (120 shorter events, 56.5 us)
Async XLA Ops:
  9.7 1.0 copy-start.3
  29.1 7.5 %copy-start.27 = (s32[128]{0:T(128)S(1)}, s32[128]{0:T(128)}, u32[]{:S(2)}) copy-start(s32[128]{0:T(128)} %param.7) | copy-start | bytes 1540
  29.1 31.2 %all-to-all-start = ((bf16[16,2,24576]{2,1,0:T(2,128)(2,1)}), bf16[16,2,24576]{2,1,0:T(2,128)(2,1)}, u32[]{:S(2)}, u32[]{:S(2)}) async-start(bf16[16,2,24576]{2,1,0:T(2,128)(2,1)} %reshape.213), calls=%async_computation | async-start | bytes 3145728 | tf_op jit(solution)/shard_map/all_to_all | solution.py:86
  67.0 2.2 copy-start.19
  68.1 3.4 copy-start.20
  69.3 4.3 copy-start.9
  73.5 6.8 %copy-start.7 = (bf16[8,8,4,1024]{3,2,1,0:T(4,128)(2,1)S(1)}, bf16[8,8,4,1024]{3,2,1,0:T(4,128)(2,1)}, u32[]{:S(2)}) copy-start(bf16[8,8,4,1024]{3,2,1,0:T(4,128)(2,1)} %param.5) | copy-start | bytes 1572868
  76.0 16.6 %all-to-all-start.1 = ((bf16[16,2,8192]{2,1,0:T(2,128)(2,1)}), bf16[16,2,8192]{2,1,0:T(2,128)(2,1)S(1)}, u32[]{:S(2)}, u32[]{:S(2)}) async-start(bf16[16,2,8192]{2,1,0:T(2,128)(2,1)} %reshape.215), calls=%async_computation.1 | async-start | bytes 1048576 | tf_op jit(solution)/shard_map/all_to_all | solution.py:90
  80.4 0.8 copy-start.11
  93.5 1.4 copy-start.4
  94.2 3.1 copy-start
  97.3 0.8 copy-start.23
  108.1 2.0 copy-start.6
  180.4 2.5 copy-start.28
  182.9 1.2 copy-start.17
  182.9 1.5 copy-start.18
  206.3 4.0 copy-start.8
  206.3 29.0 %all-to-all-start.3 = ((bf16[8,2,65536]{2,1,0:T(2,128)(2,1)}), bf16[8,2,65536]{2,1,0:T(2,128)(2,1)S(1)}, u32[]{:S(2)}, u32[]{:S(2)}) async-start(bf16[8,2,65536]{2,1,0:T(2,128)(2,1)} %reshape.219), calls=%async_computation.3 | async-start | bytes 4194304 | tf_op jit(solution)/shard_map/all_to_all | solution.py:181
  210.0 176.3 %reduce-scatter.9.cloned.1.call-start = ((), (), s32[]{:S(2)}) async-start(), calls=%async_computation.12 | async-start | bytes 8912896 | tf_op jit(solution)/shard_map/reduce_scatter | solution.py:106
  255.8 3.2 copy-start.16
  258.9 4.9 copy-start.12
  258.9 4.9 copy-start.24
  263.8 1.0 copy-start.22
  264.2 6.7 %copy-start.13 = (bf16[256,1024]{1,0:T(8,128)(2,1)}, bf16[256,1024]{1,0:T(8,128)(2,1)S(1)}, u32[]{:S(2)}) copy-start(bf16[256,1024]{1,0:T(8,128)(2,1)S(1)} %get-tuple-element.11) | copy-start | bytes 1572868
  275.3 19.3 %copy-start.10 = (bf16[128,8,4,64]{0,3,2,1:T(8,128)(2,1)S(1)}, bf16[128,8,4,64]{0,3,2,1:T(8,128)(2,1)}, u32[]{:S(2)}) copy-start(bf16[128,8,4,64]{0,3,2,1:T(8,128)(2,1)} %copy-done.9) | copy-start | bytes 1572868
  295.1 4.0 copy-start.21
  302.9 2.5 copy-start.25
  302.9 2.5 copy-start.26
  314.7 4.6 copy-start.2
  314.7 33.0 %all-to-all-start.5 = ((bf16[16,2,24576]{2,1,0:T(2,128)(2,1)}), bf16[16,2,24576]{2,1,0:T(2,128)(2,1)}, u32[]{:S(2)}, u32[]{:S(2)}) async-start(bf16[16,2,24576]{2,1,0:T(2,128)(2,1)} %reshape.223), calls=%async_computation.5 | async-start | bytes 3145728 | tf_op jit(solution)/shard_map/all_to_all | solution.py:90
  319.2 172.7 %reduce-scatter.5.cloned.1.call-start = ((), (), s32[]{:S(2)}) async-start(), calls=%async_computation.10 | async-start | bytes 8912896 | tf_op jit(solution)/shard_map/reduce_scatter | solution.py:106
  319.4 1.2 copy-start.1
  365.4 126.6 %copy-start.5 = (f32[256,1024]{1,0:T(8,128)S(1)}, f32[256,1024]{1,0:T(8,128)}, u32[]{:S(2)}) copy-start(f32[256,1024]{1,0:T(8,128)} %copy-done.3) | copy-start | bytes 3145732
  365.4 126.6 %copy-start.15 = (bf16[3,256,1024]{2,1,0:T(8,128)(2,1)S(1)}, bf16[3,256,1024]{2,1,0:T(8,128)(2,1)}, u32[]{:S(2)}) copy-start(bf16[3,256,1024]{2,1,0:T(8,128)(2,1)} %reshape.205) | copy-start | bytes 4718596
  365.5 166.2 %reduce-scatter.11.cloned.1.call-start = ((), (), s32[]{:S(2)}) async-start(), calls=%async_computation.13 | async-start | bytes 589824 | tf_op jit(solution)/shard_map/reduce_scatter | solution.py:112
  386.3 184.6 %reduce-scatter.7.cloned.1.call-start = ((), (), s32[]{:S(2)}) async-start(), calls=%async_computation.11 | async-start | bytes 589824 | tf_op jit(solution)/shard_map/reduce_scatter | solution.py:112
  492.0 4.8 copy-start.14
Sparse Core Ops, SparseCore 0:
  271.0 115.2 reduce-scatter.8
  390.6 101.3 reduce-scatter.4
  494.4 37.2 reduce-scatter.10
  534.0 36.8 reduce-scatter.6
where the time goes:
time: 586 us; the launch traced here: 580 us
  waiting for transfers between devices  278 us (47%)
  local copies, waits for them, and re-layouts  128 us (22%)
  matrix products  76.6 us (13%)
  blocking collectives  49.6 us (8%)
  starting transfers between devices  20.4 us (3%)
  between operations  15 us (3%)
  other arithmetic  12.6 us (2%)
    reduce_scatter x2, waiting for transfers between devices, reduce_grads(): lax.psum_scatter(compute(jnp.int32(0), share_rows * lax.axis_size('agent'...  126 us
    reduce_scatter x2, waiting for transfers between devices, reduce_grads(): lax.psum_scatter(partial_rows, 'mode', scatter_dimension=0, tiled=True)  71.3 us
    unnamed x70, local copies, waits for them, and re-layouts  49.9 us
    all_to_all x2, waiting for transfers between devices, collect_agents(): lax.all_to_all(stacked, 'agent', split_axis=1, concat_axis=4, tiled=True)  32.2 us
    all_to_all x1, blocking collectives, local(): lax.all_to_all(outgoing_two, 'mode', split_axis=4, concat_axis=2, tiled=T...  32.1 us
    all_to_all x1, waiting for transfers between devices, local(): lax.all_to_all(returning_two, 'mode', split_axis=2, concat_axis=4, tiled=...  24.1 us
    all_to_all x1, waiting for transfers between devices, spread_agents(): lax.all_to_all(stacked, 'agent', split_axis=4, concat_axis=1, tiled=True)  23.6 us
    all_to_all x1, blocking collectives, spread_agents(): lax.all_to_all(stacked, 'agent', split_axis=4, concat_axis=1, tiled=True)  17.5 us
  transfers between devices with their start and end apart: 8, of which 8 were waited for; matrix products, arithmetic and copies ran while one was open for 10% of the time, Pallas kernels for 0%

commit v1 on v0

v1 whole, which is shorter than its diff:
```python
import functools

import jax
import jax.numpy as jnp
from jax import lax
from jax.experimental import pallas as pl
from jax.experimental.pallas import tpu as pltpu
from jax.sharding import PartitionSpec as P

epsilon = 1e-06
masked_score = -1000000000.0

BF = jnp.bfloat16
F32 = jnp.float32
D = 1024
ROWS = 256
SCALE = 0.125
MIB = 1024 * 1024


def decode(row, order):
    if order == "o":
        return row >> 5, (row >> 2) & 7, row & 3
    if order == "a":
        return row & 7, row >> 5, (row >> 3) & 3
    return (row >> 3) & 7, row & 7, row >> 6


def encode(agent, mode, step, order):
    if order == "o":
        return agent * 32 + mode * 4 + step
    if order == "a":
        return mode * 32 + step * 8 + agent
    return step * 64 + agent * 8 + mode


def reorder(values, source, target):
    rows = lax.broadcasted_iota(jnp.int32, (ROWS, ROWS), 0)
    columns = lax.broadcasted_iota(jnp.int32, (ROWS, ROWS), 1)
    chosen = encode(*decode(rows, target), source)
    table = (chosen == columns).astype(F32).astype(BF)
    return jnp.dot(table, values, preferred_element_type=F32).astype(BF)


def dot_nt(left, right):
    return lax.dot_general(left, right, (((1,), (1,)), ((), ())), preferred_element_type=F32)


def dot_tn(left, right):
    return lax.dot_general(left, right, (((0,), (0,)), ((), ())), preferred_element_type=F32)


def factor_of(wide):
    return lax.rsqrt(jnp.mean(wide * wide, -1, keepdims=True) + epsilon)


def normalize_back(values, upstream):
    wide = values.astype(F32)
    factor = factor_of(wide)
    normed = wide * factor
    return factor * (upstream - normed * jnp.mean(upstream * normed, -1, keepdims=True))


def params(limit=32):
    return pltpu.CompilerParams(vmem_limit_bytes=limit * MIB)


def cost(flops, read):
    return pl.CostEstimate(flops=int(flops), bytes_accessed=int(read), transcendentals=0)


def fixed(shape):
    return pl.BlockSpec(shape, lambda *i: (0,) * len(shape))


def stack_heads(values):
    lanes = lax.broadcasted_iota(jnp.int32, (1, 128), 1)
    first = (lanes < 64).astype(F32).astype(BF)
    second = (lanes >= 64).astype(F32).astype(BF)
    return jnp.concatenate([values * first, values * second], 0)


def beside(table):
    return jnp.concatenate([table[:128], table[128:]], 1)


def probabilities(query_stack, keys, offset):
    scores = dot_nt(query_stack, keys) * SCALE + offset
    raised = jnp.exp(scores - jnp.max(scores, -1, keepdims=True))
    return raised / jnp.sum(raised, -1, keepdims=True)


def attend(table, values):
    return jnp.dot(beside(table.astype(BF)), stack_heads(values), preferred_element_type=F32)


def attention_back(table, query_stack, keys, values, upstream):
    upstream_stack = stack_heads(upstream)
    through = dot_nt(upstream_stack, values)
    value_grad = dot_tn(table.astype(BF), upstream_stack)
    centre = jnp.sum(through * table, -1, keepdims=True)
    score_grad = (table * (through - centre) * SCALE).astype(BF)
    query_grad = jnp.dot(beside(score_grad), stack_heads(keys), preferred_element_type=F32)
    keys_grad = dot_tn(score_grad, query_stack)
    return query_grad, keys_grad, value_grad


def enter_kernel(tokens_ref, weights_ref, send_ref, tokens_out_ref, hidden_out_ref, hidden_ref):
    step = pl.program_id(0)

    @pl.when(step == 0)
    def _():
        rows = reorder(tokens_ref[...], "o", "a")
        tokens_out_ref[...] = rows
        wide = rows.astype(F32)
        hidden = (wide * factor_of(wide)).astype(BF)
        hidden_ref[...] = hidden
        for block in range(8):
            hidden_out_ref[block] = hidden[:, 128 * block : 128 * block + 128]

    result = jnp.dot(hidden_ref[...], weights_ref[0], preferred_element_type=F32).astype(BF)
    for pair in range(8):
        for half in range(2):
            send_ref[2 * pair + half] = result[
                128 * half : 128 * half + 128, 128 * pair : 128 * pair + 128
            ]


def enter(tokens, weights):
    return pl.pallas_call(
        enter_kernel,
        grid=(3,),
        in_specs=[fixed((ROWS, D)), pl.BlockSpec((1, D, D), lambda i: (i, 0, 0))],
        out_specs=[
            pl.BlockSpec((16, 128, 128), lambda i: (0, i, 0)),
            fixed((ROWS, D)),
            fixed((8, ROWS, 128)),
        ],
        out_shape=[
            jax.ShapeDtypeStruct((16, 384, 128), BF),
            jax.ShapeDtypeStruct((ROWS, D), BF),
            jax.ShapeDtypeStruct((8, ROWS, 128), BF),
        ],
        scratch_shapes=[pltpu.VMEM((ROWS, D), BF)],
        compiler_params=params(),
        cost_estimate=cost(3 * 2 * ROWS * D * D, 8 * MIB),
        name="enter",
    )(tokens, weights)


def agent_rows(block, step):
    return block[:, 8 * step : 8 * step + 8, :].reshape(128, 128).astype(BF)


def agent_forward_kernel(query_ref, keys_ref, values_ref, offset_ref, out_ref, table_ref):
    query = query_ref[...].astype(F32)
    keys = keys_ref[...].astype(F32)
    values = values_ref[...].astype(F32)
    offset = offset_ref[...]
    outs = []
    for step in range(4):
        table = probabilities(
            stack_heads(agent_rows(query, step)), agent_rows(keys, step), offset
        )
        table_ref[0, step] = table
        outs.append(attend(table, agent_rows(values, step)).reshape(16, 8, 128))
    out_ref[...] = jnp.concatenate(outs, 1).astype(BF)


def agent_specs():
    return [pl.BlockSpec((16, 32, 128), lambda i, k=k: (0, 4 * k + i, 0)) for k in range(3)]


def agent_forward(arrived, offset):
    return pl.pallas_call(
        agent_forward_kernel,
        grid=(4,),
        in_specs=agent_specs() + [fixed((1, 128))],
        out_specs=[
            pl.BlockSpec((16, 32, 128), lambda i: (0, i, 0)),
            pl.BlockSpec((1, 4, 256, 128), lambda i: (i, 0, 0, 0)),
        ],
        out_shape=[
            jax.ShapeDtypeStruct((16, 128, 128), BF),
            jax.ShapeDtypeStruct((4, 4, 256, 128), F32),
        ],
        compiler_params=params(),
        cost_estimate=cost(3e9, 4 * MIB),
        name="agent_forward",
    )(arrived, arrived, arrived, offset)


def agent_backward_kernel(
    query_ref, keys_ref, values_ref, upstream_ref, table_ref, query_out, keys_out, values_out
):
    query = query_ref[...].astype(F32)
    keys = keys_ref[...].astype(F32)
    values = values_ref[...].astype(F32)
    upstream = upstream_ref[...].astype(F32)
    outs = [[], [], []]
    for step in range(4):
        grads = attention_back(
            table_ref[0, step],
            stack_heads(agent_rows(query, step)),
            agent_rows(keys, step),
            agent_rows(values, step),
            agent_rows(upstream, step),
        )
        for kept, grad in zip(outs, grads):
            kept.append(grad.reshape(16, 8, 128))
    for ref, kept in zip((query_out, keys_out, values_out), outs):
        ref[...] = jnp.concatenate(kept, 1).astype(BF)


def agent_backward_all_kernel(q, k, v, g, table_ref, out_ref):
    agent_backward_kernel(
        q,
        k,
        v,
        g,
        table_ref,
        out_ref.at[:, 0],
        out_ref.at[:, 1],
        out_ref.at[:, 2],
    )


def agent_backward(arrived, upstream, tables):
    return pl.pallas_call(
        agent_backward_all_kernel,
        grid=(4,),
        in_specs=agent_specs()
        + [
            pl.BlockSpec((16, 32, 128), lambda i: (0, i, 0)),
            pl.BlockSpec((1, 4, 256, 128), lambda i: (i, 0, 0, 0)),
        ],
        out_specs=pl.BlockSpec((16, 3, 32, 128), lambda i: (0, 0, i, 0)),
        out_shape=jax.ShapeDtypeStruct((16, 3, 128, 128), BF),
        compiler_params=params(),
        cost_estimate=cost(6e9, 6 * MIB),
        name="agent_backward",
    )(arrived, arrived, arrived, upstream, tables)


def middle_kernel(
    tokens_ref, mixed_ref, cotangent_ref, weights_ref,
    send_ref, after_ref, hidden_out_ref, cotangent_out_ref, hidden_ref,
):
    step = pl.program_id(0)

    @pl.when(step == 0)
    def _():
        mixed = jnp.concatenate([mixed_ref[pair] for pair in range(8)], 1)
        after = (
            tokens_ref[...].astype(F32)
            + jnp.dot(mixed, weights_ref[0], preferred_element_type=F32)
        ).astype(BF)
        after = reorder(after, "a", "m")
        after_ref[...] = after
        wide = after.astype(F32)
        hidden = (wide * factor_of(wide)).astype(BF)
        hidden_ref[...] = hidden
        for block in range(8):
            hidden_out_ref[block] = hidden[:, 128 * block : 128 * block + 128]
        cotangent_out_ref[...] = reorder(cotangent_ref[...], "o", "m")

    def send(result):
        result = result.astype(BF)
        for pair in range(8):
            send_ref[pair, 0] = result[:, 128 * pair : 128 * pair + 128]

    @pl.when((step > 0) & (step < 4))
    def _():
        send(jnp.dot(hidden_ref[...], weights_ref[0], preferred_element_type=F32))

    @pl.when(step == 4)
    def _():
        send(dot_nt(cotangent_out_ref[...], weights_ref[0]))


def middle(tokens, mixed, cotangent, weights):
    return pl.pallas_call(
        middle_kernel,
        grid=(5,),
        in_specs=[
            fixed((ROWS, D)),
            fixed((8, ROWS, 128)),
            fixed((ROWS, D)),
            pl.BlockSpec((1, D, D), lambda i: (3 + i, 0, 0)),
        ],
        out_specs=[
            pl.BlockSpec((8, 1, ROWS, 128), lambda i: (0, jnp.maximum(i - 1, 0), 0, 0)),
            fixed((ROWS, D)),
            fixed((8, ROWS, 128)),
            fixed((ROWS, D)),
        ],
        out_shape=[
            jax.ShapeDtypeStruct((8, 4, ROWS, 128), BF),
            jax.ShapeDtypeStruct((ROWS, D), BF),
            jax.ShapeDtypeStruct((8, ROWS, 128), BF),
            jax.ShapeDtypeStruct((ROWS, D), BF),
        ],
        scratch_shapes=[pltpu.VMEM((ROWS, D), BF)],
        compiler_params=params(),
        cost_estimate=cost(5 * 2 * ROWS * D * D, 13 * MIB),
        name="middle",
    )(tokens, mixed, cotangent, weights)


def mode_kernel(arrived_ref, out_ref):
    rows = lax.broadcasted_iota(jnp.int32, (256, 128), 0)
    columns = lax.broadcasted_iota(jnp.int32, (256, 128), 1)
    same = ((rows >> 6) & 1) == (columns >> 6)
    offset = jnp.where(same, 0.0, -1e30).astype(F32)
    for pair in range(4):

        def take(which):
            block = arrived_ref[:, which, 16 * pair : 16 * pair + 16, :].astype(F32)
            parts = [block[:, 8 * n : 8 * n + 8, :].reshape(64, 128) for n in range(2)]
            return jnp.concatenate(parts, 0).astype(BF)

        query, keys, values, upstream = (take(which) for which in range(4))
        query_stack = stack_heads(query)
        table = probabilities(query_stack, keys, offset)
        results = (attend(table, values),) + attention_back(
            table, query_stack, keys, values, upstream
        )
        for which, result in enumerate(results):
            parts = [result[64 * n : 64 * n + 64].reshape(8, 8, 128) for n in range(2)]
            out_ref[:, which, 16 * pair : 16 * pair + 16, :] = jnp.concatenate(parts, 1).astype(BF)


def mode_attention(arrived):
    spec = pl.BlockSpec((8, 4, 64, 128), lambda i: (0, 0, i, 0))
    return pl.pallas_call(
        mode_kernel,
        grid=(4,),
        in_specs=[spec],
        out_specs=spec,
        out_shape=jax.ShapeDtypeStruct((8, 4, ROWS, 128), BF),
        compiler_params=params(),
        cost_estimate=cost(8e9, 4 * MIB),
        name="mode_attention",
    )(arrived)


def turn_kernel(
    returned_ref, cotangent_ref, after_ref, weights_ref, send_ref, grad_after_ref, total_ref
):
    step = pl.program_id(0)

    @pl.when(step < 3)
    def _():
        grads = jnp.concatenate([returned_ref[pair, 0] for pair in range(8)], 1)
        product = dot_nt(grads, weights_ref[0])

        @pl.when(step == 0)
        def _():
            total_ref[...] = product

        @pl.when(step > 0)
        def _():
            total_ref[...] += product

    @pl.when(step == 3)
    def _():
        grad_after = (
            cotangent_ref[...].astype(F32) + normalize_back(after_ref[...], total_ref[...])
        ).astype(BF)
        grad_after = reorder(grad_after, "m", "a")
        grad_after_ref[...] = grad_after
        result = dot_nt(grad_after, weights_ref[0]).astype(BF)
        for pair in range(8):
            for half in range(2):
                send_ref[2 * pair + half] = result[
                    128 * half : 128 * half + 128, 128 * pair : 128 * pair + 128
                ]


def turn(returned, cotangent, after, weights):
    return pl.pallas_call(
        turn_kernel,
        grid=(4,),
        in_specs=[
            pl.BlockSpec((8, 1, ROWS, 128), lambda i: (0, jnp.minimum(i + 1, 3), 0, 0)),
            fixed((ROWS, D)),
            fixed((ROWS, D)),
            pl.BlockSpec((1, D, D), lambda i: (jnp.where(i < 3, i + 4, 3), 0, 0)),
        ],
        out_specs=[fixed((16, 128, 128)), fixed((ROWS, D))],
        out_shape=[
            jax.ShapeDtypeStruct((16, 128, 128), BF),
            jax.ShapeDtypeStruct((ROWS, D), BF),
        ],
        scratch_shapes=[pltpu.VMEM((ROWS, D), F32)],
        compiler_params=params(),
        cost_estimate=cost(4 * 2 * ROWS * D * D, 12 * MIB),
        name="turn",
    )(returned, cotangent, after, weights)


def whole_rows(ref):
    return jnp.concatenate([ref[:, 0].reshape(8, ROWS, 128)[pair] for pair in range(8)], 1)


def leave_kernel(returned_ref, tokens_ref, grad_after_ref, weights_ref, out_ref, total_ref):
    step = pl.program_id(0)
    product = dot_nt(whole_rows(returned_ref), weights_ref[0])

    @pl.when(step == 0)
    def _():
        total_ref[...] = product

    @pl.when(step > 0)
    def _():
        total_ref[...] += product

    @pl.when(step == 2)
    def _():
        grads = (
            grad_after_ref[...].astype(F32) + normalize_back(tokens_ref[...], total_ref[...])
        ).astype(BF)
        out_ref[...] = reorder(grads, "a", "o")


def leave(returned, tokens, grad_after, weights):
    return pl.pallas_call(
        leave_kernel,
        grid=(3,),
        in_specs=[
            pl.BlockSpec((16, 1, 128, 128), lambda i: (0, i, 0, 0)),
            fixed((ROWS, D)),
            fixed((ROWS, D)),
            pl.BlockSpec((1, D, D), lambda i: (i, 0, 0)),
        ],
        out_specs=fixed((ROWS, D)),
        out_shape=jax.ShapeDtypeStruct((ROWS, D), BF),
        scratch_shapes=[pltpu.VMEM((ROWS, D), F32)],
        compiler_params=params(),
        cost_estimate=cost(3 * 2 * ROWS * D * D, 9 * MIB),
        name="leave",
    )(returned, tokens, grad_after, weights)


def weight_kernel(of_agents, add, core_ref, hidden_ref, mixed_ref, grads_ref, last_ref, *rest):
    step = pl.program_id(0)
    if add:
        arrived_ref, out_ref = rest
    else:
        (out_ref,) = rest

    def finish(left_ref, right):
        left = jnp.concatenate([left_ref[0], left_ref[1]], 1)
        product = dot_tn(left, right)
        if add:
            total = product + arrived_ref[0].astype(F32)
            out_ref[...] = total.astype(BF).reshape(8, 1, 32, D)
        else:
            out_ref[0] = product.astype(BF)

    @pl.when(step < 6)
    def _():
        if of_agents:
            right = whole_rows(grads_ref)
        else:
            right = jnp.concatenate([grads_ref[pair, 0] for pair in range(8)], 1)
        finish(hidden_ref, right)

    @pl.when(step >= 6)
    def _():
        finish(mixed_ref.at[:, 0] if not of_agents else mixed_ref, last_ref[...])


def weight_products(of_agents, core, hidden, mixed, grads, last, arrived=None):
    add = arrived is not None

    def feature(i, core_ref):
        return 2 * (i % 2) + core_ref[0]

    if of_agents:
        mixed_spec = pl.BlockSpec((2, ROWS, 128), lambda i, c: (feature(i, c), 0, 0))
        grads_spec = pl.BlockSpec(
            (16, 1, 128, 128), lambda i, c: (0, jnp.minimum(i // 2, 2), 0, 0)
        )
    else:
        mixed_spec = pl.BlockSpec((2, 1, ROWS, 128), lambda i, c: (feature(i, c), 0, 0, 0))
        grads_spec = pl.BlockSpec(
            (8, 1, ROWS, 128), lambda i, c: (0, jnp.minimum(i // 2, 2) + 1, 0, 0)
        )
    in_specs = [
        pl.BlockSpec((2, ROWS, 128), lambda i, c: (feature(i, c), 0, 0)),
        mixed_spec,
        grads_spec,
        pl.BlockSpec((ROWS, D), lambda i, c: (0, 0)),
    ]
    operands = [core, hidden, mixed, grads, last]
    if add:
        in_specs.append(pl.BlockSpec((1, ROWS, D), lambda i, c: (i, 0, 0)))
        operands.append(arrived)
        out_spec = pl.BlockSpec((8, 1, 32, D), lambda i, c: (0, i, 0, 0))
        out_shape = jax.ShapeDtypeStruct((8, 8, 32, D), BF)
    else:
        out_spec = pl.BlockSpec((1, ROWS, D), lambda i, c: (i, 0, 0))
        out_shape = jax.ShapeDtypeStruct((8, ROWS, D), BF)
    return pl.pallas_call(
        functools.partial(weight_kernel, of_agents, add),
        grid_spec=pltpu.PrefetchScalarGridSpec(
            num_scalar_prefetch=1, grid=(8,), in_specs=in_specs, out_specs=out_spec
        ),
        out_shape=out_shape,
        compiler_params=params(),
        cost_estimate=cost(4 * 2 * ROWS * D * D // 2, 8 * MIB),
        name="weights_add" if add else "weights_first",
    )(*operands)


def swap_cores(values, axis_size):
    return lax.ppermute(values, "agent", [(n, n ^ 1) for n in range(axis_size)])


def exchange(values, axis):
    return lax.all_to_all(values, axis, split_axis=0, concat_axis=0, tiled=True)


def reduce_grads(of_agents, hidden, mixed, grads, last):
    agent_size = lax.axis_size("agent")
    core = (lax.axis_index("agent") % 2).astype(jnp.int32).reshape(1)
    theirs = weight_products(of_agents, 1 - core, hidden, mixed, grads, last)
    arrived = swap_cores(theirs, agent_size)
    mine = weight_products(of_agents, core, hidden, mixed, grads, last, arrived)
    over_modes = exchange(mine.reshape(8, 256, D), "mode").reshape(8, 256, D)
    partial = jnp.sum(over_modes.astype(F32), 0).astype(BF).reshape(8, 32, D)
    groups = [list(range(c, agent_size, 2)) for c in range(2)]
    over_agents = lax.all_to_all(
        partial, "agent", split_axis=0, concat_axis=0, tiled=True, axis_index_groups=groups
    )
    return jnp.sum(over_agents.astype(F32), 0)


def local(tokens, cotangent, weights, agent_mask):
    token_rows = tokens.reshape(ROWS, D)
    grad_rows = cotangent.reshape(ROWS, D)
    offset = jnp.where(agent_mask == 1, 0.0, masked_score).astype(F32).reshape(1, 128)

    outgoing, tokens_a, hidden_one = enter(token_rows, weights)
    arrived_one = exchange(outgoing, "agent")
    mixed, tables = agent_forward(arrived_one, offset)
    mixed_one = exchange(mixed, "agent").reshape(8, ROWS, 128)
    outgoing, after, hidden_two, cotangent_m = middle(tokens_a, mixed_one, grad_rows, weights)
    arrived_two = exchange(outgoing.reshape(8, 1024, 128), "mode").reshape(8, 4, ROWS, 128)
    returning = mode_attention(arrived_two)
    returned_two = exchange(returning.reshape(8, 1024, 128), "mode").reshape(8, 4, ROWS, 128)
    outgoing, grad_after = turn(returned_two, cotangent_m, after, weights)
    upstream = exchange(outgoing, "agent")
    returning = agent_backward(arrived_one, upstream, tables)
    returned_one = exchange(returning.reshape(16, 384, 128), "agent").reshape(16, 3, 128, 128)
    token_grads = leave(returned_one, tokens_a, grad_after, weights)
    mode_weight_grads = reduce_grads(False, hidden_two, returned_two, returned_two, cotangent_m)
    agent_weight_grads = reduce_grads(True, hidden_one, mixed_one, returned_one, grad_after)
    return (token_grads.reshape(tokens.shape), agent_weight_grads, mode_weight_grads)


def solution(mesh):
    placed = (P("agent", "mode", None, None), P("agent", "mode", None, None), P(), P())
    return jax.shard_map(
        local,
        mesh=mesh,
        in_specs=placed,
        out_specs=(
            P("agent", "mode", None, None),
            P(("agent", "mode"), None),
            P(("agent", "mode"), None),
        ),
        check_vma=False,
    )
```

time: 586 us -> 365 us (0.62)
  waiting for transfers between devices: 278 us -> 155 us
  local copies, waits for them, and re-layouts: 128 us -> 38.4 us
  matrix products: 76.6 us -> 0 us
  Pallas kernels: 0 us -> 50.6 us
  blocking collectives: 49.6 us -> 75 us
  between operations: 15 us -> 0.99 us
  starting transfers between devices: 20.4 us -> 31.9 us
    reduce_scatter x4 -> x0, waiting for transfers between devices: 198 us -> none  [the longest x2 126 us: reduce_grads(): lax.psum_scatter(compute(jnp.int32(0), share_rows * lax.axis_size('agent'...]
    all_to_all x4 -> x7, waiting for transfers between devices: 79.9 us -> 155 us  [the longest x5 149 us: exchange(): return lax.all_to_all(values, axis, split_axis=0, concat_axis=0, tiled=True)]
    dot_general x19 -> x0, matrix products: 71 us -> none  [the longest x2 13.8 us: compute(): jnp.einsum('ktr,ktc->krc', lefts, rights, preferred_element_type=jnp.floa...]
    pallas_call x0 -> x11, Pallas kernels: none -> 50.6 us  [the longest x4 18 us: weight_products(): pl.pallas_call(functools.partial(weight_kernel, of_agents, add), grid_spe...]
    another operation x12 -> x0, local copies, waits for them, and re-layouts: 27.2 us -> none  [the longest x1 11.8 us: local(): jnp.stack([mixed_two, query_grad_two, keys_grad_two, value_grad_two])]
    all_to_all x2 -> x3, blocking collectives: 49.6 us -> 75 us  [exchange(): return lax.all_to_all(values, axis, split_axis=0, concat_axis=0, tiled=True)]
    reshape x8 -> x2, local copies, waits for them, and re-layouts: 18.6 us -> 1.28 us  [the longest x1 1.16 us: local(): token_rows = tokens.reshape(ROWS, D)]
    all_to_all x7 -> x0, local copies, waits for them, and re-layouts: 14.5 us -> none  [the longest x1 7.05 us: local(): lax.all_to_all(returning_two, 'mode', split_axis=2, concat_axis=4, tiled=...]
  transfers between devices with their start and end apart: 8 -> 9, of which waited for: 8 -> 6; matrix products, arithmetic and copies ran while one was open for 10% -> 3% of each run, Pallas kernels for 0% -> 8%
where the time goes in v1:
time: 365 us; the launch traced here: 363 us
  waiting for transfers between devices  155 us (42%)
  blocking collectives  75 us (21%)
  Pallas kernels  50.6 us (14%)
  local copies, waits for them, and re-layouts  38.4 us (11%)
  starting transfers between devices  31.9 us (9%)
  other arithmetic  11.6 us (3%)
    all_to_all x5, waiting for transfers between devices, exchange(): return lax.all_to_all(values, axis, split_axis=0, concat_axis=0, tiled=True)  149 us
    all_to_all x3, blocking collectives, exchange(): return lax.all_to_all(values, axis, split_axis=0, concat_axis=0, tiled=True)  75 us
    unnamed x58, local copies, waits for them, and re-layouts  36.2 us
    all_to_all x5, starting transfers between devices, exchange(): return lax.all_to_all(values, axis, split_axis=0, concat_axis=0, tiled=True)  24.2 us
    pallas_call x4, Pallas kernels, weight_products(): pl.pallas_call(functools.partial(weight_kernel, of_agents, add), grid_spe...  18 us
    pallas_call x1, Pallas kernels, mode_attention(): pl.pallas_call(mode_kernel, grid=(4,), in_specs=[spec], out_specs=spec, o...  8.67 us
    reduce_sum x2, other arithmetic, reduce_grads(): partial = jnp.sum(over_modes.astype(F32), 0).astype(BF).reshape(8, 32, D)  8 us
    all_to_all x2, starting transfers between devices, reduce_grads(): lax.all_to_all(partial, 'agent', split_axis=0, concat_axis=0, tiled=True,...  7.64 us
  transfers between devices with their start and end apart: 9, of which 6 were waited for; matrix products, arithmetic and copies ran while one was open for 3% of the time, Pallas kernels for 8%

profile of v1, /device:TPU:0, one launch (start us, length us, event | category | flops | bytes accessed | tf_op | source)
XLA Modules:
  0.0 363.2 jit_solution(4942179553037760773)
XLA Ops:
  0.6 1.2 reshape.55.tokens_ref
  1.8 5.8 %copy-done = bf16[8,1024,1024]{2,1,0:T(8,128)(2,1)S(1)} copy-done((bf16[8,1024,1024]{2,1,0:T(8,128)(2,1)S(1)}, bf16[8,1024,1024]{2,1,0:T(8,128)(2,1)}, u32[]{:S(2)}) %copy-start) | copy-done | bytes 16777240
  7.6 2.7 enter.1
  10.3 0.8 copy-done.13
  11.1 1.2 copy-done.21
  12.3 7.1 %all-to-all-start = ((bf16[16,384,128]{2,1,0:T(8,128)(2,1)}), bf16[16,384,128]{2,1,0:T(8,128)(2,1)S(1)}, u32[]{:S(2)}, u32[]{:S(2)}) async-start(bf16[16,384,128]{2,1,0:T(8,128)(2,1)} %copy-done.21), calls=%async_computation | async-start | bytes 3145728 | tf_op jit(solution)/shard_map/all_to_all | solution.py:522
  19.5 23.6 %all-to-all-done.query_ref.keys_ref.values_ref.q.k.v = bf16[16,384,128]{2,1,0:T(8,128)(2,1)S(1)} async-done(((bf16[16,384,128]{2,1,0:T(8,128)(2,1)}), bf16[16,384,128]{2,1,0:T(8,128)(2,1)S(1)}, u32[]{:S(2)}, u32[]{:S(2)}) %all-to-all-start) | async-done | bytes 1572896 | tf_op jit(solution)/shard_map/all_to_all | solution.py:522
  43.0 4.5 %agent_forward.1 = (bf16[16,128,128]{2,1,0:T(8,128)(2,1)}, f32[4,4,256,128]{3,2,1,0:T(8,128)S(1)}) custom-call(bf16[16,384,128]{2,1,0:T(8,128)(2,1)S(1)} %all-to-all-done.query_ref.keys_ref.values_ref.q.k.v, bf16[16,384,128]{2,1,0:T(8,128)(2,1)S(1)} %all-to-all-done.query_ref.keys_ref.values_ref.q.k.v, ...), custom_call_target="tpu_custom_call" | custom-call | flops 3000000000 | bytes 4194304 | tf_op jit(solution)/shard_map/agent_forward/pallas_call | solution.py:175
  47.6 1.4 copy-done.24
  48.9 4.0 %all-to-all-start.1 = ((bf16[16,128,128]{2,1,0:T(8,128)(2,1)}), bf16[16,128,128]{2,1,0:T(8,128)(2,1)S(1)}, u32[]{:S(2)}, u32[]{:S(2)}) async-start(bf16[16,128,128]{2,1,0:T(8,128)(2,1)} %get-tuple-element.16), calls=%async_computation.1 | async-start | bytes 1048576 | tf_op jit(solution)/shard_map/all_to_all | solution.py:522
  53.0 0.1 reshape.58.cotangent_ref
  53.1 12.2 %all-to-all-done.1 = bf16[16,128,128]{2,1,0:T(8,128)(2,1)S(1)} async-done(((bf16[16,128,128]{2,1,0:T(8,128)(2,1)}), bf16[16,128,128]{2,1,0:T(8,128)(2,1)S(1)}, u32[]{:S(2)}, u32[]{:S(2)}) %all-to-all-start.1) | async-done | bytes 524320 | tf_op jit(solution)/shard_map/all_to_all | solution.py:522
  65.3 5.8 %copy-done.1 = bf16[8,1024,1024]{2,1,0:T(8,128)(2,1)S(1)} copy-done((bf16[8,1024,1024]{2,1,0:T(8,128)(2,1)S(1)}, bf16[8,1024,1024]{2,1,0:T(8,128)(2,1)}, u32[]{:S(2)}) %copy-start.1) | copy-done | bytes 16777240
  71.1 4.3 %middle.1 = (bf16[8,4,256,128]{3,2,1,0:T(8,128)(2,1)S(1)}, bf16[256,1024]{1,0:T(8,128)(2,1)S(1)}, bf16[8,256,128]{2,1,0:T(8,128)(2,1)S(1)}, bf16[256,1024]{1,0:T(8,128)(2,1)S(1)}) custom-call(bf16[256,1024]{1,0:T(8,128)(2,1)S(1)} %get-tuple-element.15.tokens_ref, bf16[8,256,128]{2,1,0:T(8,128)(2,1)S(1)} %bitcast.24, ...), custom_call_target="tpu_custom_call" | custom-call | flops 2684354560 | bytes 13631488 | tf_op jit(solution)/shard_map/middle/pallas_call | solution.py:282
  75.4 31.5 %all_to_all.50 = bf16[8,1024,128]{2,1,0:T(8,128)(2,1)S(1)} all-to-all(bf16[8,1024,128]{2,1,0:T(8,128)(2,1)S(1)} %bitcast.28), channel_id=1, replica_groups=mesh['agent'=16,'mode'=8] {'mode'}, dimensions={0} | all-to-all | bytes 4194304 | tf_op jit(solution)/shard_map/all_to_all | solution.py:522
  106.9 8.7 %mode_attention.1 = bf16[8,4,256,128]{3,2,1,0:T(8,128)(2,1)S(1)} custom-call(bf16[8,4,256,128]{3,2,1,0:T(8,128)(2,1)S(1)} %bitcast.29), custom_call_target="tpu_custom_call" | custom-call | flops 8000000000 | bytes 4194304 | tf_op jit(solution)/shard_map/mode_attention/pallas_call | solution.py:335
  115.6 1.3 copy-done.12
  116.9 3.6 all-to-all-start.3
  120.6 25.3 %all-to-all-done.3 = bf16[8,1024,128]{2,1,0:T(8,128)(2,1)S(1)} async-done(((bf16[8,1024,128]{2,1,0:T(8,128)(2,1)}), bf16[8,1024,128]{2,1,0:T(8,128)(2,1)S(1)}, u32[]{:S(2)}, u32[]{:S(2)}) %all-to-all-start.3) | async-done | bytes 2097184 | tf_op jit(solution)/shard_map/all_to_all | solution.py:522
  145.9 1.0 copy-done.17
  146.9 3.1 weights_first.3
  150.1 5.8 %copy-done.2 = bf16[8,1024,1024]{2,1,0:T(8,128)(2,1)S(1)} copy-done((bf16[8,1024,1024]{2,1,0:T(8,128)(2,1)S(1)}, bf16[8,1024,1024]{2,1,0:T(8,128)(2,1)}, u32[]{:S(2)}) %copy-start.2) | copy-done | bytes 16777240
  155.9 1.0 copy-done.9
  157.0 3.9 %turn.1 = (bf16[16,128,128]{2,1,0:T(8,128)(2,1)S(1)}, bf16[256,1024]{1,0:T(8,128)(2,1)S(1)}) custom-call(bf16[8,4,256,128]{3,2,1,0:T(8,128)(2,1)S(1)} %bitcast.16, bf16[256,1024]{1,0:T(8,128)(2,1)S(1)} %copy-done.9, bf16[256,1024]{1,0:T(8,128)(2,1)S(1)} %copy-done.23, bf16[8,1024,1024]{2,1,0:T(8,128)(2,1)S(1)} %copy-done.2), custom_call_target="tpu_custom_call" | custom-call | flops 2147483648 | bytes 12582912 | tf_op jit(solution)/shard_map/turn/pallas_call | solution.py:381
  160.9 17.2 %all_to_all.51.g = bf16[16,128,128]{2,1,0:T(8,128)(2,1)S(1)} all-to-all(bf16[16,128,128]{2,1,0:T(8,128)(2,1)S(1)} %get-tuple-element.20), channel_id=1, replica_groups=mesh['agent'=16,'mode'=8] {'agent'}, dimensions={0} | all-to-all | bytes 1048576 | tf_op jit(solution)/shard_map/all_to_all | solution.py:522
  178.1 1.6 copy-done.25
  179.7 5.2 %agent_backward.1 = bf16[16,3,128,128]{3,2,1,0:T(8,128)(2,1)S(1)} custom-call(bf16[16,384,128]{2,1,0:T(8,128)(2,1)S(1)} %copy-done.20, bf16[16,384,128]{2,1,0:T(8,128)(2,1)S(1)} %copy-done.20, bf16[16,384,128]{2,1,0:T(8,128)(2,1)S(1)} %copy-done.20, bf16[16,128,128]{2,1,0:T(8,128)(2,1)S(1)} %all_to_all.51.g, f32[4,4,256,128]{3,2,1,0:T(8,128)S(1)} %copy-done.25), custom_call_target="tpu_custom_call" | custom-call | flops 6000000000 | bytes 6291456 | tf_op jit(solution)/shard_map/agent_backward/pallas_call | solution.py:229
  184.9 26.2 %all_to_all.52 = bf16[16,384,128]{2,1,0:T(8,128)(2,1)S(1)} all-to-all(bf16[16,384,128]{2,1,0:T(8,128)(2,1)S(1)} %bitcast.30), channel_id=1, replica_groups=mesh['agent'=16,'mode'=8] {'agent'}, dimensions={0} | all-to-all | bytes 3145728 | tf_op jit(solution)/shard_map/all_to_all | solution.py:522
  211.2 5.0 %weights_first.2 = bf16[8,256,1024]{2,1,0:T(8,128)(2,1)} custom-call(s32[1]{0:T(128)S(6)} %sub.4.core_ref, bf16[8,256,128]{2,1,0:T(8,128)(2,1)S(1)} %copy-done.14, bf16[8,256,128]{2,1,0:T(8,128)(2,1)S(1)} %bitcast.25, bf16[16,3,128,128]{3,2,1,0:T(8,128)(2,1)S(1)} %bitcast.19, bf16[256,1024]{1,0:T(8,128)(2,1)S(1)} %get-tuple-element.22.grad_after_ref.last_ref), custom_call_target="tpu_custom_call" | custom-call | flops 1073741824 | bytes 8388608 | tf_op jit(solution)/shard_map/weights_first/pallas_call | solution.py:505
  216.2 3.5 weights_add.3
  219.7 2.0 copy-done.7
  221.7 4.9 %all-to-all-start.8 = ((bf16[8,256,1024]{2,1,0:T(8,128)(2,1)}), bf16[8,256,1024]{2,1,0:T(8,128)(2,1)}, u32[]{:S(2)}, u32[]{:S(2)}) async-start(bf16[8,256,1024]{2,1,0:T(8,128)(2,1)} %bitcast.23), calls=%async_computation.8 | async-start | bytes 8388608 | tf_op jit(solution)/shard_map/all_to_all | solution.py:522
  226.6 6.3 %weights_add.2 = bf16[8,8,32,1024]{3,2,1,0:T(8,128)(2,1)S(1)} custom-call(s32[1]{0:T(128)} %bitcast.8.core_ref, bf16[8,256,128]{2,1,0:T(8,128)(2,1)S(1)} %copy-done.15, bf16[8,256,128]{2,1,0:T(8,128)(2,1)S(1)} %bitcast.26, bf16[16,3,128,128]{3,2,1,0:T(8,128)(2,1)S(1)} %bitcast.20, bf16[256,1024]{1,0:T(8,128)(2,1)S(1)} %get-tuple-element.22.grad_after_ref.last_ref, ...), custom_call_target="tpu_custom_call" | custom-call | flops 1073741824 | bytes 8388608 | tf_op jit(solution)/shard_map/weights_add/pallas_call | solution.py:505
  232.9 1.9 copy-done.6
  234.9 41.9 %all-to-all-done.8 = bf16[8,256,1024]{2,1,0:T(8,128)(2,1)} async-done(((bf16[8,256,1024]{2,1,0:T(8,128)(2,1)}), bf16[8,256,1024]{2,1,0:T(8,128)(2,1)}, u32[]{:S(2)}, u32[]{:S(2)}) %all-to-all-start.8) | async-done | bytes 4194336 | tf_op jit(solution)/shard_map/all_to_all | solution.py:522
  276.8 4.6 %all-to-all-start.6 = ((bf16[8,256,1024]{2,1,0:T(8,128)(2,1)}), bf16[8,256,1024]{2,1,0:T(8,128)(2,1)}, u32[]{:S(2)}, u32[]{:S(2)}) async-start(bf16[8,256,1024]{2,1,0:T(8,128)(2,1)} %bitcast.22), calls=%async_computation.6 | async-start | bytes 8388608 | tf_op jit(solution)/shard_map/all_to_all | solution.py:522
  281.3 4.0 %reduce_sum.44 = bf16[256,1024]{1,0:T(8,128)(2,1)} reduce(bf16[8,256,1024]{2,1,0:T(8,128)(2,1)} %all-to-all-done.8, bf16[]{:T(256)} %constant.30.clone.1), dimensions={0}, to_apply=%region_2.3 | reduce | flops 1835008 | bytes 4718594 | tf_op jit(solution)/shard_map/reduce_sum | solution.py:532
  285.3 45.6 %all-to-all-done.6 = bf16[8,256,1024]{2,1,0:T(8,128)(2,1)} async-done(((bf16[8,256,1024]{2,1,0:T(8,128)(2,1)}), bf16[8,256,1024]{2,1,0:T(8,128)(2,1)}, u32[]{:S(2)}, u32[]{:S(2)}) %all-to-all-start.6) | async-done | bytes 4194336 | tf_op jit(solution)/shard_map/all_to_all | solution.py:522
  330.9 3.5 all-to-all-start.9
  334.4 4.0 %reduce_sum.42 = bf16[256,1024]{1,0:T(8,128)(2,1)} reduce(bf16[8,256,1024]{2,1,0:T(8,128)(2,1)} %all-to-all-done.6, bf16[]{:T(256)} %constant.30.clone.1), dimensions={0}, to_apply=%region_0.1 | reduce | flops 1835008 | bytes 4718594 | tf_op jit(solution)/shard_map/reduce_sum | solution.py:532
  338.4 6.1 %all-to-all-done.9 = bf16[8,32,1024]{2,1,0:T(8,128)(2,1)S(1)} async-done(((bf16[8,32,1024]{2,1,0:T(8,128)(2,1)}), bf16[8,32,1024]{2,1,0:T(8,128)(2,1)S(1)}, u32[]{:S(2)}, u32[]{:S(2)}) %all-to-all-start.9) | async-done | bytes 524320 | tf_op jit(solution)/shard_map/all_to_all | solution.py:534
  344.6 0.8 copy-done.26
  345.3 4.1 %all-to-all-start.7 = ((bf16[8,32,1024]{2,1,0:T(8,128)(2,1)}), bf16[8,32,1024]{2,1,0:T(8,128)(2,1)}, u32[]{:S(2)}, u32[]{:S(2)}) async-start(bf16[8,32,1024]{2,1,0:T(8,128)(2,1)} %bitcast.10), calls=%async_computation.7 | async-start | bytes 1048576 | tf_op jit(solution)/shard_map/all_to_all | solution.py:534
  349.5 5.8 %copy-done.3 = bf16[8,1024,1024]{2,1,0:T(8,128)(2,1)S(1)} copy-done((bf16[8,1024,1024]{2,1,0:T(8,128)(2,1)S(1)}, bf16[8,1024,1024]{2,1,0:T(8,128)(2,1)}, u32[]{:S(2)}) %copy-start.3) | copy-done | bytes 16777240
  355.3 3.3 leave.1
  358.6 1.0 reshape.65
  359.6 1.8 convert_reduce_fusion
  361.4 1.8 convert_reduce_fusion.1
  (50 shorter events, 0.2 us)
Async XLA Ops:
  1.8 5.8 %copy-start = (bf16[8,1024,1024]{2,1,0:T(8,128)(2,1)S(1)}, bf16[8,1024,1024]{2,1,0:T(8,128)(2,1)}, u32[]{:S(2)}) copy-start(bf16[8,1024,1024]{2,1,0:T(8,128)(2,1)} %weights_ref.7) | copy-start | bytes 50331652
  7.6 11.9 %copy-start.28 = (s32[128]{0:T(128)S(1)}, s32[128]{0:T(128)}, u32[]{:S(2)}) copy-start(s32[128]{0:T(128)} %param.7) | copy-start | bytes 1540
  10.3 0.8 copy-start.13
  11.1 1.2 copy-start.21
  12.3 53.0 %copy-start.10 = (bf16[256,1024]{1,0:T(8,128)(2,1)}, bf16[256,1024]{1,0:T(8,128)(2,1)S(1)}, u32[]{:S(2)}) copy-start(bf16[256,1024]{1,0:T(8,128)(2,1)S(1)} %get-tuple-element.15.tokens_ref) | copy-start | bytes 1572868
  12.3 30.7 %all-to-all-start = ((bf16[16,384,128]{2,1,0:T(8,128)(2,1)}), bf16[16,384,128]{2,1,0:T(8,128)(2,1)S(1)}, u32[]{:S(2)}, u32[]{:S(2)}) async-start(bf16[16,384,128]{2,1,0:T(8,128)(2,1)} %copy-done.21), calls=%async_computation | async-start | bytes 3145728 | tf_op jit(solution)/shard_map/all_to_all | solution.py:522
  19.5 33.5 %copy-start.27 = (bf16[8,8,4,1024]{3,2,1,0:T(4,128)(2,1)S(1)}, bf16[8,8,4,1024]{3,2,1,0:T(4,128)(2,1)}, u32[]{:S(2)}) copy-start(bf16[8,8,4,1024]{3,2,1,0:T(4,128)(2,1)} %param.5) | copy-start | bytes 1572868
  43.0 4.5 %copy-start.19 = (bf16[16,384,128]{2,1,0:T(8,128)(2,1)}, bf16[16,384,128]{2,1,0:T(8,128)(2,1)S(1)}, u32[]{:S(2)}) copy-start(bf16[16,384,128]{2,1,0:T(8,128)(2,1)S(1)} %all-to-all-done.query_ref.keys_ref.values_ref.q.k.v) | copy-start | bytes 4718596
  47.6 1.4 copy-start.24
  48.9 16.4 %all-to-all-start.1 = ((bf16[16,128,128]{2,1,0:T(8,128)(2,1)}), bf16[16,128,128]{2,1,0:T(8,128)(2,1)S(1)}, u32[]{:S(2)}, u32[]{:S(2)}) async-start(bf16[16,128,128]{2,1,0:T(8,128)(2,1)} %get-tuple-element.16), calls=%async_computation.1 | async-start | bytes 1048576 | tf_op jit(solution)/shard_map/all_to_all | solution.py:522
  65.3 5.8 %copy-start.1 = (bf16[8,1024,1024]{2,1,0:T(8,128)(2,1)S(1)}, bf16[8,1024,1024]{2,1,0:T(8,128)(2,1)}, u32[]{:S(2)}) copy-start(bf16[8,1024,1024]{2,1,0:T(8,128)(2,1)} %weights_ref.7) | copy-start | bytes 50331652
  75.4 40.2 %copy-start.16 = (bf16[8,256,128]{2,1,0:T(8,128)(2,1)}, bf16[8,256,128]{2,1,0:T(8,128)(2,1)S(1)}, u32[]{:S(2)}) copy-start(bf16[8,256,128]{2,1,0:T(8,128)(2,1)S(1)} %get-tuple-element.24.hidden_ref) | copy-start | bytes 1572868
  75.4 40.2 %copy-start.22 = (bf16[256,1024]{1,0:T(8,128)(2,1)}, bf16[256,1024]{1,0:T(8,128)(2,1)S(1)}, u32[]{:S(2)}) copy-start(bf16[256,1024]{1,0:T(8,128)(2,1)S(1)} %get-tuple-element.19.after_ref) | copy-start | bytes 1572868
  75.4 70.5 %copy-start.8 = (bf16[256,1024]{1,0:T(8,128)(2,1)}, bf16[256,1024]{1,0:T(8,128)(2,1)S(1)}, u32[]{:S(2)}) copy-start(bf16[256,1024]{1,0:T(8,128)(2,1)S(1)} %get-tuple-element.18.cotangent_ref.last_ref) | copy-start | bytes 1572868
  115.6 1.3 copy-start.12
  116.9 28.9 %all-to-all-start.3 = ((bf16[8,1024,128]{2,1,0:T(8,128)(2,1)}), bf16[8,1024,128]{2,1,0:T(8,128)(2,1)S(1)}, u32[]{:S(2)}, u32[]{:S(2)}) async-start(bf16[8,1024,128]{2,1,0:T(8,128)(2,1)} %bitcast.27), calls=%async_computation.3 | async-start | bytes 4194304 | tf_op jit(solution)/shard_map/all_to_all | solution.py:522
  145.9 1.0 copy-start.17
  146.9 3.2 copy-start.23
  150.0 66.1 %collective-permute-start.1 = (bf16[8,256,1024]{2,1,0:T(8,128)(2,1)S(1)}, bf16[8,256,1024]{2,1,0:T(8,128)(2,1)S(1)}, u32[]{:S(2)}, u32[]{:S(2)}) collective-permute-start(bf16[8,256,1024]{2,1,0:T(8,128)(2,1)S(1)} %weights_first.3), channel_id=1, source_target_pairs={{0,8},{8,0},{16,24},{24,16},{32,40},{40,32},{48,56},{56,48},{64,72... | collective-permute-start | bytes 12582920 | tf_op jit(solution)/shard_map/ppermute | solution.py:518
  150.1 5.8 %copy-start.2 = (bf16[8,1024,1024]{2,1,0:T(8,128)(2,1)S(1)}, bf16[8,1024,1024]{2,1,0:T(8,128)(2,1)}, u32[]{:S(2)}) copy-start(bf16[8,1024,1024]{2,1,0:T(8,128)(2,1)} %weights_ref.7) | copy-start | bytes 50331652
  155.9 1.0 copy-start.9
  157.0 21.2 %copy-start.20 = (bf16[16,384,128]{2,1,0:T(8,128)(2,1)S(1)}, bf16[16,384,128]{2,1,0:T(8,128)(2,1)}, u32[]{:S(2)}) copy-start(bf16[16,384,128]{2,1,0:T(8,128)(2,1)} %copy-done.19) | copy-start | bytes 4718596
  178.1 1.6 copy-start.25
  179.7 31.5 %copy-start.14 = (bf16[8,256,128]{2,1,0:T(8,128)(2,1)S(1)}, bf16[8,256,128]{2,1,0:T(8,128)(2,1)}, u32[]{:S(2)}) copy-start(bf16[8,256,128]{2,1,0:T(8,128)(2,1)} %copy-done.13) | copy-start | bytes 1572868
  211.2 8.5 %copy-start.4 = (bf16[16,384,128]{2,1,0:T(8,128)(2,1)}, bf16[16,384,128]{2,1,0:T(8,128)(2,1)S(1)}, u32[]{:S(2)}) copy-start(bf16[16,384,128]{2,1,0:T(8,128)(2,1)S(1)} %all_to_all.52) | copy-start | bytes 4718596
  211.2 5.0 %copy-start.18 = (bf16[8,256,128]{2,1,0:T(8,128)(2,1)S(1)}, bf16[8,256,128]{2,1,0:T(8,128)(2,1)}, u32[]{:S(2)}) copy-start(bf16[8,256,128]{2,1,0:T(8,128)(2,1)} %copy-done.16) | copy-start | bytes 1572868
  216.2 10.4 %collective-permute-start = (bf16[8,256,1024]{2,1,0:T(8,128)(2,1)}, bf16[8,256,1024]{2,1,0:T(8,128)(2,1)}, u32[]{:S(2)}, u32[]{:S(2)}) collective-permute-start(bf16[8,256,1024]{2,1,0:T(8,128)(2,1)} %weights_first.2), channel_id=1, source_target_pairs={{0,8},{8,0},{16,24},{24,16},{32,40},{40,32},{48,56},{56,48},{64,72... | collective-permute-start | bytes 12582920 | tf_op jit(solution)/shard_map/ppermute | solution.py:518
  219.7 2.0 copy-start.7
  221.7 4.9 %copy-start.5 = (bf16[16,384,128]{2,1,0:T(8,128)(2,1)S(1)}, bf16[16,384,128]{2,1,0:T(8,128)(2,1)}, u32[]{:S(2)}) copy-start(bf16[16,384,128]{2,1,0:T(8,128)(2,1)} %copy-done.4) | copy-start | bytes 4718596
  221.7 4.9 %copy-start.15 = (bf16[8,256,128]{2,1,0:T(8,128)(2,1)S(1)}, bf16[8,256,128]{2,1,0:T(8,128)(2,1)}, u32[]{:S(2)}) copy-start(bf16[8,256,128]{2,1,0:T(8,128)(2,1)} %copy-done.13) | copy-start | bytes 1572868
  221.7 55.1 %all-to-all-start.8 = ((bf16[8,256,1024]{2,1,0:T(8,128)(2,1)}), bf16[8,256,1024]{2,1,0:T(8,128)(2,1)}, u32[]{:S(2)}, u32[]{:S(2)}) async-start(bf16[8,256,1024]{2,1,0:T(8,128)(2,1)} %bitcast.23), calls=%async_computation.8 | async-start | bytes 8388608 | tf_op jit(solution)/shard_map/all_to_all | solution.py:522
  232.9 1.9 copy-start.6
  276.8 54.2 %all-to-all-start.6 = ((bf16[8,256,1024]{2,1,0:T(8,128)(2,1)}), bf16[8,256,1024]{2,1,0:T(8,128)(2,1)}, u32[]{:S(2)}, u32[]{:S(2)}) async-start(bf16[8,256,1024]{2,1,0:T(8,128)(2,1)} %bitcast.22), calls=%async_computation.6 | async-start | bytes 8388608 | tf_op jit(solution)/shard_map/all_to_all | solution.py:522
  285.3 64.2 %copy-start.11 = (bf16[256,1024]{1,0:T(8,128)(2,1)S(1)}, bf16[256,1024]{1,0:T(8,128)(2,1)}, u32[]{:S(2)}) copy-start(bf16[256,1024]{1,0:T(8,128)(2,1)} %copy-done.10) | copy-start | bytes 1572868
  330.9 13.6 %all-to-all-start.9 = ((bf16[8,32,1024]{2,1,0:T(8,128)(2,1)}), bf16[8,32,1024]{2,1,0:T(8,128)(2,1)S(1)}, u32[]{:S(2)}, u32[]{:S(2)}) async-start(bf16[8,32,1024]{2,1,0:T(8,128)(2,1)} %bitcast.12), calls=%async_computation.9 | async-start | bytes 1048576 | tf_op jit(solution)/shard_map/all_to_all | solution.py:534
  344.5 0.8 copy-start.26
  345.3 16.0 %all-to-all-start.7 = ((bf16[8,32,1024]{2,1,0:T(8,128)(2,1)}), bf16[8,32,1024]{2,1,0:T(8,128)(2,1)}, u32[]{:S(2)}, u32[]{:S(2)}) async-start(bf16[8,32,1024]{2,1,0:T(8,128)(2,1)} %bitcast.10), calls=%async_computation.7 | async-start | bytes 1048576 | tf_op jit(solution)/shard_map/all_to_all | solution.py:534
  349.5 5.8 %copy-start.3 = (bf16[8,1024,1024]{2,1,0:T(8,128)(2,1)S(1)}, bf16[8,1024,1024]{2,1,0:T(8,128)(2,1)}, u32[]{:S(2)}) copy-start(bf16[8,1024,1024]{2,1,0:T(8,128)(2,1)} %weights_ref.7) | copy-start | bytes 50331652

commit v2 on v1

--- a/solution.py
+++ b/solution.py
@@ -61,12 +61,23 @@
     return factor * (upstream - normed * jnp.mean(upstream * normed, -1, keepdims=True))
 
 
+def weight_specs(slot):
+    return [pl.BlockSpec((1, 256, D), lambda i, *c, q=q: (slot(i), q, 0)) for q in range(4)]
+
+
+def joined(refs):
+    return jnp.concatenate([ref[0] for ref in refs], 0)
+
+
 def params(limit=32):
     return pltpu.CompilerParams(vmem_limit_bytes=limit * MIB)
 
 
 def cost(flops, read):
     return pl.CostEstimate(flops=int(flops), bytes_accessed=int(read), transcendentals=0)
+
+
+unused = pl.BlockSpec(memory_space=pl.ANY)
 
 
 def fixed(shape):
@@ -105,7 +116,10 @@
     return query_grad, keys_grad, value_grad
 
 
-def enter_kernel(tokens_ref, weights_ref, send_ref, tokens_out_ref, hidden_out_ref, hidden_ref):
+def enter_kernel(
+    ids_ref, tokens_ref, w0, w1, w2, w3,
+    send_ref, tokens_out_ref, keep_ref, give_ref, hidden_ref,
+):
     step = pl.program_id(0)
 
     @pl.when(step == 0)
@@ -115,10 +129,20 @@
         wide = rows.astype(F32)
         hidden = (wide * factor_of(wide)).astype(BF)
         hidden_ref[...] = hidden
-        for block in range(8):
-            hidden_out_ref[block] = hidden[:, 128 * block : 128 * block + 128]
-
-    result = jnp.dot(hidden_ref[...], weights_ref[0], preferred_element_type=F32).astype(BF)
+        core = ids_ref[0]
+
+        @pl.when(core == 0)
+        def _():
+            keep_ref[...] = hidden[:128]
+            give_ref[...] = hidden[128:]
+
+        @pl.when(core == 1)
+        def _():
+            keep_ref[...] = hidden[128:]
+            give_ref[...] = hidden[:128]
+
+    weights = joined((w0, w1, w2, w3))
+    result = jnp.dot(hidden_ref[...], weights, preferred_element_type=F32).astype(BF)
     for pair in range(8):
         for half in range(2):
             send_ref[2 * pair + half] = result[
@@ -126,26 +150,31 @@
             ]
 
 
-def enter(tokens, weights):
+def enter(ids, tokens, weights):
     return pl.pallas_call(
         enter_kernel,
-        grid=(3,),
-        in_specs=[fixed((ROWS, D)), pl.BlockSpec((1, D, D), lambda i: (i, 0, 0))],
-        out_specs=[
-            pl.BlockSpec((16, 128, 128), lambda i: (0, i, 0)),
-            fixed((ROWS, D)),
-            fixed((8, ROWS, 128)),
-        ],
+        grid_spec=pltpu.PrefetchScalarGridSpec(
+            num_scalar_prefetch=1,
+            grid=(3,),
+            in_specs=[fixed((ROWS, D))] + weight_specs(lambda i: i),
+            out_specs=[
+                pl.BlockSpec((16, 128, 128), lambda i, c: (0, i, 0)),
+                fixed((ROWS, D)),
+                fixed((128, D)),
+                fixed((128, D)),
+            ],
+            scratch_shapes=[pltpu.VMEM((ROWS, D), BF)],
+        ),
         out_shape=[
             jax.ShapeDtypeStruct((16, 384, 128), BF),
             jax.ShapeDtypeStruct((ROWS, D), BF),
-            jax.ShapeDtypeStruct((8, ROWS, 128), BF),
+            jax.ShapeDtypeStruct((128, D), BF),
+            jax.ShapeDtypeStruct((128, D), BF),
         ],
-        scratch_shapes=[pltpu.VMEM((ROWS, D), BF)],
-        compiler_params=params(),
+        compiler_params=params(52),
         cost_estimate=cost(3 * 2 * ROWS * D * D, 8 * MIB),
         name="enter",
-    )(tokens, weights)
+    )(ids, tokens, *[weights] * 4)
 
 
 def agent_rows(block, step):
@@ -212,7 +241,8 @@
         ref[...] = jnp.concatenate(kept, 1).astype(BF)
 
 
-def agent_backward_all_kernel(q, k, v, g, table_ref, out_ref):
+def agent_backward_all_kernel(q, k, v, g, table_ref, *rest):
+    out_ref = rest[-1]
     agent_backward_kernel(
         q,
         k,
@@ -225,7 +255,7 @@
     )
 
 
-def agent_backward(arrived, upstream, tables):
+def agent_backward(arrived, upstream, tables, waits=()):
     return pl.pallas_call(
         agent_backward_all_kernel,
         grid=(4,),
@@ -233,19 +263,21 @@
         + [
             pl.BlockSpec((16, 32, 128), lambda i: (0, i, 0)),
             pl.BlockSpec((1, 4, 256, 128), lambda i: (i, 0, 0, 0)),
-        ],
+        ]
+        + [unused] * len(waits),
         out_specs=pl.BlockSpec((16, 3, 32, 128), lambda i: (0, 0, i, 0)),
         out_shape=jax.ShapeDtypeStruct((16, 3, 128, 128), BF),
         compiler_params=params(),
         cost_estimate=cost(6e9, 6 * MIB),
         name="agent_backward",
-    )(arrived, arrived, arrived, upstream, tables)
+    )(arrived, arrived, arrived, upstream, tables, *waits)
 
 
 def middle_kernel(
-    tokens_ref, mixed_ref, cotangent_ref, weights_ref,
-    send_ref, after_ref, hidden_out_ref, cotangent_out_ref, hidden_ref,
+    tokens_ref, mixed_ref, cotangent_ref, w0, w1, w2, w3, *rest
 ):
+    send_ref, after_ref, hidden_out_ref, cotangent_out_ref, hidden_ref = rest[-5:]
+    quarters = (w0, w1, w2, w3)
     step = pl.program_id(0)
 
     @pl.when(step == 0)
@@ -253,7 +285,7 @@
         mixed = jnp.concatenate([mixed_ref[pair] for pair in range(8)], 1)
         after = (
             tokens_ref[...].astype(F32)
-            + jnp.dot(mixed, weights_ref[0], preferred_element_type=F32)
+            + jnp.dot(mixed, joined(quarters), preferred_element_type=F32)
         ).astype(BF)
         after = reorder(after, "a", "m")
         after_ref[...] = after
@@ -271,14 +303,14 @@
 
     @pl.when((step > 0) & (step < 4))
     def _():
-        send(jnp.dot(hidden_ref[...], weights_ref[0], preferred_element_type=F32))
+        send(jnp.dot(hidden_ref[...], joined(quarters), preferred_element_type=F32))
 
     @pl.when(step == 4)
     def _():
-        send(dot_nt(cotangent_out_ref[...], weights_ref[0]))
-
-
-def middle(tokens, mixed, cotangent, weights):
+        send(dot_nt(cotangent_out_ref[...], joined(quarters)))
+
+
+def middle(tokens, mixed, cotangent, weights, waits=()):
     return pl.pallas_call(
         middle_kernel,
         grid=(5,),
@@ -286,8 +318,9 @@
             fixed((ROWS, D)),
             fixed((8, ROWS, 128)),
             fixed((ROWS, D)),
-            pl.BlockSpec((1, D, D), lambda i: (3 + i, 0, 0)),
-        ],
+        ]
+        + weight_specs(lambda i: 3 + i)
+        + [unused] * len(waits),
         out_specs=[
             pl.BlockSpec((8, 1, ROWS, 128), lambda i: (0, jnp.maximum(i - 1, 0), 0, 0)),
             fixed((ROWS, D)),
@@ -301,13 +334,14 @@
             jax.ShapeDtypeStruct((ROWS, D), BF),
         ],
         scratch_shapes=[pltpu.VMEM((ROWS, D), BF)],
-        compiler_params=params(),
+        compiler_params=params(52),
         cost_estimate=cost(5 * 2 * ROWS * D * D, 13 * MIB),
         name="middle",
-    )(tokens, mixed, cotangent, weights)
-
-
-def mode_kernel(arrived_ref, out_ref):
+    )(tokens, mixed, cotangent, *[weights] * 4, *waits)
+
+
+def mode_kernel(arrived_ref, *rest):
+    out_ref = rest[-1]
     rows = lax.broadcasted_iota(jnp.int32, (256, 128), 0)
     columns = lax.broadcasted_iota(jnp.int32, (256, 128), 1)
     same = ((rows >> 6) & 1) == (columns >> 6)
@@ -330,29 +364,29 @@
             out_ref[:, which, 16 * pair : 16 * pair + 16, :] = jnp.concatenate(parts, 1).astype(BF)
 
 
-def mode_attention(arrived):
+def mode_attention(arrived, after=()):
     spec = pl.BlockSpec((8, 4, 64, 128), lambda i: (0, 0, i, 0))
     return pl.pallas_call(
         mode_kernel,
         grid=(4,),
-        in_specs=[spec],
+        in_specs=[spec] + [unused] * len(after),
         out_specs=spec,
         out_shape=jax.ShapeDtypeStruct((8, 4, ROWS, 128), BF),
         compiler_params=params(),
         cost_estimate=cost(8e9, 4 * MIB),
         name="mode_attention",
-    )(arrived)
-
-
-def turn_kernel(
-    returned_ref, cotangent_ref, after_ref, weights_ref, send_ref, grad_after_ref, total_ref
-):
+    )(arrived, *after)
+
+
+def turn_kernel(returned_ref, cotangent_ref, after_ref, w0, w1, w2, w3, *rest):
+    quarters = (w0, w1, w2, w3)
+    send_ref, grad_after_ref, total_ref = rest[-3:]
     step = pl.program_id(0)
 
     @pl.when(step < 3)
     def _():
         grads = jnp.concatenate([returned_ref[pair, 0] for pair in range(8)], 1)
-        product = dot_nt(grads, weights_ref[0])
+        product = dot_nt(grads, joined(quarters))
 
         @pl.when(step == 0)
         def _():
@@ -369,7 +403,7 @@
         ).astype(BF)
         grad_after = reorder(grad_after, "m", "a")
         grad_after_ref[...] = grad_after
-        result = dot_nt(grad_after, weights_ref[0]).astype(BF)
+        result = dot_nt(grad_after, joined(quarters)).astype(BF)
         for pair in range(8):
             for half in range(2):
                 send_ref[2 * pair + half] = result[
@@ -377,7 +411,7 @@
                 ]
 
 
-def turn(returned, cotangent, after, weights):
+def turn(returned, cotangent, after, weights, waits=()):
     return pl.pallas_call(
         turn_kernel,
         grid=(4,),
@@ -385,27 +419,29 @@
             pl.BlockSpec((8, 1, ROWS, 128), lambda i: (0, jnp.minimum(i + 1, 3), 0, 0)),
             fixed((ROWS, D)),
             fixed((ROWS, D)),
-            pl.BlockSpec((1, D, D), lambda i: (jnp.where(i < 3, i + 4, 3), 0, 0)),
-        ],
+        ]
+        + weight_specs(lambda i: jnp.where(i < 3, i + 4, 3))
+        + [unused] * len(waits),
         out_specs=[fixed((16, 128, 128)), fixed((ROWS, D))],
         out_shape=[
             jax.ShapeDtypeStruct((16, 128, 128), BF),
             jax.ShapeDtypeStruct((ROWS, D), BF),
         ],
         scratch_shapes=[pltpu.VMEM((ROWS, D), F32)],
-        compiler_params=params(),
+        compiler_params=params(52),
         cost_estimate=cost(4 * 2 * ROWS * D * D, 12 * MIB),
         name="turn",
-    )(returned, cotangent, after, weights)
+    )(returned, cotangent, after, *[weights] * 4, *waits)
 
 
 def whole_rows(ref):
     return jnp.concatenate([ref[:, 0].reshape(8, ROWS, 128)[pair] for pair in range(8)], 1)
 
 
-def leave_kernel(returned_ref, tokens_ref, grad_after_ref, weights_ref, out_ref, total_ref):
+def leave_kernel(returned_ref, tokens_ref, grad_after_ref, w0, w1, w2, w3, *rest):
+    out_ref, total_ref = rest[-2:]
     step = pl.program_id(0)
-    product = dot_nt(whole_rows(returned_ref), weights_ref[0])
+    product = dot_nt(whole_rows(returned_ref), joined((w0, w1, w2, w3)))
 
     @pl.when(step == 0)
     def _():
@@ -423,7 +459,7 @@
         out_ref[...] = reorder(grads, "a", "o")
 
 
-def leave(returned, tokens, grad_after, weights):
+def leave(returned, tokens, grad_after, weights, waits=()):
     return pl.pallas_call(
         leave_kernel,
         grid=(3,),
@@ -431,132 +467,330 @@
             pl.BlockSpec((16, 1, 128, 128), lambda i: (0, i, 0, 0)),
             fixed((ROWS, D)),
             fixed((ROWS, D)),
-            pl.BlockSpec((1, D, D), lambda i: (i, 0, 0)),
-        ],
+        ]
+        + weight_specs(lambda i: i)
+        + [unused] * len(waits),
         out_specs=fixed((ROWS, D)),
         out_shape=jax.ShapeDtypeStruct((ROWS, D), BF),
         scratch_shapes=[pltpu.VMEM((ROWS, D), F32)],
-        compiler_params=params(),
+        compiler_params=params(52),
         cost_estimate=cost(3 * 2 * ROWS * D * D, 9 * MIB),
         name="leave",
-    )(returned, tokens, grad_after, weights)
-
-
-def weight_kernel(of_agents, add, core_ref, hidden_ref, mixed_ref, grads_ref, last_ref, *rest):
-    step = pl.program_id(0)
-    if add:
-        arrived_ref, out_ref = rest
-    else:
-        (out_ref,) = rest
-
-    def finish(left_ref, right):
-        left = jnp.concatenate([left_ref[0], left_ref[1]], 1)
-        product = dot_tn(left, right)
-        if add:
-            total = product + arrived_ref[0].astype(F32)
-            out_ref[...] = total.astype(BF).reshape(8, 1, 32, D)
-        else:
-            out_ref[0] = product.astype(BF)
-
-    @pl.when(step < 6)
-    def _():
-        if of_agents:
-            right = whole_rows(grads_ref)
-        else:
-            right = jnp.concatenate([grads_ref[pair, 0] for pair in range(8)], 1)
-        finish(hidden_ref, right)
-
-    @pl.when(step >= 6)
-    def _():
-        finish(mixed_ref.at[:, 0] if not of_agents else mixed_ref, last_ref[...])
-
-
-def weight_products(of_agents, core, hidden, mixed, grads, last, arrived=None):
-    add = arrived is not None
-
-    def feature(i, core_ref):
-        return 2 * (i % 2) + core_ref[0]
-
-    if of_agents:
-        mixed_spec = pl.BlockSpec((2, ROWS, 128), lambda i, c: (feature(i, c), 0, 0))
-        grads_spec = pl.BlockSpec(
-            (16, 1, 128, 128), lambda i, c: (0, jnp.minimum(i // 2, 2), 0, 0)
-        )
-    else:
-        mixed_spec = pl.BlockSpec((2, 1, ROWS, 128), lambda i, c: (feature(i, c), 0, 0, 0))
-        grads_spec = pl.BlockSpec(
-            (8, 1, ROWS, 128), lambda i, c: (0, jnp.minimum(i // 2, 2) + 1, 0, 0)
-        )
-    in_specs = [
-        pl.BlockSpec((2, ROWS, 128), lambda i, c: (feature(i, c), 0, 0)),
-        mixed_spec,
-        grads_spec,
-        pl.BlockSpec((ROWS, D), lambda i, c: (0, 0)),
-    ]
-    operands = [core, hidden, mixed, grads, last]
-    if add:
-        in_specs.append(pl.BlockSpec((1, ROWS, D), lambda i, c: (i, 0, 0)))
-        operands.append(arrived)
-        out_spec = pl.BlockSpec((8, 1, 32, D), lambda i, c: (0, i, 0, 0))
-        out_shape = jax.ShapeDtypeStruct((8, 8, 32, D), BF)
-    else:
-        out_spec = pl.BlockSpec((1, ROWS, D), lambda i, c: (i, 0, 0))
-        out_shape = jax.ShapeDtypeStruct((8, ROWS, D), BF)
+    )(returned, tokens, grad_after, *[weights] * 4, *waits)
+
+
+CORE, MODE, CHIP, Z, YLO, X, YHI = range(7)
+
+
+def swap(values, axis, bits):
+    size = lax.axis_size(axis)
+    return lax.ppermute(values, axis, [(n, n ^ bits) for n in range(size)])
+
+
+def swap_all(parts, axis, bit):
+    return [parts[0]] + [swap(parts[o], axis, o * bit) for o in range(1, 4)]
+
+
+def prefetched(kernel, ids, operands, in_specs, out_specs, out_shape, name, grid=(), scratch=()):
     return pl.pallas_call(
-        functools.partial(weight_kernel, of_agents, add),
+        kernel,
         grid_spec=pltpu.PrefetchScalarGridSpec(
-            num_scalar_prefetch=1, grid=(8,), in_specs=in_specs, out_specs=out_spec
+            num_scalar_prefetch=1,
+            grid=grid,
+            in_specs=in_specs,
+            out_specs=out_specs,
+            scratch_shapes=list(scratch),
         ),
         out_shape=out_shape,
         compiler_params=params(),
-        cost_estimate=cost(4 * 2 * ROWS * D * D // 2, 8 * MIB),
-        name="weights_add" if add else "weights_first",
-    )(*operands)
-
-
-def swap_cores(values, axis_size):
-    return lax.ppermute(values, "agent", [(n, n ^ 1) for n in range(axis_size)])
+        cost_estimate=cost(1e9, 5 * MIB),
+        name=name,
+    )(ids, *operands)
+
+
+def rows_of(values, start, count):
+    return values[pl.ds(pl.multiple_of(start, count), count), :]
+
+
+def early_kernel(add, ids_ref, hidden_ref, mixed_ref, grads_ref, last_ref, *rest):
+    step = pl.program_id(0)
+
+    def finish(first, second, right):
+        product = dot_tn(jnp.concatenate([first, second], 1), right)
+        if add:
+            arrived_ref, total_ref = rest[0], rest[-1]
+            total_ref[...] = product + arrived_ref[0].astype(F32)
+            for partner, out_ref in enumerate(rest[-5:-1]):
+                out_ref[0] = rows_of(total_ref, (ids_ref[Z] ^ partner) * 64, 64).astype(BF)
+        else:
+            rest[-1][0] = product.astype(BF)
+
+    @pl.when(step < 6)
+    def _():
+        right = jnp.concatenate([grads_ref[pair, 0] for pair in range(8)], 1)
+        finish(hidden_ref[0], hidden_ref[1], right)
+
+    @pl.when(step >= 6)
+    def _():
+        finish(mixed_ref[0, 0], mixed_ref[1, 0], last_ref[...])
+
+
+def early_products(ids, hidden, returned, last, arrived=None, waits=()):
+    def feature(i, ids_ref):
+        return 2 * (i % 2) + ids_ref[CORE]
+
+    in_specs = [
+        pl.BlockSpec((2, ROWS, 128), lambda i, c: (feature(i, c), 0, 0)),
+        pl.BlockSpec((2, 1, ROWS, 128), lambda i, c: (feature(i, c), 0, 0, 0)),
+        pl.BlockSpec((8, 1, ROWS, 128), lambda i, c: (0, jnp.minimum(i // 2, 2) + 1, 0, 0)),
+        pl.BlockSpec((ROWS, D), lambda i, c: (0, 0)),
+    ]
+    operands = [hidden, returned, returned, last]
+    if arrived is None:
+        return prefetched(
+            functools.partial(early_kernel, False), ids, operands + list(waits),
+            in_specs + [unused] * len(waits),
+            pl.BlockSpec((1, ROWS, D), lambda i, c: (i, 0, 0)),
+            jax.ShapeDtypeStruct((8, ROWS, D), BF), "early_first", (8,),
+        )
+    return prefetched(
+        functools.partial(early_kernel, True), ids, operands + [arrived, *waits],
+        in_specs + [pl.BlockSpec((1, ROWS, D), lambda i, c: (i, 0, 0))] + [unused] * len(waits),
+        [pl.BlockSpec((1, 64, D), lambda i, c: (i, 0, 0))] * 4,
+        [jax.ShapeDtypeStruct((8, 64, D), BF)] * 4, "early_add", (8,),
+        [pltpu.VMEM((ROWS, D), F32)],
+    )
+
+
+def sum_split_kernel(split, count, inputs, ids_ref, *refs):
+    total_ref = refs[-1]
+    total = refs[0][0].astype(F32)
+    for ref in refs[1:inputs]:
+        total += ref[0].astype(F32)
+    total_ref[...] = total
+    share = total_ref.shape[0] // count
+    for partner, out_ref in enumerate(refs[inputs:-1]):
+        out_ref[0] = rows_of(total_ref, (ids_ref[split] ^ partner) * share, share).astype(BF)
+
+
+def sum_split(ids, parts, split, count, name):
+    blocks, rows, columns = parts[0].shape
+    return prefetched(
+        functools.partial(sum_split_kernel, split, count, len(parts)), ids, parts,
+        [pl.BlockSpec((1, rows, columns), lambda i, c: (i, 0, 0))] * len(parts),
+        [pl.BlockSpec((1, rows // count, columns), lambda i, c: (i, 0, 0))] * count,
+        [jax.ShapeDtypeStruct((blocks, rows // count, columns), BF)] * count, name, (blocks,),
+        [pltpu.VMEM((rows, columns), F32)],
+    )
+
+
+def early_chips_kernel(ids_ref, own_ref, arrived_ref, *rest):
+    for partner, out_ref in enumerate(rest[-4:]):
+        for n in range(2):
+            block = (ids_ref[X] ^ partner) * 2 + n
+            out_ref[n] = (own_ref[block].astype(F32) + arrived_ref[block].astype(F32)).astype(BF)
+
+
+def early_last_kernel(ids_ref, *refs):
+    for partner, out_ref in enumerate(refs[4:]):
+        block = ids_ref[YHI] ^ partner
+        total = refs[0][block].astype(F32)
+        for ref in refs[1:4]:
+            total += ref[block].astype(F32)
+        out_ref[...] = total.astype(BF)
+
+
+def early_sums(ids, parts, waits):
+    keep, give = sum_split(ids, parts, YLO, 2, "early_z")
+    arrived = swap(give, "mode", 1)
+    whole = pl.BlockSpec(memory_space=pltpu.VMEM)
+    parts = prefetched(
+        early_chips_kernel, ids, [keep, arrived, *waits],
+        [whole] * 2 + [unused] * len(waits), [whole] * 4,
+        [jax.ShapeDtypeStruct((2, 32, D), BF)] * 4, "early_chips",
+    )
+    keep, give = prefetched(
+        early_last_kernel, ids, swap_all(parts, "agent", 4), [whole] * 4, [whole] * 2,
+        [jax.ShapeDtypeStruct((32, D), BF)] * 2, "early_last",
+    )
+    return keep.astype(F32) + swap(give, "agent", 2).astype(F32)
+
+
+WIDE = 384 + D
+
+
+def gather_hidden(keep, give):
+    chip = jnp.concatenate([keep, swap(give, "agent", 1)], 0)
+    here = jnp.stack([chip, swap(chip, "agent", 2)])
+    return here
+
+
+def late_kernel(ids_ref, *refs):
+    hiddens, first_ref, second_ref, mixed_ref, after_ref, mine_ref, theirs_ref, total_ref = (
+        refs[:4],
+        *refs[4:8],
+        *refs[-3:],
+    )
+    step = pl.program_id(0)
+    core = ids_ref[CORE]
+
+    @pl.when(step == 0)
+    def _():
+        total_ref[...] = jnp.zeros_like(total_ref)
+
+    for partner, ref in enumerate(hiddens):
+
+        @pl.when(step // 2 == partner)
+        def _(ref=ref):
+            right = jnp.concatenate(
+                [
+                    jnp.concatenate([source[0, slot] for slot in range(3)], 1)
+                    for source in (first_ref, second_ref)
+                ],
+                0,
+            )
+            total_ref[...] += dot_tn(right, ref[0])
+
+    for block in range(4):
+
+        @pl.when(step == 8 + block)
+        def _(block=block):
+            rows = total_ref[:, 256 * block : 256 * block + 256].T.astype(BF)
+            left = jnp.concatenate([mixed_ref[0], mixed_ref[1]], 1)
+            other = dot_tn(left, after_ref[...]).astype(BF)
+
+            @pl.when(core == block % 2)
+            def _():
+                mine_ref[block // 2, :, :384] = rows
+                mine_ref[block // 2, :, 384:] = other
+
+            @pl.when(core != block % 2)
+            def _():
+                theirs_ref[block // 2, :, :384] = rows
+                theirs_ref[block // 2, :, 384:] = other
+
+
+def late_products(ids, hiddens, grads, mixed, grad_after, waits):
+    def source(i, c, other):
+        chip = (c[X] ^ jnp.minimum(i // 2, 3)) * 2 + (c[YHI] ^ (i % 2))
+        return 2 * chip + (c[CORE] ^ other)
+
+    in_specs = [
+        pl.BlockSpec((1, ROWS, D), lambda i, c, o=o: (jnp.clip(i - 2 * o, 0, 1), 0, 0))
+        for o in range(4)
+    ]
+    in_specs += [
+        pl.BlockSpec((1, 3, 128, 128), lambda i, c, o=o: (source(i, c, o), 0, 0, 0))
+        for o in range(2)
+    ]
+    in_specs += [
+        pl.BlockSpec((2, ROWS, 128), lambda i, c: (jnp.clip(i - 8, 0, 3), 0, 0)),
+        pl.BlockSpec((ROWS, D), lambda i, c: (0, 0)),
+    ]
+    return prefetched(
+        late_kernel, ids, list(hiddens) + [grads, grads, mixed, grad_after, *waits],
+        in_specs + [unused] * len(waits),
+        [pl.BlockSpec((2, ROWS, WIDE), lambda i, c: (0, 0, 0))] * 2,
+        [jax.ShapeDtypeStruct((2, ROWS, WIDE), BF)] * 2, "late_products", (12,),
+        [pltpu.VMEM((384, D), F32)],
+    )
+
+
+def late_chips_kernel(ids_ref, own_ref, arrived_ref, *rest):
+    outs, total_ref = rest[:-1], rest[-1]
+    total_ref[...] = own_ref[...].astype(F32) + arrived_ref[...].astype(F32)
+    for partner, out_ref in enumerate(outs):
+        slot = jnp.minimum(ids_ref[X] ^ partner, 2)
+        lanes = pl.ds(pl.multiple_of(slot * 128, 128), 128)
+        out_ref[:, :, :128] = total_ref[:, :, lanes].astype(BF)
+        out_ref[:, :, 128:] = total_ref[:, :, 384:].astype(BF)
+
+
+def late_turn_kernel(ids_ref, *refs):
+    for other, out_ref in enumerate(refs[4:]):
+        row = ids_ref[YHI] ^ other
+        total = refs[0][row, :, 128:].astype(F32)
+        for ref in refs[1:4]:
+            total += ref[row, :, 128:].astype(F32)
+        for partner, ref in enumerate(refs[:4]):
+            out_ref[partner, :, :128] = ref[row, :, :128]
+            out_ref[partner, :, 128:] = total[:, 256 * partner : 256 * partner + 256].astype(BF)
+
+
+def late_last_kernel(ids_ref, keep_ref, arrived_ref, out_ref):
+    @pl.when(ids_ref[X] < 3)
+    def _():
+        for other, ref in enumerate((keep_ref, arrived_ref)):
+            for partner in range(4):
+                pair = (ids_ref[X] ^ partner) * 2 + (ids_ref[YHI] ^ other)
+                lanes = pl.ds(pl.multiple_of(pair * 128, 128), 128)
+                out_ref[:, lanes] = ref[partner, :, :128].astype(F32)
+
+    @pl.when(ids_ref[X] == 3)
+    def _():
+        for partner in range(4):
+            out_ref[:, 256 * partner : 256 * partner + 256] = keep_ref[partner, :, 128:].astype(
+                F32
+            ) + arrived_ref[partner, :, 128:].astype(F32)
+
+
+def late_sums(ids, mine, theirs):
+    whole = pl.BlockSpec(memory_space=pltpu.VMEM)
+    parts = sum_split(ids, [mine, swap(theirs, "agent", 1)], Z, 4, "late_add")
+    keep, give = sum_split(ids, swap_all(parts, "mode", 2), YLO, 2, "late_z")
+    parts = prefetched(
+        late_chips_kernel, ids, [keep, swap(give, "mode", 1)], [whole] * 2, [whole] * 4,
+        [jax.ShapeDtypeStruct((2, 32, 128 + D), BF)] * 4, "late_chips", (),
+        [pltpu.VMEM((2, 32, WIDE), F32)],
+    )
+    keep, give = prefetched(
+        late_turn_kernel, ids, swap_all(parts, "agent", 4), [whole] * 4, [whole] * 2,
+        [jax.ShapeDtypeStruct((4, 32, 384), BF)] * 2, "late_turn",
+    )
+    return prefetched(
+        late_last_kernel, ids, [keep, swap(give, "agent", 2)], [whole] * 2, whole,
+        jax.ShapeDtypeStruct((32, D), F32), "late_last",
+    )
 
 
 def exchange(values, axis):
     return lax.all_to_all(values, axis, split_axis=0, concat_axis=0, tiled=True)
 
 
-def reduce_grads(of_agents, hidden, mixed, grads, last):
-    agent_size = lax.axis_size("agent")
-    core = (lax.axis_index("agent") % 2).astype(jnp.int32).reshape(1)
-    theirs = weight_products(of_agents, 1 - core, hidden, mixed, grads, last)
-    arrived = swap_cores(theirs, agent_size)
-    mine = weight_products(of_agents, core, hidden, mixed, grads, last, arrived)
-    over_modes = exchange(mine.reshape(8, 256, D), "mode").reshape(8, 256, D)
-    partial = jnp.sum(over_modes.astype(F32), 0).astype(BF).reshape(8, 32, D)
-    groups = [list(range(c, agent_size, 2)) for c in range(2)]
-    over_agents = lax.all_to_all(
-        partial, "agent", split_axis=0, concat_axis=0, tiled=True, axis_index_groups=groups
-    )
-    return jnp.sum(over_agents.astype(F32), 0)
-
-
 def local(tokens, cotangent, weights, agent_mask):
+    agent, mode = lax.axis_index("agent"), lax.axis_index("mode")
+    ids = jnp.stack(
+        [agent & 1, mode, agent >> 1, mode >> 1, mode & 1, agent >> 2, (agent >> 1) & 1]
+    ).astype(jnp.int32)
+    other_ids = ids.at[CORE].set(1 - ids[CORE])
     token_rows = tokens.reshape(ROWS, D)
     grad_rows = cotangent.reshape(ROWS, D)
     offset = jnp.where(agent_mask == 1, 0.0, masked_score).astype(F32).reshape(1, 128)
 
-    outgoing, tokens_a, hidden_one = enter(token_rows, weights)
+    outgoing, tokens_a, hidden_keep, hidden_give = enter(ids, token_rows, weights)
     arrived_one = exchange(outgoing, "agent")
+    hidden_here = gather_hidden(hidden_keep, hidden_give)
     mixed, tables = agent_forward(arrived_one, offset)
     mixed_one = exchange(mixed, "agent").reshape(8, ROWS, 128)
-    outgoing, after, hidden_two, cotangent_m = middle(tokens_a, mixed_one, grad_rows, weights)
+    outgoing, after, hidden_two, cotangent_m = middle(
+        tokens_a, mixed_one, grad_rows, weights, [hidden_here]
+    )
     arrived_two = exchange(outgoing.reshape(8, 1024, 128), "mode").reshape(8, 4, ROWS, 128)
-    returning = mode_attention(arrived_two)
+    hiddens = [hidden_here] + [swap(hidden_here, "agent", 4 * o) for o in range(1, 4)]
+    returning = mode_attention(arrived_two, hiddens[1::2])
     returned_two = exchange(returning.reshape(8, 1024, 128), "mode").reshape(8, 4, ROWS, 128)
-    outgoing, grad_after = turn(returned_two, cotangent_m, after, weights)
+    early = (hidden_two, returned_two, cotangent_m)
+    theirs = early_products(other_ids, *early, None, hiddens[2:3])
+    outgoing, grad_after = turn(returned_two, cotangent_m, after, weights, [theirs])
+    parts = early_products(ids, *early, swap(theirs, "agent", 1), [grad_after])
     upstream = exchange(outgoing, "agent")
-    returning = agent_backward(arrived_one, upstream, tables)
+    returning = agent_backward(arrived_one, upstream, tables, parts[:1])
+    parts = swap_all(parts, "mode", 2)
     returned_one = exchange(returning.reshape(16, 384, 128), "agent").reshape(16, 3, 128, 128)
+    late_parts = late_products(ids, hiddens, returning, mixed_one, grad_after, parts[1::2])
     token_grads = leave(returned_one, tokens_a, grad_after, weights)
-    mode_weight_grads = reduce_grads(False, hidden_two, returned_two, returned_two, cotangent_m)
-    agent_weight_grads = reduce_grads(True, hidden_one, mixed_one, returned_one, grad_after)
+    agent_weight_grads = late_sums(ids, *late_parts)
+    mode_weight_grads = early_sums(ids, parts, [token_grads])
     return (token_grads.reshape(tokens.shape), agent_weight_grads, mode_weight_grads)
 
 

time: 365 us -> 303 us (0.83)
  blocking collectives: 75 us -> 0 us
  waiting for transfers between devices: 155 us -> 114 us
  starting transfers between devices: 31.9 us -> 67.9 us
  Pallas kernels: 50.6 us -> 86 us
  local copies, waits for them, and re-layouts: 38.4 us -> 29.3 us
  other arithmetic: 11.6 us -> 2.82 us
    all_to_all x5 -> x6, waiting for transfers between devices: 149 us -> 28.5 us  [exchange(): return lax.all_to_all(values, axis, split_axis=0, concat_axis=0, tiled=True)]
    ppermute x2 -> x23, waiting for transfers between devices: 0.01 us -> 85.8 us  [swap(): return lax.ppermute(values, axis, [(n, n ^ bits) for n in range(size)])]
    all_to_all x3 -> x0, blocking collectives: 75 us -> none  [exchange(): return lax.all_to_all(values, axis, split_axis=0, concat_axis=0, tiled=True)]
    ppermute x2 -> x23, starting transfers between devices: 0.09 us -> 33.7 us  [swap(): return lax.ppermute(values, axis, [(n, n ^ bits) for n in range(size)])]
    pallas_call x6 -> x13, Pallas kernels: 29.4 us -> 53.2 us  [the longest x11 37.8 us: prefetched(): pl.pallas_call(kernel, grid_spec=pltpu.PrefetchScalarGridSpec(num_scalar_...]
    reduce_sum x4 -> x0, other arithmetic: 11.6 us -> none  [the longest x2 8 us: reduce_grads(): partial = jnp.sum(over_modes.astype(F32), 0).astype(BF).reshape(8, 32, D)]
    unnamed x58 -> x76, local copies, waits for them, and re-layouts: 36.2 us -> 26.1 us
    all_to_all x5 -> x6, starting transfers between devices: 24.2 us -> 34.2 us  [exchange(): return lax.all_to_all(values, axis, split_axis=0, concat_axis=0, tiled=True)]
  transfers between devices with their start and end apart: 9 -> 29, of which waited for: 6 -> 14; matrix products, arithmetic and copies ran while one was open for 3% -> 2% of each run, Pallas kernels for 8% -> 15%
where the time goes in v2:
time: 303 us; the launch traced here: 301 us
  waiting for transfers between devices  114 us (38%)
  Pallas kernels  86 us (28%)
  starting transfers between devices  67.9 us (22%)
  local copies, waits for them, and re-layouts  29.3 us (10%)
    ppermute x23, waiting for transfers between devices, swap(): return lax.ppermute(values, axis, [(n, n ^ bits) for n in range(size)])  85.8 us
    pallas_call x11, Pallas kernels, prefetched(): pl.pallas_call(kernel, grid_spec=pltpu.PrefetchScalarGridSpec(num_scalar_...  37.8 us
    all_to_all x6, starting transfers between devices, exchange(): return lax.all_to_all(values, axis, split_axis=0, concat_axis=0, tiled=True)  34.2 us
    ppermute x23, starting transfers between devices, swap(): return lax.ppermute(values, axis, [(n, n ^ bits) for n in range(size)])  33.7 us
    all_to_all x6, waiting for transfers between devices, exchange(): return lax.all_to_all(values, axis, split_axis=0, concat_axis=0, tiled=True)  28.5 us
    unnamed x76, local copies, waits for them, and re-layouts  26.1 us
    pallas_call x1, Pallas kernels, middle(): pl.pallas_call(middle_kernel, grid=(5,), in_specs=[fixed((ROWS, D)), fixe...  8.92 us
    pallas_call x1, Pallas kernels, mode_attention(): pl.pallas_call(mode_kernel, grid=(4,), in_specs=[spec] + [unused] * len(a...  8.67 us
  transfers between devices with their start and end apart: 29, of which 14 were waited for; matrix products, arithmetic and copies ran while one was open for 2% of the time, Pallas kernels for 15%

profile of v2, /device:TPU:0, one launch (start us, length us, event | category | flops | bytes accessed | tf_op | source)
XLA Modules:
  0.0 301.2 jit_solution(17053248940205979282)
XLA Ops:
  1.9 6.7 %enter.1 = (bf16[16,384,128]{2,1,0:T(8,128)(2,1)}, bf16[256,1024]{1,0:T(8,128)(2,1)S(1)}, bf16[128,1024]{1,0:T(8,128)(2,1)S(1)}, bf16[128,1024]{1,0:T(8,128)(2,1)S(1)}) custom-call(s32[7]{0:T(128)S(1)} %stack.40.ids_ref, bf16[256,1024]{1,0:T(8,128)(2,1)S(1)} %reshape.64.tokens_ref, bf16[8,1024,1024]{2,1,0:T(8,128)(2,1)} %w3.7, bf16[8,1024,1024]{2,1,0:T(8,128)(2,1)} %w3.7, ...), custom_call_target="tpu_custom_call" | custom-call | flops 1610612736 | bytes 8388608 | tf_op jit(solution)/shard_map/enter/pallas_call | solution.py:154
  9.4 7.2 %all-to-all-start = ((bf16[16,384,128]{2,1,0:T(8,128)(2,1)}), bf16[16,384,128]{2,1,0:T(8,128)(2,1)S(1)}, u32[]{:S(2)}, u32[]{:S(2)}) async-start(bf16[16,384,128]{2,1,0:T(8,128)(2,1)} %get-tuple-element.53), calls=%async_computation | async-start | bytes 3145728 | tf_op jit(solution)/shard_map/all_to_all | solution.py:757
  18.3 3.4 %collective-permute-start.1 = (bf16[256,1024]{1,0:T(8,128)(2,1)S(1)}, bf16[256,1024]{1,0:T(8,128)(2,1)}, u32[]{:S(2)}, u32[]{:S(2)}) collective-permute-start(bf16[256,1024]{1,0:T(8,128)(2,1)S(1)} %constant_dynamic-update-slice_fusion), channel_id=1, source_target_pairs={{0,16},{8,24},{16,0},{24,8},{32,48},{40,56},{48,32},{56,40},{64,80... | collective-permute-start | bytes 1572872 | tf_op jit(solution)/shard_map/ppermute | solution.py:487
  21.7 18.5 %all-to-all-done.query_ref.keys_ref.values_ref.q.k.v = bf16[16,384,128]{2,1,0:T(8,128)(2,1)S(1)} async-done(((bf16[16,384,128]{2,1,0:T(8,128)(2,1)}), bf16[16,384,128]{2,1,0:T(8,128)(2,1)S(1)}, u32[]{:S(2)}, u32[]{:S(2)}) %all-to-all-start) | async-done | bytes 1572896 | tf_op jit(solution)/shard_map/all_to_all | solution.py:757
  40.3 4.5 %agent_forward.1 = (bf16[16,128,128]{2,1,0:T(8,128)(2,1)}, f32[4,4,256,128]{3,2,1,0:T(8,128)S(1)}) custom-call(bf16[16,384,128]{2,1,0:T(8,128)(2,1)S(1)} %all-to-all-done.query_ref.keys_ref.values_ref.q.k.v, bf16[16,384,128]{2,1,0:T(8,128)(2,1)S(1)} %all-to-all-done.query_ref.keys_ref.values_ref.q.k.v, ...), custom_call_target="tpu_custom_call" | custom-call | flops 3000000000 | bytes 4194304 | tf_op jit(solution)/shard_map/agent_forward/pallas_call | solution.py:204
  44.8 1.3 copy-done.33
  46.1 4.2 %all-to-all-start.1 = ((bf16[16,128,128]{2,1,0:T(8,128)(2,1)}), bf16[16,128,128]{2,1,0:T(8,128)(2,1)S(1)}, u32[]{:S(2)}, u32[]{:S(2)}) async-start(bf16[16,128,128]{2,1,0:T(8,128)(2,1)} %get-tuple-element.55), calls=%async_computation.1 | async-start | bytes 1048576 | tf_op jit(solution)/shard_map/all_to_all | solution.py:757
  51.3 2.1 pad_maximum_fusion.rest_0_.refs_0_
  53.5 9.3 %all-to-all-done.1 = bf16[16,128,128]{2,1,0:T(8,128)(2,1)S(1)} async-done(((bf16[16,128,128]{2,1,0:T(8,128)(2,1)}), bf16[16,128,128]{2,1,0:T(8,128)(2,1)S(1)}, u32[]{:S(2)}, u32[]{:S(2)}) %all-to-all-start.1) | async-done | bytes 524320 | tf_op jit(solution)/shard_map/all_to_all | solution.py:757
  63.5 8.9 %middle.1 = (bf16[8,4,256,128]{3,2,1,0:T(8,128)(2,1)}, bf16[256,1024]{1,0:T(8,128)(2,1)S(1)}, bf16[8,256,128]{2,1,0:T(8,128)(2,1)S(1)}, bf16[256,1024]{1,0:T(8,128)(2,1)S(1)}) custom-call(bf16[256,1024]{1,0:T(8,128)(2,1)} %copy-done.12, bf16[8,256,128]{2,1,0:T(8,128)(2,1)} %bitcast.24, bf16[256,1024]{1,0:T(8,128)(2,1)} %reshape.67.cotangent_ref, ...), custom_call_target="tpu_custom_call" | custom-call | flops 2684354560 | bytes 13631488 | tf_op jit(solution)/shard_map/middle/pallas_call | solution.py:314
  74.9 5.6 %all-to-all-start.2 = ((bf16[8,1024,128]{2,1,0:T(8,128)(2,1)}), bf16[8,1024,128]{2,1,0:T(8,128)(2,1)S(1)}, u32[]{:S(2)}, u32[]{:S(2)}) async-start(bf16[8,1024,128]{2,1,0:T(8,128)(2,1)} %bitcast.28), calls=%async_computation.2 | async-start | bytes 4194304 | tf_op jit(solution)/shard_map/all_to_all | solution.py:757
  81.5 24.2 %collective-permute-done.3.rest_1_.refs_3_ = bf16[2,256,1024]{2,1,0:T(8,128)(2,1)S(1)} collective-permute-done((bf16[2,256,1024]{2,1,0:T(8,128)(2,1)S(1)}, bf16[2,256,1024]{2,1,0:T(8,128)(2,1)S(1)}, u32[]{:S(2)}, u32[]{:S(2)}) %collective-permute-start.3) | collective-permute-done | bytes 1048608 | tf_op jit(solution)/shard_map/ppermute | solution.py:487
  107.7 1.2 copy-done.24
  110.1 8.7 %mode_attention.1 = bf16[8,4,256,128]{3,2,1,0:T(8,128)(2,1)S(1)} custom-call(bf16[8,4,256,128]{3,2,1,0:T(8,128)(2,1)S(1)} %bitcast.26, bf16[2,256,1024]{2,1,0:T(8,128)(2,1)S(1)} %copy-done.27, bf16[2,256,1024]{2,1,0:T(8,128)(2,1)S(1)} %copy-done.24), custom_call_target="tpu_custom_call" | custom-call | flops 8000000000 | bytes 4194304 | tf_op jit(solution)/shard_map/mode_attention/pallas_call | solution.py:369
  118.8 1.3 copy-done.14
  120.1 5.3 %all-to-all-start.3 = ((bf16[8,1024,128]{2,1,0:T(8,128)(2,1)}), bf16[8,1024,128]{2,1,0:T(8,128)(2,1)S(1)}, u32[]{:S(2)}, u32[]{:S(2)}) async-start(bf16[8,1024,128]{2,1,0:T(8,128)(2,1)} %bitcast.27), calls=%async_computation.3 | async-start | bytes 4194304 | tf_op jit(solution)/shard_map/all_to_all | solution.py:757
  126.1 23.4 %collective-permute-done.4.rest_0_.refs_2_ = bf16[2,256,1024]{2,1,0:T(8,128)(2,1)} collective-permute-done((bf16[2,256,1024]{2,1,0:T(8,128)(2,1)S(1)}, bf16[2,256,1024]{2,1,0:T(8,128)(2,1)}, u32[]{:S(2)}, u32[]{:S(2)}) %collective-permute-start.4) | collective-permute-done | bytes 1048608 | tf_op jit(solution)/shard_map/ppermute | solution.py:487
  150.3 1.4 copy-done.7
  152.7 5.7 %early_first.1.rest_0_ = bf16[8,256,1024]{2,1,0:T(8,128)(2,1)} custom-call(s32[7]{0:T(128)S(1)} %constant_dynamic-update-slice_fusion.2.ids_ref, bf16[8,256,128]{2,1,0:T(8,128)(2,1)S(1)} %copy-done.16, bf16[8,4,256,128]{3,2,1,0:T(8,128)(2,1)S(1)} %bitcast.19, bf16[8,4,256,128]{3,2,1,0:T(8,128)(2,1)S(1)} %bitcast.20, bf16[256,1024]{1,0:T(8,128)(2,1)S(1)} %copy-done.7, ...), custom_call_target="tpu_custom_call" | custom-call | flops 1000000000 | bytes 5242880 | tf_op jit(solution)/shard_map/early_first/pallas_call | solution.py:495
  158.4 6.7 %turn.1 = (bf16[16,128,128]{2,1,0:T(8,128)(2,1)S(1)}, bf16[256,1024]{1,0:T(8,128)(2,1)S(1)}) custom-call(bf16[8,4,256,128]{3,2,1,0:T(8,128)(2,1)} %bitcast.21, bf16[256,1024]{1,0:T(8,128)(2,1)S(1)} %copy-done.8, bf16[256,1024]{1,0:T(8,128)(2,1)} %copy-done.29, bf16[8,1024,1024]{2,1,0:T(8,128)(2,1)} %w3.7, bf16[8,1024,1024]{2,1,0:T(8,128)(2,1)} %w3.7, ...), custom_call_target="tpu_custom_call" | custom-call | flops 2147483648 | bytes 12582912 | tf_op jit(solution)/shard_map/turn/pallas_call | solution.py:415
  166.7 4.8 %all-to-all-start.4 = ((bf16[16,128,128]{2,1,0:T(8,128)(2,1)}), bf16[16,128,128]{2,1,0:T(8,128)(2,1)}, u32[]{:S(2)}, u32[]{:S(2)}) async-start(bf16[16,128,128]{2,1,0:T(8,128)(2,1)} %copy-done.30), calls=%async_computation.4 | async-start | bytes 1048576 | tf_op jit(solution)/shard_map/all_to_all | solution.py:757
  174.7 8.3 %early_add.1 = (bf16[8,64,1024]{2,1,0:T(8,128)(2,1)S(1)}, bf16[8,64,1024]{2,1,0:T(8,128)(2,1)}, bf16[8,64,1024]{2,1,0:T(8,128)(2,1)}, bf16[8,64,1024]{2,1,0:T(8,128)(2,1)}) custom-call(s32[7]{0:T(128)S(1)} %stack.40.ids_ref, bf16[8,256,128]{2,1,0:T(8,128)(2,1)S(1)} %copy-done.17, bf16[8,4,256,128]{3,2,1,0:T(8,128)(2,1)S(1)} %bitcast.22, ...), custom_call_target="tpu_custom_call" | custom-call | flops 1000000000 | bytes 5242880 | tf_op jit(solution)/shard_map/early_add/pallas_call | solution.py:495
  185.0 2.1 collective-permute-start.7
  187.0 1.4 copy-done.19
  189.7 1.6 copy-done.34
  191.3 7.0 %agent_backward.1.refs_4_.refs_5_ = bf16[16,3,128,128]{3,2,1,0:T(8,128)(2,1)} custom-call(bf16[16,384,128]{2,1,0:T(8,128)(2,1)S(1)} %copy-done.19, bf16[16,384,128]{2,1,0:T(8,128)(2,1)S(1)} %copy-done.19, bf16[16,384,128]{2,1,0:T(8,128)(2,1)S(1)} %copy-done.19, bf16[16,128,128]{2,1,0:T(8,128)(2,1)} %all-to-all-done.4.g, f32[4,4,256,128]{3,2,1,0:T(8,128)S(1)} %copy-done.34, ...), custom_call_target="tpu_custom_call" | custom-call | flops 6000000000 | bytes 6291456 | tf_op jit(solution)/shard_map/agent_backward/pallas_call | solution.py:259
  198.3 11.3 %collective-permute-done.6.refs_8_.refs_1_ = bf16[8,64,1024]{2,1,0:T(8,128)(2,1)S(1)} collective-permute-done((bf16[8,64,1024]{2,1,0:T(8,128)(2,1)}, bf16[8,64,1024]{2,1,0:T(8,128)(2,1)S(1)}, u32[]{:S(2)}, u32[]{:S(2)}) %collective-permute-start.6) | collective-permute-done | bytes 1048608 | tf_op jit(solution)/shard_map/ppermute | solution.py:487
  209.6 2.0 collective-permute-done.7.refs_9_.refs_3_
  211.7 11.0 %late_products.1 = (bf16[2,256,1408]{2,1,0:T(8,128)(2,1)S(1)}, bf16[2,256,1408]{2,1,0:T(8,128)(2,1)}) custom-call(s32[7]{0:T(128)S(1)} %stack.40.ids_ref, bf16[2,256,1024]{2,1,0:T(8,128)(2,1)S(1)} %copy-done.2, bf16[2,256,1024]{2,1,0:T(8,128)(2,1)S(1)} %copy-done.28, bf16[2,256,1024]{2,1,0:T(8,128)(2,1)} %collective-permute-done.4.rest_0_.refs_2_, ...), custom_call_target="tpu_custom_call" | custom-call | flops 1000000000 | bytes 5242880 | tf_op jit(solution)/shard_map/late_products/pallas_call | solution.py:495
  223.8 1.5 collective-permute-start.17
  225.3 7.0 %all-to-all-start.5 = ((bf16[16,384,128]{2,1,0:T(8,128)(2,1)}), bf16[16,384,128]{2,1,0:T(8,128)(2,1)}, u32[]{:S(2)}, u32[]{:S(2)}) async-start(bf16[16,384,128]{2,1,0:T(8,128)(2,1)} %bitcast.16), calls=%async_computation.5 | async-start | bytes 3145728 | tf_op jit(solution)/shard_map/all_to_all | solution.py:757
  232.3 1.4 copy-done.32
  233.7 2.3 late_add.1
  236.0 1.5 collective-permute-start.9
  238.6 2.2 collective-permute-start.11
  240.8 10.7 %collective-permute-done.17.refs_2_ = bf16[8,64,1024]{2,1,0:T(8,128)(2,1)S(1)} collective-permute-done((bf16[8,64,1024]{2,1,0:T(8,128)(2,1)}, bf16[8,64,1024]{2,1,0:T(8,128)(2,1)S(1)}, u32[]{:S(2)}, u32[]{:S(2)}) %collective-permute-start.17) | collective-permute-done | bytes 1048608 | tf_op jit(solution)/shard_map/ppermute | solution.py:487
  251.5 5.9 %early_z.1 = (bf16[8,32,1024]{2,1,0:T(8,128)(2,1)S(1)}, bf16[8,32,1024]{2,1,0:T(8,128)(2,1)}) custom-call(s32[7]{0:T(128)S(1)} %stack.40.ids_ref, bf16[8,64,1024]{2,1,0:T(8,128)(2,1)S(1)} %copy-done.22, bf16[8,64,1024]{2,1,0:T(8,128)(2,1)S(1)} %collective-permute-done.6.refs_8_.refs_1_, bf16[8,64,1024]{2,1,0:T(8,128)(2,1)S(1)} %collective-permute-done.17.refs_2_, ...), custom_call_target="tpu_custom_call" | custom-call | flops 1000000000 | bytes 5242880 | tf_op jit(solution)/shard_map/early_z/pallas_call | solution.py:495
  258.6 7.9 %collective-permute-done.10.refs_2_ = bf16[2,64,1408]{2,1,0:T(8,128)(2,1)S(1)} collective-permute-done((bf16[2,64,1408]{2,1,0:T(8,128)(2,1)S(1)}, bf16[2,64,1408]{2,1,0:T(8,128)(2,1)S(1)}, u32[]{:S(2)}, u32[]{:S(2)}) %collective-permute-start.10) | collective-permute-done | bytes 360480 | tf_op jit(solution)/shard_map/ppermute | solution.py:487
  268.5 5.7 %leave.1.rest_0_ = bf16[256,1024]{1,0:T(8,128)(2,1)S(1)} custom-call(bf16[16,3,128,128]{3,2,1,0:T(8,128)(2,1)} %bitcast.17.returned_ref, bf16[256,1024]{1,0:T(8,128)(2,1)S(1)} %copy-done.13, bf16[256,1024]{1,0:T(8,128)(2,1)S(1)} %copy-done.5, bf16[8,1024,1024]{2,1,0:T(8,128)(2,1)} %w3.7, bf16[8,1024,1024]{2,1,0:T(8,128)(2,1)} %w3.7, ...), custom_call_target="tpu_custom_call" | custom-call | flops 1610612736 | bytes 9437184 | tf_op jit(solution)/shard_map/leave/pallas_call | solution.py:463
  274.9 1.6 collective-permute-start.19
  276.5 2.7 collective-permute-start.20
  280.8 3.9 %collective-permute-start.14 = (bf16[2,32,1152]{2,1,0:T(8,128)(2,1)S(1)}, bf16[2,32,1152]{2,1,0:T(8,128)(2,1)S(1)}, u32[]{:S(2)}, u32[]{:S(2)}) collective-permute-start(bf16[2,32,1152]{2,1,0:T(8,128)(2,1)S(1)} %get-tuple-element.78), channel_id=1, source_target_pairs={{0,64},{8,72},{16,80},{24,88},{32,96},{40,104},{48,112},{56,120},{... | collective-permute-start | bytes 442376 | tf_op jit(solution)/shard_map/ppermute | solution.py:487
  286.1 1.4 collective-permute-done.21.refs_3_
  288.1 3.7 %collective-permute-start.22 = (bf16[32,1024]{1,0:T(8,128)(2,1)S(1)}, bf16[32,1024]{1,0:T(8,128)(2,1)S(1)}, u32[]{:S(2)}, u32[]{:S(2)}) collective-permute-start(bf16[32,1024]{1,0:T(8,128)(2,1)S(1)} %get-tuple-element.90), channel_id=1, source_target_pairs={{0,16},{8,24},{16,0},{24,8},{32,48},{40,56},{48,32},{56,40},{64,80... | collective-permute-start | bytes 196616 | tf_op jit(solution)/shard_map/ppermute | solution.py:487
  291.7 1.4 collective-permute-done.15.refs_3_
  293.7 3.7 %collective-permute-start.16 = (bf16[4,32,384]{2,1,0:T(8,128)(2,1)S(1)}, bf16[4,32,384]{2,1,0:T(8,128)(2,1)S(1)}, u32[]{:S(2)}, u32[]{:S(2)}) collective-permute-start(bf16[4,32,384]{2,1,0:T(8,128)(2,1)S(1)} %get-tuple-element.81), channel_id=1, source_target_pairs={{0,16},{8,24},{16,0},{24,8},{32,48},{40,56},{48,32},{56,40},{64,80... | collective-permute-start | bytes 294920 | tf_op jit(solution)/shard_map/ppermute | solution.py:487
  298.1 1.9 collective-permute-done.16.arrived_ref
  300.0 1.2 late_last.1
  (113 shorter events, 33.2 us)
Async XLA Ops:
  9.4 7.7 %copy-start.36 = (s32[128]{0:T(128)S(1)}, s32[128]{0:T(128)}, u32[]{:S(2)}) copy-start(s32[128]{0:T(128)} %param.9) | copy-start | bytes 1540
  9.4 30.9 %all-to-all-start = ((bf16[16,384,128]{2,1,0:T(8,128)(2,1)}), bf16[16,384,128]{2,1,0:T(8,128)(2,1)S(1)}, u32[]{:S(2)}, u32[]{:S(2)}) async-start(bf16[16,384,128]{2,1,0:T(8,128)(2,1)} %get-tuple-element.53), calls=%async_computation | async-start | bytes 3145728 | tf_op jit(solution)/shard_map/all_to_all | solution.py:757
  16.7 1.6 collective-permute-start
  18.3 32.1 %copy-start.35 = (bf16[8,8,4,1024]{3,2,1,0:T(4,128)(2,1)S(1)}, bf16[8,8,4,1024]{3,2,1,0:T(4,128)(2,1)}, u32[]{:S(2)}) copy-start(bf16[8,8,4,1024]{3,2,1,0:T(4,128)(2,1)} %param.7) | copy-start | bytes 1572868
  18.3 33.0 %collective-permute-start.1 = (bf16[256,1024]{1,0:T(8,128)(2,1)S(1)}, bf16[256,1024]{1,0:T(8,128)(2,1)}, u32[]{:S(2)}, u32[]{:S(2)}) collective-permute-start(bf16[256,1024]{1,0:T(8,128)(2,1)S(1)} %constant_dynamic-update-slice_fusion), channel_id=1, source_target_pairs={{0,16},{8,24},{16,0},{24,8},{32,48},{40,56},{48,32},{56,40},{64,80... | collective-permute-start | bytes 1572872 | tf_op jit(solution)/shard_map/ppermute | solution.py:487
  40.3 4.5 %copy-start.18 = (bf16[16,384,128]{2,1,0:T(8,128)(2,1)}, bf16[16,384,128]{2,1,0:T(8,128)(2,1)S(1)}, u32[]{:S(2)}) copy-start(bf16[16,384,128]{2,1,0:T(8,128)(2,1)S(1)} %all-to-all-done.query_ref.keys_ref.values_ref.q.k.v) | copy-start | bytes 4718596
  44.8 1.3 copy-start.33
  46.1 16.6 %all-to-all-start.1 = ((bf16[16,128,128]{2,1,0:T(8,128)(2,1)}), bf16[16,128,128]{2,1,0:T(8,128)(2,1)S(1)}, u32[]{:S(2)}, u32[]{:S(2)}) async-start(bf16[16,128,128]{2,1,0:T(8,128)(2,1)} %get-tuple-element.55), calls=%async_computation.1 | async-start | bytes 1048576 | tf_op jit(solution)/shard_map/all_to_all | solution.py:757
  74.9 5.6 %copy-start.2 = (bf16[2,256,1024]{2,1,0:T(8,128)(2,1)S(1)}, bf16[2,256,1024]{2,1,0:T(8,128)(2,1)}, u32[]{:S(2)}) copy-start(bf16[2,256,1024]{2,1,0:T(8,128)(2,1)} %pad_maximum_fusion.rest_0_.refs_0_) | copy-start | bytes 3145732
  74.9 32.8 %all-to-all-start.2 = ((bf16[8,1024,128]{2,1,0:T(8,128)(2,1)}), bf16[8,1024,128]{2,1,0:T(8,128)(2,1)S(1)}, u32[]{:S(2)}, u32[]{:S(2)}) async-start(bf16[8,1024,128]{2,1,0:T(8,128)(2,1)} %bitcast.28), calls=%async_computation.2 | async-start | bytes 4194304 | tf_op jit(solution)/shard_map/all_to_all | solution.py:757
  80.4 25.3 %collective-permute-start.3 = (bf16[2,256,1024]{2,1,0:T(8,128)(2,1)S(1)}, bf16[2,256,1024]{2,1,0:T(8,128)(2,1)S(1)}, u32[]{:S(2)}, u32[]{:S(2)}) collective-permute-start(bf16[2,256,1024]{2,1,0:T(8,128)(2,1)S(1)} %copy-done.2), channel_id=1, source_target_pairs={{0,96},{8,104},{16,112},{24,120},{32,64},{40,72},{48,80},{56,88},{... | collective-permute-start | bytes 3145736 | tf_op jit(solution)/shard_map/ppermute | solution.py:487
  81.4 25.3 %collective-permute-start.2 = (bf16[2,256,1024]{2,1,0:T(8,128)(2,1)S(1)}, bf16[2,256,1024]{2,1,0:T(8,128)(2,1)S(1)}, u32[]{:S(2)}, u32[]{:S(2)}) collective-permute-start(bf16[2,256,1024]{2,1,0:T(8,128)(2,1)S(1)} %copy-done.2), channel_id=1, source_target_pairs={{0,32},{8,40},{16,48},{24,56},{32,0},{40,8},{48,16},{56,24},{64,96... | collective-permute-start | bytes 3145736 | tf_op jit(solution)/shard_map/ppermute | solution.py:487
  118.8 1.3 copy-start.14
  120.1 30.1 %all-to-all-start.3 = ((bf16[8,1024,128]{2,1,0:T(8,128)(2,1)}), bf16[8,1024,128]{2,1,0:T(8,128)(2,1)S(1)}, u32[]{:S(2)}, u32[]{:S(2)}) async-start(bf16[8,1024,128]{2,1,0:T(8,128)(2,1)} %bitcast.27), calls=%async_computation.3 | async-start | bytes 4194304 | tf_op jit(solution)/shard_map/all_to_all | solution.py:757
  125.5 24.1 %collective-permute-start.4 = (bf16[2,256,1024]{2,1,0:T(8,128)(2,1)S(1)}, bf16[2,256,1024]{2,1,0:T(8,128)(2,1)}, u32[]{:S(2)}, u32[]{:S(2)}) collective-permute-start(bf16[2,256,1024]{2,1,0:T(8,128)(2,1)S(1)} %copy-done.2), channel_id=1, source_target_pairs={{0,64},{8,72},{16,80},{24,88},{32,96},{40,104},{48,112},{56,120},{... | collective-permute-start | bytes 3145736 | tf_op jit(solution)/shard_map/ppermute | solution.py:487
  150.3 8.1 %copy-start = (bf16[8,1024,128]{2,1,0:T(8,128)(2,1)}, bf16[8,1024,128]{2,1,0:T(8,128)(2,1)S(1)}, u32[]{:S(2)}) copy-start(bf16[8,1024,128]{2,1,0:T(8,128)(2,1)S(1)} %all-to-all-done.3) | copy-start | bytes 6291460
  150.3 1.4 copy-start.7
  152.7 5.7 %copy-start.8 = (bf16[256,1024]{1,0:T(8,128)(2,1)S(1)}, bf16[256,1024]{1,0:T(8,128)(2,1)}, u32[]{:S(2)}) copy-start(bf16[256,1024]{1,0:T(8,128)(2,1)} %copy-done.6) | copy-start | bytes 1572868
  158.4 13.2 %collective-permute-start.5 = (bf16[8,256,1024]{2,1,0:T(8,128)(2,1)}, bf16[8,256,1024]{2,1,0:T(8,128)(2,1)}, u32[]{:S(2)}, u32[]{:S(2)}) collective-permute-start(bf16[8,256,1024]{2,1,0:T(8,128)(2,1)} %early_first.1.rest_0_), channel_id=1, source_target_pairs={{0,8},{8,0},{16,24},{24,16},{32,40},{40,32},{48,56},{56,48},{64,72... | collective-permute-start | bytes 12582920 | tf_op jit(solution)/shard_map/ppermute | solution.py:487
  158.4 13.2 %copy-start.1 = (bf16[8,1024,128]{2,1,0:T(8,128)(2,1)S(1)}, bf16[8,1024,128]{2,1,0:T(8,128)(2,1)}, u32[]{:S(2)}) copy-start(bf16[8,1024,128]{2,1,0:T(8,128)(2,1)} %copy-done) | copy-start | bytes 6291460
  166.7 20.3 %all-to-all-start.4 = ((bf16[16,128,128]{2,1,0:T(8,128)(2,1)}), bf16[16,128,128]{2,1,0:T(8,128)(2,1)}, u32[]{:S(2)}, u32[]{:S(2)}) async-start(bf16[16,128,128]{2,1,0:T(8,128)(2,1)} %copy-done.30), calls=%async_computation.4 | async-start | bytes 1048576 | tf_op jit(solution)/shard_map/all_to_all | solution.py:757
  184.0 25.6 %collective-permute-start.6 = (bf16[8,64,1024]{2,1,0:T(8,128)(2,1)}, bf16[8,64,1024]{2,1,0:T(8,128)(2,1)S(1)}, u32[]{:S(2)}, u32[]{:S(2)}) collective-permute-start(bf16[8,64,1024]{2,1,0:T(8,128)(2,1)} %get-tuple-element.66), channel_id=1, source_target_pairs={{0,2},{1,3},{2,0},{3,1},{4,6},{5,7},{6,4},{7,5},{8,10},{9,11},{10,... | collective-permute-start | bytes 3145736 | tf_op jit(solution)/shard_map/ppermute | solution.py:487
  185.0 26.7 %collective-permute-start.7 = (bf16[8,64,1024]{2,1,0:T(8,128)(2,1)}, bf16[8,64,1024]{2,1,0:T(8,128)(2,1)}, u32[]{:S(2)}, u32[]{:S(2)}) collective-permute-start(bf16[8,64,1024]{2,1,0:T(8,128)(2,1)} %get-tuple-element.67), channel_id=1, source_target_pairs={{0,6},{1,7},{2,4},{3,5},{4,2},{5,3},{6,0},{7,1},{8,14},{9,15},{10,... | collective-permute-start | bytes 3145736 | tf_op jit(solution)/shard_map/ppermute | solution.py:487
  187.0 1.4 copy-start.19
  189.7 1.6 copy-start.34
  191.3 20.4 %copy-start.5 = (bf16[256,1024]{1,0:T(8,128)(2,1)S(1)}, bf16[256,1024]{1,0:T(8,128)(2,1)}, u32[]{:S(2)}) copy-start(bf16[256,1024]{1,0:T(8,128)(2,1)} %copy-done.3) | copy-start | bytes 1572868
  191.3 20.4 %copy-start.11 = (bf16[16,128,128]{2,1,0:T(8,128)(2,1)S(1)}, bf16[16,128,128]{2,1,0:T(8,128)(2,1)}, u32[]{:S(2)}) copy-start(bf16[16,128,128]{2,1,0:T(8,128)(2,1)} %copy-done.10) | copy-start | bytes 1572868
  191.3 20.4 %copy-start.25 = (bf16[2,256,1024]{2,1,0:T(8,128)(2,1)S(1)}, bf16[2,256,1024]{2,1,0:T(8,128)(2,1)}, u32[]{:S(2)}) copy-start(bf16[2,256,1024]{2,1,0:T(8,128)(2,1)} %copy-done.23) | copy-start | bytes 3145732
  191.3 20.4 %copy-start.28 = (bf16[2,256,1024]{2,1,0:T(8,128)(2,1)S(1)}, bf16[2,256,1024]{2,1,0:T(8,128)(2,1)}, u32[]{:S(2)}) copy-start(bf16[2,256,1024]{2,1,0:T(8,128)(2,1)} %copy-done.26) | copy-start | bytes 3145732
  223.8 8.5 %collective-permute-start.8 = (bf16[2,256,1408]{2,1,0:T(8,128)(2,1)}, bf16[2,256,1408]{2,1,0:T(8,128)(2,1)}, u32[]{:S(2)}, u32[]{:S(2)}) collective-permute-start(bf16[2,256,1408]{2,1,0:T(8,128)(2,1)} %get-tuple-element.69), channel_id=1, source_target_pairs={{0,8},{8,0},{16,24},{24,16},{32,40},{40,32},{48,56},{56,48},{64,72... | collective-permute-start | bytes 4325384 | tf_op jit(solution)/shard_map/ppermute | solution.py:487
  223.8 27.7 %collective-permute-start.17 = (bf16[8,64,1024]{2,1,0:T(8,128)(2,1)}, bf16[8,64,1024]{2,1,0:T(8,128)(2,1)S(1)}, u32[]{:S(2)}, u32[]{:S(2)}) collective-permute-start(bf16[8,64,1024]{2,1,0:T(8,128)(2,1)} %get-tuple-element.82), channel_id=1, source_target_pairs={{0,4},{1,5},{2,6},{3,7},{4,0},{5,1},{6,2},{7,3},{8,12},{9,13},{10,... | collective-permute-start | bytes 3145736 | tf_op jit(solution)/shard_map/ppermute | solution.py:487
  225.3 43.2 %all-to-all-start.5 = ((bf16[16,384,128]{2,1,0:T(8,128)(2,1)}), bf16[16,384,128]{2,1,0:T(8,128)(2,1)}, u32[]{:S(2)}, u32[]{:S(2)}) async-start(bf16[16,384,128]{2,1,0:T(8,128)(2,1)} %bitcast.16), calls=%async_computation.5 | async-start | bytes 3145728 | tf_op jit(solution)/shard_map/all_to_all | solution.py:757
  232.3 19.2 %copy-start.22 = (bf16[8,64,1024]{2,1,0:T(8,128)(2,1)S(1)}, bf16[8,64,1024]{2,1,0:T(8,128)(2,1)}, u32[]{:S(2)}) copy-start(bf16[8,64,1024]{2,1,0:T(8,128)(2,1)} %copy-done.20) | copy-start | bytes 3145732
  232.3 1.4 copy-start.32
  236.0 22.6 %collective-permute-start.9 = (bf16[2,64,1408]{2,1,0:T(8,128)(2,1)S(1)}, bf16[2,64,1408]{2,1,0:T(8,128)(2,1)S(1)}, u32[]{:S(2)}, u32[]{:S(2)}) collective-permute-start(bf16[2,64,1408]{2,1,0:T(8,128)(2,1)S(1)} %get-tuple-element.71), channel_id=1, source_target_pairs={{0,2},{1,3},{2,0},{3,1},{4,6},{5,7},{6,4},{7,5},{8,10},{9,11},{10,... | collective-permute-start | bytes 1081352 | tf_op jit(solution)/shard_map/ppermute | solution.py:487
  237.6 29.0 %collective-permute-start.10 = (bf16[2,64,1408]{2,1,0:T(8,128)(2,1)S(1)}, bf16[2,64,1408]{2,1,0:T(8,128)(2,1)S(1)}, u32[]{:S(2)}, u32[]{:S(2)}) collective-permute-start(bf16[2,64,1408]{2,1,0:T(8,128)(2,1)S(1)} %get-tuple-element.72), channel_id=1, source_target_pairs={{0,4},{1,5},{2,6},{3,7},{4,0},{5,1},{6,2},{7,3},{8,12},{9,13},{10,... | collective-permute-start | bytes 1081352 | tf_op jit(solution)/shard_map/ppermute | solution.py:487
  238.6 27.9 %collective-permute-start.11 = (bf16[2,64,1408]{2,1,0:T(8,128)(2,1)S(1)}, bf16[2,64,1408]{2,1,0:T(8,128)(2,1)S(1)}, u32[]{:S(2)}, u32[]{:S(2)}) collective-permute-start(bf16[2,64,1408]{2,1,0:T(8,128)(2,1)S(1)} %get-tuple-element.73), channel_id=1, source_target_pairs={{0,6},{1,7},{2,4},{3,5},{4,2},{5,3},{6,0},{7,1},{8,14},{9,15},{10,... | collective-permute-start | bytes 1081352 | tf_op jit(solution)/shard_map/ppermute | solution.py:487
  257.4 11.1 %copy-start.13 = (bf16[256,1024]{1,0:T(8,128)(2,1)S(1)}, bf16[256,1024]{1,0:T(8,128)(2,1)}, u32[]{:S(2)}) copy-start(bf16[256,1024]{1,0:T(8,128)(2,1)} %copy-done.12) | copy-start | bytes 1572868
  257.4 16.8 %collective-permute-start.18 = (bf16[8,32,1024]{2,1,0:T(8,128)(2,1)}, bf16[8,32,1024]{2,1,0:T(8,128)(2,1)S(1)}, u32[]{:S(2)}, u32[]{:S(2)}) collective-permute-start(bf16[8,32,1024]{2,1,0:T(8,128)(2,1)} %get-tuple-element.84), channel_id=1, source_target_pairs={{0,1},{1,0},{2,3},{3,2},{4,5},{5,4},{6,7},{7,6},{8,9},{9,8},{10,11... | collective-permute-start | bytes 1572872 | tf_op jit(solution)/shard_map/ppermute | solution.py:487
  267.4 12.2 %collective-permute-start.12 = (bf16[2,32,1408]{2,1,0:T(8,128)(2,1)S(1)}, bf16[2,32,1408]{2,1,0:T(8,128)(2,1)S(1)}, u32[]{:S(2)}, u32[]{:S(2)}) collective-permute-start(bf16[2,32,1408]{2,1,0:T(8,128)(2,1)S(1)} %get-tuple-element.75), channel_id=1, source_target_pairs={{0,1},{1,0},{2,3},{3,2},{4,5},{5,4},{6,7},{7,6},{8,9},{9,8},{10,11... | collective-permute-start | bytes 540680 | tf_op jit(solution)/shard_map/ppermute | solution.py:487
  274.9 9.8 %collective-permute-start.19 = (bf16[2,32,1024]{2,1,0:T(8,128)(2,1)S(1)}, bf16[2,32,1024]{2,1,0:T(8,128)(2,1)S(1)}, u32[]{:S(2)}, u32[]{:S(2)}) collective-permute-start(bf16[2,32,1024]{2,1,0:T(8,128)(2,1)S(1)} %get-tuple-element.86), channel_id=1, source_target_pairs={{0,32},{8,40},{16,48},{24,56},{32,0},{40,8},{48,16},{56,24},{64,96... | collective-permute-start | bytes 393224 | tf_op jit(solution)/shard_map/ppermute | solution.py:487
  276.5 9.5 %collective-permute-start.20 = (bf16[2,32,1024]{2,1,0:T(8,128)(2,1)S(1)}, bf16[2,32,1024]{2,1,0:T(8,128)(2,1)S(1)}, u32[]{:S(2)}, u32[]{:S(2)}) collective-permute-start(bf16[2,32,1024]{2,1,0:T(8,128)(2,1)S(1)} %get-tuple-element.87), channel_id=1, source_target_pairs={{0,64},{8,72},{16,80},{24,88},{32,96},{40,104},{48,112},{56,120},{... | collective-permute-start | bytes 393224 | tf_op jit(solution)/shard_map/ppermute | solution.py:487
  279.2 8.2 %collective-permute-start.21 = (bf16[2,32,1024]{2,1,0:T(8,128)(2,1)S(1)}, bf16[2,32,1024]{2,1,0:T(8,128)(2,1)S(1)}, u32[]{:S(2)}, u32[]{:S(2)}) collective-permute-start(bf16[2,32,1024]{2,1,0:T(8,128)(2,1)S(1)} %get-tuple-element.88), channel_id=1, source_target_pairs={{0,96},{8,104},{16,112},{24,120},{32,64},{40,72},{48,80},{56,88},{... | collective-permute-start | bytes 393224 | tf_op jit(solution)/shard_map/ppermute | solution.py:487
  280.3 11.4 %collective-permute-start.13 = (bf16[2,32,1152]{2,1,0:T(8,128)(2,1)S(1)}, bf16[2,32,1152]{2,1,0:T(8,128)(2,1)S(1)}, u32[]{:S(2)}, u32[]{:S(2)}) collective-permute-start(bf16[2,32,1152]{2,1,0:T(8,128)(2,1)S(1)} %get-tuple-element.77), channel_id=1, source_target_pairs={{0,32},{8,40},{16,48},{24,56},{32,0},{40,8},{48,16},{56,24},{64,96... | collective-permute-start | bytes 442376 | tf_op jit(solution)/shard_map/ppermute | solution.py:487
  280.8 11.0 %collective-permute-start.14 = (bf16[2,32,1152]{2,1,0:T(8,128)(2,1)S(1)}, bf16[2,32,1152]{2,1,0:T(8,128)(2,1)S(1)}, u32[]{:S(2)}, u32[]{:S(2)}) collective-permute-start(bf16[2,32,1152]{2,1,0:T(8,128)(2,1)S(1)} %get-tuple-element.78), channel_id=1, source_target_pairs={{0,64},{8,72},{16,80},{24,88},{32,96},{40,104},{48,112},{56,120},{... | collective-permute-start | bytes 442376 | tf_op jit(solution)/shard_map/ppermute | solution.py:487
  284.7 8.5 %collective-permute-start.15 = (bf16[2,32,1152]{2,1,0:T(8,128)(2,1)S(1)}, bf16[2,32,1152]{2,1,0:T(8,128)(2,1)S(1)}, u32[]{:S(2)}, u32[]{:S(2)}) collective-permute-start(bf16[2,32,1152]{2,1,0:T(8,128)(2,1)S(1)} %get-tuple-element.79), channel_id=1, source_target_pairs={{0,96},{8,104},{16,112},{24,120},{32,64},{40,72},{48,80},{56,88},{... | collective-permute-start | bytes 442376 | tf_op jit(solution)/shard_map/ppermute | solution.py:487
  288.1 9.3 %collective-permute-start.22 = (bf16[32,1024]{1,0:T(8,128)(2,1)S(1)}, bf16[32,1024]{1,0:T(8,128)(2,1)S(1)}, u32[]{:S(2)}, u32[]{:S(2)}) collective-permute-start(bf16[32,1024]{1,0:T(8,128)(2,1)S(1)} %get-tuple-element.90), channel_id=1, source_target_pairs={{0,16},{8,24},{16,0},{24,8},{32,48},{40,56},{48,32},{56,40},{64,80... | collective-permute-start | bytes 196616 | tf_op jit(solution)/shard_map/ppermute | solution.py:487
  293.7 6.3 %collective-permute-start.16 = (bf16[4,32,384]{2,1,0:T(8,128)(2,1)S(1)}, bf16[4,32,384]{2,1,0:T(8,128)(2,1)S(1)}, u32[]{:S(2)}, u32[]{:S(2)}) collective-permute-start(bf16[4,32,384]{2,1,0:T(8,128)(2,1)S(1)} %get-tuple-element.81), channel_id=1, source_target_pairs={{0,16},{8,24},{16,0},{24,8},{32,48},{40,56},{48,32},{56,40},{64,80... | collective-permute-start | bytes 294920 | tf_op jit(solution)/shard_map/ppermute | solution.py:487
  (18 other events, 17.6 us)

commit v3 on v2

--- a/solution.py
+++ b/solution.py
@@ -520,8 +520,15 @@
         if add:
             arrived_ref, total_ref = rest[0], rest[-1]
             total_ref[...] = product + arrived_ref[0].astype(F32)
-            for partner, out_ref in enumerate(rest[-5:-1]):
-                out_ref[0] = rows_of(total_ref, (ids_ref[Z] ^ partner) * 64, 64).astype(BF)
+            for columns in range(2):
+                for give in range(2):
+                    out_ref = rest[2 * columns + give - 5]
+                    near, far = ((0, 3), (1, 2))[give] if columns == 0 else ((0, 1), (3, 2))[give]
+                    for place, partner in enumerate((near, far)):
+                        rows = rows_of(total_ref, (ids_ref[Z] ^ partner) * 64, 64)
+                        out_ref[0, 64 * place : 64 * place + 64] = rows[
+                            :, 512 * columns : 512 * columns + 512
+                        ].astype(BF)
         else:
             rest[-1][0] = product.astype(BF)
 
@@ -556,8 +563,8 @@
     return prefetched(
         functools.partial(early_kernel, True), ids, operands + [arrived, *waits],
         in_specs + [pl.BlockSpec((1, ROWS, D), lambda i, c: (i, 0, 0))] + [unused] * len(waits),
-        [pl.BlockSpec((1, 64, D), lambda i, c: (i, 0, 0))] * 4,
-        [jax.ShapeDtypeStruct((8, 64, D), BF)] * 4, "early_add", (8,),
+        [pl.BlockSpec((1, 128, 512), lambda i, c: (i, 0, 0))] * 4,
+        [jax.ShapeDtypeStruct((8, 128, 512), BF)] * 4, "early_add", (8,),
         [pltpu.VMEM((ROWS, D), F32)],
     )
 
@@ -569,15 +576,16 @@
         total += ref[0].astype(F32)
     total_ref[...] = total
     share = total_ref.shape[0] // count
-    for partner, out_ref in enumerate(refs[inputs:-1]):
+    for partner, out_ref in enumerate(refs[-1 - count : -1]):
         out_ref[0] = rows_of(total_ref, (ids_ref[split] ^ partner) * share, share).astype(BF)
 
 
-def sum_split(ids, parts, split, count, name):
+def sum_split(ids, parts, split, count, name, waits=()):
     blocks, rows, columns = parts[0].shape
     return prefetched(
-        functools.partial(sum_split_kernel, split, count, len(parts)), ids, parts,
-        [pl.BlockSpec((1, rows, columns), lambda i, c: (i, 0, 0))] * len(parts),
+        functools.partial(sum_split_kernel, split, count, len(parts)), ids, [*parts, *waits],
+        [pl.BlockSpec((1, rows, columns), lambda i, c: (i, 0, 0))] * len(parts)
+        + [unused] * len(waits),
         [pl.BlockSpec((1, rows // count, columns), lambda i, c: (i, 0, 0))] * count,
         [jax.ShapeDtypeStruct((blocks, rows // count, columns), BF)] * count, name, (blocks,),
         [pltpu.VMEM((rows, columns), F32)],
@@ -600,18 +608,55 @@
         out_ref[...] = total.astype(BF)
 
 
-def early_sums(ids, parts, waits):
-    keep, give = sum_split(ids, parts, YLO, 2, "early_z")
+def early_half_kernel(ids_ref, left_ref, left_in, right_ref, right_in, own_ref, *outs):
+    for columns, (ref, arrived) in enumerate(((left_ref, left_in), (right_ref, right_in))):
+        total = (ref[0].astype(F32) + arrived[0].astype(F32)).astype(BF)
+        own_ref[0, :, 512 * columns : 512 * columns + 512] = total[:64]
+        outs[columns][0] = total[64:]
+
+
+def early_half(ids, parts):
+    left, left_give, right, right_give = parts
+    operands = [left, swap(left_give, "mode", 2), right, swap(right_give, "mode", 6)]
+    narrow = pl.BlockSpec((1, 64, 512), lambda i, c: (i, 0, 0))
+    return prefetched(
+        early_half_kernel, ids, operands,
+        [pl.BlockSpec((1, 128, 512), lambda i, c: (i, 0, 0))] * 4,
+        [pl.BlockSpec((1, 64, D), lambda i, c: (i, 0, 0)), narrow, narrow],
+        [jax.ShapeDtypeStruct((8, 64, D), BF)] + [jax.ShapeDtypeStruct((8, 64, 512), BF)] * 2,
+        "early_half", (8,),
+    )
+
+
+def early_z_kernel(ids_ref, own_ref, left_ref, right_ref, keep_ref, give_ref):
+    for other, out_ref in enumerate((keep_ref, give_ref)):
+        first = pl.multiple_of((ids_ref[YLO] ^ other) * 32, 32)
+        for columns, ref in enumerate((left_ref, right_ref)):
+            lanes = slice(512 * columns, 512 * columns + 512)
+            out_ref[:, :, lanes] = (
+                own_ref[:, pl.ds(first, 32), lanes].astype(F32)
+                + ref[:, pl.ds(first, 32), :].astype(F32)
+            ).astype(BF)
+
+
+def early_sums(ids, own, left, right, waits):
+    narrow = pl.BlockSpec((2, 64, 512), lambda i, c: (i, 0, 0))
+    keep, give = prefetched(
+        early_z_kernel, ids, [own, left, right],
+        [pl.BlockSpec((2, 64, D), lambda i, c: (i, 0, 0)), narrow, narrow],
+        [pl.BlockSpec((2, 32, D), lambda i, c: (i, 0, 0))] * 2,
+        [jax.ShapeDtypeStruct((8, 32, D), BF)] * 2, "early_z", (4,),
+    )
     arrived = swap(give, "mode", 1)
-    whole = pl.BlockSpec(memory_space=pltpu.VMEM)
     parts = prefetched(
         early_chips_kernel, ids, [keep, arrived, *waits],
-        [whole] * 2 + [unused] * len(waits), [whole] * 4,
-        [jax.ShapeDtypeStruct((2, 32, D), BF)] * 4, "early_chips",
+        [fixed((8, 32, D))] * 2 + [unused] * len(waits), [fixed((2, 32, D))] * 4,
+        [jax.ShapeDtypeStruct((2, 32, D), BF)] * 4, "early_chips", (1,),
     )
     keep, give = prefetched(
-        early_last_kernel, ids, swap_all(parts, "agent", 4), [whole] * 4, [whole] * 2,
-        [jax.ShapeDtypeStruct((32, D), BF)] * 2, "early_last",
+        early_last_kernel, ids, swap_all(parts, "agent", 4),
+        [fixed((2, 32, D))] * 4, [fixed((32, D))] * 2,
+        [jax.ShapeDtypeStruct((32, D), BF)] * 2, "early_last", (1,),
     )
     return keep.astype(F32) + swap(give, "agent", 2).astype(F32)
 
@@ -626,10 +671,10 @@
 
 
 def late_kernel(ids_ref, *refs):
-    hiddens, first_ref, second_ref, mixed_ref, after_ref, mine_ref, theirs_ref, total_ref = (
+    hiddens, first_ref, second_ref, mixed_ref, after_ref, mine_ref, *theirs_refs, total_ref = (
         refs[:4],
         *refs[4:8],
-        *refs[-3:],
+        *refs[-4:],
     )
     step = pl.program_id(0)
     core = ids_ref[CORE]
@@ -666,8 +711,8 @@
 
             @pl.when(core != block % 2)
             def _():
-                theirs_ref[block // 2, :, :384] = rows
-                theirs_ref[block // 2, :, 384:] = other
+                theirs_refs[block // 2][:, :384] = rows
+                theirs_refs[block // 2][:, 384:] = other
 
 
 def late_products(ids, hiddens, grads, mixed, grad_after, waits):
@@ -690,8 +735,10 @@
     return prefetched(
         late_kernel, ids, list(hiddens) + [grads, grads, mixed, grad_after, *waits],
         in_specs + [unused] * len(waits),
-        [pl.BlockSpec((2, ROWS, WIDE), lambda i, c: (0, 0, 0))] * 2,
-        [jax.ShapeDtypeStruct((2, ROWS, WIDE), BF)] * 2, "late_products", (12,),
+        [pl.BlockSpec((2, ROWS, WIDE), lambda i, c: (0, 0, 0))]
+        + [pl.BlockSpec((ROWS, WIDE), lambda i, c: (0, 0))] * 2,
+        [jax.ShapeDtypeStruct((2, ROWS, WIDE), BF)]
+        + [jax.ShapeDtypeStruct((ROWS, WIDE), BF)] * 2, "late_products", (12,),
         [pltpu.VMEM((384, D), F32)],
     )
 
@@ -734,22 +781,39 @@
             ) + arrived_ref[partner, :, 128:].astype(F32)
 
 
-def late_sums(ids, mine, theirs):
-    whole = pl.BlockSpec(memory_space=pltpu.VMEM)
-    parts = sum_split(ids, [mine, swap(theirs, "agent", 1)], Z, 4, "late_add")
+def late_add_kernel(ids_ref, mine_ref, first_ref, second_ref, *rest):
+    total_ref = rest[-1]
+    for block, ref in enumerate((first_ref, second_ref)):
+        total_ref[...] = mine_ref[block].astype(F32) + ref[...].astype(F32)
+        for partner, out_ref in enumerate(rest[-5:-1]):
+            out_ref[block] = rows_of(total_ref, (ids_ref[Z] ^ partner) * 64, 64).astype(BF)
+
+
+def late_sums(ids, mine, first, second, waits):
+    parts = prefetched(
+        late_add_kernel, ids,
+        [mine, swap(first, "agent", 1), swap(second, "agent", 1), *waits],
+        [fixed((2, ROWS, WIDE))] + [fixed((ROWS, WIDE))] * 2 + [unused] * len(waits),
+        [fixed((2, 64, WIDE))] * 4,
+        [jax.ShapeDtypeStruct((2, 64, WIDE), BF)] * 4, "late_add", (1,),
+        [pltpu.VMEM((ROWS, WIDE), F32)],
+    )
     keep, give = sum_split(ids, swap_all(parts, "mode", 2), YLO, 2, "late_z")
     parts = prefetched(
-        late_chips_kernel, ids, [keep, swap(give, "mode", 1)], [whole] * 2, [whole] * 4,
-        [jax.ShapeDtypeStruct((2, 32, 128 + D), BF)] * 4, "late_chips", (),
+        late_chips_kernel, ids, [keep, swap(give, "mode", 1)],
+        [fixed((2, 32, WIDE))] * 2, [fixed((2, 32, 128 + D))] * 4,
+        [jax.ShapeDtypeStruct((2, 32, 128 + D), BF)] * 4, "late_chips", (1,),
         [pltpu.VMEM((2, 32, WIDE), F32)],
     )
     keep, give = prefetched(
-        late_turn_kernel, ids, swap_all(parts, "agent", 4), [whole] * 4, [whole] * 2,
-        [jax.ShapeDtypeStruct((4, 32, 384), BF)] * 2, "late_turn",
+        late_turn_kernel, ids, swap_all(parts, "agent", 4),
+        [fixed((2, 32, 128 + D))] * 4, [fixed((4, 32, 384))] * 2,
+        [jax.ShapeDtypeStruct((4, 32, 384), BF)] * 2, "late_turn", (1,),
     )
     return prefetched(
-        late_last_kernel, ids, [keep, swap(give, "agent", 2)], [whole] * 2, whole,
-        jax.ShapeDtypeStruct((32, D), F32), "late_last",
+        late_last_kernel, ids, [keep, swap(give, "agent", 2)],
+        [fixed((4, 32, 384))] * 2, fixed((32, D)),
+        jax.ShapeDtypeStruct((32, D), F32), "late_last", (1,),
     )
 
 
@@ -781,16 +845,19 @@
     returned_two = exchange(returning.reshape(8, 1024, 128), "mode").reshape(8, 4, ROWS, 128)
     early = (hidden_two, returned_two, cotangent_m)
     theirs = early_products(other_ids, *early, None, hiddens[2:3])
-    outgoing, grad_after = turn(returned_two, cotangent_m, after, weights, [theirs])
-    parts = early_products(ids, *early, swap(theirs, "agent", 1), [grad_after])
+    parts = early_products(ids, *early, swap(theirs, "agent", 1))
+    outgoing, grad_after = turn(returned_two, cotangent_m, after, weights, parts[:1])
     upstream = exchange(outgoing, "agent")
-    returning = agent_backward(arrived_one, upstream, tables, parts[:1])
-    parts = swap_all(parts, "mode", 2)
+    own, left, right = early_half(ids, parts)
+    returning = agent_backward(arrived_one, upstream, tables, [own])
+    left, right = swap(left, "mode", 6), swap(right, "mode", 2)
     returned_one = exchange(returning.reshape(16, 384, 128), "agent").reshape(16, 3, 128, 128)
-    late_parts = late_products(ids, hiddens, returning, mixed_one, grad_after, parts[1::2])
+    late_parts = late_products(
+        ids, hiddens, returning, mixed_one, grad_after, [left, right]
+    )
     token_grads = leave(returned_one, tokens_a, grad_after, weights)
-    agent_weight_grads = late_sums(ids, *late_parts)
-    mode_weight_grads = early_sums(ids, parts, [token_grads])
+    agent_weight_grads = late_sums(ids, *late_parts, [])
+    mode_weight_grads = early_sums(ids, own, left, right, [token_grads])
     return (token_grads.reshape(tokens.shape), agent_weight_grads, mode_weight_grads)
 
 

time: 303 us -> 297 us (0.980)
  Pallas kernels: 86 us -> 81 us
    pallas_call x11 -> x12, Pallas kernels: 37.8 us -> 33.8 us  [prefetched(): pl.pallas_call(kernel, grid_spec=pltpu.PrefetchScalarGridSpec(num_scalar_...]
    unnamed x76 -> x74, local copies, waits for them, and re-layouts: 26.1 us -> 23.1 us
    ppermute x23 -> x25, waiting for transfers between devices: 85.8 us -> 88.1 us  [swap(): return lax.ppermute(values, axis, [(n, n ^ bits) for n in range(size)])]
    ppermute x23 -> x25, starting transfers between devices: 33.7 us -> 35.6 us  [swap(): return lax.ppermute(values, axis, [(n, n ^ bits) for n in range(size)])]
  transfers between devices with their start and end apart: 29 -> 31, of which waited for: 14 -> 17; matrix products, arithmetic and copies ran while one was open for 2% -> 2% of each run, Pallas kernels for 15% -> 16%
where the time goes in v3:
time: 297 us; the launch traced here: 295 us
  waiting for transfers between devices  117 us (39%)
  Pallas kernels  81 us (27%)
  starting transfers between devices  67.4 us (23%)
  local copies, waits for them, and re-layouts  26.3 us (9%)
    ppermute x25, waiting for transfers between devices, swap(): return lax.ppermute(values, axis, [(n, n ^ bits) for n in range(size)])  88.1 us
    ppermute x25, starting transfers between devices, swap(): return lax.ppermute(values, axis, [(n, n ^ bits) for n in range(size)])  35.6 us
    pallas_call x12, Pallas kernels, prefetched(): pl.pallas_call(kernel, grid_spec=pltpu.PrefetchScalarGridSpec(num_scalar_...  33.8 us
    all_to_all x6, starting transfers between devices, exchange(): return lax.all_to_all(values, axis, split_axis=0, concat_axis=0, tiled=True)  31.8 us
    all_to_all x6, waiting for transfers between devices, exchange(): return lax.all_to_all(values, axis, split_axis=0, concat_axis=0, tiled=True)  28.5 us
    unnamed x74, local copies, waits for them, and re-layouts  23.1 us
    pallas_call x1, Pallas kernels, middle(): pl.pallas_call(middle_kernel, grid=(5,), in_specs=[fixed((ROWS, D)), fixe...  8.94 us
    pallas_call x1, Pallas kernels, mode_attention(): pl.pallas_call(mode_kernel, grid=(4,), in_specs=[spec] + [unused] * len(a...  8.67 us
  transfers between devices with their start and end apart: 31, of which 17 were waited for; matrix products, arithmetic and copies ran while one was open for 2% of the time, Pallas kernels for 16%

profile of v3, /device:TPU:0, one launch (start us, length us, event | category | flops | bytes accessed | tf_op | source)
XLA Modules:
  0.0 295.1 jit_solution(14244484520752823871)
XLA Ops:
  1.9 6.8 %enter.1 = (bf16[16,384,128]{2,1,0:T(8,128)(2,1)}, bf16[256,1024]{1,0:T(8,128)(2,1)S(1)}, bf16[128,1024]{1,0:T(8,128)(2,1)S(1)}, bf16[128,1024]{1,0:T(8,128)(2,1)S(1)}) custom-call(s32[7]{0:T(128)S(1)} %stack.40.ids_ref, bf16[256,1024]{1,0:T(8,128)(2,1)S(1)} %reshape.64.tokens_ref, bf16[8,1024,1024]{2,1,0:T(8,128)(2,1)} %w3.7, bf16[8,1024,1024]{2,1,0:T(8,128)(2,1)} %w3.7, ...), custom_call_target="tpu_custom_call" | custom-call | flops 1610612736 | bytes 8388608 | tf_op jit(solution)/shard_map/enter/pallas_call | solution.py:154
  9.4 7.2 %all-to-all-start = ((bf16[16,384,128]{2,1,0:T(8,128)(2,1)}), bf16[16,384,128]{2,1,0:T(8,128)(2,1)S(1)}, u32[]{:S(2)}, u32[]{:S(2)}) async-start(bf16[16,384,128]{2,1,0:T(8,128)(2,1)} %get-tuple-element.57), calls=%async_computation | async-start | bytes 3145728 | tf_op jit(solution)/shard_map/all_to_all | solution.py:821
  18.4 3.4 %collective-permute-start.1 = (bf16[256,1024]{1,0:T(8,128)(2,1)S(1)}, bf16[256,1024]{1,0:T(8,128)(2,1)}, u32[]{:S(2)}, u32[]{:S(2)}) collective-permute-start(bf16[256,1024]{1,0:T(8,128)(2,1)S(1)} %constant_dynamic-update-slice_fusion), channel_id=1, source_target_pairs={{0,16},{8,24},{16,0},{24,8},{32,48},{40,56},{48,32},{56,40},{64,80... | collective-permute-start | bytes 1572872 | tf_op jit(solution)/shard_map/ppermute | solution.py:487
  21.8 18.5 %all-to-all-done.query_ref.keys_ref.values_ref.q.k.v = bf16[16,384,128]{2,1,0:T(8,128)(2,1)S(1)} async-done(((bf16[16,384,128]{2,1,0:T(8,128)(2,1)}), bf16[16,384,128]{2,1,0:T(8,128)(2,1)S(1)}, u32[]{:S(2)}, u32[]{:S(2)}) %all-to-all-start) | async-done | bytes 1572896 | tf_op jit(solution)/shard_map/all_to_all | solution.py:821
  40.3 4.5 %agent_forward.1 = (bf16[16,128,128]{2,1,0:T(8,128)(2,1)}, f32[4,4,256,128]{3,2,1,0:T(8,128)S(1)}) custom-call(bf16[16,384,128]{2,1,0:T(8,128)(2,1)S(1)} %all-to-all-done.query_ref.keys_ref.values_ref.q.k.v, bf16[16,384,128]{2,1,0:T(8,128)(2,1)S(1)} %all-to-all-done.query_ref.keys_ref.values_ref.q.k.v, ...), custom_call_target="tpu_custom_call" | custom-call | flops 3000000000 | bytes 4194304 | tf_op jit(solution)/shard_map/agent_forward/pallas_call | solution.py:204
  44.9 1.3 copy-done.32
  46.2 4.2 %all-to-all-start.1 = ((bf16[16,128,128]{2,1,0:T(8,128)(2,1)}), bf16[16,128,128]{2,1,0:T(8,128)(2,1)S(1)}, u32[]{:S(2)}, u32[]{:S(2)}) async-start(bf16[16,128,128]{2,1,0:T(8,128)(2,1)} %get-tuple-element.59), calls=%async_computation.1 | async-start | bytes 1048576 | tf_op jit(solution)/shard_map/all_to_all | solution.py:821
  51.4 2.1 pad_maximum_fusion.rest_0_.refs_0_
  53.5 9.3 %all-to-all-done.1 = bf16[16,128,128]{2,1,0:T(8,128)(2,1)S(1)} async-done(((bf16[16,128,128]{2,1,0:T(8,128)(2,1)}), bf16[16,128,128]{2,1,0:T(8,128)(2,1)S(1)}, u32[]{:S(2)}, u32[]{:S(2)}) %all-to-all-start.1) | async-done | bytes 524320 | tf_op jit(solution)/shard_map/all_to_all | solution.py:821
  63.6 8.9 %middle.1 = (bf16[8,4,256,128]{3,2,1,0:T(8,128)(2,1)}, bf16[256,1024]{1,0:T(8,128)(2,1)S(1)}, bf16[8,256,128]{2,1,0:T(8,128)(2,1)S(1)}, bf16[256,1024]{1,0:T(8,128)(2,1)S(1)}) custom-call(bf16[256,1024]{1,0:T(8,128)(2,1)} %copy-done.9, bf16[8,256,128]{2,1,0:T(8,128)(2,1)} %bitcast.24, bf16[256,1024]{1,0:T(8,128)(2,1)} %reshape.67.cotangent_ref, ...), custom_call_target="tpu_custom_call" | custom-call | flops 2684354560 | bytes 13631488 | tf_op jit(solution)/shard_map/middle/pallas_call | solution.py:314
  74.9 5.6 %all-to-all-start.2 = ((bf16[8,1024,128]{2,1,0:T(8,128)(2,1)}), bf16[8,1024,128]{2,1,0:T(8,128)(2,1)S(1)}, u32[]{:S(2)}, u32[]{:S(2)}) async-start(bf16[8,1024,128]{2,1,0:T(8,128)(2,1)} %bitcast.28), calls=%async_computation.2 | async-start | bytes 4194304 | tf_op jit(solution)/shard_map/all_to_all | solution.py:821
  81.6 24.2 %collective-permute-done.3.rest_1_.refs_3_ = bf16[2,256,1024]{2,1,0:T(8,128)(2,1)S(1)} collective-permute-done((bf16[2,256,1024]{2,1,0:T(8,128)(2,1)S(1)}, bf16[2,256,1024]{2,1,0:T(8,128)(2,1)S(1)}, u32[]{:S(2)}, u32[]{:S(2)}) %collective-permute-start.3) | collective-permute-done | bytes 1048608 | tf_op jit(solution)/shard_map/ppermute | solution.py:487
  110.2 8.7 %mode_attention.1 = bf16[8,4,256,128]{3,2,1,0:T(8,128)(2,1)S(1)} custom-call(bf16[8,4,256,128]{3,2,1,0:T(8,128)(2,1)S(1)} %bitcast.26, bf16[2,256,1024]{2,1,0:T(8,128)(2,1)S(1)} %copy-done.21, bf16[2,256,1024]{2,1,0:T(8,128)(2,1)S(1)} %copy-done.18), custom_call_target="tpu_custom_call" | custom-call | flops 8000000000 | bytes 4194304 | tf_op jit(solution)/shard_map/mode_attention/pallas_call | solution.py:369
  118.9 1.3 copy-done.11
  120.3 5.3 %all-to-all-start.3 = ((bf16[8,1024,128]{2,1,0:T(8,128)(2,1)}), bf16[8,1024,128]{2,1,0:T(8,128)(2,1)S(1)}, u32[]{:S(2)}, u32[]{:S(2)}) async-start(bf16[8,1024,128]{2,1,0:T(8,128)(2,1)} %bitcast.27), calls=%async_computation.3 | async-start | bytes 4194304 | tf_op jit(solution)/shard_map/all_to_all | solution.py:821
  126.3 23.4 %collective-permute-done.4.rest_0_.refs_2_ = bf16[2,256,1024]{2,1,0:T(8,128)(2,1)} collective-permute-done((bf16[2,256,1024]{2,1,0:T(8,128)(2,1)S(1)}, bf16[2,256,1024]{2,1,0:T(8,128)(2,1)}, u32[]{:S(2)}, u32[]{:S(2)}) %collective-permute-start.4) | collective-permute-done | bytes 1048608 | tf_op jit(solution)/shard_map/ppermute | solution.py:487
  150.4 1.4 copy-done.5
  152.9 3.7 %early_first.1 = bf16[8,256,1024]{2,1,0:T(8,128)(2,1)S(1)} custom-call(s32[7]{0:T(128)S(1)} %constant_dynamic-update-slice_fusion.2.ids_ref, bf16[8,256,128]{2,1,0:T(8,128)(2,1)S(1)} %copy-done.13, bf16[8,4,256,128]{3,2,1,0:T(8,128)(2,1)S(1)} %bitcast.19, bf16[8,4,256,128]{3,2,1,0:T(8,128)(2,1)S(1)} %bitcast.20, bf16[256,1024]{1,0:T(8,128)(2,1)S(1)} %copy-done.5, ...), custom_call_target="tpu_custom_call" | custom-call | flops 1000000000 | bytes 5242880 | tf_op jit(solution)/shard_map/early_first/pallas_call | solution.py:495
  156.7 7.1 %collective-permute-done.5.rest_0_ = bf16[8,256,1024]{2,1,0:T(8,128)(2,1)S(1)} collective-permute-done((bf16[8,256,1024]{2,1,0:T(8,128)(2,1)S(1)}, bf16[8,256,1024]{2,1,0:T(8,128)(2,1)S(1)}, u32[]{:S(2)}, u32[]{:S(2)}) %collective-permute-start.5) | collective-permute-done | bytes 4194336 | tf_op jit(solution)/shard_map/ppermute | solution.py:487
  163.8 5.6 %early_add.1 = (bf16[8,128,512]{2,1,0:T(8,128)(2,1)S(1)}, bf16[8,128,512]{2,1,0:T(8,128)(2,1)}, bf16[8,128,512]{2,1,0:T(8,128)(2,1)S(1)}, bf16[8,128,512]{2,1,0:T(8,128)(2,1)}) custom-call(s32[7]{0:T(128)S(1)} %stack.40.ids_ref, bf16[8,256,128]{2,1,0:T(8,128)(2,1)S(1)} %copy-done.14, bf16[8,4,256,128]{3,2,1,0:T(8,128)(2,1)S(1)} %bitcast.21, ...), custom_call_target="tpu_custom_call" | custom-call | flops 1000000000 | bytes 5242880 | tf_op jit(solution)/shard_map/early_add/pallas_call | solution.py:495
  171.4 2.1 collective-permute-start.7
  173.5 6.6 %turn.1 = (bf16[16,128,128]{2,1,0:T(8,128)(2,1)S(1)}, bf16[256,1024]{1,0:T(8,128)(2,1)S(1)}) custom-call(bf16[8,4,256,128]{3,2,1,0:T(8,128)(2,1)} %bitcast.23, bf16[256,1024]{1,0:T(8,128)(2,1)S(1)} %copy-done.6, bf16[256,1024]{1,0:T(8,128)(2,1)} %copy-done.25, bf16[8,1024,1024]{2,1,0:T(8,128)(2,1)} %w3.7, bf16[8,1024,1024]{2,1,0:T(8,128)(2,1)} %w3.7, ...), custom_call_target="tpu_custom_call" | custom-call | flops 2147483648 | bytes 12582912 | tf_op jit(solution)/shard_map/turn/pallas_call | solution.py:415
  180.9 4.6 %all-to-all-start.4 = ((bf16[16,128,128]{2,1,0:T(8,128)(2,1)}), bf16[16,128,128]{2,1,0:T(8,128)(2,1)S(1)}, u32[]{:S(2)}, u32[]{:S(2)}) async-start(bf16[16,128,128]{2,1,0:T(8,128)(2,1)} %copy-done.26), calls=%async_computation.4 | async-start | bytes 1048576 | tf_op jit(solution)/shard_map/all_to_all | solution.py:821
  185.5 10.3 %collective-permute-done.6.left_in = bf16[8,128,512]{2,1,0:T(8,128)(2,1)} collective-permute-done((bf16[8,128,512]{2,1,0:T(8,128)(2,1)}, bf16[8,128,512]{2,1,0:T(8,128)(2,1)}, u32[]{:S(2)}, u32[]{:S(2)}) %collective-permute-start.6) | collective-permute-done | bytes 1048608 | tf_op jit(solution)/shard_map/ppermute | solution.py:487
  195.9 2.0 collective-permute-done.7.right_in
  199.1 6.1 %early_half.1 = (bf16[8,64,1024]{2,1,0:T(8,128)(2,1)S(1)}, bf16[8,64,512]{2,1,0:T(8,128)(2,1)}, bf16[8,64,512]{2,1,0:T(8,128)(2,1)}) custom-call(s32[7]{0:T(128)S(1)} %stack.40.ids_ref, bf16[8,128,512]{2,1,0:T(8,128)(2,1)S(1)} %copy-done.8, bf16[8,128,512]{2,1,0:T(8,128)(2,1)} %collective-permute-done.6.left_in, bf16[8,128,512]{2,1,0:T(8,128)(2,1)S(1)} %copy-done.24, ...), custom_call_target="tpu_custom_call" | custom-call | flops 1000000000 | bytes 5242880 | tf_op jit(solution)/shard_map/early_half/pallas_call | solution.py:495
  206.2 2.1 collective-permute-start.8
  208.2 1.4 copy-done.16
  210.9 1.6 copy-done.33
  212.5 5.9 %agent_backward.1.refs_4_.refs_5_ = bf16[16,3,128,128]{3,2,1,0:T(8,128)(2,1)} custom-call(bf16[16,384,128]{2,1,0:T(8,128)(2,1)S(1)} %copy-done.16, bf16[16,384,128]{2,1,0:T(8,128)(2,1)S(1)} %copy-done.16, bf16[16,384,128]{2,1,0:T(8,128)(2,1)S(1)} %copy-done.16, bf16[16,128,128]{2,1,0:T(8,128)(2,1)S(1)} %all-to-all-done.4.g, ...), custom_call_target="tpu_custom_call" | custom-call | flops 6000000000 | bytes 6291456 | tf_op jit(solution)/shard_map/agent_backward/pallas_call | solution.py:259
  218.4 4.8 %all-to-all-start.5 = ((bf16[16,384,128]{2,1,0:T(8,128)(2,1)}), bf16[16,384,128]{2,1,0:T(8,128)(2,1)}, u32[]{:S(2)}, u32[]{:S(2)}) async-start(bf16[16,384,128]{2,1,0:T(8,128)(2,1)} %bitcast.16), calls=%async_computation.5 | async-start | bytes 3145728 | tf_op jit(solution)/shard_map/all_to_all | solution.py:821
  224.5 9.9 %late_products.1 = (bf16[2,256,1408]{2,1,0:T(8,128)(2,1)S(1)}, bf16[256,1408]{1,0:T(8,128)(2,1)S(1)}, bf16[256,1408]{1,0:T(8,128)(2,1)S(1)}) custom-call(s32[7]{0:T(128)S(1)} %stack.40.ids_ref, bf16[2,256,1024]{2,1,0:T(8,128)(2,1)S(1)} %copy-done.1, bf16[2,256,1024]{2,1,0:T(8,128)(2,1)S(1)} %copy-done.22, ...), custom_call_target="tpu_custom_call" | custom-call | flops 1000000000 | bytes 5242880 | tf_op jit(solution)/shard_map/late_products/pallas_call | solution.py:495
  235.0 1.7 collective-permute-done.10.first_ref
  238.8 2.1 collective-permute-start.12
  241.6 2.1 collective-permute-start.14
  243.7 2.8 early_z.1
  246.5 1.3 collective-permute-start.20
  247.8 2.4 collective-permute-done.12.refs_1_
  250.2 8.1 %collective-permute-done.13.refs_2_ = bf16[2,64,1408]{2,1,0:T(8,128)(2,1)S(1)} collective-permute-done((bf16[2,64,1408]{2,1,0:T(8,128)(2,1)S(1)}, bf16[2,64,1408]{2,1,0:T(8,128)(2,1)S(1)}, u32[]{:S(2)}, u32[]{:S(2)}) %collective-permute-start.13) | collective-permute-done | bytes 360480 | tf_op jit(solution)/shard_map/ppermute | solution.py:487
  258.3 2.7 collective-permute-done.14.refs_3_
  263.0 5.8 %leave.1.rest_0_ = bf16[256,1024]{1,0:T(8,128)(2,1)S(1)} custom-call(bf16[16,3,128,128]{3,2,1,0:T(8,128)(2,1)} %bitcast.17.returned_ref, bf16[256,1024]{1,0:T(8,128)(2,1)S(1)} %copy-done.10, bf16[256,1024]{1,0:T(8,128)(2,1)S(1)} %get-tuple-element.73.grad_after_ref.refs_7_, bf16[8,1024,1024]{2,1,0:T(8,128)(2,1)} %w3.7, bf16[8,1024,1024]{2,1,0:T(8,128)(2,1)} %w3.7, ...), custom_call_target="tpu_custom_call" | custom-call | flops 1610612736 | bytes 9437184 | tf_op jit(solution)/shard_map/leave/pallas_call | solution.py:463
  269.5 1.8 collective-permute-start.21
  271.2 2.7 collective-permute-start.22
  275.5 3.9 %collective-permute-start.17 = (bf16[2,32,1152]{2,1,0:T(8,128)(2,1)S(1)}, bf16[2,32,1152]{2,1,0:T(8,128)(2,1)S(1)}, u32[]{:S(2)}, u32[]{:S(2)}) collective-permute-start(bf16[2,32,1152]{2,1,0:T(8,128)(2,1)S(1)} %get-tuple-element.87), channel_id=1, source_target_pairs={{0,64},{8,72},{16,80},{24,88},{32,96},{40,104},{48,112},{56,120},{... | collective-permute-start | bytes 442376 | tf_op jit(solution)/shard_map/ppermute | solution.py:487
  282.4 3.7 %collective-permute-start.24 = (bf16[32,1024]{1,0:T(8,128)(2,1)S(1)}, bf16[32,1024]{1,0:T(8,128)(2,1)S(1)}, u32[]{:S(2)}, u32[]{:S(2)}) collective-permute-start(bf16[32,1024]{1,0:T(8,128)(2,1)S(1)} %get-tuple-element.98), channel_id=1, source_target_pairs={{0,16},{8,24},{16,0},{24,8},{32,48},{40,56},{48,32},{56,40},{64,80... | collective-permute-start | bytes 196616 | tf_op jit(solution)/shard_map/ppermute | solution.py:487
  287.6 3.7 %collective-permute-start.19 = (bf16[4,32,384]{2,1,0:T(8,128)(2,1)S(1)}, bf16[4,32,384]{2,1,0:T(8,128)(2,1)S(1)}, u32[]{:S(2)}, u32[]{:S(2)}) collective-permute-start(bf16[4,32,384]{2,1,0:T(8,128)(2,1)S(1)} %get-tuple-element.90), channel_id=1, source_target_pairs={{0,16},{8,24},{16,0},{24,8},{32,48},{40,56},{48,32},{56,40},{64,80... | collective-permute-start | bytes 294920 | tf_op jit(solution)/shard_map/ppermute | solution.py:487
  292.0 1.9 collective-permute-done.19.arrived_ref
  293.9 1.2 late_last.1
  (116 shorter events, 36.2 us)
Async XLA Ops:
  9.4 7.7 %copy-start.35 = (s32[128]{0:T(128)S(1)}, s32[128]{0:T(128)}, u32[]{:S(2)}) copy-start(s32[128]{0:T(128)} %param.9) | copy-start | bytes 1540
  9.4 30.9 %all-to-all-start = ((bf16[16,384,128]{2,1,0:T(8,128)(2,1)}), bf16[16,384,128]{2,1,0:T(8,128)(2,1)S(1)}, u32[]{:S(2)}, u32[]{:S(2)}) async-start(bf16[16,384,128]{2,1,0:T(8,128)(2,1)} %get-tuple-element.57), calls=%async_computation | async-start | bytes 3145728 | tf_op jit(solution)/shard_map/all_to_all | solution.py:821
  16.7 1.6 collective-permute-start
  18.3 32.1 %copy-start.34 = (bf16[8,8,4,1024]{3,2,1,0:T(4,128)(2,1)S(1)}, bf16[8,8,4,1024]{3,2,1,0:T(4,128)(2,1)}, u32[]{:S(2)}) copy-start(bf16[8,8,4,1024]{3,2,1,0:T(4,128)(2,1)} %param.7) | copy-start | bytes 1572868
  18.4 33.0 %collective-permute-start.1 = (bf16[256,1024]{1,0:T(8,128)(2,1)S(1)}, bf16[256,1024]{1,0:T(8,128)(2,1)}, u32[]{:S(2)}, u32[]{:S(2)}) collective-permute-start(bf16[256,1024]{1,0:T(8,128)(2,1)S(1)} %constant_dynamic-update-slice_fusion), channel_id=1, source_target_pairs={{0,16},{8,24},{16,0},{24,8},{32,48},{40,56},{48,32},{56,40},{64,80... | collective-permute-start | bytes 1572872 | tf_op jit(solution)/shard_map/ppermute | solution.py:487
  40.3 4.6 %copy-start.15 = (bf16[16,384,128]{2,1,0:T(8,128)(2,1)}, bf16[16,384,128]{2,1,0:T(8,128)(2,1)S(1)}, u32[]{:S(2)}) copy-start(bf16[16,384,128]{2,1,0:T(8,128)(2,1)S(1)} %all-to-all-done.query_ref.keys_ref.values_ref.q.k.v) | copy-start | bytes 4718596
  46.2 16.6 %all-to-all-start.1 = ((bf16[16,128,128]{2,1,0:T(8,128)(2,1)}), bf16[16,128,128]{2,1,0:T(8,128)(2,1)S(1)}, u32[]{:S(2)}, u32[]{:S(2)}) async-start(bf16[16,128,128]{2,1,0:T(8,128)(2,1)} %get-tuple-element.59), calls=%async_computation.1 | async-start | bytes 1048576 | tf_op jit(solution)/shard_map/all_to_all | solution.py:821
  74.9 5.6 %copy-start.1 = (bf16[2,256,1024]{2,1,0:T(8,128)(2,1)S(1)}, bf16[2,256,1024]{2,1,0:T(8,128)(2,1)}, u32[]{:S(2)}) copy-start(bf16[2,256,1024]{2,1,0:T(8,128)(2,1)} %pad_maximum_fusion.rest_0_.refs_0_) | copy-start | bytes 3145732
  74.9 32.8 %all-to-all-start.2 = ((bf16[8,1024,128]{2,1,0:T(8,128)(2,1)}), bf16[8,1024,128]{2,1,0:T(8,128)(2,1)S(1)}, u32[]{:S(2)}, u32[]{:S(2)}) async-start(bf16[8,1024,128]{2,1,0:T(8,128)(2,1)} %bitcast.28), calls=%async_computation.2 | async-start | bytes 4194304 | tf_op jit(solution)/shard_map/all_to_all | solution.py:821
  80.5 25.3 %collective-permute-start.3 = (bf16[2,256,1024]{2,1,0:T(8,128)(2,1)S(1)}, bf16[2,256,1024]{2,1,0:T(8,128)(2,1)S(1)}, u32[]{:S(2)}, u32[]{:S(2)}) collective-permute-start(bf16[2,256,1024]{2,1,0:T(8,128)(2,1)S(1)} %copy-done.1), channel_id=1, source_target_pairs={{0,96},{8,104},{16,112},{24,120},{32,64},{40,72},{48,80},{56,88},{... | collective-permute-start | bytes 3145736 | tf_op jit(solution)/shard_map/ppermute | solution.py:487
  81.4 25.4 %collective-permute-start.2 = (bf16[2,256,1024]{2,1,0:T(8,128)(2,1)S(1)}, bf16[2,256,1024]{2,1,0:T(8,128)(2,1)S(1)}, u32[]{:S(2)}, u32[]{:S(2)}) collective-permute-start(bf16[2,256,1024]{2,1,0:T(8,128)(2,1)S(1)} %copy-done.1), channel_id=1, source_target_pairs={{0,32},{8,40},{16,48},{24,56},{32,0},{40,8},{48,16},{56,24},{64,96... | collective-permute-start | bytes 3145736 | tf_op jit(solution)/shard_map/ppermute | solution.py:487
  120.3 30.1 %all-to-all-start.3 = ((bf16[8,1024,128]{2,1,0:T(8,128)(2,1)}), bf16[8,1024,128]{2,1,0:T(8,128)(2,1)S(1)}, u32[]{:S(2)}, u32[]{:S(2)}) async-start(bf16[8,1024,128]{2,1,0:T(8,128)(2,1)} %bitcast.27), calls=%async_computation.3 | async-start | bytes 4194304 | tf_op jit(solution)/shard_map/all_to_all | solution.py:821
  125.6 24.1 %collective-permute-start.4 = (bf16[2,256,1024]{2,1,0:T(8,128)(2,1)S(1)}, bf16[2,256,1024]{2,1,0:T(8,128)(2,1)}, u32[]{:S(2)}, u32[]{:S(2)}) collective-permute-start(bf16[2,256,1024]{2,1,0:T(8,128)(2,1)S(1)} %copy-done.1), channel_id=1, source_target_pairs={{0,64},{8,72},{16,80},{24,88},{32,96},{40,104},{48,112},{56,120},{... | collective-permute-start | bytes 3145736 | tf_op jit(solution)/shard_map/ppermute | solution.py:487
  150.4 13.4 %copy-start = (bf16[8,1024,128]{2,1,0:T(8,128)(2,1)}, bf16[8,1024,128]{2,1,0:T(8,128)(2,1)S(1)}, u32[]{:S(2)}) copy-start(bf16[8,1024,128]{2,1,0:T(8,128)(2,1)S(1)} %all-to-all-done.3) | copy-start | bytes 6291460
  152.9 10.9 %copy-start.6 = (bf16[256,1024]{1,0:T(8,128)(2,1)S(1)}, bf16[256,1024]{1,0:T(8,128)(2,1)}, u32[]{:S(2)}) copy-start(bf16[256,1024]{1,0:T(8,128)(2,1)} %copy-done.4) | copy-start | bytes 1572868
  152.9 10.9 %copy-start.14 = (bf16[8,256,128]{2,1,0:T(8,128)(2,1)S(1)}, bf16[8,256,128]{2,1,0:T(8,128)(2,1)}, u32[]{:S(2)}) copy-start(bf16[8,256,128]{2,1,0:T(8,128)(2,1)} %copy-done.12) | copy-start | bytes 1572868
  156.6 7.2 %collective-permute-start.5 = (bf16[8,256,1024]{2,1,0:T(8,128)(2,1)S(1)}, bf16[8,256,1024]{2,1,0:T(8,128)(2,1)S(1)}, u32[]{:S(2)}, u32[]{:S(2)}) collective-permute-start(bf16[8,256,1024]{2,1,0:T(8,128)(2,1)S(1)} %early_first.1), channel_id=1, source_target_pairs={{0,8},{8,0},{16,24},{24,16},{32,40},{40,32},{48,56},{56,48},{64,72... | collective-permute-start | bytes 12582920 | tf_op jit(solution)/shard_map/ppermute | solution.py:487
  170.4 9.7 %copy-start.23 = (bf16[8,128,512]{2,1,0:T(8,128)(2,1)}, bf16[8,128,512]{2,1,0:T(8,128)(2,1)S(1)}, u32[]{:S(2)}) copy-start(bf16[8,128,512]{2,1,0:T(8,128)(2,1)S(1)} %get-tuple-element.70.right_ref) | copy-start | bytes 3145732
  170.4 25.5 %collective-permute-start.6 = (bf16[8,128,512]{2,1,0:T(8,128)(2,1)}, bf16[8,128,512]{2,1,0:T(8,128)(2,1)}, u32[]{:S(2)}, u32[]{:S(2)}) collective-permute-start(bf16[8,128,512]{2,1,0:T(8,128)(2,1)} %get-tuple-element.69), channel_id=1, source_target_pairs={{0,2},{1,3},{2,0},{3,1},{4,6},{5,7},{6,4},{7,5},{8,10},{9,11},{10,... | collective-permute-start | bytes 3145736 | tf_op jit(solution)/shard_map/ppermute | solution.py:487
  171.4 26.4 %collective-permute-start.7 = (bf16[8,128,512]{2,1,0:T(8,128)(2,1)}, bf16[8,128,512]{2,1,0:T(8,128)(2,1)}, u32[]{:S(2)}, u32[]{:S(2)}) collective-permute-start(bf16[8,128,512]{2,1,0:T(8,128)(2,1)} %get-tuple-element.71), channel_id=1, source_target_pairs={{0,6},{1,7},{2,4},{3,5},{4,2},{5,3},{6,0},{7,1},{8,14},{9,15},{10,... | collective-permute-start | bytes 3145736 | tf_op jit(solution)/shard_map/ppermute | solution.py:487
  173.5 24.4 %copy-start.8 = (bf16[8,128,512]{2,1,0:T(8,128)(2,1)S(1)}, bf16[8,128,512]{2,1,0:T(8,128)(2,1)}, u32[]{:S(2)}) copy-start(bf16[8,128,512]{2,1,0:T(8,128)(2,1)} %copy-done.7) | copy-start | bytes 3145732
  180.9 27.3 %all-to-all-start.4 = ((bf16[16,128,128]{2,1,0:T(8,128)(2,1)}), bf16[16,128,128]{2,1,0:T(8,128)(2,1)S(1)}, u32[]{:S(2)}, u32[]{:S(2)}) async-start(bf16[16,128,128]{2,1,0:T(8,128)(2,1)} %copy-done.26), calls=%async_computation.4 | async-start | bytes 1048576 | tf_op jit(solution)/shard_map/all_to_all | solution.py:821
  206.2 17.1 %collective-permute-start.8 = (bf16[8,64,512]{2,1,0:T(8,128)(2,1)}, bf16[8,64,512]{2,1,0:T(8,128)(2,1)}, u32[]{:S(2)}, u32[]{:S(2)}) collective-permute-start(bf16[8,64,512]{2,1,0:T(8,128)(2,1)} %get-tuple-element.74), channel_id=1, source_target_pairs={{0,6},{1,7},{2,4},{3,5},{4,2},{5,3},{6,0},{7,1},{8,14},{9,15},{10,... | collective-permute-start | bytes 1572872 | tf_op jit(solution)/shard_map/ppermute | solution.py:487
  208.2 15.0 %collective-permute-start.9 = (bf16[8,64,512]{2,1,0:T(8,128)(2,1)}, bf16[8,64,512]{2,1,0:T(8,128)(2,1)}, u32[]{:S(2)}, u32[]{:S(2)}) collective-permute-start(bf16[8,64,512]{2,1,0:T(8,128)(2,1)} %get-tuple-element.75), channel_id=1, source_target_pairs={{0,2},{1,3},{2,0},{3,1},{4,6},{5,7},{6,4},{7,5},{8,10},{9,11},{10,... | collective-permute-start | bytes 1572872 | tf_op jit(solution)/shard_map/ppermute | solution.py:487
  208.2 1.4 copy-start.16
  210.9 1.6 copy-start.33
  218.4 4.8 %copy-start.3 = (bf16[16,128,128]{2,1,0:T(8,128)(2,1)S(1)}, bf16[16,128,128]{2,1,0:T(8,128)(2,1)}, u32[]{:S(2)}) copy-start(bf16[16,128,128]{2,1,0:T(8,128)(2,1)} %copy-done.2) | copy-start | bytes 1572868
  218.4 4.8 %copy-start.19 = (bf16[2,256,1024]{2,1,0:T(8,128)(2,1)S(1)}, bf16[2,256,1024]{2,1,0:T(8,128)(2,1)}, u32[]{:S(2)}) copy-start(bf16[2,256,1024]{2,1,0:T(8,128)(2,1)} %copy-done.17) | copy-start | bytes 3145732
  218.4 44.6 %all-to-all-start.5 = ((bf16[16,384,128]{2,1,0:T(8,128)(2,1)}), bf16[16,384,128]{2,1,0:T(8,128)(2,1)}, u32[]{:S(2)}, u32[]{:S(2)}) async-start(bf16[16,384,128]{2,1,0:T(8,128)(2,1)} %bitcast.16), calls=%async_computation.5 | async-start | bytes 3145728 | tf_op jit(solution)/shard_map/all_to_all | solution.py:821
  234.4 9.3 %copy-start.29 = (bf16[8,64,1024]{2,1,0:T(8,128)(2,1)S(1)}, bf16[8,64,1024]{2,1,0:T(8,128)(2,1)}, u32[]{:S(2)}) copy-start(bf16[8,64,1024]{2,1,0:T(8,128)(2,1)} %copy-done.27) | copy-start | bytes 3145732
  234.4 2.3 collective-permute-start.10
  234.8 2.9 collective-permute-start.11
  238.8 11.4 %collective-permute-start.12 = (bf16[2,64,1408]{2,1,0:T(8,128)(2,1)S(1)}, bf16[2,64,1408]{2,1,0:T(8,128)(2,1)S(1)}, u32[]{:S(2)}, u32[]{:S(2)}) collective-permute-start(bf16[2,64,1408]{2,1,0:T(8,128)(2,1)S(1)} %get-tuple-element.80), channel_id=1, source_target_pairs={{0,2},{1,3},{2,0},{3,1},{4,6},{5,7},{6,4},{7,5},{8,10},{9,11},{10,... | collective-permute-start | bytes 1081352 | tf_op jit(solution)/shard_map/ppermute | solution.py:487
  240.9 17.4 %collective-permute-start.13 = (bf16[2,64,1408]{2,1,0:T(8,128)(2,1)S(1)}, bf16[2,64,1408]{2,1,0:T(8,128)(2,1)S(1)}, u32[]{:S(2)}, u32[]{:S(2)}) collective-permute-start(bf16[2,64,1408]{2,1,0:T(8,128)(2,1)S(1)} %get-tuple-element.81), channel_id=1, source_target_pairs={{0,4},{1,5},{2,6},{3,7},{4,0},{5,1},{6,2},{7,3},{8,12},{9,13},{10,... | collective-permute-start | bytes 1081352 | tf_op jit(solution)/shard_map/ppermute | solution.py:487
  241.6 19.3 %collective-permute-start.14 = (bf16[2,64,1408]{2,1,0:T(8,128)(2,1)S(1)}, bf16[2,64,1408]{2,1,0:T(8,128)(2,1)S(1)}, u32[]{:S(2)}, u32[]{:S(2)}) collective-permute-start(bf16[2,64,1408]{2,1,0:T(8,128)(2,1)S(1)} %get-tuple-element.82), channel_id=1, source_target_pairs={{0,6},{1,7},{2,4},{3,5},{4,2},{5,3},{6,0},{7,1},{8,14},{9,15},{10,... | collective-permute-start | bytes 1081352 | tf_op jit(solution)/shard_map/ppermute | solution.py:487
  246.5 15.3 %copy-start.30 = (bf16[8,32,1024]{2,1,0:T(8,128)(2,1)}, bf16[8,32,1024]{2,1,0:T(8,128)(2,1)S(1)}, u32[]{:S(2)}) copy-start(bf16[8,32,1024]{2,1,0:T(8,128)(2,1)S(1)} %get-tuple-element.91.own_ref) | copy-start | bytes 1572868
  246.5 16.5 %copy-start.10 = (bf16[256,1024]{1,0:T(8,128)(2,1)S(1)}, bf16[256,1024]{1,0:T(8,128)(2,1)}, u32[]{:S(2)}) copy-start(bf16[256,1024]{1,0:T(8,128)(2,1)} %copy-done.9) | copy-start | bytes 1572868
  246.5 22.3 %collective-permute-start.20 = (bf16[8,32,1024]{2,1,0:T(8,128)(2,1)S(1)}, bf16[8,32,1024]{2,1,0:T(8,128)(2,1)S(1)}, u32[]{:S(2)}, u32[]{:S(2)}) collective-permute-start(bf16[8,32,1024]{2,1,0:T(8,128)(2,1)S(1)} %get-tuple-element.92), channel_id=1, source_target_pairs={{0,1},{1,0},{2,3},{3,2},{4,5},{5,4},{6,7},{7,6},{8,9},{9,8},{10,11... | collective-permute-start | bytes 1572872 | tf_op jit(solution)/shard_map/ppermute | solution.py:487
  261.8 12.4 %collective-permute-start.15 = (bf16[2,32,1408]{2,1,0:T(8,128)(2,1)S(1)}, bf16[2,32,1408]{2,1,0:T(8,128)(2,1)S(1)}, u32[]{:S(2)}, u32[]{:S(2)}) collective-permute-start(bf16[2,32,1408]{2,1,0:T(8,128)(2,1)S(1)} %get-tuple-element.84), channel_id=1, source_target_pairs={{0,1},{1,0},{2,3},{3,2},{4,5},{5,4},{6,7},{7,6},{8,9},{9,8},{10,11... | collective-permute-start | bytes 540680 | tf_op jit(solution)/shard_map/ppermute | solution.py:487
  263.0 5.8 %copy-start.31 = (bf16[8,32,1024]{2,1,0:T(8,128)(2,1)S(1)}, bf16[8,32,1024]{2,1,0:T(8,128)(2,1)}, u32[]{:S(2)}) copy-start(bf16[8,32,1024]{2,1,0:T(8,128)(2,1)} %copy-done.30) | copy-start | bytes 1572868
  269.5 9.9 %collective-permute-start.21 = (bf16[2,32,1024]{2,1,0:T(8,128)(2,1)S(1)}, bf16[2,32,1024]{2,1,0:T(8,128)(2,1)S(1)}, u32[]{:S(2)}, u32[]{:S(2)}) collective-permute-start(bf16[2,32,1024]{2,1,0:T(8,128)(2,1)S(1)} %get-tuple-element.94), channel_id=1, source_target_pairs={{0,32},{8,40},{16,48},{24,56},{32,0},{40,8},{48,16},{56,24},{64,96... | collective-permute-start | bytes 393224 | tf_op jit(solution)/shard_map/ppermute | solution.py:487
  271.2 9.4 %collective-permute-start.22 = (bf16[2,32,1024]{2,1,0:T(8,128)(2,1)S(1)}, bf16[2,32,1024]{2,1,0:T(8,128)(2,1)S(1)}, u32[]{:S(2)}, u32[]{:S(2)}) collective-permute-start(bf16[2,32,1024]{2,1,0:T(8,128)(2,1)S(1)} %get-tuple-element.95), channel_id=1, source_target_pairs={{0,64},{8,72},{16,80},{24,88},{32,96},{40,104},{48,112},{56,120},{... | collective-permute-start | bytes 393224 | tf_op jit(solution)/shard_map/ppermute | solution.py:487
  274.0 7.8 %collective-permute-start.23 = (bf16[2,32,1024]{2,1,0:T(8,128)(2,1)S(1)}, bf16[2,32,1024]{2,1,0:T(8,128)(2,1)S(1)}, u32[]{:S(2)}, u32[]{:S(2)}) collective-permute-start(bf16[2,32,1024]{2,1,0:T(8,128)(2,1)S(1)} %get-tuple-element.96), channel_id=1, source_target_pairs={{0,96},{8,104},{16,112},{24,120},{32,64},{40,72},{48,80},{56,88},{... | collective-permute-start | bytes 393224 | tf_op jit(solution)/shard_map/ppermute | solution.py:487
  274.9 11.2 %collective-permute-start.16 = (bf16[2,32,1152]{2,1,0:T(8,128)(2,1)S(1)}, bf16[2,32,1152]{2,1,0:T(8,128)(2,1)S(1)}, u32[]{:S(2)}, u32[]{:S(2)}) collective-permute-start(bf16[2,32,1152]{2,1,0:T(8,128)(2,1)S(1)} %get-tuple-element.86), channel_id=1, source_target_pairs={{0,32},{8,40},{16,48},{24,56},{32,0},{40,8},{48,16},{56,24},{64,96... | collective-permute-start | bytes 442376 | tf_op jit(solution)/shard_map/ppermute | solution.py:487
  275.5 10.7 %collective-permute-start.17 = (bf16[2,32,1152]{2,1,0:T(8,128)(2,1)S(1)}, bf16[2,32,1152]{2,1,0:T(8,128)(2,1)S(1)}, u32[]{:S(2)}, u32[]{:S(2)}) collective-permute-start(bf16[2,32,1152]{2,1,0:T(8,128)(2,1)S(1)} %get-tuple-element.87), channel_id=1, source_target_pairs={{0,64},{8,72},{16,80},{24,88},{32,96},{40,104},{48,112},{56,120},{... | collective-permute-start | bytes 442376 | tf_op jit(solution)/shard_map/ppermute | solution.py:487
  279.4 7.6 %collective-permute-start.18 = (bf16[2,32,1152]{2,1,0:T(8,128)(2,1)S(1)}, bf16[2,32,1152]{2,1,0:T(8,128)(2,1)S(1)}, u32[]{:S(2)}, u32[]{:S(2)}) collective-permute-start(bf16[2,32,1152]{2,1,0:T(8,128)(2,1)S(1)} %get-tuple-element.88), channel_id=1, source_target_pairs={{0,96},{8,104},{16,112},{24,120},{32,64},{40,72},{48,80},{56,88},{... | collective-permute-start | bytes 442376 | tf_op jit(solution)/shard_map/ppermute | solution.py:487
  282.4 8.9 %collective-permute-start.24 = (bf16[32,1024]{1,0:T(8,128)(2,1)S(1)}, bf16[32,1024]{1,0:T(8,128)(2,1)S(1)}, u32[]{:S(2)}, u32[]{:S(2)}) collective-permute-start(bf16[32,1024]{1,0:T(8,128)(2,1)S(1)} %get-tuple-element.98), channel_id=1, source_target_pairs={{0,16},{8,24},{16,0},{24,8},{32,48},{40,56},{48,32},{56,40},{64,80... | collective-permute-start | bytes 196616 | tf_op jit(solution)/shard_map/ppermute | solution.py:487
  287.6 6.3 %collective-permute-start.19 = (bf16[4,32,384]{2,1,0:T(8,128)(2,1)S(1)}, bf16[4,32,384]{2,1,0:T(8,128)(2,1)S(1)}, u32[]{:S(2)}, u32[]{:S(2)}) collective-permute-start(bf16[4,32,384]{2,1,0:T(8,128)(2,1)S(1)} %get-tuple-element.90), channel_id=1, source_target_pairs={{0,16},{8,24},{16,0},{24,8},{32,48},{40,56},{48,32},{56,40},{64,80... | collective-permute-start | bytes 294920 | tf_op jit(solution)/shard_map/ppermute | solution.py:487
  (19 other events, 20.0 us)

commit v4 on v3

--- a/solution.py
+++ b/solution.py
@@ -61,12 +61,36 @@
     return factor * (upstream - normed * jnp.mean(upstream * normed, -1, keepdims=True))
 
 
-def weight_specs(slot):
-    return [pl.BlockSpec((1, 256, D), lambda i, *c, q=q: (slot(i), q, 0)) for q in range(4)]
-
-
-def joined(refs):
-    return jnp.concatenate([ref[0] for ref in refs], 0)
+def fetch(slots, weights_ref, held_ref, sems_ref):
+    copies = [
+        pltpu.make_async_copy(weights_ref.at[slot], held_ref.at[n], sems_ref.at[n])
+        for n, slot in enumerate(slots)
+    ]
+    step = pl.program_id(0)
+
+    @pl.when(step == 0)
+    def _():
+        for copy in copies:
+            copy.start()
+
+    def ready():
+        for n, copy in enumerate(copies):
+
+            @pl.when(step == n)
+            def _(copy=copy):
+                copy.wait()
+
+        return held_ref[step]
+
+    return ready
+
+
+def pinned(operand):
+    return pltpu.with_memory_space_constraint(operand, pltpu.HBM)
+
+
+def held(count):
+    return [pltpu.VMEM((count, D, D), BF), pltpu.SemaphoreType.DMA((count,))]
 
 
 def params(limit=32):
@@ -117,10 +141,11 @@
 
 
 def enter_kernel(
-    ids_ref, tokens_ref, w0, w1, w2, w3,
-    send_ref, tokens_out_ref, keep_ref, give_ref, hidden_ref,
+    ids_ref, tokens_ref, weights_ref,
+    send_ref, tokens_out_ref, keep_ref, give_ref, hidden_ref, held_ref, sems_ref,
 ):
     step = pl.program_id(0)
+    ready = fetch((0, 1, 2), weights_ref, held_ref, sems_ref)
 
     @pl.when(step == 0)
     def _():
@@ -141,8 +166,7 @@
             keep_ref[...] = hidden[128:]
             give_ref[...] = hidden[:128]
 
-    weights = joined((w0, w1, w2, w3))
-    result = jnp.dot(hidden_ref[...], weights, preferred_element_type=F32).astype(BF)
+    result = jnp.dot(hidden_ref[...], ready(), preferred_element_type=F32).astype(BF)
     for pair in range(8):
         for half in range(2):
             send_ref[2 * pair + half] = result[
@@ -156,25 +180,25 @@
         grid_spec=pltpu.PrefetchScalarGridSpec(
             num_scalar_prefetch=1,
             grid=(3,),
-            in_specs=[fixed((ROWS, D))] + weight_specs(lambda i: i),
+            in_specs=[fixed((ROWS, D)), unused],
             out_specs=[
                 pl.BlockSpec((16, 128, 128), lambda i, c: (0, i, 0)),
                 fixed((ROWS, D)),
                 fixed((128, D)),
                 fixed((128, D)),
             ],
-            scratch_shapes=[pltpu.VMEM((ROWS, D), BF)],
+            scratch_shapes=[pltpu.VMEM((ROWS, D), BF)] + held(3),
         ),
         out_shape=[
             jax.ShapeDtypeStruct((16, 384, 128), BF),
-            jax.ShapeDtypeStruct((ROWS, D), BF),
-            jax.ShapeDtypeStruct((128, D), BF),
+            pltpu.HBM((ROWS, D), BF),
+            pltpu.HBM((128, D), BF),
             jax.ShapeDtypeStruct((128, D), BF),
         ],
-        compiler_params=params(52),
+        compiler_params=params(45),
         cost_estimate=cost(3 * 2 * ROWS * D * D, 8 * MIB),
         name="enter",
-    )(ids, tokens, *[weights] * 4)
+    )(ids, tokens, pinned(weights))
 
 
 def agent_rows(block, step):
@@ -211,7 +235,7 @@
         ],
         out_shape=[
             jax.ShapeDtypeStruct((16, 128, 128), BF),
-            jax.ShapeDtypeStruct((4, 4, 256, 128), F32),
+            pltpu.HBM((4, 4, 256, 128), F32),
         ],
         compiler_params=params(),
         cost_estimate=cost(3e9, 4 * MIB),
@@ -270,22 +294,23 @@
         compiler_params=params(),
         cost_estimate=cost(6e9, 6 * MIB),
         name="agent_backward",
-    )(arrived, arrived, arrived, upstream, tables, *waits)
+    )(arrived, arrived, arrived, upstream, tables, *map(pinned, waits))
 
 
 def middle_kernel(
-    tokens_ref, mixed_ref, cotangent_ref, w0, w1, w2, w3, *rest
+    tokens_ref, mixed_ref, cotangent_ref, weights_ref, *rest
 ):
-    send_ref, after_ref, hidden_out_ref, cotangent_out_ref, hidden_ref = rest[-5:]
-    quarters = (w0, w1, w2, w3)
+    send_ref, after_ref, hidden_out_ref, cotangent_out_ref, hidden_ref = rest[-7:-2]
     step = pl.program_id(0)
+    ready = fetch((3, 4, 5, 6, 7), weights_ref, *rest[-2:])
+    matrix = ready()
 
     @pl.when(step == 0)
     def _():
         mixed = jnp.concatenate([mixed_ref[pair] for pair in range(8)], 1)
         after = (
             tokens_ref[...].astype(F32)
-            + jnp.dot(mixed, joined(quarters), preferred_element_type=F32)
+            + jnp.dot(mixed, matrix, preferred_element_type=F32)
         ).astype(BF)
         after = reorder(after, "a", "m")
         after_ref[...] = after
@@ -303,11 +328,11 @@
 
     @pl.when((step > 0) & (step < 4))
     def _():
-        send(jnp.dot(hidden_ref[...], joined(quarters), preferred_element_type=F32))
+        send(jnp.dot(hidden_ref[...], matrix, preferred_element_type=F32))
 
     @pl.when(step == 4)
     def _():
-        send(dot_nt(cotangent_out_ref[...], joined(quarters)))
+        send(dot_nt(cotangent_out_ref[...], matrix))
 
 
 def middle(tokens, mixed, cotangent, weights, waits=()):
@@ -318,8 +343,8 @@
             fixed((ROWS, D)),
             fixed((8, ROWS, 128)),
             fixed((ROWS, D)),
+            unused,
         ]
-        + weight_specs(lambda i: 3 + i)
         + [unused] * len(waits),
         out_specs=[
             pl.BlockSpec((8, 1, ROWS, 128), lambda i: (0, jnp.maximum(i - 1, 0), 0, 0)),
@@ -329,15 +354,15 @@
         ],
         out_shape=[
             jax.ShapeDtypeStruct((8, 4, ROWS, 128), BF),
-            jax.ShapeDtypeStruct((ROWS, D), BF),
-            jax.ShapeDtypeStruct((8, ROWS, 128), BF),
-            jax.ShapeDtypeStruct((ROWS, D), BF),
+            pltpu.HBM((ROWS, D), BF),
+            pltpu.HBM((8, ROWS, 128), BF),
+            pltpu.HBM((ROWS, D), BF),
         ],
-        scratch_shapes=[pltpu.VMEM((ROWS, D), BF)],
-        compiler_params=params(52),
+        scratch_shapes=[pltpu.VMEM((ROWS, D), BF)] + held(5),
+        compiler_params=params(45),
         cost_estimate=cost(5 * 2 * ROWS * D * D, 13 * MIB),
         name="middle",
-    )(tokens, mixed, cotangent, *[weights] * 4, *waits)
+    )(tokens, mixed, cotangent, pinned(weights), *map(pinned, waits))
 
 
 def mode_kernel(arrived_ref, *rest):
@@ -371,22 +396,23 @@
         grid=(4,),
         in_specs=[spec] + [unused] * len(after),
         out_specs=spec,
-        out_shape=jax.ShapeDtypeStruct((8, 4, ROWS, 128), BF),
+        out_shape=pltpu.HBM((8, 4, ROWS, 128), BF),
         compiler_params=params(),
         cost_estimate=cost(8e9, 4 * MIB),
         name="mode_attention",
-    )(arrived, *after)
-
-
-def turn_kernel(returned_ref, cotangent_ref, after_ref, w0, w1, w2, w3, *rest):
-    quarters = (w0, w1, w2, w3)
-    send_ref, grad_after_ref, total_ref = rest[-3:]
+    )(arrived, *map(pinned, after))
+
+
+def turn_kernel(returned_ref, cotangent_ref, after_ref, weights_ref, *rest):
+    send_ref, grad_after_ref, total_ref = rest[-5:-2]
     step = pl.program_id(0)
+    ready = fetch((4, 5, 6, 3), weights_ref, *rest[-2:])
+    matrix = ready()
 
     @pl.when(step < 3)
     def _():
         grads = jnp.concatenate([returned_ref[pair, 0] for pair in range(8)], 1)
-        product = dot_nt(grads, joined(quarters))
+        product = dot_nt(grads, matrix)
 
         @pl.when(step == 0)
         def _():
@@ -403,7 +429,7 @@
         ).astype(BF)
         grad_after = reorder(grad_after, "m", "a")
         grad_after_ref[...] = grad_after
-        result = dot_nt(grad_after, joined(quarters)).astype(BF)
+        result = dot_nt(grad_after, matrix).astype(BF)
         for pair in range(8):
             for half in range(2):
                 send_ref[2 * pair + half] = result[
@@ -419,29 +445,30 @@
             pl.BlockSpec((8, 1, ROWS, 128), lambda i: (0, jnp.minimum(i + 1, 3), 0, 0)),
             fixed((ROWS, D)),
             fixed((ROWS, D)),
+            unused,
         ]
-        + weight_specs(lambda i: jnp.where(i < 3, i + 4, 3))
         + [unused] * len(waits),
         out_specs=[fixed((16, 128, 128)), fixed((ROWS, D))],
         out_shape=[
-            jax.ShapeDtypeStruct((16, 128, 128), BF),
-            jax.ShapeDtypeStruct((ROWS, D), BF),
+            pltpu.HBM((16, 128, 128), BF),
+            pltpu.HBM((ROWS, D), BF),
         ],
-        scratch_shapes=[pltpu.VMEM((ROWS, D), F32)],
-        compiler_params=params(52),
+        scratch_shapes=[pltpu.VMEM((ROWS, D), F32)] + held(4),
+        compiler_params=params(45),
         cost_estimate=cost(4 * 2 * ROWS * D * D, 12 * MIB),
         name="turn",
-    )(returned, cotangent, after, *[weights] * 4, *waits)
+    )(returned, cotangent, after, pinned(weights), *map(pinned, waits))
 
 
 def whole_rows(ref):
     return jnp.concatenate([ref[:, 0].reshape(8, ROWS, 128)[pair] for pair in range(8)], 1)
 
 
-def leave_kernel(returned_ref, tokens_ref, grad_after_ref, w0, w1, w2, w3, *rest):
-    out_ref, total_ref = rest[-2:]
+def leave_kernel(returned_ref, tokens_ref, grad_after_ref, weights_ref, *rest):
+    out_ref, total_ref = rest[-4:-2]
     step = pl.program_id(0)
-    product = dot_nt(whole_rows(returned_ref), joined((w0, w1, w2, w3)))
+    ready = fetch((0, 1, 2), weights_ref, *rest[-2:])
+    product = dot_nt(whole_rows(returned_ref), ready())
 
     @pl.when(step == 0)
     def _():
@@ -467,16 +494,16 @@
             pl.BlockSpec((16, 1, 128, 128), lambda i: (0, i, 0, 0)),
             fixed((ROWS, D)),
             fixed((ROWS, D)),
+            unused,
         ]
-        + weight_specs(lambda i: i)
         + [unused] * len(waits),
         out_specs=fixed((ROWS, D)),
         out_shape=jax.ShapeDtypeStruct((ROWS, D), BF),
-        scratch_shapes=[pltpu.VMEM((ROWS, D), F32)],
-        compiler_params=params(52),
+        scratch_shapes=[pltpu.VMEM((ROWS, D), F32)] + held(3),
+        compiler_params=params(45),
         cost_estimate=cost(3 * 2 * ROWS * D * D, 9 * MIB),
         name="leave",
-    )(returned, tokens, grad_after, *[weights] * 4, *waits)
+    )(returned, tokens, grad_after, pinned(weights), *map(pinned, waits))
 
 
 CORE, MODE, CHIP, Z, YLO, X, YHI = range(7)
@@ -555,16 +582,16 @@
     operands = [hidden, returned, returned, last]
     if arrived is None:
         return prefetched(
-            functools.partial(early_kernel, False), ids, operands + list(waits),
+            functools.partial(early_kernel, False), ids, operands + [pinned(wait) for wait in waits],
             in_specs + [unused] * len(waits),
             pl.BlockSpec((1, ROWS, D), lambda i, c: (i, 0, 0)),
             jax.ShapeDtypeStruct((8, ROWS, D), BF), "early_first", (8,),
         )
     return prefetched(
-        functools.partial(early_kernel, True), ids, operands + [arrived, *waits],
+        functools.partial(early_kernel, True), ids, operands + [arrived, *map(pinned, waits)],
         in_specs + [pl.BlockSpec((1, ROWS, D), lambda i, c: (i, 0, 0))] + [unused] * len(waits),
         [pl.BlockSpec((1, 128, 512), lambda i, c: (i, 0, 0))] * 4,
-        [jax.ShapeDtypeStruct((8, 128, 512), BF)] * 4, "early_add", (8,),
+        [pltpu.HBM((8, 128, 512), BF), jax.ShapeDtypeStruct((8, 128, 512), BF)] * 2, "early_add", (8,),
         [pltpu.VMEM((ROWS, D), F32)],
     )
 
@@ -583,7 +610,7 @@
 def sum_split(ids, parts, split, count, name, waits=()):
     blocks, rows, columns = parts[0].shape
     return prefetched(
-        functools.partial(sum_split_kernel, split, count, len(parts)), ids, [*parts, *waits],
+        functools.partial(sum_split_kernel, split, count, len(parts)), ids, [*parts, *map(pinned, waits)],
         [pl.BlockSpec((1, rows, columns), lambda i, c: (i, 0, 0))] * len(parts)
         + [unused] * len(waits),
         [pl.BlockSpec((1, rows // count, columns), lambda i, c: (i, 0, 0))] * count,
@@ -592,39 +619,23 @@
     )
 
 
-def early_chips_kernel(ids_ref, own_ref, arrived_ref, *rest):
-    for partner, out_ref in enumerate(rest[-4:]):
-        for n in range(2):
-            block = (ids_ref[X] ^ partner) * 2 + n
-            out_ref[n] = (own_ref[block].astype(F32) + arrived_ref[block].astype(F32)).astype(BF)
-
-
-def early_last_kernel(ids_ref, *refs):
-    for partner, out_ref in enumerate(refs[4:]):
-        block = ids_ref[YHI] ^ partner
-        total = refs[0][block].astype(F32)
-        for ref in refs[1:4]:
-            total += ref[block].astype(F32)
-        out_ref[...] = total.astype(BF)
-
-
 def early_half_kernel(ids_ref, left_ref, left_in, right_ref, right_in, own_ref, *outs):
     for columns, (ref, arrived) in enumerate(((left_ref, left_in), (right_ref, right_in))):
-        total = (ref[0].astype(F32) + arrived[0].astype(F32)).astype(BF)
-        own_ref[0, :, 512 * columns : 512 * columns + 512] = total[:64]
-        outs[columns][0] = total[64:]
+        total = (ref[...].astype(F32) + arrived[...].astype(F32)).astype(BF)
+        own_ref[:, :, 512 * columns : 512 * columns + 512] = total[:, :64]
+        outs[columns][...] = total[:, 64:]
 
 
 def early_half(ids, parts):
     left, left_give, right, right_give = parts
     operands = [left, swap(left_give, "mode", 2), right, swap(right_give, "mode", 6)]
-    narrow = pl.BlockSpec((1, 64, 512), lambda i, c: (i, 0, 0))
+    narrow = pl.BlockSpec((2, 64, 512), lambda i, c: (i, 0, 0))
     return prefetched(
         early_half_kernel, ids, operands,
-        [pl.BlockSpec((1, 128, 512), lambda i, c: (i, 0, 0))] * 4,
-        [pl.BlockSpec((1, 64, D), lambda i, c: (i, 0, 0)), narrow, narrow],
-        [jax.ShapeDtypeStruct((8, 64, D), BF)] + [jax.ShapeDtypeStruct((8, 64, 512), BF)] * 2,
-        "early_half", (8,),
+        [pl.BlockSpec((2, 128, 512), lambda i, c: (i, 0, 0))] * 4,
+        [pl.BlockSpec((2, 64, D), lambda i, c: (i, 0, 0)), narrow, narrow],
+        [pltpu.HBM((8, 64, D), BF)] + [jax.ShapeDtypeStruct((8, 64, 512), BF)] * 2,
+        "early_half", (4,),
     )
 
 
@@ -639,26 +650,15 @@
             ).astype(BF)
 
 
-def early_sums(ids, own, left, right, waits):
+def early_sums(ids, own, left, right):
     narrow = pl.BlockSpec((2, 64, 512), lambda i, c: (i, 0, 0))
     keep, give = prefetched(
         early_z_kernel, ids, [own, left, right],
         [pl.BlockSpec((2, 64, D), lambda i, c: (i, 0, 0)), narrow, narrow],
         [pl.BlockSpec((2, 32, D), lambda i, c: (i, 0, 0))] * 2,
-        [jax.ShapeDtypeStruct((8, 32, D), BF)] * 2, "early_z", (4,),
-    )
-    arrived = swap(give, "mode", 1)
-    parts = prefetched(
-        early_chips_kernel, ids, [keep, arrived, *waits],
-        [fixed((8, 32, D))] * 2 + [unused] * len(waits), [fixed((2, 32, D))] * 4,
-        [jax.ShapeDtypeStruct((2, 32, D), BF)] * 4, "early_chips", (1,),
-    )
-    keep, give = prefetched(
-        early_last_kernel, ids, swap_all(parts, "agent", 4),
-        [fixed((2, 32, D))] * 4, [fixed((32, D))] * 2,
-        [jax.ShapeDtypeStruct((32, D), BF)] * 2, "early_last", (1,),
-    )
-    return keep.astype(F32) + swap(give, "agent", 2).astype(F32)
+        [pltpu.HBM((8, 32, D), BF), jax.ShapeDtypeStruct((8, 32, D), BF)], "early_z", (4,),
+    )
+    return keep, swap(give, "mode", 1)
 
 
 WIDE = 384 + D
@@ -733,7 +733,7 @@
         pl.BlockSpec((ROWS, D), lambda i, c: (0, 0)),
     ]
     return prefetched(
-        late_kernel, ids, list(hiddens) + [grads, grads, mixed, grad_after, *waits],
+        late_kernel, ids, list(hiddens) + [grads, grads, mixed, grad_after, *map(pinned, waits)],
         in_specs + [unused] * len(waits),
         [pl.BlockSpec((2, ROWS, WIDE), lambda i, c: (0, 0, 0))]
         + [pl.BlockSpec((ROWS, WIDE), lambda i, c: (0, 0))] * 2,
@@ -743,42 +743,77 @@
     )
 
 
-def late_chips_kernel(ids_ref, own_ref, arrived_ref, *rest):
+def chips_kernel(ids_ref, early_ref, early_in, late_ref, late_in, *rest):
     outs, total_ref = rest[:-1], rest[-1]
-    total_ref[...] = own_ref[...].astype(F32) + arrived_ref[...].astype(F32)
+    total_ref[...] = late_ref[...].astype(F32) + late_in[...].astype(F32)
     for partner, out_ref in enumerate(outs):
-        slot = jnp.minimum(ids_ref[X] ^ partner, 2)
-        lanes = pl.ds(pl.multiple_of(slot * 128, 128), 128)
-        out_ref[:, :, :128] = total_ref[:, :, lanes].astype(BF)
-        out_ref[:, :, 128:] = total_ref[:, :, 384:].astype(BF)
-
-
-def late_turn_kernel(ids_ref, *refs):
+        chip_x = ids_ref[X] ^ partner
+        lanes = pl.ds(pl.multiple_of(jnp.minimum(chip_x, 2) * 128, 128), 128)
+        for n in range(2):
+            block = chip_x * 2 + n
+            out_ref[n, :, :D] = (early_ref[block].astype(F32) + early_in[block].astype(F32)).astype(
+                BF
+            )
+        out_ref[:, :, D : D + 128] = total_ref[:, :, lanes].astype(BF)
+        out_ref[:, :, D + 128 :] = total_ref[:, :, 384:].astype(BF)
+
+
+def cross_kernel(ids_ref, *refs):
     for other, out_ref in enumerate(refs[4:]):
         row = ids_ref[YHI] ^ other
-        total = refs[0][row, :, 128:].astype(F32)
-        for ref in refs[1:4]:
-            total += ref[row, :, 128:].astype(F32)
+        for source, target in ((0, 0), (D + 128, 384)):
+            total = refs[0][row, :, source : source + D].astype(F32)
+            for ref in refs[1:4]:
+                total += ref[row, :, source : source + D].astype(F32)
+            for place in range(4):
+                out_ref[place, :, target : target + 256] = total[
+                    :, 256 * place : 256 * place + 256
+                ].astype(BF)
         for partner, ref in enumerate(refs[:4]):
-            out_ref[partner, :, :128] = ref[row, :, :128]
-            out_ref[partner, :, 128:] = total[:, 256 * partner : 256 * partner + 256].astype(BF)
-
-
-def late_last_kernel(ids_ref, keep_ref, arrived_ref, out_ref):
+            out_ref[partner, :, 256:384] = ref[row, :, D : D + 128]
+
+
+def last_kernel(ids_ref, keep_ref, arrived_ref, agent_ref, mode_ref):
+    for place in range(4):
+        lanes = slice(256 * place, 256 * place + 256)
+        mode_ref[:, lanes] = keep_ref[place, :, :256].astype(F32) + arrived_ref[
+            place, :, :256
+        ].astype(F32)
+
     @pl.when(ids_ref[X] < 3)
     def _():
         for other, ref in enumerate((keep_ref, arrived_ref)):
             for partner in range(4):
                 pair = (ids_ref[X] ^ partner) * 2 + (ids_ref[YHI] ^ other)
                 lanes = pl.ds(pl.multiple_of(pair * 128, 128), 128)
-                out_ref[:, lanes] = ref[partner, :, :128].astype(F32)
+                agent_ref[:, lanes] = ref[partner, :, 256:384].astype(F32)
 
     @pl.when(ids_ref[X] == 3)
     def _():
-        for partner in range(4):
-            out_ref[:, 256 * partner : 256 * partner + 256] = keep_ref[partner, :, 128:].astype(
-                F32
-            ) + arrived_ref[partner, :, 128:].astype(F32)
+        for place in range(4):
+            lanes = slice(256 * place, 256 * place + 256)
+            agent_ref[:, lanes] = keep_ref[place, :, 384:].astype(F32) + arrived_ref[
+                place, :, 384:
+            ].astype(F32)
+
+
+def chip_sums(ids, early, late):
+    parts = prefetched(
+        chips_kernel, ids, [*early, *late],
+        [fixed((8, 32, D))] * 2 + [fixed((2, 32, WIDE))] * 2, [fixed((2, 32, 128 + 2 * D))] * 4,
+        [jax.ShapeDtypeStruct((2, 32, 128 + 2 * D), BF)] * 4, "chips", (1,),
+        [pltpu.VMEM((2, 32, WIDE), F32)],
+    )
+    keep, give = prefetched(
+        cross_kernel, ids, swap_all(parts, "agent", 4),
+        [fixed((2, 32, 128 + 2 * D))] * 4, [fixed((4, 32, 640))] * 2,
+        [jax.ShapeDtypeStruct((4, 32, 640), BF)] * 2, "cross", (1,),
+    )
+    return prefetched(
+        last_kernel, ids, [keep, swap(give, "agent", 2)],
+        [fixed((4, 32, 640))] * 2, [fixed((32, D))] * 2,
+        [jax.ShapeDtypeStruct((32, D), F32)] * 2, "last", (1,),
+    )
 
 
 def late_add_kernel(ids_ref, mine_ref, first_ref, second_ref, *rest):
@@ -792,29 +827,14 @@
 def late_sums(ids, mine, first, second, waits):
     parts = prefetched(
         late_add_kernel, ids,
-        [mine, swap(first, "agent", 1), swap(second, "agent", 1), *waits],
-        [fixed((2, ROWS, WIDE))] + [fixed((ROWS, WIDE))] * 2 + [unused] * len(waits),
+        [mine, swap(first, "agent", 1), swap(second, "agent", 1)],
+        [fixed((2, ROWS, WIDE))] + [fixed((ROWS, WIDE))] * 2,
         [fixed((2, 64, WIDE))] * 4,
-        [jax.ShapeDtypeStruct((2, 64, WIDE), BF)] * 4, "late_add", (1,),
+        [pltpu.HBM((2, 64, WIDE), BF)] + [jax.ShapeDtypeStruct((2, 64, WIDE), BF)] * 3, "late_add", (1,),
         [pltpu.VMEM((ROWS, WIDE), F32)],
     )
-    keep, give = sum_split(ids, swap_all(parts, "mode", 2), YLO, 2, "late_z")
-    parts = prefetched(
-        late_chips_kernel, ids, [keep, swap(give, "mode", 1)],
-        [fixed((2, 32, WIDE))] * 2, [fixed((2, 32, 128 + D))] * 4,
-        [jax.ShapeDtypeStruct((2, 32, 128 + D), BF)] * 4, "late_chips", (1,),
-        [pltpu.VMEM((2, 32, WIDE), F32)],
-    )
-    keep, give = prefetched(
-        late_turn_kernel, ids, swap_all(parts, "agent", 4),
-        [fixed((2, 32, 128 + D))] * 4, [fixed((4, 32, 384))] * 2,
-        [jax.ShapeDtypeStruct((4, 32, 384), BF)] * 2, "late_turn", (1,),
-    )
-    return prefetched(
-        late_last_kernel, ids, [keep, swap(give, "agent", 2)],
-        [fixed((4, 32, 384))] * 2, fixed((32, D)),
-        jax.ShapeDtypeStruct((32, D), F32), "late_last", (1,),
-    )
+    keep, give = sum_split(ids, swap_all(parts, "mode", 2), YLO, 2, "late_z", waits)
+    return keep, swap(give, "mode", 1)
 
 
 def exchange(values, axis):
@@ -856,8 +876,9 @@
         ids, hiddens, returning, mixed_one, grad_after, [left, right]
     )
     token_grads = leave(returned_one, tokens_a, grad_after, weights)
-    agent_weight_grads = late_sums(ids, *late_parts, [])
-    mode_weight_grads = early_sums(ids, own, left, right, [token_grads])
+    late = late_sums(ids, *late_parts, [token_grads])
+    early = early_sums(ids, own, left, right)
+    agent_weight_grads, mode_weight_grads = chip_sums(ids, early, late)
     return (token_grads.reshape(tokens.shape), agent_weight_grads, mode_weight_grads)
 
 

time: 297 us -> 285 us (0.960)
  local copies, waits for them, and re-layouts: 26.3 us -> 14.1 us
  waiting for transfers between devices: 117 us -> 126 us
  starting transfers between devices: 67.4 us -> 59 us
    unnamed x74 -> x58, local copies, waits for them, and re-layouts: 23.1 us -> 11.7 us
    ppermute x25 -> x21, waiting for transfers between devices: 88.1 us -> 96.9 us  [swap(): return lax.ppermute(values, axis, [(n, n ^ bits) for n in range(size)])]
    ppermute x25 -> x21, starting transfers between devices: 35.6 us -> 26.9 us  [swap(): return lax.ppermute(values, axis, [(n, n ^ bits) for n in range(size)])]
    pallas_call x12 -> x10, Pallas kernels: 33.8 us -> 35 us  [prefetched(): pl.pallas_call(kernel, grid_spec=pltpu.PrefetchScalarGridSpec(num_scalar_...]
  transfers between devices with their start and end apart: 31 -> 27, of which waited for: 17 -> 19; matrix products, arithmetic and copies ran while one was open for 2% -> 1% of each run, Pallas kernels for 16% -> 16%
where the time goes in v4:
time: 285 us; the launch traced here: 283 us
  waiting for transfers between devices  126 us (44%)
  Pallas kernels  80.7 us (28%)
  starting transfers between devices  59 us (21%)
  local copies, waits for them, and re-layouts  14.1 us (5%)
    ppermute x21, waiting for transfers between devices, swap(): return lax.ppermute(values, axis, [(n, n ^ bits) for n in range(size)])  96.9 us
    pallas_call x10, Pallas kernels, prefetched(): pl.pallas_call(kernel, grid_spec=pltpu.PrefetchScalarGridSpec(num_scalar_...  35 us
    all_to_all x6, starting transfers between devices, exchange(): return lax.all_to_all(values, axis, split_axis=0, concat_axis=0, tiled=True)  32.1 us
    all_to_all x6, waiting for transfers between devices, exchange(): return lax.all_to_all(values, axis, split_axis=0, concat_axis=0, tiled=True)  29.3 us
    ppermute x21, starting transfers between devices, swap(): return lax.ppermute(values, axis, [(n, n ^ bits) for n in range(size)])  26.9 us
    unnamed x58, local copies, waits for them, and re-layouts  11.7 us
    pallas_call x1, Pallas kernels, mode_attention(): pl.pallas_call(mode_kernel, grid=(4,), in_specs=[spec] + [unused] * len(a...  9.46 us
    pallas_call x1, Pallas kernels, middle(): pl.pallas_call(middle_kernel, grid=(5,), in_specs=[fixed((ROWS, D)), fixe...  7.95 us
  transfers between devices with their start and end apart: 27, of which 19 were waited for; matrix products, arithmetic and copies ran while one was open for 1% of the time, Pallas kernels for 16%

profile of v4, /device:TPU:0, one launch (start us, length us, event | category | flops | bytes accessed | tf_op | source)
XLA Modules:
  0.0 283.1 jit_solution(4026480300021041417)
XLA Ops:
  1.9 5.5 %enter.1 = (bf16[16,384,128]{2,1,0:T(8,128)(2,1)}, bf16[256,1024]{1,0:T(8,128)(2,1)}, bf16[128,1024]{1,0:T(8,128)(2,1)}, bf16[128,1024]{1,0:T(8,128)(2,1)S(1)}) custom-call(s32[7]{0:T(128)S(1)} %stack.40.ids_ref, bf16[256,1024]{1,0:T(8,128)(2,1)S(1)} %reshape.64.tokens_ref, bf16[8,1024,1024]{2,1,0:T(8,128)(2,1)} %weights_ref.7), custom_call_target="tpu_custom_call" | custom-call | flops 1610612736 | bytes 8388608 | tf_op jit(solution)/shard_map/enter/pallas_call | solution.py:178
  7.4 7.3 %all-to-all-start = ((bf16[16,384,128]{2,1,0:T(8,128)(2,1)}), bf16[16,384,128]{2,1,0:T(8,128)(2,1)S(1)}, u32[]{:S(2)}, u32[]{:S(2)}) async-start(bf16[16,384,128]{2,1,0:T(8,128)(2,1)} %get-tuple-element.53), calls=%async_computation | async-start | bytes 3145728 | tf_op jit(solution)/shard_map/all_to_all | solution.py:841
  16.3 3.4 %collective-permute-start.1 = (bf16[256,1024]{1,0:T(8,128)(2,1)S(1)}, bf16[256,1024]{1,0:T(8,128)(2,1)}, u32[]{:S(2)}, u32[]{:S(2)}) collective-permute-start(bf16[256,1024]{1,0:T(8,128)(2,1)S(1)} %constant_dynamic-update-slice_fusion), channel_id=1, source_target_pairs={{0,16},{8,24},{16,0},{24,8},{32,48},{40,56},{48,32},{56,40},{64,80... | collective-permute-start | bytes 1572872 | tf_op jit(solution)/shard_map/ppermute | solution.py:514
  19.8 18.5 %all-to-all-done.query_ref.keys_ref.values_ref.q.k.v = bf16[16,384,128]{2,1,0:T(8,128)(2,1)S(1)} async-done(((bf16[16,384,128]{2,1,0:T(8,128)(2,1)}), bf16[16,384,128]{2,1,0:T(8,128)(2,1)S(1)}, u32[]{:S(2)}, u32[]{:S(2)}) %all-to-all-start) | async-done | bytes 1572896 | tf_op jit(solution)/shard_map/all_to_all | solution.py:841
  38.3 4.7 %agent_forward.1 = (bf16[16,128,128]{2,1,0:T(8,128)(2,1)}, f32[4,4,256,128]{3,2,1,0:T(8,128)}) custom-call(bf16[16,384,128]{2,1,0:T(8,128)(2,1)S(1)} %all-to-all-done.query_ref.keys_ref.values_ref.q.k.v, bf16[16,384,128]{2,1,0:T(8,128)(2,1)S(1)} %all-to-all-done.query_ref.keys_ref.values_ref.q.k.v, ...), custom_call_target="tpu_custom_call" | custom-call | flops 3000000000 | bytes 4194304 | tf_op jit(solution)/shard_map/agent_forward/pallas_call | solution.py:228
  43.0 4.4 %all-to-all-start.1 = ((bf16[16,128,128]{2,1,0:T(8,128)(2,1)}), bf16[16,128,128]{2,1,0:T(8,128)(2,1)S(1)}, u32[]{:S(2)}, u32[]{:S(2)}) async-start(bf16[16,128,128]{2,1,0:T(8,128)(2,1)} %get-tuple-element.55), calls=%async_computation.1 | async-start | bytes 1048576 | tf_op jit(solution)/shard_map/all_to_all | solution.py:841
  47.6 2.1 pad_maximum_fusion.rest_0_.refs_0_
  49.7 10.1 %all-to-all-done.1 = bf16[16,128,128]{2,1,0:T(8,128)(2,1)S(1)} async-done(((bf16[16,128,128]{2,1,0:T(8,128)(2,1)}), bf16[16,128,128]{2,1,0:T(8,128)(2,1)S(1)}, u32[]{:S(2)}, u32[]{:S(2)}) %all-to-all-start.1) | async-done | bytes 524320 | tf_op jit(solution)/shard_map/all_to_all | solution.py:841
  59.8 8.0 %middle.1 = (bf16[8,4,256,128]{3,2,1,0:T(8,128)(2,1)S(1)}, bf16[256,1024]{1,0:T(8,128)(2,1)}, bf16[8,256,128]{2,1,0:T(8,128)(2,1)}, bf16[256,1024]{1,0:T(8,128)(2,1)}) custom-call(bf16[256,1024]{1,0:T(8,128)(2,1)S(1)} %copy-done.6, bf16[8,256,128]{2,1,0:T(8,128)(2,1)S(1)} %bitcast.25, bf16[256,1024]{1,0:T(8,128)(2,1)S(1)} %reshape.67.cotangent_ref, ...), custom_call_target="tpu_custom_call" | custom-call | flops 2684354560 | bytes 13631488 | tf_op jit(solution)/shard_map/middle/pallas_call | solution.py:339
  69.1 5.6 %all-to-all-start.2 = ((bf16[8,1024,128]{2,1,0:T(8,128)(2,1)}), bf16[8,1024,128]{2,1,0:T(8,128)(2,1)S(1)}, u32[]{:S(2)}, u32[]{:S(2)}) async-start(bf16[8,1024,128]{2,1,0:T(8,128)(2,1)} %bitcast.27), calls=%async_computation.2 | async-start | bytes 4194304 | tf_op jit(solution)/shard_map/all_to_all | solution.py:841
  75.7 24.2 %collective-permute-done.3.rest_1_.refs_3_ = bf16[2,256,1024]{2,1,0:T(8,128)(2,1)S(1)} collective-permute-done((bf16[2,256,1024]{2,1,0:T(8,128)(2,1)S(1)}, bf16[2,256,1024]{2,1,0:T(8,128)(2,1)S(1)}, u32[]{:S(2)}, u32[]{:S(2)}) %collective-permute-start.3) | collective-permute-done | bytes 1048608 | tf_op jit(solution)/shard_map/ppermute | solution.py:514
  101.0 9.5 %mode_attention.1 = bf16[8,4,256,128]{3,2,1,0:T(8,128)(2,1)} custom-call(bf16[8,4,256,128]{3,2,1,0:T(8,128)(2,1)S(1)} %bitcast.28, bf16[2,256,1024]{2,1,0:T(8,128)(2,1)} %collective-permute-done.2.rest_0_.refs_1_, bf16[2,256,1024]{2,1,0:T(8,128)(2,1)} %copy-done.17), custom_call_target="tpu_custom_call" | custom-call | flops 8000000000 | bytes 4194304 | tf_op jit(solution)/shard_map/mode_attention/pallas_call | solution.py:394
  110.5 5.3 %all-to-all-start.3 = ((bf16[8,1024,128]{2,1,0:T(8,128)(2,1)}), bf16[8,1024,128]{2,1,0:T(8,128)(2,1)S(1)}, u32[]{:S(2)}, u32[]{:S(2)}) async-start(bf16[8,1024,128]{2,1,0:T(8,128)(2,1)} %bitcast.29), calls=%async_computation.3 | async-start | bytes 4194304 | tf_op jit(solution)/shard_map/all_to_all | solution.py:841
  116.5 23.4 %collective-permute-done.4.rest_0_.refs_2_ = bf16[2,256,1024]{2,1,0:T(8,128)(2,1)} collective-permute-done((bf16[2,256,1024]{2,1,0:T(8,128)(2,1)S(1)}, bf16[2,256,1024]{2,1,0:T(8,128)(2,1)}, u32[]{:S(2)}, u32[]{:S(2)}) %collective-permute-start.4) | collective-permute-done | bytes 1048608 | tf_op jit(solution)/shard_map/ppermute | solution.py:514
  142.7 3.7 %early_first.1 = bf16[8,256,1024]{2,1,0:T(8,128)(2,1)S(1)} custom-call(s32[7]{0:T(128)S(1)} %constant_dynamic-update-slice_fusion.2.ids_ref, bf16[8,256,128]{2,1,0:T(8,128)(2,1)S(1)} %copy-done.13, bf16[8,4,256,128]{3,2,1,0:T(8,128)(2,1)S(1)} %bitcast.19, bf16[8,4,256,128]{3,2,1,0:T(8,128)(2,1)S(1)} %bitcast.20, bf16[256,1024]{1,0:T(8,128)(2,1)S(1)} %copy-done.3, ...), custom_call_target="tpu_custom_call" | custom-call | flops 1000000000 | bytes 5242880 | tf_op jit(solution)/shard_map/early_first/pallas_call | solution.py:522
  146.5 7.1 %collective-permute-done.5.rest_0_ = bf16[8,256,1024]{2,1,0:T(8,128)(2,1)S(1)} collective-permute-done((bf16[8,256,1024]{2,1,0:T(8,128)(2,1)S(1)}, bf16[8,256,1024]{2,1,0:T(8,128)(2,1)S(1)}, u32[]{:S(2)}, u32[]{:S(2)}) %collective-permute-start.5) | collective-permute-done | bytes 4194336 | tf_op jit(solution)/shard_map/ppermute | solution.py:514
  153.7 6.0 %early_add.1 = (bf16[8,128,512]{2,1,0:T(8,128)(2,1)}, bf16[8,128,512]{2,1,0:T(8,128)(2,1)}, bf16[8,128,512]{2,1,0:T(8,128)(2,1)}, bf16[8,128,512]{2,1,0:T(8,128)(2,1)}) custom-call(s32[7]{0:T(128)S(1)} %stack.40.ids_ref, bf16[8,256,128]{2,1,0:T(8,128)(2,1)S(1)} %copy-done.14, bf16[8,4,256,128]{3,2,1,0:T(8,128)(2,1)S(1)} %bitcast.21, ...), custom_call_target="tpu_custom_call" | custom-call | flops 1000000000 | bytes 5242880 | tf_op jit(solution)/shard_map/early_add/pallas_call | solution.py:522
  160.7 2.1 collective-permute-start.7
  162.8 7.1 %turn.1 = (bf16[16,128,128]{2,1,0:T(8,128)(2,1)}, bf16[256,1024]{1,0:T(8,128)(2,1)}) custom-call(bf16[8,4,256,128]{3,2,1,0:T(8,128)(2,1)S(1)} %bitcast.23, bf16[256,1024]{1,0:T(8,128)(2,1)S(1)} %copy-done.4, bf16[256,1024]{1,0:T(8,128)(2,1)S(1)} %copy-done.20, bf16[8,1024,1024]{2,1,0:T(8,128)(2,1)} %weights_ref.7, ...), custom_call_target="tpu_custom_call" | custom-call | flops 2147483648 | bytes 12582912 | tf_op jit(solution)/shard_map/turn/pallas_call | solution.py:441
  169.8 4.8 %all-to-all-start.4 = ((bf16[16,128,128]{2,1,0:T(8,128)(2,1)}), bf16[16,128,128]{2,1,0:T(8,128)(2,1)S(1)}, u32[]{:S(2)}, u32[]{:S(2)}) async-start(bf16[16,128,128]{2,1,0:T(8,128)(2,1)} %get-tuple-element.63), calls=%async_computation.4 | async-start | bytes 1048576 | tf_op jit(solution)/shard_map/all_to_all | solution.py:841
  174.7 10.5 %collective-permute-done.6.left_in = bf16[8,128,512]{2,1,0:T(8,128)(2,1)} collective-permute-done((bf16[8,128,512]{2,1,0:T(8,128)(2,1)}, bf16[8,128,512]{2,1,0:T(8,128)(2,1)}, u32[]{:S(2)}, u32[]{:S(2)}) %collective-permute-start.6) | collective-permute-done | bytes 1048608 | tf_op jit(solution)/shard_map/ppermute | solution.py:514
  185.2 2.0 collective-permute-done.7.right_in
  189.6 4.3 %early_half.1 = (bf16[8,64,1024]{2,1,0:T(8,128)(2,1)}, bf16[8,64,512]{2,1,0:T(8,128)(2,1)}, bf16[8,64,512]{2,1,0:T(8,128)(2,1)}) custom-call(s32[7]{0:T(128)S(1)} %stack.40.ids_ref, bf16[8,128,512]{2,1,0:T(8,128)(2,1)S(1)} %copy-done.5, bf16[8,128,512]{2,1,0:T(8,128)(2,1)} %collective-permute-done.6.left_in, bf16[8,128,512]{2,1,0:T(8,128)(2,1)S(1)} %copy-done.19, ...), custom_call_target="tpu_custom_call" | custom-call | flops 1000000000 | bytes 5242880 | tf_op jit(solution)/shard_map/early_half/pallas_call | solution.py:522
  193.9 2.1 collective-permute-start.8
  196.0 1.6 copy-done.24
  197.6 5.9 %agent_backward.1.refs_4_.refs_5_ = bf16[16,3,128,128]{3,2,1,0:T(8,128)(2,1)} custom-call(bf16[16,384,128]{2,1,0:T(8,128)(2,1)S(1)} %copy-done.16, bf16[16,384,128]{2,1,0:T(8,128)(2,1)S(1)} %copy-done.16, bf16[16,384,128]{2,1,0:T(8,128)(2,1)S(1)} %copy-done.16, bf16[16,128,128]{2,1,0:T(8,128)(2,1)S(1)} %all-to-all-done.4.g, ...), custom_call_target="tpu_custom_call" | custom-call | flops 6000000000 | bytes 6291456 | tf_op jit(solution)/shard_map/agent_backward/pallas_call | solution.py:283
  203.5 4.8 %all-to-all-start.5 = ((bf16[16,384,128]{2,1,0:T(8,128)(2,1)}), bf16[16,384,128]{2,1,0:T(8,128)(2,1)S(1)}, u32[]{:S(2)}, u32[]{:S(2)}) async-start(bf16[16,384,128]{2,1,0:T(8,128)(2,1)} %bitcast.16), calls=%async_computation.5 | async-start | bytes 3145728 | tf_op jit(solution)/shard_map/all_to_all | solution.py:841
  211.1 10.2 %late_products.1 = (bf16[2,256,1408]{2,1,0:T(8,128)(2,1)S(1)}, bf16[256,1408]{1,0:T(8,128)(2,1)S(1)}, bf16[256,1408]{1,0:T(8,128)(2,1)S(1)}) custom-call(s32[7]{0:T(128)S(1)} %stack.40.ids_ref, bf16[2,256,1024]{2,1,0:T(8,128)(2,1)S(1)} %copy-done, bf16[2,256,1024]{2,1,0:T(8,128)(2,1)} %collective-permute-done.2.rest_0_.refs_1_, ...), custom_call_target="tpu_custom_call" | custom-call | flops 1000000000 | bytes 5242880 | tf_op jit(solution)/shard_map/late_products/pallas_call | solution.py:522
  221.9 1.7 collective-permute-done.11.first_ref
  224.6 2.2 late_add.1
  226.8 1.5 collective-permute-start.13
  228.3 1.4 collective-permute-start.14
  229.7 1.7 collective-permute-start.15
  231.5 4.0 %early_z.1 = (bf16[8,32,1024]{2,1,0:T(8,128)(2,1)}, bf16[8,32,1024]{2,1,0:T(8,128)(2,1)}) custom-call(s32[7]{0:T(128)S(1)} %stack.40.ids_ref, bf16[8,64,1024]{2,1,0:T(8,128)(2,1)S(1)} %copy-done.21, bf16[8,64,512]{2,1,0:T(8,128)(2,1)} %collective-permute-done.8.left_ref.refs_8_, bf16[8,64,512]{2,1,0:T(8,128)(2,1)} %collective-permute-done.9.right_ref.refs_9_), custom_call_target="tpu_custom_call" | custom-call | flops 1000000000 | bytes 5242880 | tf_op jit(solution)/shard_map/early_z/pallas_call | solution.py:522
  235.5 1.5 collective-permute-start.10
  236.9 5.0 %leave.1.refs_4_ = bf16[256,1024]{1,0:T(8,128)(2,1)S(1)} custom-call(bf16[16,3,128,128]{3,2,1,0:T(8,128)(2,1)S(1)} %bitcast.24, bf16[256,1024]{1,0:T(8,128)(2,1)S(1)} %copy-done.7, bf16[256,1024]{1,0:T(8,128)(2,1)S(1)} %copy-done.9, bf16[8,1024,1024]{2,1,0:T(8,128)(2,1)} %weights_ref.7), custom_call_target="tpu_custom_call" | custom-call | flops 1610612736 | bytes 9437184 | tf_op jit(solution)/shard_map/leave/pallas_call | solution.py:490
  242.8 3.5 %collective-permute-done.14.refs_2_ = bf16[2,64,1408]{2,1,0:T(8,128)(2,1)} collective-permute-done((bf16[2,64,1408]{2,1,0:T(8,128)(2,1)}, bf16[2,64,1408]{2,1,0:T(8,128)(2,1)}, u32[]{:S(2)}, u32[]{:S(2)}) %collective-permute-start.14) | collective-permute-done | bytes 360480 | tf_op jit(solution)/shard_map/ppermute | solution.py:514
  246.3 2.4 collective-permute-done.15.refs_3_
  248.7 2.0 late_z.1
  250.7 1.5 collective-permute-start.16
  252.2 4.0 %collective-permute-done.16.late_in = bf16[2,32,1408]{2,1,0:T(8,128)(2,1)S(1)} collective-permute-done((bf16[2,32,1408]{2,1,0:T(8,128)(2,1)S(1)}, bf16[2,32,1408]{2,1,0:T(8,128)(2,1)S(1)}, u32[]{:S(2)}, u32[]{:S(2)}) %collective-permute-start.16) | collective-permute-done | bytes 180256 | tf_op jit(solution)/shard_map/ppermute | solution.py:514
  257.0 1.5 collective-permute-start.17
  258.6 2.7 collective-permute-start.18
  261.8 4.4 %collective-permute-done.17.refs_1_ = bf16[2,32,2176]{2,1,0:T(8,128)(2,1)S(1)} collective-permute-done((bf16[2,32,2176]{2,1,0:T(8,128)(2,1)S(1)}, bf16[2,32,2176]{2,1,0:T(8,128)(2,1)S(1)}, u32[]{:S(2)}, u32[]{:S(2)}) %collective-permute-start.17) | collective-permute-done | bytes 278560 | tf_op jit(solution)/shard_map/ppermute | solution.py:514
  266.2 5.4 %collective-permute-done.18.refs_2_ = bf16[2,32,2176]{2,1,0:T(8,128)(2,1)S(1)} collective-permute-done((bf16[2,32,2176]{2,1,0:T(8,128)(2,1)S(1)}, bf16[2,32,2176]{2,1,0:T(8,128)(2,1)S(1)}, u32[]{:S(2)}, u32[]{:S(2)}) %collective-permute-start.18) | collective-permute-done | bytes 278560 | tf_op jit(solution)/shard_map/ppermute | solution.py:514
  271.7 2.6 collective-permute-done.19.refs_3_
  275.0 3.0 %collective-permute-start.20 = (bf16[4,32,640]{2,1,0:T(8,128)(2,1)S(1)}, bf16[4,32,640]{2,1,0:T(8,128)(2,1)S(1)}, u32[]{:S(2)}, u32[]{:S(2)}) collective-permute-start(bf16[4,32,640]{2,1,0:T(8,128)(2,1)S(1)} %get-tuple-element.88), channel_id=1, source_target_pairs={{0,16},{8,24},{16,0},{24,8},{32,48},{40,56},{48,32},{56,40},{64,80... | collective-permute-start | bytes 491528 | tf_op jit(solution)/shard_map/ppermute | solution.py:514
  279.0 2.9 %collective-permute-done.20.arrived_ref = bf16[4,32,640]{2,1,0:T(8,128)(2,1)S(1)} collective-permute-done((bf16[4,32,640]{2,1,0:T(8,128)(2,1)S(1)}, bf16[4,32,640]{2,1,0:T(8,128)(2,1)S(1)}, u32[]{:S(2)}, u32[]{:S(2)}) %collective-permute-start.20) | collective-permute-done | bytes 163872 | tf_op jit(solution)/shard_map/ppermute | solution.py:514
  (89 shorter events, 23.0 us)
Async XLA Ops:
  7.4 7.7 %copy-start.26 = (bf16[128,1024]{1,0:T(8,128)(2,1)S(1)}, bf16[128,1024]{1,0:T(8,128)(2,1)}, u32[]{:S(2)}) copy-start(bf16[128,1024]{1,0:T(8,128)(2,1)} %get-tuple-element.56) | copy-start | bytes 786436
  7.4 7.7 %copy-start.27 = (s32[128]{0:T(128)S(1)}, s32[128]{0:T(128)}, u32[]{:S(2)}) copy-start(s32[128]{0:T(128)} %param.9) | copy-start | bytes 1540
  7.4 30.9 %all-to-all-start = ((bf16[16,384,128]{2,1,0:T(8,128)(2,1)}), bf16[16,384,128]{2,1,0:T(8,128)(2,1)S(1)}, u32[]{:S(2)}, u32[]{:S(2)}) async-start(bf16[16,384,128]{2,1,0:T(8,128)(2,1)} %get-tuple-element.53), calls=%async_computation | async-start | bytes 3145728 | tf_op jit(solution)/shard_map/all_to_all | solution.py:841
  14.7 1.6 collective-permute-start
  16.3 31.1 %copy-start.25 = (bf16[8,8,4,1024]{3,2,1,0:T(4,128)(2,1)S(1)}, bf16[8,8,4,1024]{3,2,1,0:T(4,128)(2,1)}, u32[]{:S(2)}) copy-start(bf16[8,8,4,1024]{3,2,1,0:T(4,128)(2,1)} %param.7) | copy-start | bytes 1572868
  16.3 31.2 %collective-permute-start.1 = (bf16[256,1024]{1,0:T(8,128)(2,1)S(1)}, bf16[256,1024]{1,0:T(8,128)(2,1)}, u32[]{:S(2)}, u32[]{:S(2)}) collective-permute-start(bf16[256,1024]{1,0:T(8,128)(2,1)S(1)} %constant_dynamic-update-slice_fusion), channel_id=1, source_target_pairs={{0,16},{8,24},{16,0},{24,8},{32,48},{40,56},{48,32},{56,40},{64,80... | collective-permute-start | bytes 1572872 | tf_op jit(solution)/shard_map/ppermute | solution.py:514
  38.3 4.7 %copy-start.15 = (bf16[16,384,128]{2,1,0:T(8,128)(2,1)}, bf16[16,384,128]{2,1,0:T(8,128)(2,1)S(1)}, u32[]{:S(2)}) copy-start(bf16[16,384,128]{2,1,0:T(8,128)(2,1)S(1)} %all-to-all-done.query_ref.keys_ref.values_ref.q.k.v) | copy-start | bytes 4718596
  43.0 16.7 %copy-start.6 = (bf16[256,1024]{1,0:T(8,128)(2,1)S(1)}, bf16[256,1024]{1,0:T(8,128)(2,1)}, u32[]{:S(2)}) copy-start(bf16[256,1024]{1,0:T(8,128)(2,1)} %get-tuple-element.54.tokens_ref) | copy-start | bytes 1572868
  43.0 16.7 %all-to-all-start.1 = ((bf16[16,128,128]{2,1,0:T(8,128)(2,1)}), bf16[16,128,128]{2,1,0:T(8,128)(2,1)S(1)}, u32[]{:S(2)}, u32[]{:S(2)}) async-start(bf16[16,128,128]{2,1,0:T(8,128)(2,1)} %get-tuple-element.55), calls=%async_computation.1 | async-start | bytes 1048576 | tf_op jit(solution)/shard_map/all_to_all | solution.py:841
  59.8 8.0 %copy-start.1 = (bf16[16,128,128]{2,1,0:T(8,128)(2,1)}, bf16[16,128,128]{2,1,0:T(8,128)(2,1)S(1)}, u32[]{:S(2)}) copy-start(bf16[16,128,128]{2,1,0:T(8,128)(2,1)S(1)} %all-to-all-done.1) | copy-start | bytes 1572868
  67.8 1.3 copy-start.12
  69.1 5.6 %copy-start = (bf16[2,256,1024]{2,1,0:T(8,128)(2,1)S(1)}, bf16[2,256,1024]{2,1,0:T(8,128)(2,1)}, u32[]{:S(2)}) copy-start(bf16[2,256,1024]{2,1,0:T(8,128)(2,1)} %pad_maximum_fusion.rest_0_.refs_0_) | copy-start | bytes 3145732
  69.1 31.9 %all-to-all-start.2 = ((bf16[8,1024,128]{2,1,0:T(8,128)(2,1)}), bf16[8,1024,128]{2,1,0:T(8,128)(2,1)S(1)}, u32[]{:S(2)}, u32[]{:S(2)}) async-start(bf16[8,1024,128]{2,1,0:T(8,128)(2,1)} %bitcast.27), calls=%async_computation.2 | async-start | bytes 4194304 | tf_op jit(solution)/shard_map/all_to_all | solution.py:841
  74.7 25.3 %collective-permute-start.3 = (bf16[2,256,1024]{2,1,0:T(8,128)(2,1)S(1)}, bf16[2,256,1024]{2,1,0:T(8,128)(2,1)S(1)}, u32[]{:S(2)}, u32[]{:S(2)}) collective-permute-start(bf16[2,256,1024]{2,1,0:T(8,128)(2,1)S(1)} %copy-done), channel_id=1, source_target_pairs={{0,96},{8,104},{16,112},{24,120},{32,64},{40,72},{48,80},{56,88},{... | collective-permute-start | bytes 3145736 | tf_op jit(solution)/shard_map/ppermute | solution.py:514
  75.6 25.4 %collective-permute-start.2 = (bf16[2,256,1024]{2,1,0:T(8,128)(2,1)S(1)}, bf16[2,256,1024]{2,1,0:T(8,128)(2,1)}, u32[]{:S(2)}, u32[]{:S(2)}) collective-permute-start(bf16[2,256,1024]{2,1,0:T(8,128)(2,1)S(1)} %copy-done), channel_id=1, source_target_pairs={{0,32},{8,40},{16,48},{24,56},{32,0},{40,8},{48,16},{56,24},{64,96... | collective-permute-start | bytes 3145736 | tf_op jit(solution)/shard_map/ppermute | solution.py:514
  110.5 30.1 %all-to-all-start.3 = ((bf16[8,1024,128]{2,1,0:T(8,128)(2,1)}), bf16[8,1024,128]{2,1,0:T(8,128)(2,1)S(1)}, u32[]{:S(2)}, u32[]{:S(2)}) async-start(bf16[8,1024,128]{2,1,0:T(8,128)(2,1)} %bitcast.29), calls=%async_computation.3 | async-start | bytes 4194304 | tf_op jit(solution)/shard_map/all_to_all | solution.py:841
  115.8 24.1 %collective-permute-start.4 = (bf16[2,256,1024]{2,1,0:T(8,128)(2,1)S(1)}, bf16[2,256,1024]{2,1,0:T(8,128)(2,1)}, u32[]{:S(2)}, u32[]{:S(2)}) collective-permute-start(bf16[2,256,1024]{2,1,0:T(8,128)(2,1)S(1)} %copy-done), channel_id=1, source_target_pairs={{0,64},{8,72},{16,80},{24,88},{32,96},{40,104},{48,112},{56,120},{... | collective-permute-start | bytes 3145736 | tf_op jit(solution)/shard_map/ppermute | solution.py:514
  142.7 11.0 %copy-start.4 = (bf16[256,1024]{1,0:T(8,128)(2,1)S(1)}, bf16[256,1024]{1,0:T(8,128)(2,1)}, u32[]{:S(2)}) copy-start(bf16[256,1024]{1,0:T(8,128)(2,1)} %get-tuple-element.59.last_ref.cotangent_ref) | copy-start | bytes 1572868
  142.7 11.0 %copy-start.14 = (bf16[8,256,128]{2,1,0:T(8,128)(2,1)S(1)}, bf16[8,256,128]{2,1,0:T(8,128)(2,1)}, u32[]{:S(2)}) copy-start(bf16[8,256,128]{2,1,0:T(8,128)(2,1)} %get-tuple-element.61.hidden_ref) | copy-start | bytes 1572868
  146.4 16.4 %copy-start.20 = (bf16[256,1024]{1,0:T(8,128)(2,1)S(1)}, bf16[256,1024]{1,0:T(8,128)(2,1)}, u32[]{:S(2)}) copy-start(bf16[256,1024]{1,0:T(8,128)(2,1)} %get-tuple-element.60.after_ref) | copy-start | bytes 1572868
  146.4 7.2 %collective-permute-start.5 = (bf16[8,256,1024]{2,1,0:T(8,128)(2,1)S(1)}, bf16[8,256,1024]{2,1,0:T(8,128)(2,1)S(1)}, u32[]{:S(2)}, u32[]{:S(2)}) collective-permute-start(bf16[8,256,1024]{2,1,0:T(8,128)(2,1)S(1)} %early_first.1), channel_id=1, source_target_pairs={{0,8},{8,0},{16,24},{24,16},{32,40},{40,32},{48,56},{56,48},{64,72... | collective-permute-start | bytes 12582920 | tf_op jit(solution)/shard_map/ppermute | solution.py:514
  159.6 25.5 %collective-permute-start.6 = (bf16[8,128,512]{2,1,0:T(8,128)(2,1)}, bf16[8,128,512]{2,1,0:T(8,128)(2,1)}, u32[]{:S(2)}, u32[]{:S(2)}) collective-permute-start(bf16[8,128,512]{2,1,0:T(8,128)(2,1)} %get-tuple-element.65), channel_id=1, source_target_pairs={{0,2},{1,3},{2,0},{3,1},{4,6},{5,7},{6,4},{7,5},{8,10},{9,11},{10,... | collective-permute-start | bytes 3145736 | tf_op jit(solution)/shard_map/ppermute | solution.py:514
  160.7 26.4 %collective-permute-start.7 = (bf16[8,128,512]{2,1,0:T(8,128)(2,1)}, bf16[8,128,512]{2,1,0:T(8,128)(2,1)}, u32[]{:S(2)}, u32[]{:S(2)}) collective-permute-start(bf16[8,128,512]{2,1,0:T(8,128)(2,1)} %get-tuple-element.67), channel_id=1, source_target_pairs={{0,6},{1,7},{2,4},{3,5},{4,2},{5,3},{6,0},{7,1},{8,14},{9,15},{10,... | collective-permute-start | bytes 3145736 | tf_op jit(solution)/shard_map/ppermute | solution.py:514
  169.8 26.1 %all-to-all-start.4 = ((bf16[16,128,128]{2,1,0:T(8,128)(2,1)}), bf16[16,128,128]{2,1,0:T(8,128)(2,1)S(1)}, u32[]{:S(2)}, u32[]{:S(2)}) async-start(bf16[16,128,128]{2,1,0:T(8,128)(2,1)} %get-tuple-element.63), calls=%async_computation.4 | async-start | bytes 1048576 | tf_op jit(solution)/shard_map/all_to_all | solution.py:841
  187.1 1.2 copy-start.5
  189.6 6.4 %copy-start.16 = (bf16[16,384,128]{2,1,0:T(8,128)(2,1)S(1)}, bf16[16,384,128]{2,1,0:T(8,128)(2,1)}, u32[]{:S(2)}) copy-start(bf16[16,384,128]{2,1,0:T(8,128)(2,1)} %copy-done.15) | copy-start | bytes 4718596
  193.9 14.4 %collective-permute-start.8 = (bf16[8,64,512]{2,1,0:T(8,128)(2,1)}, bf16[8,64,512]{2,1,0:T(8,128)(2,1)}, u32[]{:S(2)}, u32[]{:S(2)}) collective-permute-start(bf16[8,64,512]{2,1,0:T(8,128)(2,1)} %get-tuple-element.70), channel_id=1, source_target_pairs={{0,6},{1,7},{2,4},{3,5},{4,2},{5,3},{6,0},{7,1},{8,14},{9,15},{10,... | collective-permute-start | bytes 1572872 | tf_op jit(solution)/shard_map/ppermute | solution.py:514
  196.0 12.9 %collective-permute-start.9 = (bf16[8,64,512]{2,1,0:T(8,128)(2,1)}, bf16[8,64,512]{2,1,0:T(8,128)(2,1)}, u32[]{:S(2)}, u32[]{:S(2)}) collective-permute-start(bf16[8,64,512]{2,1,0:T(8,128)(2,1)} %get-tuple-element.71), channel_id=1, source_target_pairs={{0,2},{1,3},{2,0},{3,1},{4,6},{5,7},{6,4},{7,5},{8,10},{9,11},{10,... | collective-permute-start | bytes 1572872 | tf_op jit(solution)/shard_map/ppermute | solution.py:514
  196.0 1.6 copy-start.24
  203.5 5.3 %copy-start.2 = (bf16[16,128,128]{2,1,0:T(8,128)(2,1)S(1)}, bf16[16,128,128]{2,1,0:T(8,128)(2,1)}, u32[]{:S(2)}) copy-start(bf16[16,128,128]{2,1,0:T(8,128)(2,1)} %copy-done.1) | copy-start | bytes 1572868
  203.5 33.4 %all-to-all-start.5 = ((bf16[16,384,128]{2,1,0:T(8,128)(2,1)}), bf16[16,384,128]{2,1,0:T(8,128)(2,1)S(1)}, u32[]{:S(2)}, u32[]{:S(2)}) async-start(bf16[16,384,128]{2,1,0:T(8,128)(2,1)} %bitcast.16), calls=%async_computation.5 | async-start | bytes 3145728 | tf_op jit(solution)/shard_map/all_to_all | solution.py:841
  221.3 10.2 %copy-start.21 = (bf16[8,64,1024]{2,1,0:T(8,128)(2,1)S(1)}, bf16[8,64,1024]{2,1,0:T(8,128)(2,1)}, u32[]{:S(2)}) copy-start(bf16[8,64,1024]{2,1,0:T(8,128)(2,1)} %get-tuple-element.68.rest_0_.own_ref) | copy-start | bytes 3145732
  221.3 2.3 collective-permute-start.11
  221.4 3.2 %collective-permute-start.12 = (bf16[256,1408]{1,0:T(8,128)(2,1)S(1)}, bf16[256,1408]{1,0:T(8,128)(2,1)S(1)}, u32[]{:S(2)}, u32[]{:S(2)}) collective-permute-start(bf16[256,1408]{1,0:T(8,128)(2,1)S(1)} %get-tuple-element.76), channel_id=1, source_target_pairs={{0,8},{8,0},{16,24},{24,16},{32,40},{40,32},{48,56},{56,48},{64,72... | collective-permute-start | bytes 2162696 | tf_op jit(solution)/shard_map/ppermute | solution.py:514
  226.8 10.2 %copy-start.7 = (bf16[256,1024]{1,0:T(8,128)(2,1)S(1)}, bf16[256,1024]{1,0:T(8,128)(2,1)}, u32[]{:S(2)}) copy-start(bf16[256,1024]{1,0:T(8,128)(2,1)} %get-tuple-element.54.tokens_ref) | copy-start | bytes 1572868
  226.8 10.2 %copy-start.9 = (bf16[256,1024]{1,0:T(8,128)(2,1)S(1)}, bf16[256,1024]{1,0:T(8,128)(2,1)}, u32[]{:S(2)}) copy-start(bf16[256,1024]{1,0:T(8,128)(2,1)} %get-tuple-element.69.grad_after_ref.refs_7_) | copy-start | bytes 1572868
  226.8 16.0 %collective-permute-start.13 = (bf16[2,64,1408]{2,1,0:T(8,128)(2,1)}, bf16[2,64,1408]{2,1,0:T(8,128)(2,1)}, u32[]{:S(2)}, u32[]{:S(2)}) collective-permute-start(bf16[2,64,1408]{2,1,0:T(8,128)(2,1)} %get-tuple-element.78), channel_id=1, source_target_pairs={{0,2},{1,3},{2,0},{3,1},{4,6},{5,7},{6,4},{7,5},{8,10},{9,11},{10,... | collective-permute-start | bytes 1081352 | tf_op jit(solution)/shard_map/ppermute | solution.py:514
  228.3 18.0 %collective-permute-start.14 = (bf16[2,64,1408]{2,1,0:T(8,128)(2,1)}, bf16[2,64,1408]{2,1,0:T(8,128)(2,1)}, u32[]{:S(2)}, u32[]{:S(2)}) collective-permute-start(bf16[2,64,1408]{2,1,0:T(8,128)(2,1)} %get-tuple-element.79), channel_id=1, source_target_pairs={{0,4},{1,5},{2,6},{3,7},{4,0},{5,1},{6,2},{7,3},{8,12},{9,13},{10,... | collective-permute-start | bytes 1081352 | tf_op jit(solution)/shard_map/ppermute | solution.py:514
  229.7 18.9 %collective-permute-start.15 = (bf16[2,64,1408]{2,1,0:T(8,128)(2,1)S(1)}, bf16[2,64,1408]{2,1,0:T(8,128)(2,1)}, u32[]{:S(2)}, u32[]{:S(2)}) collective-permute-start(bf16[2,64,1408]{2,1,0:T(8,128)(2,1)S(1)} %get-tuple-element.80), channel_id=1, source_target_pairs={{0,6},{1,7},{2,4},{3,5},{4,2},{5,3},{6,0},{7,1},{8,14},{9,15},{10,... | collective-permute-start | bytes 1081352 | tf_op jit(solution)/shard_map/ppermute | solution.py:514
  235.5 16.8 %collective-permute-start.10 = (bf16[8,32,1024]{2,1,0:T(8,128)(2,1)}, bf16[8,32,1024]{2,1,0:T(8,128)(2,1)S(1)}, u32[]{:S(2)}, u32[]{:S(2)}) collective-permute-start(bf16[8,32,1024]{2,1,0:T(8,128)(2,1)} %get-tuple-element.73), channel_id=1, source_target_pairs={{0,1},{1,0},{2,3},{3,2},{4,5},{5,4},{6,7},{7,6},{8,9},{9,8},{10,11... | collective-permute-start | bytes 1572872 | tf_op jit(solution)/shard_map/ppermute | solution.py:514
  236.9 11.7 %copy-start.22 = (bf16[2,64,1408]{2,1,0:T(8,128)(2,1)S(1)}, bf16[2,64,1408]{2,1,0:T(8,128)(2,1)}, u32[]{:S(2)}) copy-start(bf16[2,64,1408]{2,1,0:T(8,128)(2,1)} %get-tuple-element.77.refs_0_) | copy-start | bytes 1081348
  242.8 13.5 %copy-start.23 = (bf16[8,32,1024]{2,1,0:T(8,128)(2,1)S(1)}, bf16[8,32,1024]{2,1,0:T(8,128)(2,1)}, u32[]{:S(2)}) copy-start(bf16[8,32,1024]{2,1,0:T(8,128)(2,1)} %get-tuple-element.72.early_ref) | copy-start | bytes 1572868
  250.7 5.6 %collective-permute-start.16 = (bf16[2,32,1408]{2,1,0:T(8,128)(2,1)S(1)}, bf16[2,32,1408]{2,1,0:T(8,128)(2,1)S(1)}, u32[]{:S(2)}, u32[]{:S(2)}) collective-permute-start(bf16[2,32,1408]{2,1,0:T(8,128)(2,1)S(1)} %get-tuple-element.82), channel_id=1, source_target_pairs={{0,1},{1,0},{2,3},{3,2},{4,5},{5,4},{6,7},{7,6},{8,9},{9,8},{10,11... | collective-permute-start | bytes 540680 | tf_op jit(solution)/shard_map/ppermute | solution.py:514
  257.0 21.0 %copy-start.11 = (bf16[256,1024]{1,0:T(8,128)(2,1)S(1)}, bf16[256,1024]{1,0:T(8,128)(2,1)}, u32[]{:S(2)}) copy-start(bf16[256,1024]{1,0:T(8,128)(2,1)} %copy-done.10) | copy-start | bytes 1572868
  257.0 9.2 %collective-permute-start.17 = (bf16[2,32,2176]{2,1,0:T(8,128)(2,1)S(1)}, bf16[2,32,2176]{2,1,0:T(8,128)(2,1)S(1)}, u32[]{:S(2)}, u32[]{:S(2)}) collective-permute-start(bf16[2,32,2176]{2,1,0:T(8,128)(2,1)S(1)} %get-tuple-element.84), channel_id=1, source_target_pairs={{0,32},{8,40},{16,48},{24,56},{32,0},{40,8},{48,16},{56,24},{64,96... | collective-permute-start | bytes 835592 | tf_op jit(solution)/shard_map/ppermute | solution.py:514
  258.6 13.1 %collective-permute-start.18 = (bf16[2,32,2176]{2,1,0:T(8,128)(2,1)S(1)}, bf16[2,32,2176]{2,1,0:T(8,128)(2,1)S(1)}, u32[]{:S(2)}, u32[]{:S(2)}) collective-permute-start(bf16[2,32,2176]{2,1,0:T(8,128)(2,1)S(1)} %get-tuple-element.85), channel_id=1, source_target_pairs={{0,64},{8,72},{16,80},{24,88},{32,96},{40,104},{48,112},{56,120},{... | collective-permute-start | bytes 835592 | tf_op jit(solution)/shard_map/ppermute | solution.py:514
  261.2 13.0 %collective-permute-start.19 = (bf16[2,32,2176]{2,1,0:T(8,128)(2,1)S(1)}, bf16[2,32,2176]{2,1,0:T(8,128)(2,1)S(1)}, u32[]{:S(2)}, u32[]{:S(2)}) collective-permute-start(bf16[2,32,2176]{2,1,0:T(8,128)(2,1)S(1)} %get-tuple-element.86), channel_id=1, source_target_pairs={{0,96},{8,104},{16,112},{24,120},{32,64},{40,72},{48,80},{56,88},{... | collective-permute-start | bytes 835592 | tf_op jit(solution)/shard_map/ppermute | solution.py:514
  275.0 6.9 %collective-permute-start.20 = (bf16[4,32,640]{2,1,0:T(8,128)(2,1)S(1)}, bf16[4,32,640]{2,1,0:T(8,128)(2,1)S(1)}, u32[]{:S(2)}, u32[]{:S(2)}) collective-permute-start(bf16[4,32,640]{2,1,0:T(8,128)(2,1)S(1)} %get-tuple-element.88), channel_id=1, source_target_pairs={{0,16},{8,24},{16,0},{24,8},{32,48},{40,56},{48,32},{56,40},{64,80... | collective-permute-start | bytes 491528 | tf_op jit(solution)/shard_map/ppermute | solution.py:514
  (7 other events, 7.5 us)

commit v5 on v4

--- a/solution.py
+++ b/solution.py
@@ -627,11 +627,9 @@
 
 
 def early_half(ids, parts):
-    left, left_give, right, right_give = parts
-    operands = [left, swap(left_give, "mode", 2), right, swap(right_give, "mode", 6)]
     narrow = pl.BlockSpec((2, 64, 512), lambda i, c: (i, 0, 0))
     return prefetched(
-        early_half_kernel, ids, operands,
+        early_half_kernel, ids, parts,
         [pl.BlockSpec((2, 128, 512), lambda i, c: (i, 0, 0))] * 4,
         [pl.BlockSpec((2, 64, D), lambda i, c: (i, 0, 0)), narrow, narrow],
         [pltpu.HBM((8, 64, D), BF)] + [jax.ShapeDtypeStruct((8, 64, 512), BF)] * 2,
@@ -865,16 +863,15 @@
     returned_two = exchange(returning.reshape(8, 1024, 128), "mode").reshape(8, 4, ROWS, 128)
     early = (hidden_two, returned_two, cotangent_m)
     theirs = early_products(other_ids, *early, None, hiddens[2:3])
-    parts = early_products(ids, *early, swap(theirs, "agent", 1))
-    outgoing, grad_after = turn(returned_two, cotangent_m, after, weights, parts[:1])
+    outgoing, grad_after = turn(returned_two, cotangent_m, after, weights, [theirs])
     upstream = exchange(outgoing, "agent")
-    own, left, right = early_half(ids, parts)
-    returning = agent_backward(arrived_one, upstream, tables, [own])
+    parts = early_products(ids, *early, swap(theirs, "agent", 1), [grad_after])
+    arrived_half = swap(parts[1], "mode", 2)
+    returning = agent_backward(arrived_one, upstream, tables, [])
+    own, left, right = early_half(ids, [parts[0], arrived_half, parts[2], swap(parts[3], "mode", 6)])
     left, right = swap(left, "mode", 6), swap(right, "mode", 2)
     returned_one = exchange(returning.reshape(16, 384, 128), "agent").reshape(16, 3, 128, 128)
-    late_parts = late_products(
-        ids, hiddens, returning, mixed_one, grad_after, [left, right]
-    )
+    late_parts = late_products(ids, hiddens, returning, mixed_one, grad_after, [])
     token_grads = leave(returned_one, tokens_a, grad_after, weights)
     late = late_sums(ids, *late_parts, [token_grads])
     early = early_sums(ids, own, left, right)

time: 285 us -> 278 us (0.975)
  waiting for transfers between devices: 126 us -> 114 us
  Pallas kernels: 80.7 us -> 85.2 us
    ppermute x21, waiting for transfers between devices: 96.9 us -> 84.3 us  [swap(): return lax.ppermute(values, axis, [(n, n ^ bits) for n in range(size)])]
    pallas_call x10, Pallas kernels: 35 us -> 38.7 us  [prefetched(): pl.pallas_call(kernel, grid_spec=pltpu.PrefetchScalarGridSpec(num_scalar_...]
  transfers between devices with their start and end apart: 27 -> 27, of which waited for: 19 -> 14; matrix products, arithmetic and copies ran while one was open for 1% -> 1% of each run, Pallas kernels for 16% -> 19%
where the time goes in v5:
time: 278 us; the launch traced here: 276 us
  waiting for transfers between devices  114 us (41%)
  Pallas kernels  85.2 us (31%)
  starting transfers between devices  59.3 us (21%)
  local copies, waits for them, and re-layouts  15 us (5%)
    ppermute x21, waiting for transfers between devices, swap(): return lax.ppermute(values, axis, [(n, n ^ bits) for n in range(size)])  84.3 us
    pallas_call x10, Pallas kernels, prefetched(): pl.pallas_call(kernel, grid_spec=pltpu.PrefetchScalarGridSpec(num_scalar_...  38.7 us
    all_to_all x6, starting transfers between devices, exchange(): return lax.all_to_all(values, axis, split_axis=0, concat_axis=0, tiled=True)  34.6 us
    all_to_all x6, waiting for transfers between devices, exchange(): return lax.all_to_all(values, axis, split_axis=0, concat_axis=0, tiled=True)  29.4 us
    ppermute x21, starting transfers between devices, swap(): return lax.ppermute(values, axis, [(n, n ^ bits) for n in range(size)])  24.7 us
    unnamed x58, local copies, waits for them, and re-layouts  12.6 us
    pallas_call x1, Pallas kernels, mode_attention(): pl.pallas_call(mode_kernel, grid=(4,), in_specs=[spec] + [unused] * len(a...  9.43 us
    pallas_call x1, Pallas kernels, middle(): pl.pallas_call(middle_kernel, grid=(5,), in_specs=[fixed((ROWS, D)), fixe...  7.98 us
  transfers between devices with their start and end apart: 27, of which 14 were waited for; matrix products, arithmetic and copies ran while one was open for 1% of the time, Pallas kernels for 19%

profile of v5, /device:TPU:0, one launch (start us, length us, event | category | flops | bytes accessed | tf_op | source)
XLA Modules:
  0.0 276.3 jit_solution(13911010180886256859)
XLA Ops:
  0.6 1.2 reshape.64.tokens_ref
  1.9 5.5 %enter.1 = (bf16[16,384,128]{2,1,0:T(8,128)(2,1)}, bf16[256,1024]{1,0:T(8,128)(2,1)}, bf16[128,1024]{1,0:T(8,128)(2,1)}, bf16[128,1024]{1,0:T(8,128)(2,1)S(1)}) custom-call(s32[7]{0:T(128)S(1)} %stack.40.ids_ref, bf16[256,1024]{1,0:T(8,128)(2,1)S(1)} %reshape.64.tokens_ref, bf16[8,1024,1024]{2,1,0:T(8,128)(2,1)} %weights_ref.7), custom_call_target="tpu_custom_call" | custom-call | flops 1610612736 | bytes 8388608 | tf_op jit(solution)/shard_map/enter/pallas_call | solution.py:178
  7.4 7.3 %all-to-all-start = ((bf16[16,384,128]{2,1,0:T(8,128)(2,1)}), bf16[16,384,128]{2,1,0:T(8,128)(2,1)S(1)}, u32[]{:S(2)}, u32[]{:S(2)}) async-start(bf16[16,384,128]{2,1,0:T(8,128)(2,1)} %get-tuple-element.53), calls=%async_computation | async-start | bytes 3145728 | tf_op jit(solution)/shard_map/all_to_all | solution.py:839
  16.3 3.4 %collective-permute-start.1 = (bf16[256,1024]{1,0:T(8,128)(2,1)S(1)}, bf16[256,1024]{1,0:T(8,128)(2,1)}, u32[]{:S(2)}, u32[]{:S(2)}) collective-permute-start(bf16[256,1024]{1,0:T(8,128)(2,1)S(1)} %constant_dynamic-update-slice_fusion), channel_id=1, source_target_pairs={{0,16},{8,24},{16,0},{24,8},{32,48},{40,56},{48,32},{56,40},{64,80... | collective-permute-start | bytes 1572872 | tf_op jit(solution)/shard_map/ppermute | solution.py:514
  19.8 18.5 %all-to-all-done.query_ref.keys_ref.values_ref.q.k.v = bf16[16,384,128]{2,1,0:T(8,128)(2,1)S(1)} async-done(((bf16[16,384,128]{2,1,0:T(8,128)(2,1)}), bf16[16,384,128]{2,1,0:T(8,128)(2,1)S(1)}, u32[]{:S(2)}, u32[]{:S(2)}) %all-to-all-start) | async-done | bytes 1572896 | tf_op jit(solution)/shard_map/all_to_all | solution.py:839
  38.3 4.8 %agent_forward.1 = (bf16[16,128,128]{2,1,0:T(8,128)(2,1)}, f32[4,4,256,128]{3,2,1,0:T(8,128)}) custom-call(bf16[16,384,128]{2,1,0:T(8,128)(2,1)S(1)} %all-to-all-done.query_ref.keys_ref.values_ref.q.k.v, bf16[16,384,128]{2,1,0:T(8,128)(2,1)S(1)} %all-to-all-done.query_ref.keys_ref.values_ref.q.k.v, ...), custom_call_target="tpu_custom_call" | custom-call | flops 3000000000 | bytes 4194304 | tf_op jit(solution)/shard_map/agent_forward/pallas_call | solution.py:228
  43.1 4.4 %all-to-all-start.1 = ((bf16[16,128,128]{2,1,0:T(8,128)(2,1)}), bf16[16,128,128]{2,1,0:T(8,128)(2,1)S(1)}, u32[]{:S(2)}, u32[]{:S(2)}) async-start(bf16[16,128,128]{2,1,0:T(8,128)(2,1)} %get-tuple-element.55), calls=%async_computation.1 | async-start | bytes 1048576 | tf_op jit(solution)/shard_map/all_to_all | solution.py:839
  47.6 2.1 pad_maximum_fusion.rest_0_.refs_0_
  49.7 10.1 %all-to-all-done.1 = bf16[16,128,128]{2,1,0:T(8,128)(2,1)S(1)} async-done(((bf16[16,128,128]{2,1,0:T(8,128)(2,1)}), bf16[16,128,128]{2,1,0:T(8,128)(2,1)S(1)}, u32[]{:S(2)}, u32[]{:S(2)}) %all-to-all-start.1) | async-done | bytes 524320 | tf_op jit(solution)/shard_map/all_to_all | solution.py:839
  59.8 8.0 %middle.1 = (bf16[8,4,256,128]{3,2,1,0:T(8,128)(2,1)S(1)}, bf16[256,1024]{1,0:T(8,128)(2,1)}, bf16[8,256,128]{2,1,0:T(8,128)(2,1)}, bf16[256,1024]{1,0:T(8,128)(2,1)}) custom-call(bf16[256,1024]{1,0:T(8,128)(2,1)S(1)} %copy-done.7, bf16[8,256,128]{2,1,0:T(8,128)(2,1)S(1)} %bitcast.25, bf16[256,1024]{1,0:T(8,128)(2,1)S(1)} %reshape.67.cotangent_ref, ...), custom_call_target="tpu_custom_call" | custom-call | flops 2684354560 | bytes 13631488 | tf_op jit(solution)/shard_map/middle/pallas_call | solution.py:339
  67.8 1.3 copy-done.11
  69.1 5.6 %all-to-all-start.2 = ((bf16[8,1024,128]{2,1,0:T(8,128)(2,1)}), bf16[8,1024,128]{2,1,0:T(8,128)(2,1)S(1)}, u32[]{:S(2)}, u32[]{:S(2)}) async-start(bf16[8,1024,128]{2,1,0:T(8,128)(2,1)} %bitcast.27), calls=%async_computation.2 | async-start | bytes 4194304 | tf_op jit(solution)/shard_map/all_to_all | solution.py:839
  75.7 24.2 %collective-permute-done.3.rest_1_.refs_3_ = bf16[2,256,1024]{2,1,0:T(8,128)(2,1)S(1)} collective-permute-done((bf16[2,256,1024]{2,1,0:T(8,128)(2,1)S(1)}, bf16[2,256,1024]{2,1,0:T(8,128)(2,1)S(1)}, u32[]{:S(2)}, u32[]{:S(2)}) %collective-permute-start.3) | collective-permute-done | bytes 1048608 | tf_op jit(solution)/shard_map/ppermute | solution.py:514
  101.0 9.4 %mode_attention.1 = bf16[8,4,256,128]{3,2,1,0:T(8,128)(2,1)} custom-call(bf16[8,4,256,128]{3,2,1,0:T(8,128)(2,1)S(1)} %bitcast.28, bf16[2,256,1024]{2,1,0:T(8,128)(2,1)} %collective-permute-done.2.rest_0_.refs_1_, bf16[2,256,1024]{2,1,0:T(8,128)(2,1)} %copy-done.16), custom_call_target="tpu_custom_call" | custom-call | flops 8000000000 | bytes 4194304 | tf_op jit(solution)/shard_map/mode_attention/pallas_call | solution.py:394
  110.4 5.3 %all-to-all-start.3 = ((bf16[8,1024,128]{2,1,0:T(8,128)(2,1)}), bf16[8,1024,128]{2,1,0:T(8,128)(2,1)S(1)}, u32[]{:S(2)}, u32[]{:S(2)}) async-start(bf16[8,1024,128]{2,1,0:T(8,128)(2,1)} %bitcast.29), calls=%async_computation.3 | async-start | bytes 4194304 | tf_op jit(solution)/shard_map/all_to_all | solution.py:839
  116.4 23.4 %collective-permute-done.4.rest_0_.refs_2_ = bf16[2,256,1024]{2,1,0:T(8,128)(2,1)} collective-permute-done((bf16[2,256,1024]{2,1,0:T(8,128)(2,1)S(1)}, bf16[2,256,1024]{2,1,0:T(8,128)(2,1)}, u32[]{:S(2)}, u32[]{:S(2)}) %collective-permute-start.4) | collective-permute-done | bytes 1048608 | tf_op jit(solution)/shard_map/ppermute | solution.py:514
  142.6 5.7 %early_first.1.rest_0_ = bf16[8,256,1024]{2,1,0:T(8,128)(2,1)} custom-call(s32[7]{0:T(128)S(1)} %constant_dynamic-update-slice_fusion.2.ids_ref, bf16[8,256,128]{2,1,0:T(8,128)(2,1)S(1)} %copy-done.12, bf16[8,4,256,128]{3,2,1,0:T(8,128)(2,1)S(1)} %bitcast.19, bf16[8,4,256,128]{3,2,1,0:T(8,128)(2,1)S(1)} %bitcast.20, bf16[256,1024]{1,0:T(8,128)(2,1)S(1)} %copy-done.4, ...), custom_call_target="tpu_custom_call" | custom-call | flops 1000000000 | bytes 5242880 | tf_op jit(solution)/shard_map/early_first/pallas_call | solution.py:522
  148.3 7.1 %turn.1 = (bf16[16,128,128]{2,1,0:T(8,128)(2,1)}, bf16[256,1024]{1,0:T(8,128)(2,1)}) custom-call(bf16[8,4,256,128]{3,2,1,0:T(8,128)(2,1)S(1)} %bitcast.21, bf16[256,1024]{1,0:T(8,128)(2,1)S(1)} %copy-done.5, bf16[256,1024]{1,0:T(8,128)(2,1)S(1)} %copy-done.20, bf16[8,1024,1024]{2,1,0:T(8,128)(2,1)} %weights_ref.7, bf16[8,256,1024]{2,1,0:T(8,128)(2,1)} %early_first.1.rest_0_), custom_call_target="tpu_custom_call" | custom-call | flops 2147483648 | bytes 12582912 | tf_op jit(solution)/shard_map/turn/pallas_call | solution.py:441
  155.4 4.8 %all-to-all-start.4 = ((bf16[16,128,128]{2,1,0:T(8,128)(2,1)}), bf16[16,128,128]{2,1,0:T(8,128)(2,1)}, u32[]{:S(2)}, u32[]{:S(2)}) async-start(bf16[16,128,128]{2,1,0:T(8,128)(2,1)} %get-tuple-element.62), calls=%async_computation.4 | async-start | bytes 1048576 | tf_op jit(solution)/shard_map/all_to_all | solution.py:839
  162.4 8.5 %early_add.1 = (bf16[8,128,512]{2,1,0:T(8,128)(2,1)}, bf16[8,128,512]{2,1,0:T(8,128)(2,1)}, bf16[8,128,512]{2,1,0:T(8,128)(2,1)}, bf16[8,128,512]{2,1,0:T(8,128)(2,1)}) custom-call(s32[7]{0:T(128)S(1)} %stack.40.ids_ref, bf16[8,256,128]{2,1,0:T(8,128)(2,1)S(1)} %copy-done.13, bf16[8,4,256,128]{3,2,1,0:T(8,128)(2,1)S(1)} %bitcast.22, ...), custom_call_target="tpu_custom_call" | custom-call | flops 1000000000 | bytes 5242880 | tf_op jit(solution)/shard_map/early_add/pallas_call | solution.py:522
  171.8 2.1 collective-permute-start.7
  173.9 1.4 copy-done.15
  175.3 1.6 copy-done.24
  176.9 6.8 %agent_backward.1.refs_4_.refs_5_ = bf16[16,3,128,128]{3,2,1,0:T(8,128)(2,1)} custom-call(bf16[16,384,128]{2,1,0:T(8,128)(2,1)S(1)} %copy-done.15, bf16[16,384,128]{2,1,0:T(8,128)(2,1)S(1)} %copy-done.15, bf16[16,384,128]{2,1,0:T(8,128)(2,1)S(1)} %copy-done.15, bf16[16,128,128]{2,1,0:T(8,128)(2,1)} %all-to-all-done.4.g, f32[4,4,256,128]{3,2,1,0:T(8,128)S(1)} %copy-done.24), custom_call_target="tpu_custom_call" | custom-call | flops 6000000000 | bytes 6291456 | tf_op jit(solution)/shard_map/agent_backward/pallas_call | solution.py:283
  183.7 7.3 %all-to-all-start.5 = ((bf16[16,384,128]{2,1,0:T(8,128)(2,1)}), bf16[16,384,128]{2,1,0:T(8,128)(2,1)S(1)}, u32[]{:S(2)}, u32[]{:S(2)}) async-start(bf16[16,384,128]{2,1,0:T(8,128)(2,1)} %bitcast.16), calls=%async_computation.5 | async-start | bytes 3145728 | tf_op jit(solution)/shard_map/all_to_all | solution.py:839
  192.0 1.2 copy-done.17
  193.3 10.2 %late_products.1 = (bf16[2,256,1408]{2,1,0:T(8,128)(2,1)S(1)}, bf16[256,1408]{1,0:T(8,128)(2,1)S(1)}, bf16[256,1408]{1,0:T(8,128)(2,1)S(1)}) custom-call(s32[7]{0:T(128)S(1)} %stack.40.ids_ref, bf16[2,256,1024]{2,1,0:T(8,128)(2,1)S(1)} %copy-done, bf16[2,256,1024]{2,1,0:T(8,128)(2,1)} %collective-permute-done.2.rest_0_.refs_1_, ...), custom_call_target="tpu_custom_call" | custom-call | flops 1000000000 | bytes 5242880 | tf_op jit(solution)/shard_map/late_products/pallas_call | solution.py:522
  204.1 4.2 %early_half.1 = (bf16[8,64,1024]{2,1,0:T(8,128)(2,1)}, bf16[8,64,512]{2,1,0:T(8,128)(2,1)S(1)}, bf16[8,64,512]{2,1,0:T(8,128)(2,1)S(1)}) custom-call(s32[7]{0:T(128)S(1)} %stack.40.ids_ref, bf16[8,128,512]{2,1,0:T(8,128)(2,1)S(1)} %copy-done.18, bf16[8,128,512]{2,1,0:T(8,128)(2,1)} %collective-permute-done.6.left_in, bf16[8,128,512]{2,1,0:T(8,128)(2,1)S(1)} %copy-done.19, ...), custom_call_target="tpu_custom_call" | custom-call | flops 1000000000 | bytes 5242880 | tf_op jit(solution)/shard_map/early_half/pallas_call | solution.py:522
  208.3 1.2 collective-permute-start.8
  209.5 2.1 late_add.1
  211.6 2.0 collective-permute-start.13
  213.7 1.5 collective-permute-start.14
  215.2 1.2 collective-permute-start.15
  216.3 7.9 %collective-permute-done.8.left_ref = bf16[8,64,512]{2,1,0:T(8,128)(2,1)S(1)} collective-permute-done((bf16[8,64,512]{2,1,0:T(8,128)(2,1)S(1)}, bf16[8,64,512]{2,1,0:T(8,128)(2,1)S(1)}, u32[]{:S(2)}, u32[]{:S(2)}) %collective-permute-start.8) | collective-permute-done | bytes 524320 | tf_op jit(solution)/shard_map/ppermute | solution.py:514
  224.3 2.2 early_z.1
  227.3 5.0 %leave.1.refs_4_ = bf16[256,1024]{1,0:T(8,128)(2,1)S(1)} custom-call(bf16[16,3,128,128]{3,2,1,0:T(8,128)(2,1)S(1)} %bitcast.24, bf16[256,1024]{1,0:T(8,128)(2,1)S(1)} %copy-done.8, bf16[256,1024]{1,0:T(8,128)(2,1)S(1)} %copy-done.1, bf16[8,1024,1024]{2,1,0:T(8,128)(2,1)} %weights_ref.7), custom_call_target="tpu_custom_call" | custom-call | flops 1610612736 | bytes 9437184 | tf_op jit(solution)/shard_map/leave/pallas_call | solution.py:490
  233.2 7.4 %collective-permute-done.14.refs_2_ = bf16[2,64,1408]{2,1,0:T(8,128)(2,1)} collective-permute-done((bf16[2,64,1408]{2,1,0:T(8,128)(2,1)}, bf16[2,64,1408]{2,1,0:T(8,128)(2,1)}, u32[]{:S(2)}, u32[]{:S(2)}) %collective-permute-start.14) | collective-permute-done | bytes 360480 | tf_op jit(solution)/shard_map/ppermute | solution.py:514
  240.5 2.0 late_z.1
  243.5 4.9 %collective-permute-done.16.late_in = bf16[2,32,1408]{2,1,0:T(8,128)(2,1)S(1)} collective-permute-done((bf16[2,32,1408]{2,1,0:T(8,128)(2,1)S(1)}, bf16[2,32,1408]{2,1,0:T(8,128)(2,1)S(1)}, u32[]{:S(2)}, u32[]{:S(2)}) %collective-permute-start.16) | collective-permute-done | bytes 180256 | tf_op jit(solution)/shard_map/ppermute | solution.py:514
  248.4 1.8 chips.1
  250.2 1.4 collective-permute-start.17
  251.7 2.7 collective-permute-start.18
  255.0 4.9 %collective-permute-done.17.refs_1_ = bf16[2,32,2176]{2,1,0:T(8,128)(2,1)S(1)} collective-permute-done((bf16[2,32,2176]{2,1,0:T(8,128)(2,1)S(1)}, bf16[2,32,2176]{2,1,0:T(8,128)(2,1)S(1)}, u32[]{:S(2)}, u32[]{:S(2)}) %collective-permute-start.17) | collective-permute-done | bytes 278560 | tf_op jit(solution)/shard_map/ppermute | solution.py:514
  259.9 4.9 %collective-permute-done.18.refs_2_ = bf16[2,32,2176]{2,1,0:T(8,128)(2,1)S(1)} collective-permute-done((bf16[2,32,2176]{2,1,0:T(8,128)(2,1)S(1)}, bf16[2,32,2176]{2,1,0:T(8,128)(2,1)S(1)}, u32[]{:S(2)}, u32[]{:S(2)}) %collective-permute-start.18) | collective-permute-done | bytes 278560 | tf_op jit(solution)/shard_map/ppermute | solution.py:514
  264.8 2.6 collective-permute-done.19.refs_3_
  268.1 3.0 %collective-permute-start.20 = (bf16[4,32,640]{2,1,0:T(8,128)(2,1)S(1)}, bf16[4,32,640]{2,1,0:T(8,128)(2,1)S(1)}, u32[]{:S(2)}, u32[]{:S(2)}) collective-permute-start(bf16[4,32,640]{2,1,0:T(8,128)(2,1)S(1)} %get-tuple-element.88), channel_id=1, source_target_pairs={{0,16},{8,24},{16,0},{24,8},{32,48},{40,56},{48,32},{56,40},{64,80... | collective-permute-start | bytes 491528 | tf_op jit(solution)/shard_map/ppermute | solution.py:514
  272.1 2.9 %collective-permute-done.20.arrived_ref = bf16[4,32,640]{2,1,0:T(8,128)(2,1)S(1)} collective-permute-done((bf16[4,32,640]{2,1,0:T(8,128)(2,1)S(1)}, bf16[4,32,640]{2,1,0:T(8,128)(2,1)S(1)}, u32[]{:S(2)}, u32[]{:S(2)}) %collective-permute-start.20) | collective-permute-done | bytes 163872 | tf_op jit(solution)/shard_map/ppermute | solution.py:514
  275.0 1.3 last.1
  (89 shorter events, 17.1 us)
Async XLA Ops:
  7.4 7.7 %copy-start.26 = (bf16[128,1024]{1,0:T(8,128)(2,1)S(1)}, bf16[128,1024]{1,0:T(8,128)(2,1)}, u32[]{:S(2)}) copy-start(bf16[128,1024]{1,0:T(8,128)(2,1)} %get-tuple-element.56) | copy-start | bytes 786436
  7.4 7.7 %copy-start.27 = (s32[128]{0:T(128)S(1)}, s32[128]{0:T(128)}, u32[]{:S(2)}) copy-start(s32[128]{0:T(128)} %param.9) | copy-start | bytes 1540
  7.4 30.9 %all-to-all-start = ((bf16[16,384,128]{2,1,0:T(8,128)(2,1)}), bf16[16,384,128]{2,1,0:T(8,128)(2,1)S(1)}, u32[]{:S(2)}, u32[]{:S(2)}) async-start(bf16[16,384,128]{2,1,0:T(8,128)(2,1)} %get-tuple-element.53), calls=%async_computation | async-start | bytes 3145728 | tf_op jit(solution)/shard_map/all_to_all | solution.py:839
  14.7 1.6 collective-permute-start
  16.3 31.1 %copy-start.25 = (bf16[8,8,4,1024]{3,2,1,0:T(4,128)(2,1)S(1)}, bf16[8,8,4,1024]{3,2,1,0:T(4,128)(2,1)}, u32[]{:S(2)}) copy-start(bf16[8,8,4,1024]{3,2,1,0:T(4,128)(2,1)} %param.7) | copy-start | bytes 1572868
  16.3 31.2 %collective-permute-start.1 = (bf16[256,1024]{1,0:T(8,128)(2,1)S(1)}, bf16[256,1024]{1,0:T(8,128)(2,1)}, u32[]{:S(2)}, u32[]{:S(2)}) collective-permute-start(bf16[256,1024]{1,0:T(8,128)(2,1)S(1)} %constant_dynamic-update-slice_fusion), channel_id=1, source_target_pairs={{0,16},{8,24},{16,0},{24,8},{32,48},{40,56},{48,32},{56,40},{64,80... | collective-permute-start | bytes 1572872 | tf_op jit(solution)/shard_map/ppermute | solution.py:514
  38.3 4.8 %copy-start.14 = (bf16[16,384,128]{2,1,0:T(8,128)(2,1)}, bf16[16,384,128]{2,1,0:T(8,128)(2,1)S(1)}, u32[]{:S(2)}) copy-start(bf16[16,384,128]{2,1,0:T(8,128)(2,1)S(1)} %all-to-all-done.query_ref.keys_ref.values_ref.q.k.v) | copy-start | bytes 4718596
  43.1 16.7 %copy-start.7 = (bf16[256,1024]{1,0:T(8,128)(2,1)S(1)}, bf16[256,1024]{1,0:T(8,128)(2,1)}, u32[]{:S(2)}) copy-start(bf16[256,1024]{1,0:T(8,128)(2,1)} %get-tuple-element.54.tokens_ref) | copy-start | bytes 1572868
  43.1 16.7 %all-to-all-start.1 = ((bf16[16,128,128]{2,1,0:T(8,128)(2,1)}), bf16[16,128,128]{2,1,0:T(8,128)(2,1)S(1)}, u32[]{:S(2)}, u32[]{:S(2)}) async-start(bf16[16,128,128]{2,1,0:T(8,128)(2,1)} %get-tuple-element.55), calls=%async_computation.1 | async-start | bytes 1048576 | tf_op jit(solution)/shard_map/all_to_all | solution.py:839
  59.8 8.0 %copy-start.2 = (bf16[16,128,128]{2,1,0:T(8,128)(2,1)}, bf16[16,128,128]{2,1,0:T(8,128)(2,1)S(1)}, u32[]{:S(2)}) copy-start(bf16[16,128,128]{2,1,0:T(8,128)(2,1)S(1)} %all-to-all-done.1) | copy-start | bytes 1572868
  67.8 1.3 copy-start.11
  69.1 5.6 %copy-start = (bf16[2,256,1024]{2,1,0:T(8,128)(2,1)S(1)}, bf16[2,256,1024]{2,1,0:T(8,128)(2,1)}, u32[]{:S(2)}) copy-start(bf16[2,256,1024]{2,1,0:T(8,128)(2,1)} %pad_maximum_fusion.rest_0_.refs_0_) | copy-start | bytes 3145732
  69.1 31.9 %all-to-all-start.2 = ((bf16[8,1024,128]{2,1,0:T(8,128)(2,1)}), bf16[8,1024,128]{2,1,0:T(8,128)(2,1)S(1)}, u32[]{:S(2)}, u32[]{:S(2)}) async-start(bf16[8,1024,128]{2,1,0:T(8,128)(2,1)} %bitcast.27), calls=%async_computation.2 | async-start | bytes 4194304 | tf_op jit(solution)/shard_map/all_to_all | solution.py:839
  74.7 25.3 %collective-permute-start.3 = (bf16[2,256,1024]{2,1,0:T(8,128)(2,1)S(1)}, bf16[2,256,1024]{2,1,0:T(8,128)(2,1)S(1)}, u32[]{:S(2)}, u32[]{:S(2)}) collective-permute-start(bf16[2,256,1024]{2,1,0:T(8,128)(2,1)S(1)} %copy-done), channel_id=1, source_target_pairs={{0,96},{8,104},{16,112},{24,120},{32,64},{40,72},{48,80},{56,88},{... | collective-permute-start | bytes 3145736 | tf_op jit(solution)/shard_map/ppermute | solution.py:514
  75.6 25.3 %collective-permute-start.2 = (bf16[2,256,1024]{2,1,0:T(8,128)(2,1)S(1)}, bf16[2,256,1024]{2,1,0:T(8,128)(2,1)}, u32[]{:S(2)}, u32[]{:S(2)}) collective-permute-start(bf16[2,256,1024]{2,1,0:T(8,128)(2,1)S(1)} %copy-done), channel_id=1, source_target_pairs={{0,32},{8,40},{16,48},{24,56},{32,0},{40,8},{48,16},{56,24},{64,96... | collective-permute-start | bytes 3145736 | tf_op jit(solution)/shard_map/ppermute | solution.py:514
  110.4 30.1 %all-to-all-start.3 = ((bf16[8,1024,128]{2,1,0:T(8,128)(2,1)}), bf16[8,1024,128]{2,1,0:T(8,128)(2,1)S(1)}, u32[]{:S(2)}, u32[]{:S(2)}) async-start(bf16[8,1024,128]{2,1,0:T(8,128)(2,1)} %bitcast.29), calls=%async_computation.3 | async-start | bytes 4194304 | tf_op jit(solution)/shard_map/all_to_all | solution.py:839
  115.7 24.1 %collective-permute-start.4 = (bf16[2,256,1024]{2,1,0:T(8,128)(2,1)S(1)}, bf16[2,256,1024]{2,1,0:T(8,128)(2,1)}, u32[]{:S(2)}, u32[]{:S(2)}) collective-permute-start(bf16[2,256,1024]{2,1,0:T(8,128)(2,1)S(1)} %copy-done), channel_id=1, source_target_pairs={{0,64},{8,72},{16,80},{24,88},{32,96},{40,104},{48,112},{56,120},{... | collective-permute-start | bytes 3145736 | tf_op jit(solution)/shard_map/ppermute | solution.py:514
  142.6 5.7 %copy-start.5 = (bf16[256,1024]{1,0:T(8,128)(2,1)S(1)}, bf16[256,1024]{1,0:T(8,128)(2,1)}, u32[]{:S(2)}) copy-start(bf16[256,1024]{1,0:T(8,128)(2,1)} %get-tuple-element.59.last_ref.cotangent_ref) | copy-start | bytes 1572868
  142.6 5.7 %copy-start.20 = (bf16[256,1024]{1,0:T(8,128)(2,1)S(1)}, bf16[256,1024]{1,0:T(8,128)(2,1)}, u32[]{:S(2)}) copy-start(bf16[256,1024]{1,0:T(8,128)(2,1)} %get-tuple-element.60.after_ref) | copy-start | bytes 1572868
  148.3 12.0 %collective-permute-start.5 = (bf16[8,256,1024]{2,1,0:T(8,128)(2,1)}, bf16[8,256,1024]{2,1,0:T(8,128)(2,1)}, u32[]{:S(2)}, u32[]{:S(2)}) collective-permute-start(bf16[8,256,1024]{2,1,0:T(8,128)(2,1)} %early_first.1.rest_0_), channel_id=1, source_target_pairs={{0,8},{8,0},{16,24},{24,16},{32,40},{40,32},{48,56},{56,48},{64,72... | collective-permute-start | bytes 12582920 | tf_op jit(solution)/shard_map/ppermute | solution.py:514
  155.4 18.5 %all-to-all-start.4 = ((bf16[16,128,128]{2,1,0:T(8,128)(2,1)}), bf16[16,128,128]{2,1,0:T(8,128)(2,1)}, u32[]{:S(2)}, u32[]{:S(2)}) async-start(bf16[16,128,128]{2,1,0:T(8,128)(2,1)} %get-tuple-element.62), calls=%async_computation.4 | async-start | bytes 1048576 | tf_op jit(solution)/shard_map/all_to_all | solution.py:839
  170.8 33.3 %collective-permute-start.6 = (bf16[8,128,512]{2,1,0:T(8,128)(2,1)}, bf16[8,128,512]{2,1,0:T(8,128)(2,1)}, u32[]{:S(2)}, u32[]{:S(2)}) collective-permute-start(bf16[8,128,512]{2,1,0:T(8,128)(2,1)} %get-tuple-element.66), channel_id=1, source_target_pairs={{0,2},{1,3},{2,0},{3,1},{4,6},{5,7},{6,4},{7,5},{8,10},{9,11},{10,... | collective-permute-start | bytes 3145736 | tf_op jit(solution)/shard_map/ppermute | solution.py:514
  171.8 32.3 %collective-permute-start.7 = (bf16[8,128,512]{2,1,0:T(8,128)(2,1)}, bf16[8,128,512]{2,1,0:T(8,128)(2,1)}, u32[]{:S(2)}, u32[]{:S(2)}) collective-permute-start(bf16[8,128,512]{2,1,0:T(8,128)(2,1)} %get-tuple-element.68), channel_id=1, source_target_pairs={{0,6},{1,7},{2,4},{3,5},{4,2},{5,3},{6,0},{7,1},{8,14},{9,15},{10,... | collective-permute-start | bytes 3145736 | tf_op jit(solution)/shard_map/ppermute | solution.py:514
  173.9 1.4 copy-start.15
  175.3 1.6 copy-start.24
  183.7 7.3 %copy-start.1 = (bf16[256,1024]{1,0:T(8,128)(2,1)S(1)}, bf16[256,1024]{1,0:T(8,128)(2,1)}, u32[]{:S(2)}) copy-start(bf16[256,1024]{1,0:T(8,128)(2,1)} %get-tuple-element.64.grad_after_ref.rest_1_.refs_7_) | copy-start | bytes 1572868
  183.7 43.6 %all-to-all-start.5 = ((bf16[16,384,128]{2,1,0:T(8,128)(2,1)}), bf16[16,384,128]{2,1,0:T(8,128)(2,1)S(1)}, u32[]{:S(2)}, u32[]{:S(2)}) async-start(bf16[16,384,128]{2,1,0:T(8,128)(2,1)} %bitcast.16), calls=%async_computation.5 | async-start | bytes 3145728 | tf_op jit(solution)/shard_map/all_to_all | solution.py:839
  192.0 1.2 copy-start.17
  193.2 10.9 %copy-start.18 = (bf16[8,128,512]{2,1,0:T(8,128)(2,1)S(1)}, bf16[8,128,512]{2,1,0:T(8,128)(2,1)}, u32[]{:S(2)}) copy-start(bf16[8,128,512]{2,1,0:T(8,128)(2,1)} %get-tuple-element.65.left_ref) | copy-start | bytes 3145732
  193.2 10.9 %copy-start.19 = (bf16[8,128,512]{2,1,0:T(8,128)(2,1)S(1)}, bf16[8,128,512]{2,1,0:T(8,128)(2,1)}, u32[]{:S(2)}) copy-start(bf16[8,128,512]{2,1,0:T(8,128)(2,1)} %get-tuple-element.67.right_ref) | copy-start | bytes 3145732
  203.5 6.0 %collective-permute-start.11 = (bf16[256,1408]{1,0:T(8,128)(2,1)S(1)}, bf16[256,1408]{1,0:T(8,128)(2,1)S(1)}, u32[]{:S(2)}, u32[]{:S(2)}) collective-permute-start(bf16[256,1408]{1,0:T(8,128)(2,1)S(1)} %get-tuple-element.75), channel_id=1, source_target_pairs={{0,8},{8,0},{16,24},{24,16},{32,40},{40,32},{48,56},{56,48},{64,72... | collective-permute-start | bytes 2162696 | tf_op jit(solution)/shard_map/ppermute | solution.py:514
  204.0 5.5 %collective-permute-start.12 = (bf16[256,1408]{1,0:T(8,128)(2,1)S(1)}, bf16[256,1408]{1,0:T(8,128)(2,1)S(1)}, u32[]{:S(2)}, u32[]{:S(2)}) collective-permute-start(bf16[256,1408]{1,0:T(8,128)(2,1)S(1)} %get-tuple-element.76), channel_id=1, source_target_pairs={{0,8},{8,0},{16,24},{24,16},{32,40},{40,32},{48,56},{56,48},{64,72... | collective-permute-start | bytes 2162696 | tf_op jit(solution)/shard_map/ppermute | solution.py:514
  208.3 15.9 %copy-start.21 = (bf16[8,64,1024]{2,1,0:T(8,128)(2,1)S(1)}, bf16[8,64,1024]{2,1,0:T(8,128)(2,1)}, u32[]{:S(2)}) copy-start(bf16[8,64,1024]{2,1,0:T(8,128)(2,1)} %get-tuple-element.69.own_ref) | copy-start | bytes 3145732
  208.3 15.9 %collective-permute-start.8 = (bf16[8,64,512]{2,1,0:T(8,128)(2,1)S(1)}, bf16[8,64,512]{2,1,0:T(8,128)(2,1)S(1)}, u32[]{:S(2)}, u32[]{:S(2)}) collective-permute-start(bf16[8,64,512]{2,1,0:T(8,128)(2,1)S(1)} %get-tuple-element.70), channel_id=1, source_target_pairs={{0,6},{1,7},{2,4},{3,5},{4,2},{5,3},{6,0},{7,1},{8,14},{9,15},{10,... | collective-permute-start | bytes 1572872 | tf_op jit(solution)/shard_map/ppermute | solution.py:514
  209.5 14.8 %collective-permute-start.9 = (bf16[8,64,512]{2,1,0:T(8,128)(2,1)S(1)}, bf16[8,64,512]{2,1,0:T(8,128)(2,1)S(1)}, u32[]{:S(2)}, u32[]{:S(2)}) collective-permute-start(bf16[8,64,512]{2,1,0:T(8,128)(2,1)S(1)} %get-tuple-element.71), channel_id=1, source_target_pairs={{0,2},{1,3},{2,0},{3,1},{4,6},{5,7},{6,4},{7,5},{8,10},{9,11},{10,... | collective-permute-start | bytes 1572872 | tf_op jit(solution)/shard_map/ppermute | solution.py:514
  211.6 15.7 %copy-start.8 = (bf16[256,1024]{1,0:T(8,128)(2,1)S(1)}, bf16[256,1024]{1,0:T(8,128)(2,1)}, u32[]{:S(2)}) copy-start(bf16[256,1024]{1,0:T(8,128)(2,1)} %get-tuple-element.54.tokens_ref) | copy-start | bytes 1572868
  211.6 21.5 %collective-permute-start.13 = (bf16[2,64,1408]{2,1,0:T(8,128)(2,1)}, bf16[2,64,1408]{2,1,0:T(8,128)(2,1)}, u32[]{:S(2)}, u32[]{:S(2)}) collective-permute-start(bf16[2,64,1408]{2,1,0:T(8,128)(2,1)} %get-tuple-element.78), channel_id=1, source_target_pairs={{0,2},{1,3},{2,0},{3,1},{4,6},{5,7},{6,4},{7,5},{8,10},{9,11},{10,... | collective-permute-start | bytes 1081352 | tf_op jit(solution)/shard_map/ppermute | solution.py:514
  213.7 26.9 %collective-permute-start.14 = (bf16[2,64,1408]{2,1,0:T(8,128)(2,1)}, bf16[2,64,1408]{2,1,0:T(8,128)(2,1)}, u32[]{:S(2)}, u32[]{:S(2)}) collective-permute-start(bf16[2,64,1408]{2,1,0:T(8,128)(2,1)} %get-tuple-element.79), channel_id=1, source_target_pairs={{0,4},{1,5},{2,6},{3,7},{4,0},{5,1},{6,2},{7,3},{8,12},{9,13},{10,... | collective-permute-start | bytes 1081352 | tf_op jit(solution)/shard_map/ppermute | solution.py:514
  215.2 25.4 %collective-permute-start.15 = (bf16[2,64,1408]{2,1,0:T(8,128)(2,1)S(1)}, bf16[2,64,1408]{2,1,0:T(8,128)(2,1)}, u32[]{:S(2)}, u32[]{:S(2)}) collective-permute-start(bf16[2,64,1408]{2,1,0:T(8,128)(2,1)S(1)} %get-tuple-element.80), channel_id=1, source_target_pairs={{0,6},{1,7},{2,4},{3,5},{4,2},{5,3},{6,0},{7,1},{8,14},{9,15},{10,... | collective-permute-start | bytes 1081352 | tf_op jit(solution)/shard_map/ppermute | solution.py:514
  226.4 22.0 %collective-permute-start.10 = (bf16[8,32,1024]{2,1,0:T(8,128)(2,1)}, bf16[8,32,1024]{2,1,0:T(8,128)(2,1)}, u32[]{:S(2)}, u32[]{:S(2)}) collective-permute-start(bf16[8,32,1024]{2,1,0:T(8,128)(2,1)} %get-tuple-element.73), channel_id=1, source_target_pairs={{0,1},{1,0},{2,3},{3,2},{4,5},{5,4},{6,7},{7,6},{8,9},{9,8},{10,11... | collective-permute-start | bytes 1572872 | tf_op jit(solution)/shard_map/ppermute | solution.py:514
  227.3 13.2 %copy-start.22 = (bf16[2,64,1408]{2,1,0:T(8,128)(2,1)S(1)}, bf16[2,64,1408]{2,1,0:T(8,128)(2,1)}, u32[]{:S(2)}) copy-start(bf16[2,64,1408]{2,1,0:T(8,128)(2,1)} %get-tuple-element.77.refs_0_) | copy-start | bytes 1081348
  233.1 15.3 %copy-start.23 = (bf16[8,32,1024]{2,1,0:T(8,128)(2,1)S(1)}, bf16[8,32,1024]{2,1,0:T(8,128)(2,1)}, u32[]{:S(2)}) copy-start(bf16[8,32,1024]{2,1,0:T(8,128)(2,1)} %get-tuple-element.72.early_ref) | copy-start | bytes 1572868
  242.6 5.9 %collective-permute-start.16 = (bf16[2,32,1408]{2,1,0:T(8,128)(2,1)S(1)}, bf16[2,32,1408]{2,1,0:T(8,128)(2,1)S(1)}, u32[]{:S(2)}, u32[]{:S(2)}) collective-permute-start(bf16[2,32,1408]{2,1,0:T(8,128)(2,1)S(1)} %get-tuple-element.82), channel_id=1, source_target_pairs={{0,1},{1,0},{2,3},{3,2},{4,5},{5,4},{6,7},{7,6},{8,9},{9,8},{10,11... | collective-permute-start | bytes 540680 | tf_op jit(solution)/shard_map/ppermute | solution.py:514
  250.2 20.9 %copy-start.10 = (bf16[256,1024]{1,0:T(8,128)(2,1)S(1)}, bf16[256,1024]{1,0:T(8,128)(2,1)}, u32[]{:S(2)}) copy-start(bf16[256,1024]{1,0:T(8,128)(2,1)} %copy-done.9) | copy-start | bytes 1572868
  250.2 9.7 %collective-permute-start.17 = (bf16[2,32,2176]{2,1,0:T(8,128)(2,1)S(1)}, bf16[2,32,2176]{2,1,0:T(8,128)(2,1)S(1)}, u32[]{:S(2)}, u32[]{:S(2)}) collective-permute-start(bf16[2,32,2176]{2,1,0:T(8,128)(2,1)S(1)} %get-tuple-element.84), channel_id=1, source_target_pairs={{0,32},{8,40},{16,48},{24,56},{32,0},{40,8},{48,16},{56,24},{64,96... | collective-permute-start | bytes 835592 | tf_op jit(solution)/shard_map/ppermute | solution.py:514
  251.7 13.1 %collective-permute-start.18 = (bf16[2,32,2176]{2,1,0:T(8,128)(2,1)S(1)}, bf16[2,32,2176]{2,1,0:T(8,128)(2,1)S(1)}, u32[]{:S(2)}, u32[]{:S(2)}) collective-permute-start(bf16[2,32,2176]{2,1,0:T(8,128)(2,1)S(1)} %get-tuple-element.85), channel_id=1, source_target_pairs={{0,64},{8,72},{16,80},{24,88},{32,96},{40,104},{48,112},{56,120},{... | collective-permute-start | bytes 835592 | tf_op jit(solution)/shard_map/ppermute | solution.py:514
  254.4 13.0 %collective-permute-start.19 = (bf16[2,32,2176]{2,1,0:T(8,128)(2,1)S(1)}, bf16[2,32,2176]{2,1,0:T(8,128)(2,1)S(1)}, u32[]{:S(2)}, u32[]{:S(2)}) collective-permute-start(bf16[2,32,2176]{2,1,0:T(8,128)(2,1)S(1)} %get-tuple-element.86), channel_id=1, source_target_pairs={{0,96},{8,104},{16,112},{24,120},{32,64},{40,72},{48,80},{56,88},{... | collective-permute-start | bytes 835592 | tf_op jit(solution)/shard_map/ppermute | solution.py:514
  268.1 6.9 %collective-permute-start.20 = (bf16[4,32,640]{2,1,0:T(8,128)(2,1)S(1)}, bf16[4,32,640]{2,1,0:T(8,128)(2,1)S(1)}, u32[]{:S(2)}, u32[]{:S(2)}) collective-permute-start(bf16[4,32,640]{2,1,0:T(8,128)(2,1)S(1)} %get-tuple-element.88), channel_id=1, source_target_pairs={{0,16},{8,24},{16,0},{24,8},{32,48},{40,56},{48,32},{56,40},{64,80... | collective-permute-start | bytes 491528 | tf_op jit(solution)/shard_map/ppermute | solution.py:514
  (7 other events, 7.0 us)

commit v6 on v5

--- a/solution.py
+++ b/solution.py
@@ -294,7 +294,7 @@
         compiler_params=params(),
         cost_estimate=cost(6e9, 6 * MIB),
         name="agent_backward",
-    )(arrived, arrived, arrived, upstream, tables, *map(pinned, waits))
+    )(*[pinned(arrived)] * 3, upstream, pinned(tables), *map(pinned, waits))
 
 
 def middle_kernel(
@@ -353,7 +353,7 @@
             fixed((ROWS, D)),
         ],
         out_shape=[
-            jax.ShapeDtypeStruct((8, 4, ROWS, 128), BF),
+            pltpu.HBM((8, 4, ROWS, 128), BF),
             pltpu.HBM((ROWS, D), BF),
             pltpu.HBM((8, ROWS, 128), BF),
             pltpu.HBM((ROWS, D), BF),
@@ -457,7 +457,7 @@
         compiler_params=params(45),
         cost_estimate=cost(4 * 2 * ROWS * D * D, 12 * MIB),
         name="turn",
-    )(returned, cotangent, after, pinned(weights), *map(pinned, waits))
+    )(returned, cotangent, after, pinned(weights), *waits)
 
 
 def whole_rows(ref):
@@ -579,7 +579,7 @@
         pl.BlockSpec((8, 1, ROWS, 128), lambda i, c: (0, jnp.minimum(i // 2, 2) + 1, 0, 0)),
         pl.BlockSpec((ROWS, D), lambda i, c: (0, 0)),
     ]
-    operands = [hidden, returned, returned, last]
+    operands = [pinned(hidden), returned, returned, pinned(last)]
     if arrived is None:
         return prefetched(
             functools.partial(early_kernel, False), ids, operands + [pinned(wait) for wait in waits],
@@ -731,7 +731,7 @@
         pl.BlockSpec((ROWS, D), lambda i, c: (0, 0)),
     ]
     return prefetched(
-        late_kernel, ids, list(hiddens) + [grads, grads, mixed, grad_after, *map(pinned, waits)],
+        late_kernel, ids, list(map(pinned, hiddens)) + [grads, grads, pinned(mixed), grad_after, *map(pinned, waits)],
         in_specs + [unused] * len(waits),
         [pl.BlockSpec((2, ROWS, WIDE), lambda i, c: (0, 0, 0))]
         + [pl.BlockSpec((ROWS, WIDE), lambda i, c: (0, 0))] * 2,

time: 278 us -> 271 us (0.975)
  local copies, waits for them, and re-layouts: 15 us -> 4.28 us
  Pallas kernels: 85.2 us -> 89.2 us
    unnamed x58 -> x36, local copies, waits for them, and re-layouts: 12.6 us -> 1.89 us
    pallas_call x10, Pallas kernels: 38.7 us -> 42.1 us  [prefetched(): pl.pallas_call(kernel, grid_spec=pltpu.PrefetchScalarGridSpec(num_scalar_...]
  transfers between devices with their start and end apart: 27 -> 27, of which waited for: 14 -> 14; matrix products, arithmetic and copies ran while one was open for 1% -> 1% of each run, Pallas kernels for 19% -> 20%
where the time goes in v6:
time: 271 us; the launch traced here: 270 us
  waiting for transfers between devices  114 us (42%)
  Pallas kernels  89.2 us (33%)
  starting transfers between devices  59.3 us (22%)
  local copies, waits for them, and re-layouts  4.28 us (2%)
    ppermute x21, waiting for transfers between devices, swap(): return lax.ppermute(values, axis, [(n, n ^ bits) for n in range(size)])  84.7 us
    pallas_call x10, Pallas kernels, prefetched(): pl.pallas_call(kernel, grid_spec=pltpu.PrefetchScalarGridSpec(num_scalar_...  42.1 us
    all_to_all x6, starting transfers between devices, exchange(): return lax.all_to_all(values, axis, split_axis=0, concat_axis=0, tiled=True)  34.4 us
    all_to_all x6, waiting for transfers between devices, exchange(): return lax.all_to_all(values, axis, split_axis=0, concat_axis=0, tiled=True)  29.3 us
    ppermute x21, starting transfers between devices, swap(): return lax.ppermute(values, axis, [(n, n ^ bits) for n in range(size)])  24.8 us
    pallas_call x1, Pallas kernels, mode_attention(): pl.pallas_call(mode_kernel, grid=(4,), in_specs=[spec] + [unused] * len(a...  9.42 us
    pallas_call x1, Pallas kernels, middle(): pl.pallas_call(middle_kernel, grid=(5,), in_specs=[fixed((ROWS, D)), fixe...  8.07 us
    pallas_call x1, Pallas kernels, agent_backward(): pl.pallas_call(agent_backward_all_kernel, grid=(4,), in_specs=agent_specs...  7.15 us
  transfers between devices with their start and end apart: 27, of which 14 were waited for; matrix products, arithmetic and copies ran while one was open for 1% of the time, Pallas kernels for 20%

profile of v6, /device:TPU:0, one launch (start us, length us, event | category | flops | bytes accessed | tf_op | source)
XLA Modules:
  0.0 269.8 jit_solution(10406488143835895600)
XLA Ops:
  0.6 1.2 reshape.64.tokens_ref
  1.9 5.5 %enter.1 = (bf16[16,384,128]{2,1,0:T(8,128)(2,1)}, bf16[256,1024]{1,0:T(8,128)(2,1)}, bf16[128,1024]{1,0:T(8,128)(2,1)}, bf16[128,1024]{1,0:T(8,128)(2,1)S(1)}) custom-call(s32[7]{0:T(128)S(1)} %stack.40.ids_ref, bf16[256,1024]{1,0:T(8,128)(2,1)S(1)} %reshape.64.tokens_ref, bf16[8,1024,1024]{2,1,0:T(8,128)(2,1)} %weights_ref.7), custom_call_target="tpu_custom_call" | custom-call | flops 1610612736 | bytes 8388608 | tf_op jit(solution)/shard_map/enter/pallas_call | solution.py:178
  7.4 7.3 %all-to-all-start = ((bf16[16,384,128]{2,1,0:T(8,128)(2,1)}), bf16[16,384,128]{2,1,0:T(8,128)(2,1)S(1)}, u32[]{:S(2)}, u32[]{:S(2)}) async-start(bf16[16,384,128]{2,1,0:T(8,128)(2,1)} %get-tuple-element.53), calls=%async_computation | async-start | bytes 3145728 | tf_op jit(solution)/shard_map/all_to_all | solution.py:839
  15.2 1.2 collective-permute-done
  16.3 3.4 %collective-permute-start.1 = (bf16[256,1024]{1,0:T(8,128)(2,1)S(1)}, bf16[256,1024]{1,0:T(8,128)(2,1)}, u32[]{:S(2)}, u32[]{:S(2)}) collective-permute-start(bf16[256,1024]{1,0:T(8,128)(2,1)S(1)} %constant_dynamic-update-slice_fusion), channel_id=1, source_target_pairs={{0,16},{8,24},{16,0},{24,8},{32,48},{40,56},{48,32},{56,40},{64,80... | collective-permute-start | bytes 1572872 | tf_op jit(solution)/shard_map/ppermute | solution.py:514
  19.8 18.5 %all-to-all-done.query_ref.keys_ref.values_ref.q.k.v = bf16[16,384,128]{2,1,0:T(8,128)(2,1)S(1)} async-done(((bf16[16,384,128]{2,1,0:T(8,128)(2,1)}), bf16[16,384,128]{2,1,0:T(8,128)(2,1)S(1)}, u32[]{:S(2)}, u32[]{:S(2)}) %all-to-all-start) | async-done | bytes 1572896 | tf_op jit(solution)/shard_map/all_to_all | solution.py:839
  38.3 4.8 %agent_forward.1 = (bf16[16,128,128]{2,1,0:T(8,128)(2,1)}, f32[4,4,256,128]{3,2,1,0:T(8,128)}) custom-call(bf16[16,384,128]{2,1,0:T(8,128)(2,1)S(1)} %all-to-all-done.query_ref.keys_ref.values_ref.q.k.v, bf16[16,384,128]{2,1,0:T(8,128)(2,1)S(1)} %all-to-all-done.query_ref.keys_ref.values_ref.q.k.v, ...), custom_call_target="tpu_custom_call" | custom-call | flops 3000000000 | bytes 4194304 | tf_op jit(solution)/shard_map/agent_forward/pallas_call | solution.py:228
  43.1 4.4 %all-to-all-start.1 = ((bf16[16,128,128]{2,1,0:T(8,128)(2,1)}), bf16[16,128,128]{2,1,0:T(8,128)(2,1)S(1)}, u32[]{:S(2)}, u32[]{:S(2)}) async-start(bf16[16,128,128]{2,1,0:T(8,128)(2,1)} %get-tuple-element.55), calls=%async_computation.1 | async-start | bytes 1048576 | tf_op jit(solution)/shard_map/all_to_all | solution.py:839
  47.6 2.1 pad_maximum_fusion.rest_0_.refs_0_
  49.8 10.1 %all-to-all-done.1 = bf16[16,128,128]{2,1,0:T(8,128)(2,1)S(1)} async-done(((bf16[16,128,128]{2,1,0:T(8,128)(2,1)}), bf16[16,128,128]{2,1,0:T(8,128)(2,1)S(1)}, u32[]{:S(2)}, u32[]{:S(2)}) %all-to-all-start.1) | async-done | bytes 524320 | tf_op jit(solution)/shard_map/all_to_all | solution.py:839
  59.8 8.1 %middle.1 = (bf16[8,4,256,128]{3,2,1,0:T(8,128)(2,1)}, bf16[256,1024]{1,0:T(8,128)(2,1)}, bf16[8,256,128]{2,1,0:T(8,128)(2,1)}, bf16[256,1024]{1,0:T(8,128)(2,1)}) custom-call(bf16[256,1024]{1,0:T(8,128)(2,1)S(1)} %copy-done.3, bf16[8,256,128]{2,1,0:T(8,128)(2,1)S(1)} %bitcast.25, bf16[256,1024]{1,0:T(8,128)(2,1)S(1)} %reshape.67.cotangent_ref, ...), custom_call_target="tpu_custom_call" | custom-call | flops 2684354560 | bytes 13631488 | tf_op jit(solution)/shard_map/middle/pallas_call | solution.py:339
  67.9 5.5 %all-to-all-start.2 = ((bf16[8,1024,128]{2,1,0:T(8,128)(2,1)}), bf16[8,1024,128]{2,1,0:T(8,128)(2,1)S(1)}, u32[]{:S(2)}, u32[]{:S(2)}) async-start(bf16[8,1024,128]{2,1,0:T(8,128)(2,1)} %bitcast.28), calls=%async_computation.2 | async-start | bytes 4194304 | tf_op jit(solution)/shard_map/all_to_all | solution.py:839
  74.3 24.4 %collective-permute-done.3.rest_1_.refs_3_ = bf16[2,256,1024]{2,1,0:T(8,128)(2,1)S(1)} collective-permute-done((bf16[2,256,1024]{2,1,0:T(8,128)(2,1)}, bf16[2,256,1024]{2,1,0:T(8,128)(2,1)S(1)}, u32[]{:S(2)}, u32[]{:S(2)}) %collective-permute-start.3) | collective-permute-done | bytes 1048608 | tf_op jit(solution)/shard_map/ppermute | solution.py:514
  98.8 1.0 copy-done.13
  99.8 9.4 %mode_attention.1 = bf16[8,4,256,128]{3,2,1,0:T(8,128)(2,1)} custom-call(bf16[8,4,256,128]{3,2,1,0:T(8,128)(2,1)S(1)} %bitcast.27, bf16[2,256,1024]{2,1,0:T(8,128)(2,1)} %collective-permute-done.2.rest_0_.refs_1_, bf16[2,256,1024]{2,1,0:T(8,128)(2,1)} %copy-done.13), custom_call_target="tpu_custom_call" | custom-call | flops 8000000000 | bytes 4194304 | tf_op jit(solution)/shard_map/mode_attention/pallas_call | solution.py:394
  109.2 5.4 %all-to-all-start.3 = ((bf16[8,1024,128]{2,1,0:T(8,128)(2,1)}), bf16[8,1024,128]{2,1,0:T(8,128)(2,1)S(1)}, u32[]{:S(2)}, u32[]{:S(2)}) async-start(bf16[8,1024,128]{2,1,0:T(8,128)(2,1)} %bitcast.29), calls=%async_computation.3 | async-start | bytes 4194304 | tf_op jit(solution)/shard_map/all_to_all | solution.py:839
  115.3 23.7 %collective-permute-done.4.rest_0_.refs_2_ = bf16[2,256,1024]{2,1,0:T(8,128)(2,1)} collective-permute-done((bf16[2,256,1024]{2,1,0:T(8,128)(2,1)}, bf16[2,256,1024]{2,1,0:T(8,128)(2,1)}, u32[]{:S(2)}, u32[]{:S(2)}) %collective-permute-start.4) | collective-permute-done | bytes 1048608 | tf_op jit(solution)/shard_map/ppermute | solution.py:514
  139.4 7.9 %early_first.1.rest_0_ = bf16[8,256,1024]{2,1,0:T(8,128)(2,1)} custom-call(s32[7]{0:T(128)S(1)} %constant_dynamic-update-slice_fusion.2.ids_ref, bf16[8,256,128]{2,1,0:T(8,128)(2,1)} %get-tuple-element.61.hidden_ref, bf16[8,4,256,128]{3,2,1,0:T(8,128)(2,1)S(1)} %bitcast.19, bf16[8,4,256,128]{3,2,1,0:T(8,128)(2,1)S(1)} %bitcast.20, ...), custom_call_target="tpu_custom_call" | custom-call | flops 1000000000 | bytes 5242880 | tf_op jit(solution)/shard_map/early_first/pallas_call | solution.py:522
  147.3 7.1 %turn.1 = (bf16[16,128,128]{2,1,0:T(8,128)(2,1)}, bf16[256,1024]{1,0:T(8,128)(2,1)}) custom-call(bf16[8,4,256,128]{3,2,1,0:T(8,128)(2,1)S(1)} %bitcast.21, bf16[256,1024]{1,0:T(8,128)(2,1)S(1)} %copy-done.2, bf16[256,1024]{1,0:T(8,128)(2,1)S(1)} %copy-done.9, bf16[8,1024,1024]{2,1,0:T(8,128)(2,1)} %weights_ref.7, bf16[8,256,1024]{2,1,0:T(8,128)(2,1)} %early_first.1.rest_0_), custom_call_target="tpu_custom_call" | custom-call | flops 2147483648 | bytes 12582912 | tf_op jit(solution)/shard_map/turn/pallas_call | solution.py:441
  154.4 4.8 %all-to-all-start.4 = ((bf16[16,128,128]{2,1,0:T(8,128)(2,1)}), bf16[16,128,128]{2,1,0:T(8,128)(2,1)S(1)}, u32[]{:S(2)}, u32[]{:S(2)}) async-start(bf16[16,128,128]{2,1,0:T(8,128)(2,1)} %get-tuple-element.62), calls=%async_computation.4 | async-start | bytes 1048576 | tf_op jit(solution)/shard_map/all_to_all | solution.py:839
  159.3 8.8 %early_add.1 = (bf16[8,128,512]{2,1,0:T(8,128)(2,1)}, bf16[8,128,512]{2,1,0:T(8,128)(2,1)}, bf16[8,128,512]{2,1,0:T(8,128)(2,1)}, bf16[8,128,512]{2,1,0:T(8,128)(2,1)}) custom-call(s32[7]{0:T(128)S(1)} %stack.40.ids_ref, bf16[8,256,128]{2,1,0:T(8,128)(2,1)} %get-tuple-element.61.hidden_ref, bf16[8,4,256,128]{3,2,1,0:T(8,128)(2,1)S(1)} %bitcast.22, ...), custom_call_target="tpu_custom_call" | custom-call | flops 1000000000 | bytes 5242880 | tf_op jit(solution)/shard_map/early_add/pallas_call | solution.py:522
  168.1 1.2 collective-permute-start.6
  169.3 2.1 collective-permute-start.7
  171.6 7.1 %agent_backward.1.refs_4_.refs_5_ = bf16[16,3,128,128]{3,2,1,0:T(8,128)(2,1)} custom-call(bf16[16,384,128]{2,1,0:T(8,128)(2,1)} %copy-done.6, bf16[16,384,128]{2,1,0:T(8,128)(2,1)} %copy-done.6, bf16[16,384,128]{2,1,0:T(8,128)(2,1)} %copy-done.6, bf16[16,128,128]{2,1,0:T(8,128)(2,1)S(1)} %all-to-all-done.4.g, f32[4,4,256,128]{3,2,1,0:T(8,128)} %get-tuple-element.63.table_ref), custom_call_target="tpu_custom_call" | custom-call | flops 6000000000 | bytes 6291456 | tf_op jit(solution)/shard_map/agent_backward/pallas_call | solution.py:283
  178.8 7.1 %all-to-all-start.5 = ((bf16[16,384,128]{2,1,0:T(8,128)(2,1)}), bf16[16,384,128]{2,1,0:T(8,128)(2,1)S(1)}, u32[]{:S(2)}, u32[]{:S(2)}) async-start(bf16[16,384,128]{2,1,0:T(8,128)(2,1)} %bitcast.16), calls=%async_computation.5 | async-start | bytes 3145728 | tf_op jit(solution)/shard_map/all_to_all | solution.py:839
  185.9 11.0 %late_products.1 = (bf16[2,256,1408]{2,1,0:T(8,128)(2,1)S(1)}, bf16[256,1408]{1,0:T(8,128)(2,1)S(1)}, bf16[256,1408]{1,0:T(8,128)(2,1)S(1)}) custom-call(s32[7]{0:T(128)S(1)} %stack.40.ids_ref, bf16[2,256,1024]{2,1,0:T(8,128)(2,1)} %pad_maximum_fusion.rest_0_.refs_0_, bf16[2,256,1024]{2,1,0:T(8,128)(2,1)} %collective-permute-done.2.rest_0_.refs_1_, ...), custom_call_target="tpu_custom_call" | custom-call | flops 1000000000 | bytes 5242880 | tf_op jit(solution)/shard_map/late_products/pallas_call | solution.py:522
  197.5 4.3 %early_half.1 = (bf16[8,64,1024]{2,1,0:T(8,128)(2,1)}, bf16[8,64,512]{2,1,0:T(8,128)(2,1)S(1)}, bf16[8,64,512]{2,1,0:T(8,128)(2,1)S(1)}) custom-call(s32[7]{0:T(128)S(1)} %stack.40.ids_ref, bf16[8,128,512]{2,1,0:T(8,128)(2,1)S(1)} %copy-done.7, bf16[8,128,512]{2,1,0:T(8,128)(2,1)} %collective-permute-done.6.left_in, bf16[8,128,512]{2,1,0:T(8,128)(2,1)S(1)} %copy-done.8, ...), custom_call_target="tpu_custom_call" | custom-call | flops 1000000000 | bytes 5242880 | tf_op jit(solution)/shard_map/early_half/pallas_call | solution.py:522
  201.8 1.2 collective-permute-start.8
  203.0 2.1 late_add.1
  205.2 2.0 collective-permute-start.13
  207.2 1.5 collective-permute-start.14
  208.7 1.1 collective-permute-start.15
  209.9 7.9 %collective-permute-done.8.left_ref = bf16[8,64,512]{2,1,0:T(8,128)(2,1)S(1)} collective-permute-done((bf16[8,64,512]{2,1,0:T(8,128)(2,1)S(1)}, bf16[8,64,512]{2,1,0:T(8,128)(2,1)S(1)}, u32[]{:S(2)}, u32[]{:S(2)}) %collective-permute-start.8) | collective-permute-done | bytes 524320 | tf_op jit(solution)/shard_map/ppermute | solution.py:514
  217.8 2.2 early_z.1
  220.8 5.1 %leave.1.refs_4_ = bf16[256,1024]{1,0:T(8,128)(2,1)S(1)} custom-call(bf16[16,3,128,128]{3,2,1,0:T(8,128)(2,1)S(1)} %bitcast.24, bf16[256,1024]{1,0:T(8,128)(2,1)S(1)} %copy-done.3, bf16[256,1024]{1,0:T(8,128)(2,1)S(1)} %copy-done, bf16[8,1024,1024]{2,1,0:T(8,128)(2,1)} %weights_ref.7), custom_call_target="tpu_custom_call" | custom-call | flops 1610612736 | bytes 9437184 | tf_op jit(solution)/shard_map/leave/pallas_call | solution.py:490
  226.7 7.3 %collective-permute-done.14.refs_2_ = bf16[2,64,1408]{2,1,0:T(8,128)(2,1)} collective-permute-done((bf16[2,64,1408]{2,1,0:T(8,128)(2,1)}, bf16[2,64,1408]{2,1,0:T(8,128)(2,1)}, u32[]{:S(2)}, u32[]{:S(2)}) %collective-permute-start.14) | collective-permute-done | bytes 360480 | tf_op jit(solution)/shard_map/ppermute | solution.py:514
  234.0 2.0 late_z.1
  237.0 4.9 %collective-permute-done.16.late_in = bf16[2,32,1408]{2,1,0:T(8,128)(2,1)S(1)} collective-permute-done((bf16[2,32,1408]{2,1,0:T(8,128)(2,1)S(1)}, bf16[2,32,1408]{2,1,0:T(8,128)(2,1)S(1)}, u32[]{:S(2)}, u32[]{:S(2)}) %collective-permute-start.16) | collective-permute-done | bytes 180256 | tf_op jit(solution)/shard_map/ppermute | solution.py:514
  241.9 1.8 chips.1
  243.7 1.4 collective-permute-start.17
  245.2 2.7 collective-permute-start.18
  248.5 4.9 %collective-permute-done.17.refs_1_ = bf16[2,32,2176]{2,1,0:T(8,128)(2,1)S(1)} collective-permute-done((bf16[2,32,2176]{2,1,0:T(8,128)(2,1)S(1)}, bf16[2,32,2176]{2,1,0:T(8,128)(2,1)S(1)}, u32[]{:S(2)}, u32[]{:S(2)}) %collective-permute-start.17) | collective-permute-done | bytes 278560 | tf_op jit(solution)/shard_map/ppermute | solution.py:514
  253.4 4.9 %collective-permute-done.18.refs_2_ = bf16[2,32,2176]{2,1,0:T(8,128)(2,1)S(1)} collective-permute-done((bf16[2,32,2176]{2,1,0:T(8,128)(2,1)S(1)}, bf16[2,32,2176]{2,1,0:T(8,128)(2,1)S(1)}, u32[]{:S(2)}, u32[]{:S(2)}) %collective-permute-start.18) | collective-permute-done | bytes 278560 | tf_op jit(solution)/shard_map/ppermute | solution.py:514
  258.3 2.6 collective-permute-done.19.refs_3_
  261.6 3.0 %collective-permute-start.20 = (bf16[4,32,640]{2,1,0:T(8,128)(2,1)S(1)}, bf16[4,32,640]{2,1,0:T(8,128)(2,1)S(1)}, u32[]{:S(2)}, u32[]{:S(2)}) collective-permute-start(bf16[4,32,640]{2,1,0:T(8,128)(2,1)S(1)} %get-tuple-element.88), channel_id=1, source_target_pairs={{0,16},{8,24},{16,0},{24,8},{32,48},{40,56},{48,32},{56,40},{64,80... | collective-permute-start | bytes 491528 | tf_op jit(solution)/shard_map/ppermute | solution.py:514
  264.6 1.0 reshape.75
  265.6 2.9 %collective-permute-done.20.arrived_ref = bf16[4,32,640]{2,1,0:T(8,128)(2,1)S(1)} collective-permute-done((bf16[4,32,640]{2,1,0:T(8,128)(2,1)S(1)}, bf16[4,32,640]{2,1,0:T(8,128)(2,1)S(1)}, u32[]{:S(2)}, u32[]{:S(2)}) %collective-permute-start.20) | collective-permute-done | bytes 163872 | tf_op jit(solution)/shard_map/ppermute | solution.py:514
  268.5 1.3 last.1
  (67 shorter events, 7.7 us)
Async XLA Ops:
  7.4 7.7 %copy-start.15 = (bf16[128,1024]{1,0:T(8,128)(2,1)S(1)}, bf16[128,1024]{1,0:T(8,128)(2,1)}, u32[]{:S(2)}) copy-start(bf16[128,1024]{1,0:T(8,128)(2,1)} %get-tuple-element.56) | copy-start | bytes 786436
  7.4 7.7 %copy-start.16 = (s32[128]{0:T(128)S(1)}, s32[128]{0:T(128)}, u32[]{:S(2)}) copy-start(s32[128]{0:T(128)} %param.9) | copy-start | bytes 1540
  7.4 30.9 %all-to-all-start = ((bf16[16,384,128]{2,1,0:T(8,128)(2,1)}), bf16[16,384,128]{2,1,0:T(8,128)(2,1)S(1)}, u32[]{:S(2)}, u32[]{:S(2)}) async-start(bf16[16,384,128]{2,1,0:T(8,128)(2,1)} %get-tuple-element.53), calls=%async_computation | async-start | bytes 3145728 | tf_op jit(solution)/shard_map/all_to_all | solution.py:839
  14.7 1.6 collective-permute-start
  16.3 31.1 %copy-start.14 = (bf16[8,8,4,1024]{3,2,1,0:T(4,128)(2,1)S(1)}, bf16[8,8,4,1024]{3,2,1,0:T(4,128)(2,1)}, u32[]{:S(2)}) copy-start(bf16[8,8,4,1024]{3,2,1,0:T(4,128)(2,1)} %param.7) | copy-start | bytes 1572868
  16.3 31.3 %collective-permute-start.1 = (bf16[256,1024]{1,0:T(8,128)(2,1)S(1)}, bf16[256,1024]{1,0:T(8,128)(2,1)}, u32[]{:S(2)}, u32[]{:S(2)}) collective-permute-start(bf16[256,1024]{1,0:T(8,128)(2,1)S(1)} %constant_dynamic-update-slice_fusion), channel_id=1, source_target_pairs={{0,16},{8,24},{16,0},{24,8},{32,48},{40,56},{48,32},{56,40},{64,80... | collective-permute-start | bytes 1572872 | tf_op jit(solution)/shard_map/ppermute | solution.py:514
  38.3 4.8 %copy-start.6 = (bf16[16,384,128]{2,1,0:T(8,128)(2,1)}, bf16[16,384,128]{2,1,0:T(8,128)(2,1)S(1)}, u32[]{:S(2)}) copy-start(bf16[16,384,128]{2,1,0:T(8,128)(2,1)S(1)} %all-to-all-done.query_ref.keys_ref.values_ref.q.k.v) | copy-start | bytes 4718596
  43.1 16.7 %copy-start.3 = (bf16[256,1024]{1,0:T(8,128)(2,1)S(1)}, bf16[256,1024]{1,0:T(8,128)(2,1)}, u32[]{:S(2)}) copy-start(bf16[256,1024]{1,0:T(8,128)(2,1)} %get-tuple-element.54.tokens_ref) | copy-start | bytes 1572868
  43.1 16.7 %all-to-all-start.1 = ((bf16[16,128,128]{2,1,0:T(8,128)(2,1)}), bf16[16,128,128]{2,1,0:T(8,128)(2,1)S(1)}, u32[]{:S(2)}, u32[]{:S(2)}) async-start(bf16[16,128,128]{2,1,0:T(8,128)(2,1)} %get-tuple-element.55), calls=%async_computation.1 | async-start | bytes 1048576 | tf_op jit(solution)/shard_map/all_to_all | solution.py:839
  59.8 8.1 %copy-start.1 = (bf16[16,128,128]{2,1,0:T(8,128)(2,1)}, bf16[16,128,128]{2,1,0:T(8,128)(2,1)S(1)}, u32[]{:S(2)}) copy-start(bf16[16,128,128]{2,1,0:T(8,128)(2,1)S(1)} %all-to-all-done.1) | copy-start | bytes 1572868
  67.9 31.9 %all-to-all-start.2 = ((bf16[8,1024,128]{2,1,0:T(8,128)(2,1)}), bf16[8,1024,128]{2,1,0:T(8,128)(2,1)S(1)}, u32[]{:S(2)}, u32[]{:S(2)}) async-start(bf16[8,1024,128]{2,1,0:T(8,128)(2,1)} %bitcast.28), calls=%async_computation.2 | async-start | bytes 4194304 | tf_op jit(solution)/shard_map/all_to_all | solution.py:839
  73.4 25.4 %collective-permute-start.3 = (bf16[2,256,1024]{2,1,0:T(8,128)(2,1)}, bf16[2,256,1024]{2,1,0:T(8,128)(2,1)S(1)}, u32[]{:S(2)}, u32[]{:S(2)}) collective-permute-start(bf16[2,256,1024]{2,1,0:T(8,128)(2,1)} %pad_maximum_fusion.rest_0_.refs_0_), channel_id=1, source_target_pairs={{0,96},{8,104},{16,112},{24,120},{32,64},{40,72},{48,80},{56,88},{... | collective-permute-start | bytes 3145736 | tf_op jit(solution)/shard_map/ppermute | solution.py:514
  74.2 25.6 %collective-permute-start.2 = (bf16[2,256,1024]{2,1,0:T(8,128)(2,1)}, bf16[2,256,1024]{2,1,0:T(8,128)(2,1)}, u32[]{:S(2)}, u32[]{:S(2)}) collective-permute-start(bf16[2,256,1024]{2,1,0:T(8,128)(2,1)} %pad_maximum_fusion.rest_0_.refs_0_), channel_id=1, source_target_pairs={{0,32},{8,40},{16,48},{24,56},{32,0},{40,8},{48,16},{56,24},{64,96... | collective-permute-start | bytes 3145736 | tf_op jit(solution)/shard_map/ppermute | solution.py:514
  98.8 1.0 copy-start.13
  109.2 30.2 %all-to-all-start.3 = ((bf16[8,1024,128]{2,1,0:T(8,128)(2,1)}), bf16[8,1024,128]{2,1,0:T(8,128)(2,1)S(1)}, u32[]{:S(2)}, u32[]{:S(2)}) async-start(bf16[8,1024,128]{2,1,0:T(8,128)(2,1)} %bitcast.29), calls=%async_computation.3 | async-start | bytes 4194304 | tf_op jit(solution)/shard_map/all_to_all | solution.py:839
  114.6 24.3 %collective-permute-start.4 = (bf16[2,256,1024]{2,1,0:T(8,128)(2,1)}, bf16[2,256,1024]{2,1,0:T(8,128)(2,1)}, u32[]{:S(2)}, u32[]{:S(2)}) collective-permute-start(bf16[2,256,1024]{2,1,0:T(8,128)(2,1)} %pad_maximum_fusion.rest_0_.refs_0_), channel_id=1, source_target_pairs={{0,64},{8,72},{16,80},{24,88},{32,96},{40,104},{48,112},{56,120},{... | collective-permute-start | bytes 3145736 | tf_op jit(solution)/shard_map/ppermute | solution.py:514
  139.4 7.9 %copy-start.2 = (bf16[256,1024]{1,0:T(8,128)(2,1)S(1)}, bf16[256,1024]{1,0:T(8,128)(2,1)}, u32[]{:S(2)}) copy-start(bf16[256,1024]{1,0:T(8,128)(2,1)} %get-tuple-element.59.last_ref.cotangent_ref) | copy-start | bytes 1572868
  139.4 7.9 %copy-start.9 = (bf16[256,1024]{1,0:T(8,128)(2,1)S(1)}, bf16[256,1024]{1,0:T(8,128)(2,1)}, u32[]{:S(2)}) copy-start(bf16[256,1024]{1,0:T(8,128)(2,1)} %get-tuple-element.60.after_ref) | copy-start | bytes 1572868
  147.3 11.9 %collective-permute-start.5 = (bf16[8,256,1024]{2,1,0:T(8,128)(2,1)}, bf16[8,256,1024]{2,1,0:T(8,128)(2,1)}, u32[]{:S(2)}, u32[]{:S(2)}) collective-permute-start(bf16[8,256,1024]{2,1,0:T(8,128)(2,1)} %early_first.1.rest_0_), channel_id=1, source_target_pairs={{0,8},{8,0},{16,24},{24,16},{32,40},{40,32},{48,56},{56,48},{64,72... | collective-permute-start | bytes 12582920 | tf_op jit(solution)/shard_map/ppermute | solution.py:514
  154.4 17.2 %all-to-all-start.4 = ((bf16[16,128,128]{2,1,0:T(8,128)(2,1)}), bf16[16,128,128]{2,1,0:T(8,128)(2,1)S(1)}, u32[]{:S(2)}, u32[]{:S(2)}) async-start(bf16[16,128,128]{2,1,0:T(8,128)(2,1)} %get-tuple-element.62), calls=%async_computation.4 | async-start | bytes 1048576 | tf_op jit(solution)/shard_map/all_to_all | solution.py:839
  168.1 29.4 %collective-permute-start.6 = (bf16[8,128,512]{2,1,0:T(8,128)(2,1)}, bf16[8,128,512]{2,1,0:T(8,128)(2,1)}, u32[]{:S(2)}, u32[]{:S(2)}) collective-permute-start(bf16[8,128,512]{2,1,0:T(8,128)(2,1)} %get-tuple-element.66), channel_id=1, source_target_pairs={{0,2},{1,3},{2,0},{3,1},{4,6},{5,7},{6,4},{7,5},{8,10},{9,11},{10,... | collective-permute-start | bytes 3145736 | tf_op jit(solution)/shard_map/ppermute | solution.py:514
  169.3 28.2 %collective-permute-start.7 = (bf16[8,128,512]{2,1,0:T(8,128)(2,1)}, bf16[8,128,512]{2,1,0:T(8,128)(2,1)}, u32[]{:S(2)}, u32[]{:S(2)}) collective-permute-start(bf16[8,128,512]{2,1,0:T(8,128)(2,1)} %get-tuple-element.68), channel_id=1, source_target_pairs={{0,6},{1,7},{2,4},{3,5},{4,2},{5,3},{6,0},{7,1},{8,14},{9,15},{10,... | collective-permute-start | bytes 3145736 | tf_op jit(solution)/shard_map/ppermute | solution.py:514
  178.8 7.1 %copy-start = (bf16[256,1024]{1,0:T(8,128)(2,1)S(1)}, bf16[256,1024]{1,0:T(8,128)(2,1)}, u32[]{:S(2)}) copy-start(bf16[256,1024]{1,0:T(8,128)(2,1)} %get-tuple-element.64.grad_after_ref.rest_1_.refs_7_) | copy-start | bytes 1572868
  178.8 42.1 %all-to-all-start.5 = ((bf16[16,384,128]{2,1,0:T(8,128)(2,1)}), bf16[16,384,128]{2,1,0:T(8,128)(2,1)S(1)}, u32[]{:S(2)}, u32[]{:S(2)}) async-start(bf16[16,384,128]{2,1,0:T(8,128)(2,1)} %bitcast.16), calls=%async_computation.5 | async-start | bytes 3145728 | tf_op jit(solution)/shard_map/all_to_all | solution.py:839
  185.9 11.6 %copy-start.7 = (bf16[8,128,512]{2,1,0:T(8,128)(2,1)S(1)}, bf16[8,128,512]{2,1,0:T(8,128)(2,1)}, u32[]{:S(2)}) copy-start(bf16[8,128,512]{2,1,0:T(8,128)(2,1)} %get-tuple-element.65.left_ref) | copy-start | bytes 3145732
  185.9 11.6 %copy-start.8 = (bf16[8,128,512]{2,1,0:T(8,128)(2,1)S(1)}, bf16[8,128,512]{2,1,0:T(8,128)(2,1)}, u32[]{:S(2)}) copy-start(bf16[8,128,512]{2,1,0:T(8,128)(2,1)} %get-tuple-element.67.right_ref) | copy-start | bytes 3145732
  196.9 6.1 %collective-permute-start.11 = (bf16[256,1408]{1,0:T(8,128)(2,1)S(1)}, bf16[256,1408]{1,0:T(8,128)(2,1)S(1)}, u32[]{:S(2)}, u32[]{:S(2)}) collective-permute-start(bf16[256,1408]{1,0:T(8,128)(2,1)S(1)} %get-tuple-element.75), channel_id=1, source_target_pairs={{0,8},{8,0},{16,24},{24,16},{32,40},{40,32},{48,56},{56,48},{64,72... | collective-permute-start | bytes 2162696 | tf_op jit(solution)/shard_map/ppermute | solution.py:514
  197.4 5.6 %collective-permute-start.12 = (bf16[256,1408]{1,0:T(8,128)(2,1)S(1)}, bf16[256,1408]{1,0:T(8,128)(2,1)S(1)}, u32[]{:S(2)}, u32[]{:S(2)}) collective-permute-start(bf16[256,1408]{1,0:T(8,128)(2,1)S(1)} %get-tuple-element.76), channel_id=1, source_target_pairs={{0,8},{8,0},{16,24},{24,16},{32,40},{40,32},{48,56},{56,48},{64,72... | collective-permute-start | bytes 2162696 | tf_op jit(solution)/shard_map/ppermute | solution.py:514
  201.8 16.0 %copy-start.10 = (bf16[8,64,1024]{2,1,0:T(8,128)(2,1)S(1)}, bf16[8,64,1024]{2,1,0:T(8,128)(2,1)}, u32[]{:S(2)}) copy-start(bf16[8,64,1024]{2,1,0:T(8,128)(2,1)} %get-tuple-element.69.own_ref) | copy-start | bytes 3145732
  201.8 15.9 %collective-permute-start.8 = (bf16[8,64,512]{2,1,0:T(8,128)(2,1)S(1)}, bf16[8,64,512]{2,1,0:T(8,128)(2,1)S(1)}, u32[]{:S(2)}, u32[]{:S(2)}) collective-permute-start(bf16[8,64,512]{2,1,0:T(8,128)(2,1)S(1)} %get-tuple-element.70), channel_id=1, source_target_pairs={{0,6},{1,7},{2,4},{3,5},{4,2},{5,3},{6,0},{7,1},{8,14},{9,15},{10,... | collective-permute-start | bytes 1572872 | tf_op jit(solution)/shard_map/ppermute | solution.py:514
  203.0 14.8 %collective-permute-start.9 = (bf16[8,64,512]{2,1,0:T(8,128)(2,1)S(1)}, bf16[8,64,512]{2,1,0:T(8,128)(2,1)S(1)}, u32[]{:S(2)}, u32[]{:S(2)}) collective-permute-start(bf16[8,64,512]{2,1,0:T(8,128)(2,1)S(1)} %get-tuple-element.71), channel_id=1, source_target_pairs={{0,2},{1,3},{2,0},{3,1},{4,6},{5,7},{6,4},{7,5},{8,10},{9,11},{10,... | collective-permute-start | bytes 1572872 | tf_op jit(solution)/shard_map/ppermute | solution.py:514
  205.2 21.5 %collective-permute-start.13 = (bf16[2,64,1408]{2,1,0:T(8,128)(2,1)}, bf16[2,64,1408]{2,1,0:T(8,128)(2,1)}, u32[]{:S(2)}, u32[]{:S(2)}) collective-permute-start(bf16[2,64,1408]{2,1,0:T(8,128)(2,1)} %get-tuple-element.78), channel_id=1, source_target_pairs={{0,2},{1,3},{2,0},{3,1},{4,6},{5,7},{6,4},{7,5},{8,10},{9,11},{10,... | collective-permute-start | bytes 1081352 | tf_op jit(solution)/shard_map/ppermute | solution.py:514
  207.2 26.8 %collective-permute-start.14 = (bf16[2,64,1408]{2,1,0:T(8,128)(2,1)}, bf16[2,64,1408]{2,1,0:T(8,128)(2,1)}, u32[]{:S(2)}, u32[]{:S(2)}) collective-permute-start(bf16[2,64,1408]{2,1,0:T(8,128)(2,1)} %get-tuple-element.79), channel_id=1, source_target_pairs={{0,4},{1,5},{2,6},{3,7},{4,0},{5,1},{6,2},{7,3},{8,12},{9,13},{10,... | collective-permute-start | bytes 1081352 | tf_op jit(solution)/shard_map/ppermute | solution.py:514
  208.7 25.3 %collective-permute-start.15 = (bf16[2,64,1408]{2,1,0:T(8,128)(2,1)S(1)}, bf16[2,64,1408]{2,1,0:T(8,128)(2,1)}, u32[]{:S(2)}, u32[]{:S(2)}) collective-permute-start(bf16[2,64,1408]{2,1,0:T(8,128)(2,1)S(1)} %get-tuple-element.80), channel_id=1, source_target_pairs={{0,6},{1,7},{2,4},{3,5},{4,2},{5,3},{6,0},{7,1},{8,14},{9,15},{10,... | collective-permute-start | bytes 1081352 | tf_op jit(solution)/shard_map/ppermute | solution.py:514
  219.9 22.0 %collective-permute-start.10 = (bf16[8,32,1024]{2,1,0:T(8,128)(2,1)}, bf16[8,32,1024]{2,1,0:T(8,128)(2,1)}, u32[]{:S(2)}, u32[]{:S(2)}) collective-permute-start(bf16[8,32,1024]{2,1,0:T(8,128)(2,1)} %get-tuple-element.73), channel_id=1, source_target_pairs={{0,1},{1,0},{2,3},{3,2},{4,5},{5,4},{6,7},{7,6},{8,9},{9,8},{10,11... | collective-permute-start | bytes 1572872 | tf_op jit(solution)/shard_map/ppermute | solution.py:514
  220.8 13.2 %copy-start.11 = (bf16[2,64,1408]{2,1,0:T(8,128)(2,1)S(1)}, bf16[2,64,1408]{2,1,0:T(8,128)(2,1)}, u32[]{:S(2)}) copy-start(bf16[2,64,1408]{2,1,0:T(8,128)(2,1)} %get-tuple-element.77.refs_0_) | copy-start | bytes 1081348
  225.9 0.8 copy-start.4
  226.7 15.2 %copy-start.12 = (bf16[8,32,1024]{2,1,0:T(8,128)(2,1)S(1)}, bf16[8,32,1024]{2,1,0:T(8,128)(2,1)}, u32[]{:S(2)}) copy-start(bf16[8,32,1024]{2,1,0:T(8,128)(2,1)} %get-tuple-element.72.early_ref) | copy-start | bytes 1572868
  236.0 5.9 %collective-permute-start.16 = (bf16[2,32,1408]{2,1,0:T(8,128)(2,1)S(1)}, bf16[2,32,1408]{2,1,0:T(8,128)(2,1)S(1)}, u32[]{:S(2)}, u32[]{:S(2)}) collective-permute-start(bf16[2,32,1408]{2,1,0:T(8,128)(2,1)S(1)} %get-tuple-element.82), channel_id=1, source_target_pairs={{0,1},{1,0},{2,3},{3,2},{4,5},{5,4},{6,7},{7,6},{8,9},{9,8},{10,11... | collective-permute-start | bytes 540680 | tf_op jit(solution)/shard_map/ppermute | solution.py:514
  243.7 20.9 %copy-start.5 = (bf16[256,1024]{1,0:T(8,128)(2,1)S(1)}, bf16[256,1024]{1,0:T(8,128)(2,1)}, u32[]{:S(2)}) copy-start(bf16[256,1024]{1,0:T(8,128)(2,1)} %copy-done.4) | copy-start | bytes 1572868
  243.7 9.7 %collective-permute-start.17 = (bf16[2,32,2176]{2,1,0:T(8,128)(2,1)S(1)}, bf16[2,32,2176]{2,1,0:T(8,128)(2,1)S(1)}, u32[]{:S(2)}, u32[]{:S(2)}) collective-permute-start(bf16[2,32,2176]{2,1,0:T(8,128)(2,1)S(1)} %get-tuple-element.84), channel_id=1, source_target_pairs={{0,32},{8,40},{16,48},{24,56},{32,0},{40,8},{48,16},{56,24},{64,96... | collective-permute-start | bytes 835592 | tf_op jit(solution)/shard_map/ppermute | solution.py:514
  245.2 13.1 %collective-permute-start.18 = (bf16[2,32,2176]{2,1,0:T(8,128)(2,1)S(1)}, bf16[2,32,2176]{2,1,0:T(8,128)(2,1)S(1)}, u32[]{:S(2)}, u32[]{:S(2)}) collective-permute-start(bf16[2,32,2176]{2,1,0:T(8,128)(2,1)S(1)} %get-tuple-element.85), channel_id=1, source_target_pairs={{0,64},{8,72},{16,80},{24,88},{32,96},{40,104},{48,112},{56,120},{... | collective-permute-start | bytes 835592 | tf_op jit(solution)/shard_map/ppermute | solution.py:514
  247.9 13.0 %collective-permute-start.19 = (bf16[2,32,2176]{2,1,0:T(8,128)(2,1)S(1)}, bf16[2,32,2176]{2,1,0:T(8,128)(2,1)S(1)}, u32[]{:S(2)}, u32[]{:S(2)}) collective-permute-start(bf16[2,32,2176]{2,1,0:T(8,128)(2,1)S(1)} %get-tuple-element.86), channel_id=1, source_target_pairs={{0,96},{8,104},{16,112},{24,120},{32,64},{40,72},{48,80},{56,88},{... | collective-permute-start | bytes 835592 | tf_op jit(solution)/shard_map/ppermute | solution.py:514
  261.6 6.9 %collective-permute-start.20 = (bf16[4,32,640]{2,1,0:T(8,128)(2,1)S(1)}, bf16[4,32,640]{2,1,0:T(8,128)(2,1)S(1)}, u32[]{:S(2)}, u32[]{:S(2)}) collective-permute-start(bf16[4,32,640]{2,1,0:T(8,128)(2,1)S(1)} %get-tuple-element.88), channel_id=1, source_target_pairs={{0,16},{8,24},{16,0},{24,8},{32,48},{40,56},{48,32},{56,40},{64,80... | collective-permute-start | bytes 491528 | tf_op jit(solution)/shard_map/ppermute | solution.py:514

commit v7 on v6

--- a/solution.py
+++ b/solution.py
@@ -637,8 +637,8 @@
     )
 
 
-def early_z_kernel(ids_ref, own_ref, left_ref, right_ref, keep_ref, give_ref):
-    for other, out_ref in enumerate((keep_ref, give_ref)):
+def early_z_kernel(ids_ref, own_ref, left_ref, right_ref, *rest):
+    for other, out_ref in enumerate(rest[-2:]):
         first = pl.multiple_of((ids_ref[YLO] ^ other) * 32, 32)
         for columns, ref in enumerate((left_ref, right_ref)):
             lanes = slice(512 * columns, 512 * columns + 512)
@@ -648,11 +648,11 @@
             ).astype(BF)
 
 
-def early_sums(ids, own, left, right):
+def early_sums(ids, own, left, right, waits):
     narrow = pl.BlockSpec((2, 64, 512), lambda i, c: (i, 0, 0))
     keep, give = prefetched(
-        early_z_kernel, ids, [own, left, right],
-        [pl.BlockSpec((2, 64, D), lambda i, c: (i, 0, 0)), narrow, narrow],
+        early_z_kernel, ids, [own, left, right, *map(pinned, waits)],
+        [pl.BlockSpec((2, 64, D), lambda i, c: (i, 0, 0)), narrow, narrow] + [unused] * len(waits),
         [pl.BlockSpec((2, 32, D), lambda i, c: (i, 0, 0))] * 2,
         [pltpu.HBM((8, 32, D), BF), jax.ShapeDtypeStruct((8, 32, D), BF)], "early_z", (4,),
     )
@@ -741,9 +741,11 @@
     )
 
 
-def chips_kernel(ids_ref, early_ref, early_in, late_ref, late_in, *rest):
-    outs, total_ref = rest[:-1], rest[-1]
-    total_ref[...] = late_ref[...].astype(F32) + late_in[...].astype(F32)
+def chips_kernel(ids_ref, early_ref, early_in, *rest):
+    late, outs, total_ref = rest[:4], rest[4:-1], rest[-1]
+    total_ref[...] = late[0][...].astype(F32)
+    for ref in late[1:]:
+        total_ref[...] += ref[...].astype(F32)
     for partner, out_ref in enumerate(outs):
         chip_x = ids_ref[X] ^ partner
         lanes = pl.ds(pl.multiple_of(jnp.minimum(chip_x, 2) * 128, 128), 128)
@@ -798,7 +800,7 @@
 def chip_sums(ids, early, late):
     parts = prefetched(
         chips_kernel, ids, [*early, *late],
-        [fixed((8, 32, D))] * 2 + [fixed((2, 32, WIDE))] * 2, [fixed((2, 32, 128 + 2 * D))] * 4,
+        [fixed((8, 32, D))] * 2 + [fixed((2, 32, WIDE))] * 4, [fixed((2, 32, 128 + 2 * D))] * 4,
         [jax.ShapeDtypeStruct((2, 32, 128 + 2 * D), BF)] * 4, "chips", (1,),
         [pltpu.VMEM((2, 32, WIDE), F32)],
     )
@@ -818,21 +820,24 @@
     total_ref = rest[-1]
     for block, ref in enumerate((first_ref, second_ref)):
         total_ref[...] = mine_ref[block].astype(F32) + ref[...].astype(F32)
-        for partner, out_ref in enumerate(rest[-5:-1]):
-            out_ref[block] = rows_of(total_ref, (ids_ref[Z] ^ partner) * 64, 64).astype(BF)
+        for partner, out_ref in enumerate(rest[-3:-1]):
+            for z in range(4):
+                first = z * 64 + (ids_ref[YLO] ^ partner) * 32
+                out_ref[block, 32 * z : 32 * z + 32] = rows_of(total_ref, first, 32).astype(BF)
 
 
 def late_sums(ids, mine, first, second, waits):
-    parts = prefetched(
+    keep, give = prefetched(
         late_add_kernel, ids,
         [mine, swap(first, "agent", 1), swap(second, "agent", 1)],
         [fixed((2, ROWS, WIDE))] + [fixed((ROWS, WIDE))] * 2,
-        [fixed((2, 64, WIDE))] * 4,
-        [pltpu.HBM((2, 64, WIDE), BF)] + [jax.ShapeDtypeStruct((2, 64, WIDE), BF)] * 3, "late_add", (1,),
+        [fixed((2, 128, WIDE))] * 2,
+        [pltpu.HBM((2, 128, WIDE), BF), jax.ShapeDtypeStruct((2, 128, WIDE), BF)],
+        "late_add", (1,),
         [pltpu.VMEM((ROWS, WIDE), F32)],
     )
-    keep, give = sum_split(ids, swap_all(parts, "mode", 2), YLO, 2, "late_z", waits)
-    return keep, swap(give, "mode", 1)
+    parts = sum_split(ids, [keep, swap(give, "mode", 1)], Z, 4, "late_y", waits)
+    return swap_all(parts, "mode", 2)
 
 
 def exchange(values, axis):
@@ -873,8 +878,8 @@
     returned_one = exchange(returning.reshape(16, 384, 128), "agent").reshape(16, 3, 128, 128)
     late_parts = late_products(ids, hiddens, returning, mixed_one, grad_after, [])
     token_grads = leave(returned_one, tokens_a, grad_after, weights)
-    late = late_sums(ids, *late_parts, [token_grads])
-    early = early_sums(ids, own, left, right)
+    late = late_sums(ids, *late_parts, [])
+    early = early_sums(ids, own, left, right, [token_grads])
     agent_weight_grads, mode_weight_grads = chip_sums(ids, early, late)
     return (token_grads.reshape(tokens.shape), agent_weight_grads, mode_weight_grads)
 

time: 271 us -> 265 us (0.978)
  waiting for transfers between devices: 114 us -> 106 us
    ppermute x21, waiting for transfers between devices: 84.7 us -> 73.7 us  [swap(): return lax.ppermute(values, axis, [(n, n ^ bits) for n in range(size)])]
    all_to_all x6, waiting for transfers between devices: 29.3 us -> 32.6 us  [exchange(): return lax.all_to_all(values, axis, split_axis=0, concat_axis=0, tiled=True)]
  transfers between devices with their start and end apart: 27 -> 27, of which waited for: 14 -> 17; matrix products, arithmetic and copies ran while one was open for 1% -> 1% of each run, Pallas kernels for 20% -> 21%
where the time goes in v7:
time: 265 us; the launch traced here: 264 us
  waiting for transfers between devices  106 us (40%)
  Pallas kernels  90.1 us (34%)
  starting transfers between devices  60.1 us (23%)
  local copies, waits for them, and re-layouts  4.28 us (2%)
    ppermute x21, waiting for transfers between devices, swap(): return lax.ppermute(values, axis, [(n, n ^ bits) for n in range(size)])  73.7 us
    pallas_call x10, Pallas kernels, prefetched(): pl.pallas_call(kernel, grid_spec=pltpu.PrefetchScalarGridSpec(num_scalar_...  43 us
    all_to_all x6, starting transfers between devices, exchange(): return lax.all_to_all(values, axis, split_axis=0, concat_axis=0, tiled=True)  34.4 us
    all_to_all x6, waiting for transfers between devices, exchange(): return lax.all_to_all(values, axis, split_axis=0, concat_axis=0, tiled=True)  32.6 us
    ppermute x21, starting transfers between devices, swap(): return lax.ppermute(values, axis, [(n, n ^ bits) for n in range(size)])  25.7 us
    pallas_call x1, Pallas kernels, mode_attention(): pl.pallas_call(mode_kernel, grid=(4,), in_specs=[spec] + [unused] * len(a...  9.42 us
    pallas_call x1, Pallas kernels, middle(): pl.pallas_call(middle_kernel, grid=(5,), in_specs=[fixed((ROWS, D)), fixe...  8.07 us
    pallas_call x1, Pallas kernels, agent_backward(): pl.pallas_call(agent_backward_all_kernel, grid=(4,), in_specs=agent_specs...  7.15 us
  transfers between devices with their start and end apart: 27, of which 17 were waited for; matrix products, arithmetic and copies ran while one was open for 1% of the time, Pallas kernels for 21%

profile of v7, /device:TPU:0, one launch (start us, length us, event | category | flops | bytes accessed | tf_op | source)
XLA Modules:
  0.0 263.8 jit_solution(3885961618784586823)
XLA Ops:
  0.6 1.2 reshape.64.tokens_ref
  1.9 5.5 %enter.1 = (bf16[16,384,128]{2,1,0:T(8,128)(2,1)}, bf16[256,1024]{1,0:T(8,128)(2,1)}, bf16[128,1024]{1,0:T(8,128)(2,1)}, bf16[128,1024]{1,0:T(8,128)(2,1)S(1)}) custom-call(s32[7]{0:T(128)S(1)} %stack.40.ids_ref, bf16[256,1024]{1,0:T(8,128)(2,1)S(1)} %reshape.64.tokens_ref, bf16[8,1024,1024]{2,1,0:T(8,128)(2,1)} %weights_ref.7), custom_call_target="tpu_custom_call" | custom-call | flops 1610612736 | bytes 8388608 | tf_op jit(solution)/shard_map/enter/pallas_call | solution.py:178
  7.4 7.3 %all-to-all-start = ((bf16[16,384,128]{2,1,0:T(8,128)(2,1)}), bf16[16,384,128]{2,1,0:T(8,128)(2,1)S(1)}, u32[]{:S(2)}, u32[]{:S(2)}) async-start(bf16[16,384,128]{2,1,0:T(8,128)(2,1)} %get-tuple-element.53), calls=%async_computation | async-start | bytes 3145728 | tf_op jit(solution)/shard_map/all_to_all | solution.py:844
  15.2 1.2 collective-permute-done
  16.3 3.4 %collective-permute-start.1 = (bf16[256,1024]{1,0:T(8,128)(2,1)S(1)}, bf16[256,1024]{1,0:T(8,128)(2,1)}, u32[]{:S(2)}, u32[]{:S(2)}) collective-permute-start(bf16[256,1024]{1,0:T(8,128)(2,1)S(1)} %constant_dynamic-update-slice_fusion), channel_id=1, source_target_pairs={{0,16},{8,24},{16,0},{24,8},{32,48},{40,56},{48,32},{56,40},{64,80... | collective-permute-start | bytes 1572872 | tf_op jit(solution)/shard_map/ppermute | solution.py:514
  19.8 18.5 %all-to-all-done.query_ref.keys_ref.values_ref.q.k.v = bf16[16,384,128]{2,1,0:T(8,128)(2,1)S(1)} async-done(((bf16[16,384,128]{2,1,0:T(8,128)(2,1)}), bf16[16,384,128]{2,1,0:T(8,128)(2,1)S(1)}, u32[]{:S(2)}, u32[]{:S(2)}) %all-to-all-start) | async-done | bytes 1572896 | tf_op jit(solution)/shard_map/all_to_all | solution.py:844
  38.3 4.8 %agent_forward.1 = (bf16[16,128,128]{2,1,0:T(8,128)(2,1)}, f32[4,4,256,128]{3,2,1,0:T(8,128)}) custom-call(bf16[16,384,128]{2,1,0:T(8,128)(2,1)S(1)} %all-to-all-done.query_ref.keys_ref.values_ref.q.k.v, bf16[16,384,128]{2,1,0:T(8,128)(2,1)S(1)} %all-to-all-done.query_ref.keys_ref.values_ref.q.k.v, ...), custom_call_target="tpu_custom_call" | custom-call | flops 3000000000 | bytes 4194304 | tf_op jit(solution)/shard_map/agent_forward/pallas_call | solution.py:228
  43.1 4.4 %all-to-all-start.1 = ((bf16[16,128,128]{2,1,0:T(8,128)(2,1)}), bf16[16,128,128]{2,1,0:T(8,128)(2,1)S(1)}, u32[]{:S(2)}, u32[]{:S(2)}) async-start(bf16[16,128,128]{2,1,0:T(8,128)(2,1)} %get-tuple-element.55), calls=%async_computation.1 | async-start | bytes 1048576 | tf_op jit(solution)/shard_map/all_to_all | solution.py:844
  47.6 2.1 pad_maximum_fusion.rest_0_.refs_0_
  49.8 10.1 %all-to-all-done.1 = bf16[16,128,128]{2,1,0:T(8,128)(2,1)S(1)} async-done(((bf16[16,128,128]{2,1,0:T(8,128)(2,1)}), bf16[16,128,128]{2,1,0:T(8,128)(2,1)S(1)}, u32[]{:S(2)}, u32[]{:S(2)}) %all-to-all-start.1) | async-done | bytes 524320 | tf_op jit(solution)/shard_map/all_to_all | solution.py:844
  59.8 8.1 %middle.1 = (bf16[8,4,256,128]{3,2,1,0:T(8,128)(2,1)}, bf16[256,1024]{1,0:T(8,128)(2,1)}, bf16[8,256,128]{2,1,0:T(8,128)(2,1)}, bf16[256,1024]{1,0:T(8,128)(2,1)}) custom-call(bf16[256,1024]{1,0:T(8,128)(2,1)S(1)} %copy-done.3, bf16[8,256,128]{2,1,0:T(8,128)(2,1)S(1)} %bitcast.25, bf16[256,1024]{1,0:T(8,128)(2,1)S(1)} %reshape.67.cotangent_ref, ...), custom_call_target="tpu_custom_call" | custom-call | flops 2684354560 | bytes 13631488 | tf_op jit(solution)/shard_map/middle/pallas_call | solution.py:339
  67.9 5.5 %all-to-all-start.2 = ((bf16[8,1024,128]{2,1,0:T(8,128)(2,1)}), bf16[8,1024,128]{2,1,0:T(8,128)(2,1)S(1)}, u32[]{:S(2)}, u32[]{:S(2)}) async-start(bf16[8,1024,128]{2,1,0:T(8,128)(2,1)} %bitcast.28), calls=%async_computation.2 | async-start | bytes 4194304 | tf_op jit(solution)/shard_map/all_to_all | solution.py:844
  74.3 24.4 %collective-permute-done.3.rest_1_.refs_3_ = bf16[2,256,1024]{2,1,0:T(8,128)(2,1)S(1)} collective-permute-done((bf16[2,256,1024]{2,1,0:T(8,128)(2,1)}, bf16[2,256,1024]{2,1,0:T(8,128)(2,1)S(1)}, u32[]{:S(2)}, u32[]{:S(2)}) %collective-permute-start.3) | collective-permute-done | bytes 1048608 | tf_op jit(solution)/shard_map/ppermute | solution.py:514
  99.8 9.4 %mode_attention.1 = bf16[8,4,256,128]{3,2,1,0:T(8,128)(2,1)} custom-call(bf16[8,4,256,128]{3,2,1,0:T(8,128)(2,1)S(1)} %bitcast.27, bf16[2,256,1024]{2,1,0:T(8,128)(2,1)} %collective-permute-done.2.rest_0_.refs_1_, bf16[2,256,1024]{2,1,0:T(8,128)(2,1)} %copy-done.13), custom_call_target="tpu_custom_call" | custom-call | flops 8000000000 | bytes 4194304 | tf_op jit(solution)/shard_map/mode_attention/pallas_call | solution.py:394
  109.2 5.4 %all-to-all-start.3 = ((bf16[8,1024,128]{2,1,0:T(8,128)(2,1)}), bf16[8,1024,128]{2,1,0:T(8,128)(2,1)S(1)}, u32[]{:S(2)}, u32[]{:S(2)}) async-start(bf16[8,1024,128]{2,1,0:T(8,128)(2,1)} %bitcast.29), calls=%async_computation.3 | async-start | bytes 4194304 | tf_op jit(solution)/shard_map/all_to_all | solution.py:844
  115.3 23.7 %collective-permute-done.4.rest_0_.refs_2_ = bf16[2,256,1024]{2,1,0:T(8,128)(2,1)} collective-permute-done((bf16[2,256,1024]{2,1,0:T(8,128)(2,1)}, bf16[2,256,1024]{2,1,0:T(8,128)(2,1)}, u32[]{:S(2)}, u32[]{:S(2)}) %collective-permute-start.4) | collective-permute-done | bytes 1048608 | tf_op jit(solution)/shard_map/ppermute | solution.py:514
  139.4 7.9 %early_first.1.rest_0_ = bf16[8,256,1024]{2,1,0:T(8,128)(2,1)} custom-call(s32[7]{0:T(128)S(1)} %constant_dynamic-update-slice_fusion.2.ids_ref, bf16[8,256,128]{2,1,0:T(8,128)(2,1)} %get-tuple-element.61.hidden_ref, bf16[8,4,256,128]{3,2,1,0:T(8,128)(2,1)S(1)} %bitcast.19, bf16[8,4,256,128]{3,2,1,0:T(8,128)(2,1)S(1)} %bitcast.20, ...), custom_call_target="tpu_custom_call" | custom-call | flops 1000000000 | bytes 5242880 | tf_op jit(solution)/shard_map/early_first/pallas_call | solution.py:522
  147.3 7.1 %turn.1 = (bf16[16,128,128]{2,1,0:T(8,128)(2,1)}, bf16[256,1024]{1,0:T(8,128)(2,1)}) custom-call(bf16[8,4,256,128]{3,2,1,0:T(8,128)(2,1)S(1)} %bitcast.21, bf16[256,1024]{1,0:T(8,128)(2,1)S(1)} %copy-done.2, bf16[256,1024]{1,0:T(8,128)(2,1)S(1)} %copy-done.9, bf16[8,1024,1024]{2,1,0:T(8,128)(2,1)} %weights_ref.7, bf16[8,256,1024]{2,1,0:T(8,128)(2,1)} %early_first.1.rest_0_), custom_call_target="tpu_custom_call" | custom-call | flops 2147483648 | bytes 12582912 | tf_op jit(solution)/shard_map/turn/pallas_call | solution.py:441
  154.4 4.8 %all-to-all-start.4 = ((bf16[16,128,128]{2,1,0:T(8,128)(2,1)}), bf16[16,128,128]{2,1,0:T(8,128)(2,1)S(1)}, u32[]{:S(2)}, u32[]{:S(2)}) async-start(bf16[16,128,128]{2,1,0:T(8,128)(2,1)} %get-tuple-element.62), calls=%async_computation.4 | async-start | bytes 1048576 | tf_op jit(solution)/shard_map/all_to_all | solution.py:844
  159.3 8.8 %early_add.1 = (bf16[8,128,512]{2,1,0:T(8,128)(2,1)}, bf16[8,128,512]{2,1,0:T(8,128)(2,1)}, bf16[8,128,512]{2,1,0:T(8,128)(2,1)}, bf16[8,128,512]{2,1,0:T(8,128)(2,1)}) custom-call(s32[7]{0:T(128)S(1)} %stack.40.ids_ref, bf16[8,256,128]{2,1,0:T(8,128)(2,1)} %get-tuple-element.61.hidden_ref, bf16[8,4,256,128]{3,2,1,0:T(8,128)(2,1)S(1)} %bitcast.22, ...), custom_call_target="tpu_custom_call" | custom-call | flops 1000000000 | bytes 5242880 | tf_op jit(solution)/shard_map/early_add/pallas_call | solution.py:522
  168.1 1.2 collective-permute-start.6
  169.3 2.1 collective-permute-start.7
  171.6 7.1 %agent_backward.1.refs_4_.refs_5_ = bf16[16,3,128,128]{3,2,1,0:T(8,128)(2,1)} custom-call(bf16[16,384,128]{2,1,0:T(8,128)(2,1)} %copy-done.6, bf16[16,384,128]{2,1,0:T(8,128)(2,1)} %copy-done.6, bf16[16,384,128]{2,1,0:T(8,128)(2,1)} %copy-done.6, bf16[16,128,128]{2,1,0:T(8,128)(2,1)S(1)} %all-to-all-done.4.g, f32[4,4,256,128]{3,2,1,0:T(8,128)} %get-tuple-element.63.table_ref), custom_call_target="tpu_custom_call" | custom-call | flops 6000000000 | bytes 6291456 | tf_op jit(solution)/shard_map/agent_backward/pallas_call | solution.py:283
  178.8 7.1 %all-to-all-start.5 = ((bf16[16,384,128]{2,1,0:T(8,128)(2,1)}), bf16[16,384,128]{2,1,0:T(8,128)(2,1)S(1)}, u32[]{:S(2)}, u32[]{:S(2)}) async-start(bf16[16,384,128]{2,1,0:T(8,128)(2,1)} %bitcast.16), calls=%async_computation.5 | async-start | bytes 3145728 | tf_op jit(solution)/shard_map/all_to_all | solution.py:844
  185.9 11.0 %late_products.1 = (bf16[2,256,1408]{2,1,0:T(8,128)(2,1)S(1)}, bf16[256,1408]{1,0:T(8,128)(2,1)S(1)}, bf16[256,1408]{1,0:T(8,128)(2,1)S(1)}) custom-call(s32[7]{0:T(128)S(1)} %stack.40.ids_ref, bf16[2,256,1024]{2,1,0:T(8,128)(2,1)} %pad_maximum_fusion.rest_0_.refs_0_, bf16[2,256,1024]{2,1,0:T(8,128)(2,1)} %collective-permute-done.2.rest_0_.refs_1_, ...), custom_call_target="tpu_custom_call" | custom-call | flops 1000000000 | bytes 5242880 | tf_op jit(solution)/shard_map/late_products/pallas_call | solution.py:522
  197.5 4.4 %early_half.1 = (bf16[8,64,1024]{2,1,0:T(8,128)(2,1)}, bf16[8,64,512]{2,1,0:T(8,128)(2,1)}, bf16[8,64,512]{2,1,0:T(8,128)(2,1)}) custom-call(s32[7]{0:T(128)S(1)} %stack.40.ids_ref, bf16[8,128,512]{2,1,0:T(8,128)(2,1)S(1)} %copy-done.7, bf16[8,128,512]{2,1,0:T(8,128)(2,1)} %collective-permute-done.6.left_in, bf16[8,128,512]{2,1,0:T(8,128)(2,1)S(1)} %copy-done.8, ...), custom_call_target="tpu_custom_call" | custom-call | flops 1000000000 | bytes 5242880 | tf_op jit(solution)/shard_map/early_half/pallas_call | solution.py:522
  202.0 1.2 collective-permute-start.8
  203.2 2.2 late_add.1
  206.2 3.2 %all-to-all-done.5 = bf16[16,384,128]{2,1,0:T(8,128)(2,1)S(1)} async-done(((bf16[16,384,128]{2,1,0:T(8,128)(2,1)}), bf16[16,384,128]{2,1,0:T(8,128)(2,1)S(1)}, u32[]{:S(2)}, u32[]{:S(2)}) %all-to-all-start.5) | async-done | bytes 1572896 | tf_op jit(solution)/shard_map/all_to_all | solution.py:844
  209.5 5.1 %leave.1.rest_0_ = bf16[256,1024]{1,0:T(8,128)(2,1)S(1)} custom-call(bf16[16,3,128,128]{3,2,1,0:T(8,128)(2,1)S(1)} %bitcast.24, bf16[256,1024]{1,0:T(8,128)(2,1)S(1)} %copy-done.3, bf16[256,1024]{1,0:T(8,128)(2,1)S(1)} %copy-done, bf16[8,1024,1024]{2,1,0:T(8,128)(2,1)} %weights_ref.7), custom_call_target="tpu_custom_call" | custom-call | flops 1610612736 | bytes 9437184 | tf_op jit(solution)/shard_map/leave/pallas_call | solution.py:490
  215.4 2.4 collective-permute-done.8.left_ref
  217.7 3.9 %early_z.1 = (bf16[8,32,1024]{2,1,0:T(8,128)(2,1)}, bf16[8,32,1024]{2,1,0:T(8,128)(2,1)S(1)}) custom-call(s32[7]{0:T(128)S(1)} %stack.40.ids_ref, bf16[8,64,1024]{2,1,0:T(8,128)(2,1)S(1)} %copy-done.10, bf16[8,64,512]{2,1,0:T(8,128)(2,1)} %collective-permute-done.8.left_ref, bf16[8,64,512]{2,1,0:T(8,128)(2,1)} %collective-permute-done.9.right_ref, ...), custom_call_target="tpu_custom_call" | custom-call | flops 1000000000 | bytes 5242880 | tf_op jit(solution)/shard_map/early_z/pallas_call | solution.py:522
  222.5 1.4 collective-permute-done.13.refs_1_
  223.9 1.9 late_y.1
  225.8 2.9 %collective-permute-start.14 = (bf16[2,32,1408]{2,1,0:T(8,128)(2,1)S(1)}, bf16[2,32,1408]{2,1,0:T(8,128)(2,1)S(1)}, u32[]{:S(2)}, u32[]{:S(2)}) collective-permute-start(bf16[2,32,1408]{2,1,0:T(8,128)(2,1)S(1)} %get-tuple-element.80), channel_id=1, source_target_pairs={{0,2},{1,3},{2,0},{3,1},{4,6},{5,7},{6,4},{7,5},{8,10},{9,11},{10,... | collective-permute-start | bytes 540680 | tf_op jit(solution)/shard_map/ppermute | solution.py:514
  228.7 1.6 collective-permute-start.15
  230.3 1.2 collective-permute-start.16
  231.5 2.2 collective-permute-done.14.rest_1_
  233.7 3.4 %collective-permute-done.15.rest_2_ = bf16[2,32,1408]{2,1,0:T(8,128)(2,1)S(1)} collective-permute-done((bf16[2,32,1408]{2,1,0:T(8,128)(2,1)S(1)}, bf16[2,32,1408]{2,1,0:T(8,128)(2,1)S(1)}, u32[]{:S(2)}, u32[]{:S(2)}) %collective-permute-start.15) | collective-permute-done | bytes 180256 | tf_op jit(solution)/shard_map/ppermute | solution.py:514
  237.0 1.9 collective-permute-done.16.rest_3_
  239.8 1.4 collective-permute-start.17
  241.2 2.7 %collective-permute-start.18 = (bf16[2,32,2176]{2,1,0:T(8,128)(2,1)S(1)}, bf16[2,32,2176]{2,1,0:T(8,128)(2,1)S(1)}, u32[]{:S(2)}, u32[]{:S(2)}) collective-permute-start(bf16[2,32,2176]{2,1,0:T(8,128)(2,1)S(1)} %get-tuple-element.85), channel_id=1, source_target_pairs={{0,64},{8,72},{16,80},{24,88},{32,96},{40,104},{48,112},{56,120},{... | collective-permute-start | bytes 835592 | tf_op jit(solution)/shard_map/ppermute | solution.py:514
  244.6 3.2 %collective-permute-done.17.refs_1_ = bf16[2,32,2176]{2,1,0:T(8,128)(2,1)S(1)} collective-permute-done((bf16[2,32,2176]{2,1,0:T(8,128)(2,1)S(1)}, bf16[2,32,2176]{2,1,0:T(8,128)(2,1)S(1)}, u32[]{:S(2)}, u32[]{:S(2)}) %collective-permute-start.17) | collective-permute-done | bytes 278560 | tf_op jit(solution)/shard_map/ppermute | solution.py:514
  247.7 4.7 %collective-permute-done.18.refs_2_ = bf16[2,32,2176]{2,1,0:T(8,128)(2,1)S(1)} collective-permute-done((bf16[2,32,2176]{2,1,0:T(8,128)(2,1)S(1)}, bf16[2,32,2176]{2,1,0:T(8,128)(2,1)S(1)}, u32[]{:S(2)}, u32[]{:S(2)}) %collective-permute-start.18) | collective-permute-done | bytes 278560 | tf_op jit(solution)/shard_map/ppermute | solution.py:514
  252.4 2.5 collective-permute-done.19.refs_3_
  255.7 3.0 %collective-permute-start.20 = (bf16[4,32,640]{2,1,0:T(8,128)(2,1)S(1)}, bf16[4,32,640]{2,1,0:T(8,128)(2,1)S(1)}, u32[]{:S(2)}, u32[]{:S(2)}) collective-permute-start(bf16[4,32,640]{2,1,0:T(8,128)(2,1)S(1)} %get-tuple-element.88), channel_id=1, source_target_pairs={{0,16},{8,24},{16,0},{24,8},{32,48},{40,56},{48,32},{56,40},{64,80... | collective-permute-start | bytes 491528 | tf_op jit(solution)/shard_map/ppermute | solution.py:514
  259.7 2.9 %collective-permute-done.20.arrived_ref = bf16[4,32,640]{2,1,0:T(8,128)(2,1)S(1)} collective-permute-done((bf16[4,32,640]{2,1,0:T(8,128)(2,1)S(1)}, bf16[4,32,640]{2,1,0:T(8,128)(2,1)S(1)}, u32[]{:S(2)}, u32[]{:S(2)}) %collective-permute-start.20) | collective-permute-done | bytes 163872 | tf_op jit(solution)/shard_map/ppermute | solution.py:514
  262.6 1.3 last.1
  (67 shorter events, 10.5 us)
Async XLA Ops:
  7.4 7.7 %copy-start.15 = (bf16[128,1024]{1,0:T(8,128)(2,1)S(1)}, bf16[128,1024]{1,0:T(8,128)(2,1)}, u32[]{:S(2)}) copy-start(bf16[128,1024]{1,0:T(8,128)(2,1)} %get-tuple-element.56) | copy-start | bytes 786436
  7.4 7.7 %copy-start.16 = (s32[128]{0:T(128)S(1)}, s32[128]{0:T(128)}, u32[]{:S(2)}) copy-start(s32[128]{0:T(128)} %param.9) | copy-start | bytes 1540
  7.4 30.9 %all-to-all-start = ((bf16[16,384,128]{2,1,0:T(8,128)(2,1)}), bf16[16,384,128]{2,1,0:T(8,128)(2,1)S(1)}, u32[]{:S(2)}, u32[]{:S(2)}) async-start(bf16[16,384,128]{2,1,0:T(8,128)(2,1)} %get-tuple-element.53), calls=%async_computation | async-start | bytes 3145728 | tf_op jit(solution)/shard_map/all_to_all | solution.py:844
  14.7 1.6 collective-permute-start
  16.3 31.1 %copy-start.14 = (bf16[8,8,4,1024]{3,2,1,0:T(4,128)(2,1)S(1)}, bf16[8,8,4,1024]{3,2,1,0:T(4,128)(2,1)}, u32[]{:S(2)}) copy-start(bf16[8,8,4,1024]{3,2,1,0:T(4,128)(2,1)} %param.7) | copy-start | bytes 1572868
  16.3 31.3 %collective-permute-start.1 = (bf16[256,1024]{1,0:T(8,128)(2,1)S(1)}, bf16[256,1024]{1,0:T(8,128)(2,1)}, u32[]{:S(2)}, u32[]{:S(2)}) collective-permute-start(bf16[256,1024]{1,0:T(8,128)(2,1)S(1)} %constant_dynamic-update-slice_fusion), channel_id=1, source_target_pairs={{0,16},{8,24},{16,0},{24,8},{32,48},{40,56},{48,32},{56,40},{64,80... | collective-permute-start | bytes 1572872 | tf_op jit(solution)/shard_map/ppermute | solution.py:514
  38.3 4.8 %copy-start.6 = (bf16[16,384,128]{2,1,0:T(8,128)(2,1)}, bf16[16,384,128]{2,1,0:T(8,128)(2,1)S(1)}, u32[]{:S(2)}) copy-start(bf16[16,384,128]{2,1,0:T(8,128)(2,1)S(1)} %all-to-all-done.query_ref.keys_ref.values_ref.q.k.v) | copy-start | bytes 4718596
  43.1 16.7 %copy-start.3 = (bf16[256,1024]{1,0:T(8,128)(2,1)S(1)}, bf16[256,1024]{1,0:T(8,128)(2,1)}, u32[]{:S(2)}) copy-start(bf16[256,1024]{1,0:T(8,128)(2,1)} %get-tuple-element.54.tokens_ref) | copy-start | bytes 1572868
  43.1 16.7 %all-to-all-start.1 = ((bf16[16,128,128]{2,1,0:T(8,128)(2,1)}), bf16[16,128,128]{2,1,0:T(8,128)(2,1)S(1)}, u32[]{:S(2)}, u32[]{:S(2)}) async-start(bf16[16,128,128]{2,1,0:T(8,128)(2,1)} %get-tuple-element.55), calls=%async_computation.1 | async-start | bytes 1048576 | tf_op jit(solution)/shard_map/all_to_all | solution.py:844
  59.8 8.1 %copy-start.1 = (bf16[16,128,128]{2,1,0:T(8,128)(2,1)}, bf16[16,128,128]{2,1,0:T(8,128)(2,1)S(1)}, u32[]{:S(2)}) copy-start(bf16[16,128,128]{2,1,0:T(8,128)(2,1)S(1)} %all-to-all-done.1) | copy-start | bytes 1572868
  67.9 31.9 %all-to-all-start.2 = ((bf16[8,1024,128]{2,1,0:T(8,128)(2,1)}), bf16[8,1024,128]{2,1,0:T(8,128)(2,1)S(1)}, u32[]{:S(2)}, u32[]{:S(2)}) async-start(bf16[8,1024,128]{2,1,0:T(8,128)(2,1)} %bitcast.28), calls=%async_computation.2 | async-start | bytes 4194304 | tf_op jit(solution)/shard_map/all_to_all | solution.py:844
  73.4 25.4 %collective-permute-start.3 = (bf16[2,256,1024]{2,1,0:T(8,128)(2,1)}, bf16[2,256,1024]{2,1,0:T(8,128)(2,1)S(1)}, u32[]{:S(2)}, u32[]{:S(2)}) collective-permute-start(bf16[2,256,1024]{2,1,0:T(8,128)(2,1)} %pad_maximum_fusion.rest_0_.refs_0_), channel_id=1, source_target_pairs={{0,96},{8,104},{16,112},{24,120},{32,64},{40,72},{48,80},{56,88},{... | collective-permute-start | bytes 3145736 | tf_op jit(solution)/shard_map/ppermute | solution.py:514
  74.2 25.6 %collective-permute-start.2 = (bf16[2,256,1024]{2,1,0:T(8,128)(2,1)}, bf16[2,256,1024]{2,1,0:T(8,128)(2,1)}, u32[]{:S(2)}, u32[]{:S(2)}) collective-permute-start(bf16[2,256,1024]{2,1,0:T(8,128)(2,1)} %pad_maximum_fusion.rest_0_.refs_0_), channel_id=1, source_target_pairs={{0,32},{8,40},{16,48},{24,56},{32,0},{40,8},{48,16},{56,24},{64,96... | collective-permute-start | bytes 3145736 | tf_op jit(solution)/shard_map/ppermute | solution.py:514
  98.8 1.0 copy-start.13
  109.2 30.2 %all-to-all-start.3 = ((bf16[8,1024,128]{2,1,0:T(8,128)(2,1)}), bf16[8,1024,128]{2,1,0:T(8,128)(2,1)S(1)}, u32[]{:S(2)}, u32[]{:S(2)}) async-start(bf16[8,1024,128]{2,1,0:T(8,128)(2,1)} %bitcast.29), calls=%async_computation.3 | async-start | bytes 4194304 | tf_op jit(solution)/shard_map/all_to_all | solution.py:844
  114.6 24.3 %collective-permute-start.4 = (bf16[2,256,1024]{2,1,0:T(8,128)(2,1)}, bf16[2,256,1024]{2,1,0:T(8,128)(2,1)}, u32[]{:S(2)}, u32[]{:S(2)}) collective-permute-start(bf16[2,256,1024]{2,1,0:T(8,128)(2,1)} %pad_maximum_fusion.rest_0_.refs_0_), channel_id=1, source_target_pairs={{0,64},{8,72},{16,80},{24,88},{32,96},{40,104},{48,112},{56,120},{... | collective-permute-start | bytes 3145736 | tf_op jit(solution)/shard_map/ppermute | solution.py:514
  139.4 7.9 %copy-start.2 = (bf16[256,1024]{1,0:T(8,128)(2,1)S(1)}, bf16[256,1024]{1,0:T(8,128)(2,1)}, u32[]{:S(2)}) copy-start(bf16[256,1024]{1,0:T(8,128)(2,1)} %get-tuple-element.59.last_ref.cotangent_ref) | copy-start | bytes 1572868
  139.4 7.9 %copy-start.9 = (bf16[256,1024]{1,0:T(8,128)(2,1)S(1)}, bf16[256,1024]{1,0:T(8,128)(2,1)}, u32[]{:S(2)}) copy-start(bf16[256,1024]{1,0:T(8,128)(2,1)} %get-tuple-element.60.after_ref) | copy-start | bytes 1572868
  147.3 11.9 %collective-permute-start.5 = (bf16[8,256,1024]{2,1,0:T(8,128)(2,1)}, bf16[8,256,1024]{2,1,0:T(8,128)(2,1)}, u32[]{:S(2)}, u32[]{:S(2)}) collective-permute-start(bf16[8,256,1024]{2,1,0:T(8,128)(2,1)} %early_first.1.rest_0_), channel_id=1, source_target_pairs={{0,8},{8,0},{16,24},{24,16},{32,40},{40,32},{48,56},{56,48},{64,72... | collective-permute-start | bytes 12582920 | tf_op jit(solution)/shard_map/ppermute | solution.py:514
  154.4 17.2 %all-to-all-start.4 = ((bf16[16,128,128]{2,1,0:T(8,128)(2,1)}), bf16[16,128,128]{2,1,0:T(8,128)(2,1)S(1)}, u32[]{:S(2)}, u32[]{:S(2)}) async-start(bf16[16,128,128]{2,1,0:T(8,128)(2,1)} %get-tuple-element.62), calls=%async_computation.4 | async-start | bytes 1048576 | tf_op jit(solution)/shard_map/all_to_all | solution.py:844
  168.1 29.4 %collective-permute-start.6 = (bf16[8,128,512]{2,1,0:T(8,128)(2,1)}, bf16[8,128,512]{2,1,0:T(8,128)(2,1)}, u32[]{:S(2)}, u32[]{:S(2)}) collective-permute-start(bf16[8,128,512]{2,1,0:T(8,128)(2,1)} %get-tuple-element.66), channel_id=1, source_target_pairs={{0,2},{1,3},{2,0},{3,1},{4,6},{5,7},{6,4},{7,5},{8,10},{9,11},{10,... | collective-permute-start | bytes 3145736 | tf_op jit(solution)/shard_map/ppermute | solution.py:514
  169.3 28.2 %collective-permute-start.7 = (bf16[8,128,512]{2,1,0:T(8,128)(2,1)}, bf16[8,128,512]{2,1,0:T(8,128)(2,1)}, u32[]{:S(2)}, u32[]{:S(2)}) collective-permute-start(bf16[8,128,512]{2,1,0:T(8,128)(2,1)} %get-tuple-element.68), channel_id=1, source_target_pairs={{0,6},{1,7},{2,4},{3,5},{4,2},{5,3},{6,0},{7,1},{8,14},{9,15},{10,... | collective-permute-start | bytes 3145736 | tf_op jit(solution)/shard_map/ppermute | solution.py:514
  178.8 7.1 %copy-start = (bf16[256,1024]{1,0:T(8,128)(2,1)S(1)}, bf16[256,1024]{1,0:T(8,128)(2,1)}, u32[]{:S(2)}) copy-start(bf16[256,1024]{1,0:T(8,128)(2,1)} %get-tuple-element.64.grad_after_ref.rest_1_.refs_7_) | copy-start | bytes 1572868
  178.8 30.7 %all-to-all-start.5 = ((bf16[16,384,128]{2,1,0:T(8,128)(2,1)}), bf16[16,384,128]{2,1,0:T(8,128)(2,1)S(1)}, u32[]{:S(2)}, u32[]{:S(2)}) async-start(bf16[16,384,128]{2,1,0:T(8,128)(2,1)} %bitcast.16), calls=%async_computation.5 | async-start | bytes 3145728 | tf_op jit(solution)/shard_map/all_to_all | solution.py:844
  185.9 11.6 %copy-start.7 = (bf16[8,128,512]{2,1,0:T(8,128)(2,1)S(1)}, bf16[8,128,512]{2,1,0:T(8,128)(2,1)}, u32[]{:S(2)}) copy-start(bf16[8,128,512]{2,1,0:T(8,128)(2,1)} %get-tuple-element.65.left_ref) | copy-start | bytes 3145732
  185.9 11.6 %copy-start.8 = (bf16[8,128,512]{2,1,0:T(8,128)(2,1)S(1)}, bf16[8,128,512]{2,1,0:T(8,128)(2,1)}, u32[]{:S(2)}) copy-start(bf16[8,128,512]{2,1,0:T(8,128)(2,1)} %get-tuple-element.67.right_ref) | copy-start | bytes 3145732
  196.9 6.2 %collective-permute-start.11 = (bf16[256,1408]{1,0:T(8,128)(2,1)S(1)}, bf16[256,1408]{1,0:T(8,128)(2,1)S(1)}, u32[]{:S(2)}, u32[]{:S(2)}) collective-permute-start(bf16[256,1408]{1,0:T(8,128)(2,1)S(1)} %get-tuple-element.75), channel_id=1, source_target_pairs={{0,8},{8,0},{16,24},{24,16},{32,40},{40,32},{48,56},{56,48},{64,72... | collective-permute-start | bytes 2162696 | tf_op jit(solution)/shard_map/ppermute | solution.py:514
  197.4 5.8 %collective-permute-start.12 = (bf16[256,1408]{1,0:T(8,128)(2,1)S(1)}, bf16[256,1408]{1,0:T(8,128)(2,1)S(1)}, u32[]{:S(2)}, u32[]{:S(2)}) collective-permute-start(bf16[256,1408]{1,0:T(8,128)(2,1)S(1)} %get-tuple-element.76), channel_id=1, source_target_pairs={{0,8},{8,0},{16,24},{24,16},{32,40},{40,32},{48,56},{56,48},{64,72... | collective-permute-start | bytes 2162696 | tf_op jit(solution)/shard_map/ppermute | solution.py:514
  202.0 15.8 %collective-permute-start.8 = (bf16[8,64,512]{2,1,0:T(8,128)(2,1)}, bf16[8,64,512]{2,1,0:T(8,128)(2,1)}, u32[]{:S(2)}, u32[]{:S(2)}) collective-permute-start(bf16[8,64,512]{2,1,0:T(8,128)(2,1)} %get-tuple-element.70), channel_id=1, source_target_pairs={{0,6},{1,7},{2,4},{3,5},{4,2},{5,3},{6,0},{7,1},{8,14},{9,15},{10,... | collective-permute-start | bytes 1572872 | tf_op jit(solution)/shard_map/ppermute | solution.py:514
  203.1 14.6 %collective-permute-start.9 = (bf16[8,64,512]{2,1,0:T(8,128)(2,1)}, bf16[8,64,512]{2,1,0:T(8,128)(2,1)}, u32[]{:S(2)}, u32[]{:S(2)}) collective-permute-start(bf16[8,64,512]{2,1,0:T(8,128)(2,1)} %get-tuple-element.71), channel_id=1, source_target_pairs={{0,2},{1,3},{2,0},{3,1},{4,6},{5,7},{6,4},{7,5},{8,10},{9,11},{10,... | collective-permute-start | bytes 1572872 | tf_op jit(solution)/shard_map/ppermute | solution.py:514
  205.4 18.5 %collective-permute-start.13 = (bf16[2,128,1408]{2,1,0:T(8,128)(2,1)}, bf16[2,128,1408]{2,1,0:T(8,128)(2,1)}, u32[]{:S(2)}, u32[]{:S(2)}) collective-permute-start(bf16[2,128,1408]{2,1,0:T(8,128)(2,1)} %get-tuple-element.78), channel_id=1, source_target_pairs={{0,1},{1,0},{2,3},{3,2},{4,5},{5,4},{6,7},{7,6},{8,9},{9,8},{10,11... | collective-permute-start | bytes 2162696 | tf_op jit(solution)/shard_map/ppermute | solution.py:514
  209.5 8.3 %copy-start.10 = (bf16[8,64,1024]{2,1,0:T(8,128)(2,1)S(1)}, bf16[8,64,1024]{2,1,0:T(8,128)(2,1)}, u32[]{:S(2)}) copy-start(bf16[8,64,1024]{2,1,0:T(8,128)(2,1)} %get-tuple-element.69.own_ref) | copy-start | bytes 3145732
  214.6 0.8 copy-start.4
  215.4 8.5 %copy-start.11 = (bf16[2,128,1408]{2,1,0:T(8,128)(2,1)S(1)}, bf16[2,128,1408]{2,1,0:T(8,128)(2,1)}, u32[]{:S(2)}) copy-start(bf16[2,128,1408]{2,1,0:T(8,128)(2,1)} %get-tuple-element.77.refs_0_) | copy-start | bytes 2162692
  221.6 17.3 %copy-start.12 = (bf16[8,32,1024]{2,1,0:T(8,128)(2,1)S(1)}, bf16[8,32,1024]{2,1,0:T(8,128)(2,1)}, u32[]{:S(2)}) copy-start(bf16[8,32,1024]{2,1,0:T(8,128)(2,1)} %get-tuple-element.72.early_ref) | copy-start | bytes 1572868
  221.6 17.3 %collective-permute-start.10 = (bf16[8,32,1024]{2,1,0:T(8,128)(2,1)S(1)}, bf16[8,32,1024]{2,1,0:T(8,128)(2,1)S(1)}, u32[]{:S(2)}, u32[]{:S(2)}) collective-permute-start(bf16[8,32,1024]{2,1,0:T(8,128)(2,1)S(1)} %get-tuple-element.73), channel_id=1, source_target_pairs={{0,1},{1,0},{2,3},{3,2},{4,5},{5,4},{6,7},{7,6},{8,9},{9,8},{10,11... | collective-permute-start | bytes 1572872 | tf_op jit(solution)/shard_map/ppermute | solution.py:514
  225.8 7.9 %collective-permute-start.14 = (bf16[2,32,1408]{2,1,0:T(8,128)(2,1)S(1)}, bf16[2,32,1408]{2,1,0:T(8,128)(2,1)S(1)}, u32[]{:S(2)}, u32[]{:S(2)}) collective-permute-start(bf16[2,32,1408]{2,1,0:T(8,128)(2,1)S(1)} %get-tuple-element.80), channel_id=1, source_target_pairs={{0,2},{1,3},{2,0},{3,1},{4,6},{5,7},{6,4},{7,5},{8,10},{9,11},{10,... | collective-permute-start | bytes 540680 | tf_op jit(solution)/shard_map/ppermute | solution.py:514
  228.7 8.3 %collective-permute-start.15 = (bf16[2,32,1408]{2,1,0:T(8,128)(2,1)S(1)}, bf16[2,32,1408]{2,1,0:T(8,128)(2,1)S(1)}, u32[]{:S(2)}, u32[]{:S(2)}) collective-permute-start(bf16[2,32,1408]{2,1,0:T(8,128)(2,1)S(1)} %get-tuple-element.81), channel_id=1, source_target_pairs={{0,4},{1,5},{2,6},{3,7},{4,0},{5,1},{6,2},{7,3},{8,12},{9,13},{10,... | collective-permute-start | bytes 540680 | tf_op jit(solution)/shard_map/ppermute | solution.py:514
  230.3 8.6 %collective-permute-start.16 = (bf16[2,32,1408]{2,1,0:T(8,128)(2,1)S(1)}, bf16[2,32,1408]{2,1,0:T(8,128)(2,1)S(1)}, u32[]{:S(2)}, u32[]{:S(2)}) collective-permute-start(bf16[2,32,1408]{2,1,0:T(8,128)(2,1)S(1)} %get-tuple-element.82), channel_id=1, source_target_pairs={{0,6},{1,7},{2,4},{3,5},{4,2},{5,3},{6,0},{7,1},{8,14},{9,15},{10,... | collective-permute-start | bytes 540680 | tf_op jit(solution)/shard_map/ppermute | solution.py:514
  239.8 18.9 %copy-start.5 = (bf16[256,1024]{1,0:T(8,128)(2,1)S(1)}, bf16[256,1024]{1,0:T(8,128)(2,1)}, u32[]{:S(2)}) copy-start(bf16[256,1024]{1,0:T(8,128)(2,1)} %copy-done.4) | copy-start | bytes 1572868
  239.8 7.9 %collective-permute-start.17 = (bf16[2,32,2176]{2,1,0:T(8,128)(2,1)S(1)}, bf16[2,32,2176]{2,1,0:T(8,128)(2,1)S(1)}, u32[]{:S(2)}, u32[]{:S(2)}) collective-permute-start(bf16[2,32,2176]{2,1,0:T(8,128)(2,1)S(1)} %get-tuple-element.84), channel_id=1, source_target_pairs={{0,32},{8,40},{16,48},{24,56},{32,0},{40,8},{48,16},{56,24},{64,96... | collective-permute-start | bytes 835592 | tf_op jit(solution)/shard_map/ppermute | solution.py:514
  241.2 11.3 %collective-permute-start.18 = (bf16[2,32,2176]{2,1,0:T(8,128)(2,1)S(1)}, bf16[2,32,2176]{2,1,0:T(8,128)(2,1)S(1)}, u32[]{:S(2)}, u32[]{:S(2)}) collective-permute-start(bf16[2,32,2176]{2,1,0:T(8,128)(2,1)S(1)} %get-tuple-element.85), channel_id=1, source_target_pairs={{0,64},{8,72},{16,80},{24,88},{32,96},{40,104},{48,112},{56,120},{... | collective-permute-start | bytes 835592 | tf_op jit(solution)/shard_map/ppermute | solution.py:514
  243.8 11.1 %collective-permute-start.19 = (bf16[2,32,2176]{2,1,0:T(8,128)(2,1)S(1)}, bf16[2,32,2176]{2,1,0:T(8,128)(2,1)S(1)}, u32[]{:S(2)}, u32[]{:S(2)}) collective-permute-start(bf16[2,32,2176]{2,1,0:T(8,128)(2,1)S(1)} %get-tuple-element.86), channel_id=1, source_target_pairs={{0,96},{8,104},{16,112},{24,120},{32,64},{40,72},{48,80},{56,88},{... | collective-permute-start | bytes 835592 | tf_op jit(solution)/shard_map/ppermute | solution.py:514
  255.7 6.9 %collective-permute-start.20 = (bf16[4,32,640]{2,1,0:T(8,128)(2,1)S(1)}, bf16[4,32,640]{2,1,0:T(8,128)(2,1)S(1)}, u32[]{:S(2)}, u32[]{:S(2)}) collective-permute-start(bf16[4,32,640]{2,1,0:T(8,128)(2,1)S(1)} %get-tuple-element.88), channel_id=1, source_target_pairs={{0,16},{8,24},{16,0},{24,8},{32,48},{40,56},{48,32},{56,40},{64,80... | collective-permute-start | bytes 491528 | tf_op jit(solution)/shard_map/ppermute | solution.py:514

commit v8 on v7

--- a/solution.py
+++ b/solution.py
@@ -122,7 +122,7 @@
 def probabilities(query_stack, keys, offset):
     scores = dot_nt(query_stack, keys) * SCALE + offset
     raised = jnp.exp(scores - jnp.max(scores, -1, keepdims=True))
-    return raised / jnp.sum(raised, -1, keepdims=True)
+    return raised * (1.0 / jnp.sum(raised, -1, keepdims=True))
 
 
 def attend(table, values):

time: 265 us -> 265 us (level)
  no operation moved by 1% of the time
where the time goes in v8:
time: 265 us; the launch traced here: 264 us
  waiting for transfers between devices  106 us (40%)
  Pallas kernels  90.1 us (34%)
  starting transfers between devices  60.1 us (23%)
  local copies, waits for them, and re-layouts  4.28 us (2%)
    ppermute x21, waiting for transfers between devices, swap(): return lax.ppermute(values, axis, [(n, n ^ bits) for n in range(size)])  73.7 us
    pallas_call x10, Pallas kernels, prefetched(): pl.pallas_call(kernel, grid_spec=pltpu.PrefetchScalarGridSpec(num_scalar_...  43 us
    all_to_all x6, starting transfers between devices, exchange(): return lax.all_to_all(values, axis, split_axis=0, concat_axis=0, tiled=True)  34.4 us
    all_to_all x6, waiting for transfers between devices, exchange(): return lax.all_to_all(values, axis, split_axis=0, concat_axis=0, tiled=True)  32.6 us
    ppermute x21, starting transfers between devices, swap(): return lax.ppermute(values, axis, [(n, n ^ bits) for n in range(size)])  25.7 us
    pallas_call x1, Pallas kernels, mode_attention(): pl.pallas_call(mode_kernel, grid=(4,), in_specs=[spec] + [unused] * len(a...  9.42 us
    pallas_call x1, Pallas kernels, middle(): pl.pallas_call(middle_kernel, grid=(5,), in_specs=[fixed((ROWS, D)), fixe...  8.07 us
    pallas_call x1, Pallas kernels, agent_backward(): pl.pallas_call(agent_backward_all_kernel, grid=(4,), in_specs=agent_specs...  7.15 us
  transfers between devices with their start and end apart: 27, of which 17 were waited for; matrix products, arithmetic and copies ran while one was open for 1% of the time, Pallas kernels for 21%

profile of v8, /device:TPU:0, one launch (start us, length us, event | category | flops | bytes accessed | tf_op | source)
XLA Modules:
  0.0 263.8 jit_solution(3885961618784586823)
XLA Ops:
  0.6 1.2 reshape.64.tokens_ref
  1.9 5.5 %enter.1 = (bf16[16,384,128]{2,1,0:T(8,128)(2,1)}, bf16[256,1024]{1,0:T(8,128)(2,1)}, bf16[128,1024]{1,0:T(8,128)(2,1)}, bf16[128,1024]{1,0:T(8,128)(2,1)S(1)}) custom-call(s32[7]{0:T(128)S(1)} %stack.40.ids_ref, bf16[256,1024]{1,0:T(8,128)(2,1)S(1)} %reshape.64.tokens_ref, bf16[8,1024,1024]{2,1,0:T(8,128)(2,1)} %weights_ref.7), custom_call_target="tpu_custom_call" | custom-call | flops 1610612736 | bytes 8388608 | tf_op jit(solution)/shard_map/enter/pallas_call | solution.py:178
  7.4 7.3 %all-to-all-start = ((bf16[16,384,128]{2,1,0:T(8,128)(2,1)}), bf16[16,384,128]{2,1,0:T(8,128)(2,1)S(1)}, u32[]{:S(2)}, u32[]{:S(2)}) async-start(bf16[16,384,128]{2,1,0:T(8,128)(2,1)} %get-tuple-element.53), calls=%async_computation | async-start | bytes 3145728 | tf_op jit(solution)/shard_map/all_to_all | solution.py:844
  15.2 1.2 collective-permute-done
  16.3 3.4 %collective-permute-start.1 = (bf16[256,1024]{1,0:T(8,128)(2,1)S(1)}, bf16[256,1024]{1,0:T(8,128)(2,1)}, u32[]{:S(2)}, u32[]{:S(2)}) collective-permute-start(bf16[256,1024]{1,0:T(8,128)(2,1)S(1)} %constant_dynamic-update-slice_fusion), channel_id=1, source_target_pairs={{0,16},{8,24},{16,0},{24,8},{32,48},{40,56},{48,32},{56,40},{64,80... | collective-permute-start | bytes 1572872 | tf_op jit(solution)/shard_map/ppermute | solution.py:514
  19.8 18.5 %all-to-all-done.query_ref.keys_ref.values_ref.q.k.v = bf16[16,384,128]{2,1,0:T(8,128)(2,1)S(1)} async-done(((bf16[16,384,128]{2,1,0:T(8,128)(2,1)}), bf16[16,384,128]{2,1,0:T(8,128)(2,1)S(1)}, u32[]{:S(2)}, u32[]{:S(2)}) %all-to-all-start) | async-done | bytes 1572896 | tf_op jit(solution)/shard_map/all_to_all | solution.py:844
  38.3 4.8 %agent_forward.1 = (bf16[16,128,128]{2,1,0:T(8,128)(2,1)}, f32[4,4,256,128]{3,2,1,0:T(8,128)}) custom-call(bf16[16,384,128]{2,1,0:T(8,128)(2,1)S(1)} %all-to-all-done.query_ref.keys_ref.values_ref.q.k.v, bf16[16,384,128]{2,1,0:T(8,128)(2,1)S(1)} %all-to-all-done.query_ref.keys_ref.values_ref.q.k.v, ...), custom_call_target="tpu_custom_call" | custom-call | flops 3000000000 | bytes 4194304 | tf_op jit(solution)/shard_map/agent_forward/pallas_call | solution.py:228
  43.1 4.4 %all-to-all-start.1 = ((bf16[16,128,128]{2,1,0:T(8,128)(2,1)}), bf16[16,128,128]{2,1,0:T(8,128)(2,1)S(1)}, u32[]{:S(2)}, u32[]{:S(2)}) async-start(bf16[16,128,128]{2,1,0:T(8,128)(2,1)} %get-tuple-element.55), calls=%async_computation.1 | async-start | bytes 1048576 | tf_op jit(solution)/shard_map/all_to_all | solution.py:844
  47.6 2.1 pad_maximum_fusion.rest_0_.refs_0_
  49.8 10.1 %all-to-all-done.1 = bf16[16,128,128]{2,1,0:T(8,128)(2,1)S(1)} async-done(((bf16[16,128,128]{2,1,0:T(8,128)(2,1)}), bf16[16,128,128]{2,1,0:T(8,128)(2,1)S(1)}, u32[]{:S(2)}, u32[]{:S(2)}) %all-to-all-start.1) | async-done | bytes 524320 | tf_op jit(solution)/shard_map/all_to_all | solution.py:844
  59.8 8.1 %middle.1 = (bf16[8,4,256,128]{3,2,1,0:T(8,128)(2,1)}, bf16[256,1024]{1,0:T(8,128)(2,1)}, bf16[8,256,128]{2,1,0:T(8,128)(2,1)}, bf16[256,1024]{1,0:T(8,128)(2,1)}) custom-call(bf16[256,1024]{1,0:T(8,128)(2,1)S(1)} %copy-done.3, bf16[8,256,128]{2,1,0:T(8,128)(2,1)S(1)} %bitcast.25, bf16[256,1024]{1,0:T(8,128)(2,1)S(1)} %reshape.67.cotangent_ref, ...), custom_call_target="tpu_custom_call" | custom-call | flops 2684354560 | bytes 13631488 | tf_op jit(solution)/shard_map/middle/pallas_call | solution.py:339
  67.9 5.5 %all-to-all-start.2 = ((bf16[8,1024,128]{2,1,0:T(8,128)(2,1)}), bf16[8,1024,128]{2,1,0:T(8,128)(2,1)S(1)}, u32[]{:S(2)}, u32[]{:S(2)}) async-start(bf16[8,1024,128]{2,1,0:T(8,128)(2,1)} %bitcast.28), calls=%async_computation.2 | async-start | bytes 4194304 | tf_op jit(solution)/shard_map/all_to_all | solution.py:844
  74.3 24.4 %collective-permute-done.3.rest_1_.refs_3_ = bf16[2,256,1024]{2,1,0:T(8,128)(2,1)S(1)} collective-permute-done((bf16[2,256,1024]{2,1,0:T(8,128)(2,1)}, bf16[2,256,1024]{2,1,0:T(8,128)(2,1)S(1)}, u32[]{:S(2)}, u32[]{:S(2)}) %collective-permute-start.3) | collective-permute-done | bytes 1048608 | tf_op jit(solution)/shard_map/ppermute | solution.py:514
  99.8 9.4 %mode_attention.1 = bf16[8,4,256,128]{3,2,1,0:T(8,128)(2,1)} custom-call(bf16[8,4,256,128]{3,2,1,0:T(8,128)(2,1)S(1)} %bitcast.27, bf16[2,256,1024]{2,1,0:T(8,128)(2,1)} %collective-permute-done.2.rest_0_.refs_1_, bf16[2,256,1024]{2,1,0:T(8,128)(2,1)} %copy-done.13), custom_call_target="tpu_custom_call" | custom-call | flops 8000000000 | bytes 4194304 | tf_op jit(solution)/shard_map/mode_attention/pallas_call | solution.py:394
  109.2 5.4 %all-to-all-start.3 = ((bf16[8,1024,128]{2,1,0:T(8,128)(2,1)}), bf16[8,1024,128]{2,1,0:T(8,128)(2,1)S(1)}, u32[]{:S(2)}, u32[]{:S(2)}) async-start(bf16[8,1024,128]{2,1,0:T(8,128)(2,1)} %bitcast.29), calls=%async_computation.3 | async-start | bytes 4194304 | tf_op jit(solution)/shard_map/all_to_all | solution.py:844
  115.3 23.7 %collective-permute-done.4.rest_0_.refs_2_ = bf16[2,256,1024]{2,1,0:T(8,128)(2,1)} collective-permute-done((bf16[2,256,1024]{2,1,0:T(8,128)(2,1)}, bf16[2,256,1024]{2,1,0:T(8,128)(2,1)}, u32[]{:S(2)}, u32[]{:S(2)}) %collective-permute-start.4) | collective-permute-done | bytes 1048608 | tf_op jit(solution)/shard_map/ppermute | solution.py:514
  139.4 7.9 %early_first.1.rest_0_ = bf16[8,256,1024]{2,1,0:T(8,128)(2,1)} custom-call(s32[7]{0:T(128)S(1)} %constant_dynamic-update-slice_fusion.2.ids_ref, bf16[8,256,128]{2,1,0:T(8,128)(2,1)} %get-tuple-element.61.hidden_ref, bf16[8,4,256,128]{3,2,1,0:T(8,128)(2,1)S(1)} %bitcast.19, bf16[8,4,256,128]{3,2,1,0:T(8,128)(2,1)S(1)} %bitcast.20, ...), custom_call_target="tpu_custom_call" | custom-call | flops 1000000000 | bytes 5242880 | tf_op jit(solution)/shard_map/early_first/pallas_call | solution.py:522
  147.3 7.1 %turn.1 = (bf16[16,128,128]{2,1,0:T(8,128)(2,1)}, bf16[256,1024]{1,0:T(8,128)(2,1)}) custom-call(bf16[8,4,256,128]{3,2,1,0:T(8,128)(2,1)S(1)} %bitcast.21, bf16[256,1024]{1,0:T(8,128)(2,1)S(1)} %copy-done.2, bf16[256,1024]{1,0:T(8,128)(2,1)S(1)} %copy-done.9, bf16[8,1024,1024]{2,1,0:T(8,128)(2,1)} %weights_ref.7, bf16[8,256,1024]{2,1,0:T(8,128)(2,1)} %early_first.1.rest_0_), custom_call_target="tpu_custom_call" | custom-call | flops 2147483648 | bytes 12582912 | tf_op jit(solution)/shard_map/turn/pallas_call | solution.py:441
  154.4 4.8 %all-to-all-start.4 = ((bf16[16,128,128]{2,1,0:T(8,128)(2,1)}), bf16[16,128,128]{2,1,0:T(8,128)(2,1)S(1)}, u32[]{:S(2)}, u32[]{:S(2)}) async-start(bf16[16,128,128]{2,1,0:T(8,128)(2,1)} %get-tuple-element.62), calls=%async_computation.4 | async-start | bytes 1048576 | tf_op jit(solution)/shard_map/all_to_all | solution.py:844
  159.3 8.8 %early_add.1 = (bf16[8,128,512]{2,1,0:T(8,128)(2,1)}, bf16[8,128,512]{2,1,0:T(8,128)(2,1)}, bf16[8,128,512]{2,1,0:T(8,128)(2,1)}, bf16[8,128,512]{2,1,0:T(8,128)(2,1)}) custom-call(s32[7]{0:T(128)S(1)} %stack.40.ids_ref, bf16[8,256,128]{2,1,0:T(8,128)(2,1)} %get-tuple-element.61.hidden_ref, bf16[8,4,256,128]{3,2,1,0:T(8,128)(2,1)S(1)} %bitcast.22, ...), custom_call_target="tpu_custom_call" | custom-call | flops 1000000000 | bytes 5242880 | tf_op jit(solution)/shard_map/early_add/pallas_call | solution.py:522
  168.1 1.2 collective-permute-start.6
  169.3 2.1 collective-permute-start.7
  171.6 7.1 %agent_backward.1.refs_4_.refs_5_ = bf16[16,3,128,128]{3,2,1,0:T(8,128)(2,1)} custom-call(bf16[16,384,128]{2,1,0:T(8,128)(2,1)} %copy-done.6, bf16[16,384,128]{2,1,0:T(8,128)(2,1)} %copy-done.6, bf16[16,384,128]{2,1,0:T(8,128)(2,1)} %copy-done.6, bf16[16,128,128]{2,1,0:T(8,128)(2,1)S(1)} %all-to-all-done.4.g, f32[4,4,256,128]{3,2,1,0:T(8,128)} %get-tuple-element.63.table_ref), custom_call_target="tpu_custom_call" | custom-call | flops 6000000000 | bytes 6291456 | tf_op jit(solution)/shard_map/agent_backward/pallas_call | solution.py:283
  178.8 7.1 %all-to-all-start.5 = ((bf16[16,384,128]{2,1,0:T(8,128)(2,1)}), bf16[16,384,128]{2,1,0:T(8,128)(2,1)S(1)}, u32[]{:S(2)}, u32[]{:S(2)}) async-start(bf16[16,384,128]{2,1,0:T(8,128)(2,1)} %bitcast.16), calls=%async_computation.5 | async-start | bytes 3145728 | tf_op jit(solution)/shard_map/all_to_all | solution.py:844
  185.9 11.0 %late_products.1 = (bf16[2,256,1408]{2,1,0:T(8,128)(2,1)S(1)}, bf16[256,1408]{1,0:T(8,128)(2,1)S(1)}, bf16[256,1408]{1,0:T(8,128)(2,1)S(1)}) custom-call(s32[7]{0:T(128)S(1)} %stack.40.ids_ref, bf16[2,256,1024]{2,1,0:T(8,128)(2,1)} %pad_maximum_fusion.rest_0_.refs_0_, bf16[2,256,1024]{2,1,0:T(8,128)(2,1)} %collective-permute-done.2.rest_0_.refs_1_, ...), custom_call_target="tpu_custom_call" | custom-call | flops 1000000000 | bytes 5242880 | tf_op jit(solution)/shard_map/late_products/pallas_call | solution.py:522
  197.5 4.4 %early_half.1 = (bf16[8,64,1024]{2,1,0:T(8,128)(2,1)}, bf16[8,64,512]{2,1,0:T(8,128)(2,1)}, bf16[8,64,512]{2,1,0:T(8,128)(2,1)}) custom-call(s32[7]{0:T(128)S(1)} %stack.40.ids_ref, bf16[8,128,512]{2,1,0:T(8,128)(2,1)S(1)} %copy-done.7, bf16[8,128,512]{2,1,0:T(8,128)(2,1)} %collective-permute-done.6.left_in, bf16[8,128,512]{2,1,0:T(8,128)(2,1)S(1)} %copy-done.8, ...), custom_call_target="tpu_custom_call" | custom-call | flops 1000000000 | bytes 5242880 | tf_op jit(solution)/shard_map/early_half/pallas_call | solution.py:522
  202.0 1.2 collective-permute-start.8
  203.2 2.2 late_add.1
  206.2 3.2 %all-to-all-done.5 = bf16[16,384,128]{2,1,0:T(8,128)(2,1)S(1)} async-done(((bf16[16,384,128]{2,1,0:T(8,128)(2,1)}), bf16[16,384,128]{2,1,0:T(8,128)(2,1)S(1)}, u32[]{:S(2)}, u32[]{:S(2)}) %all-to-all-start.5) | async-done | bytes 1572896 | tf_op jit(solution)/shard_map/all_to_all | solution.py:844
  209.5 5.1 %leave.1.rest_0_ = bf16[256,1024]{1,0:T(8,128)(2,1)S(1)} custom-call(bf16[16,3,128,128]{3,2,1,0:T(8,128)(2,1)S(1)} %bitcast.24, bf16[256,1024]{1,0:T(8,128)(2,1)S(1)} %copy-done.3, bf16[256,1024]{1,0:T(8,128)(2,1)S(1)} %copy-done, bf16[8,1024,1024]{2,1,0:T(8,128)(2,1)} %weights_ref.7), custom_call_target="tpu_custom_call" | custom-call | flops 1610612736 | bytes 9437184 | tf_op jit(solution)/shard_map/leave/pallas_call | solution.py:490
  215.4 2.4 collective-permute-done.8.left_ref
  217.7 3.9 %early_z.1 = (bf16[8,32,1024]{2,1,0:T(8,128)(2,1)}, bf16[8,32,1024]{2,1,0:T(8,128)(2,1)S(1)}) custom-call(s32[7]{0:T(128)S(1)} %stack.40.ids_ref, bf16[8,64,1024]{2,1,0:T(8,128)(2,1)S(1)} %copy-done.10, bf16[8,64,512]{2,1,0:T(8,128)(2,1)} %collective-permute-done.8.left_ref, bf16[8,64,512]{2,1,0:T(8,128)(2,1)} %collective-permute-done.9.right_ref, ...), custom_call_target="tpu_custom_call" | custom-call | flops 1000000000 | bytes 5242880 | tf_op jit(solution)/shard_map/early_z/pallas_call | solution.py:522
  222.5 1.4 collective-permute-done.13.refs_1_
  223.9 1.9 late_y.1
  225.8 2.9 %collective-permute-start.14 = (bf16[2,32,1408]{2,1,0:T(8,128)(2,1)S(1)}, bf16[2,32,1408]{2,1,0:T(8,128)(2,1)S(1)}, u32[]{:S(2)}, u32[]{:S(2)}) collective-permute-start(bf16[2,32,1408]{2,1,0:T(8,128)(2,1)S(1)} %get-tuple-element.80), channel_id=1, source_target_pairs={{0,2},{1,3},{2,0},{3,1},{4,6},{5,7},{6,4},{7,5},{8,10},{9,11},{10,... | collective-permute-start | bytes 540680 | tf_op jit(solution)/shard_map/ppermute | solution.py:514
  228.7 1.6 collective-permute-start.15
  230.3 1.2 collective-permute-start.16
  231.5 2.2 collective-permute-done.14.rest_1_
  233.7 3.4 %collective-permute-done.15.rest_2_ = bf16[2,32,1408]{2,1,0:T(8,128)(2,1)S(1)} collective-permute-done((bf16[2,32,1408]{2,1,0:T(8,128)(2,1)S(1)}, bf16[2,32,1408]{2,1,0:T(8,128)(2,1)S(1)}, u32[]{:S(2)}, u32[]{:S(2)}) %collective-permute-start.15) | collective-permute-done | bytes 180256 | tf_op jit(solution)/shard_map/ppermute | solution.py:514
  237.0 1.9 collective-permute-done.16.rest_3_
  239.8 1.4 collective-permute-start.17
  241.2 2.7 %collective-permute-start.18 = (bf16[2,32,2176]{2,1,0:T(8,128)(2,1)S(1)}, bf16[2,32,2176]{2,1,0:T(8,128)(2,1)S(1)}, u32[]{:S(2)}, u32[]{:S(2)}) collective-permute-start(bf16[2,32,2176]{2,1,0:T(8,128)(2,1)S(1)} %get-tuple-element.85), channel_id=1, source_target_pairs={{0,64},{8,72},{16,80},{24,88},{32,96},{40,104},{48,112},{56,120},{... | collective-permute-start | bytes 835592 | tf_op jit(solution)/shard_map/ppermute | solution.py:514
  244.6 3.2 %collective-permute-done.17.refs_1_ = bf16[2,32,2176]{2,1,0:T(8,128)(2,1)S(1)} collective-permute-done((bf16[2,32,2176]{2,1,0:T(8,128)(2,1)S(1)}, bf16[2,32,2176]{2,1,0:T(8,128)(2,1)S(1)}, u32[]{:S(2)}, u32[]{:S(2)}) %collective-permute-start.17) | collective-permute-done | bytes 278560 | tf_op jit(solution)/shard_map/ppermute | solution.py:514
  247.7 4.7 %collective-permute-done.18.refs_2_ = bf16[2,32,2176]{2,1,0:T(8,128)(2,1)S(1)} collective-permute-done((bf16[2,32,2176]{2,1,0:T(8,128)(2,1)S(1)}, bf16[2,32,2176]{2,1,0:T(8,128)(2,1)S(1)}, u32[]{:S(2)}, u32[]{:S(2)}) %collective-permute-start.18) | collective-permute-done | bytes 278560 | tf_op jit(solution)/shard_map/ppermute | solution.py:514
  252.4 2.5 collective-permute-done.19.refs_3_
  255.7 3.0 %collective-permute-start.20 = (bf16[4,32,640]{2,1,0:T(8,128)(2,1)S(1)}, bf16[4,32,640]{2,1,0:T(8,128)(2,1)S(1)}, u32[]{:S(2)}, u32[]{:S(2)}) collective-permute-start(bf16[4,32,640]{2,1,0:T(8,128)(2,1)S(1)} %get-tuple-element.88), channel_id=1, source_target_pairs={{0,16},{8,24},{16,0},{24,8},{32,48},{40,56},{48,32},{56,40},{64,80... | collective-permute-start | bytes 491528 | tf_op jit(solution)/shard_map/ppermute | solution.py:514
  259.7 2.9 %collective-permute-done.20.arrived_ref = bf16[4,32,640]{2,1,0:T(8,128)(2,1)S(1)} collective-permute-done((bf16[4,32,640]{2,1,0:T(8,128)(2,1)S(1)}, bf16[4,32,640]{2,1,0:T(8,128)(2,1)S(1)}, u32[]{:S(2)}, u32[]{:S(2)}) %collective-permute-start.20) | collective-permute-done | bytes 163872 | tf_op jit(solution)/shard_map/ppermute | solution.py:514
  262.6 1.3 last.1
  (67 shorter events, 10.5 us)
Async XLA Ops:
  7.4 7.7 %copy-start.15 = (bf16[128,1024]{1,0:T(8,128)(2,1)S(1)}, bf16[128,1024]{1,0:T(8,128)(2,1)}, u32[]{:S(2)}) copy-start(bf16[128,1024]{1,0:T(8,128)(2,1)} %get-tuple-element.56) | copy-start | bytes 786436
  7.4 7.7 %copy-start.16 = (s32[128]{0:T(128)S(1)}, s32[128]{0:T(128)}, u32[]{:S(2)}) copy-start(s32[128]{0:T(128)} %param.9) | copy-start | bytes 1540
  7.4 30.9 %all-to-all-start = ((bf16[16,384,128]{2,1,0:T(8,128)(2,1)}), bf16[16,384,128]{2,1,0:T(8,128)(2,1)S(1)}, u32[]{:S(2)}, u32[]{:S(2)}) async-start(bf16[16,384,128]{2,1,0:T(8,128)(2,1)} %get-tuple-element.53), calls=%async_computation | async-start | bytes 3145728 | tf_op jit(solution)/shard_map/all_to_all | solution.py:844
  14.7 1.6 collective-permute-start
  16.3 31.1 %copy-start.14 = (bf16[8,8,4,1024]{3,2,1,0:T(4,128)(2,1)S(1)}, bf16[8,8,4,1024]{3,2,1,0:T(4,128)(2,1)}, u32[]{:S(2)}) copy-start(bf16[8,8,4,1024]{3,2,1,0:T(4,128)(2,1)} %param.7) | copy-start | bytes 1572868
  16.3 31.3 %collective-permute-start.1 = (bf16[256,1024]{1,0:T(8,128)(2,1)S(1)}, bf16[256,1024]{1,0:T(8,128)(2,1)}, u32[]{:S(2)}, u32[]{:S(2)}) collective-permute-start(bf16[256,1024]{1,0:T(8,128)(2,1)S(1)} %constant_dynamic-update-slice_fusion), channel_id=1, source_target_pairs={{0,16},{8,24},{16,0},{24,8},{32,48},{40,56},{48,32},{56,40},{64,80... | collective-permute-start | bytes 1572872 | tf_op jit(solution)/shard_map/ppermute | solution.py:514
  38.3 4.8 %copy-start.6 = (bf16[16,384,128]{2,1,0:T(8,128)(2,1)}, bf16[16,384,128]{2,1,0:T(8,128)(2,1)S(1)}, u32[]{:S(2)}) copy-start(bf16[16,384,128]{2,1,0:T(8,128)(2,1)S(1)} %all-to-all-done.query_ref.keys_ref.values_ref.q.k.v) | copy-start | bytes 4718596
  43.1 16.7 %copy-start.3 = (bf16[256,1024]{1,0:T(8,128)(2,1)S(1)}, bf16[256,1024]{1,0:T(8,128)(2,1)}, u32[]{:S(2)}) copy-start(bf16[256,1024]{1,0:T(8,128)(2,1)} %get-tuple-element.54.tokens_ref) | copy-start | bytes 1572868
  43.1 16.7 %all-to-all-start.1 = ((bf16[16,128,128]{2,1,0:T(8,128)(2,1)}), bf16[16,128,128]{2,1,0:T(8,128)(2,1)S(1)}, u32[]{:S(2)}, u32[]{:S(2)}) async-start(bf16[16,128,128]{2,1,0:T(8,128)(2,1)} %get-tuple-element.55), calls=%async_computation.1 | async-start | bytes 1048576 | tf_op jit(solution)/shard_map/all_to_all | solution.py:844
  59.8 8.1 %copy-start.1 = (bf16[16,128,128]{2,1,0:T(8,128)(2,1)}, bf16[16,128,128]{2,1,0:T(8,128)(2,1)S(1)}, u32[]{:S(2)}) copy-start(bf16[16,128,128]{2,1,0:T(8,128)(2,1)S(1)} %all-to-all-done.1) | copy-start | bytes 1572868
  67.9 31.9 %all-to-all-start.2 = ((bf16[8,1024,128]{2,1,0:T(8,128)(2,1)}), bf16[8,1024,128]{2,1,0:T(8,128)(2,1)S(1)}, u32[]{:S(2)}, u32[]{:S(2)}) async-start(bf16[8,1024,128]{2,1,0:T(8,128)(2,1)} %bitcast.28), calls=%async_computation.2 | async-start | bytes 4194304 | tf_op jit(solution)/shard_map/all_to_all | solution.py:844
  73.4 25.4 %collective-permute-start.3 = (bf16[2,256,1024]{2,1,0:T(8,128)(2,1)}, bf16[2,256,1024]{2,1,0:T(8,128)(2,1)S(1)}, u32[]{:S(2)}, u32[]{:S(2)}) collective-permute-start(bf16[2,256,1024]{2,1,0:T(8,128)(2,1)} %pad_maximum_fusion.rest_0_.refs_0_), channel_id=1, source_target_pairs={{0,96},{8,104},{16,112},{24,120},{32,64},{40,72},{48,80},{56,88},{... | collective-permute-start | bytes 3145736 | tf_op jit(solution)/shard_map/ppermute | solution.py:514
  74.2 25.6 %collective-permute-start.2 = (bf16[2,256,1024]{2,1,0:T(8,128)(2,1)}, bf16[2,256,1024]{2,1,0:T(8,128)(2,1)}, u32[]{:S(2)}, u32[]{:S(2)}) collective-permute-start(bf16[2,256,1024]{2,1,0:T(8,128)(2,1)} %pad_maximum_fusion.rest_0_.refs_0_), channel_id=1, source_target_pairs={{0,32},{8,40},{16,48},{24,56},{32,0},{40,8},{48,16},{56,24},{64,96... | collective-permute-start | bytes 3145736 | tf_op jit(solution)/shard_map/ppermute | solution.py:514
  98.8 1.0 copy-start.13
  109.2 30.2 %all-to-all-start.3 = ((bf16[8,1024,128]{2,1,0:T(8,128)(2,1)}), bf16[8,1024,128]{2,1,0:T(8,128)(2,1)S(1)}, u32[]{:S(2)}, u32[]{:S(2)}) async-start(bf16[8,1024,128]{2,1,0:T(8,128)(2,1)} %bitcast.29), calls=%async_computation.3 | async-start | bytes 4194304 | tf_op jit(solution)/shard_map/all_to_all | solution.py:844
  114.6 24.3 %collective-permute-start.4 = (bf16[2,256,1024]{2,1,0:T(8,128)(2,1)}, bf16[2,256,1024]{2,1,0:T(8,128)(2,1)}, u32[]{:S(2)}, u32[]{:S(2)}) collective-permute-start(bf16[2,256,1024]{2,1,0:T(8,128)(2,1)} %pad_maximum_fusion.rest_0_.refs_0_), channel_id=1, source_target_pairs={{0,64},{8,72},{16,80},{24,88},{32,96},{40,104},{48,112},{56,120},{... | collective-permute-start | bytes 3145736 | tf_op jit(solution)/shard_map/ppermute | solution.py:514
  139.4 7.9 %copy-start.2 = (bf16[256,1024]{1,0:T(8,128)(2,1)S(1)}, bf16[256,1024]{1,0:T(8,128)(2,1)}, u32[]{:S(2)}) copy-start(bf16[256,1024]{1,0:T(8,128)(2,1)} %get-tuple-element.59.last_ref.cotangent_ref) | copy-start | bytes 1572868
  139.4 7.9 %copy-start.9 = (bf16[256,1024]{1,0:T(8,128)(2,1)S(1)}, bf16[256,1024]{1,0:T(8,128)(2,1)}, u32[]{:S(2)}) copy-start(bf16[256,1024]{1,0:T(8,128)(2,1)} %get-tuple-element.60.after_ref) | copy-start | bytes 1572868
  147.3 11.9 %collective-permute-start.5 = (bf16[8,256,1024]{2,1,0:T(8,128)(2,1)}, bf16[8,256,1024]{2,1,0:T(8,128)(2,1)}, u32[]{:S(2)}, u32[]{:S(2)}) collective-permute-start(bf16[8,256,1024]{2,1,0:T(8,128)(2,1)} %early_first.1.rest_0_), channel_id=1, source_target_pairs={{0,8},{8,0},{16,24},{24,16},{32,40},{40,32},{48,56},{56,48},{64,72... | collective-permute-start | bytes 12582920 | tf_op jit(solution)/shard_map/ppermute | solution.py:514
  154.4 17.2 %all-to-all-start.4 = ((bf16[16,128,128]{2,1,0:T(8,128)(2,1)}), bf16[16,128,128]{2,1,0:T(8,128)(2,1)S(1)}, u32[]{:S(2)}, u32[]{:S(2)}) async-start(bf16[16,128,128]{2,1,0:T(8,128)(2,1)} %get-tuple-element.62), calls=%async_computation.4 | async-start | bytes 1048576 | tf_op jit(solution)/shard_map/all_to_all | solution.py:844
  168.1 29.4 %collective-permute-start.6 = (bf16[8,128,512]{2,1,0:T(8,128)(2,1)}, bf16[8,128,512]{2,1,0:T(8,128)(2,1)}, u32[]{:S(2)}, u32[]{:S(2)}) collective-permute-start(bf16[8,128,512]{2,1,0:T(8,128)(2,1)} %get-tuple-element.66), channel_id=1, source_target_pairs={{0,2},{1,3},{2,0},{3,1},{4,6},{5,7},{6,4},{7,5},{8,10},{9,11},{10,... | collective-permute-start | bytes 3145736 | tf_op jit(solution)/shard_map/ppermute | solution.py:514
  169.3 28.2 %collective-permute-start.7 = (bf16[8,128,512]{2,1,0:T(8,128)(2,1)}, bf16[8,128,512]{2,1,0:T(8,128)(2,1)}, u32[]{:S(2)}, u32[]{:S(2)}) collective-permute-start(bf16[8,128,512]{2,1,0:T(8,128)(2,1)} %get-tuple-element.68), channel_id=1, source_target_pairs={{0,6},{1,7},{2,4},{3,5},{4,2},{5,3},{6,0},{7,1},{8,14},{9,15},{10,... | collective-permute-start | bytes 3145736 | tf_op jit(solution)/shard_map/ppermute | solution.py:514
  178.8 7.1 %copy-start = (bf16[256,1024]{1,0:T(8,128)(2,1)S(1)}, bf16[256,1024]{1,0:T(8,128)(2,1)}, u32[]{:S(2)}) copy-start(bf16[256,1024]{1,0:T(8,128)(2,1)} %get-tuple-element.64.grad_after_ref.rest_1_.refs_7_) | copy-start | bytes 1572868
  178.8 30.7 %all-to-all-start.5 = ((bf16[16,384,128]{2,1,0:T(8,128)(2,1)}), bf16[16,384,128]{2,1,0:T(8,128)(2,1)S(1)}, u32[]{:S(2)}, u32[]{:S(2)}) async-start(bf16[16,384,128]{2,1,0:T(8,128)(2,1)} %bitcast.16), calls=%async_computation.5 | async-start | bytes 3145728 | tf_op jit(solution)/shard_map/all_to_all | solution.py:844
  185.9 11.6 %copy-start.7 = (bf16[8,128,512]{2,1,0:T(8,128)(2,1)S(1)}, bf16[8,128,512]{2,1,0:T(8,128)(2,1)}, u32[]{:S(2)}) copy-start(bf16[8,128,512]{2,1,0:T(8,128)(2,1)} %get-tuple-element.65.left_ref) | copy-start | bytes 3145732
  185.9 11.6 %copy-start.8 = (bf16[8,128,512]{2,1,0:T(8,128)(2,1)S(1)}, bf16[8,128,512]{2,1,0:T(8,128)(2,1)}, u32[]{:S(2)}) copy-start(bf16[8,128,512]{2,1,0:T(8,128)(2,1)} %get-tuple-element.67.right_ref) | copy-start | bytes 3145732
  196.9 6.2 %collective-permute-start.11 = (bf16[256,1408]{1,0:T(8,128)(2,1)S(1)}, bf16[256,1408]{1,0:T(8,128)(2,1)S(1)}, u32[]{:S(2)}, u32[]{:S(2)}) collective-permute-start(bf16[256,1408]{1,0:T(8,128)(2,1)S(1)} %get-tuple-element.75), channel_id=1, source_target_pairs={{0,8},{8,0},{16,24},{24,16},{32,40},{40,32},{48,56},{56,48},{64,72... | collective-permute-start | bytes 2162696 | tf_op jit(solution)/shard_map/ppermute | solution.py:514
  197.4 5.8 %collective-permute-start.12 = (bf16[256,1408]{1,0:T(8,128)(2,1)S(1)}, bf16[256,1408]{1,0:T(8,128)(2,1)S(1)}, u32[]{:S(2)}, u32[]{:S(2)}) collective-permute-start(bf16[256,1408]{1,0:T(8,128)(2,1)S(1)} %get-tuple-element.76), channel_id=1, source_target_pairs={{0,8},{8,0},{16,24},{24,16},{32,40},{40,32},{48,56},{56,48},{64,72... | collective-permute-start | bytes 2162696 | tf_op jit(solution)/shard_map/ppermute | solution.py:514
  202.0 15.8 %collective-permute-start.8 = (bf16[8,64,512]{2,1,0:T(8,128)(2,1)}, bf16[8,64,512]{2,1,0:T(8,128)(2,1)}, u32[]{:S(2)}, u32[]{:S(2)}) collective-permute-start(bf16[8,64,512]{2,1,0:T(8,128)(2,1)} %get-tuple-element.70), channel_id=1, source_target_pairs={{0,6},{1,7},{2,4},{3,5},{4,2},{5,3},{6,0},{7,1},{8,14},{9,15},{10,... | collective-permute-start | bytes 1572872 | tf_op jit(solution)/shard_map/ppermute | solution.py:514
  203.1 14.6 %collective-permute-start.9 = (bf16[8,64,512]{2,1,0:T(8,128)(2,1)}, bf16[8,64,512]{2,1,0:T(8,128)(2,1)}, u32[]{:S(2)}, u32[]{:S(2)}) collective-permute-start(bf16[8,64,512]{2,1,0:T(8,128)(2,1)} %get-tuple-element.71), channel_id=1, source_target_pairs={{0,2},{1,3},{2,0},{3,1},{4,6},{5,7},{6,4},{7,5},{8,10},{9,11},{10,... | collective-permute-start | bytes 1572872 | tf_op jit(solution)/shard_map/ppermute | solution.py:514
  205.4 18.5 %collective-permute-start.13 = (bf16[2,128,1408]{2,1,0:T(8,128)(2,1)}, bf16[2,128,1408]{2,1,0:T(8,128)(2,1)}, u32[]{:S(2)}, u32[]{:S(2)}) collective-permute-start(bf16[2,128,1408]{2,1,0:T(8,128)(2,1)} %get-tuple-element.78), channel_id=1, source_target_pairs={{0,1},{1,0},{2,3},{3,2},{4,5},{5,4},{6,7},{7,6},{8,9},{9,8},{10,11... | collective-permute-start | bytes 2162696 | tf_op jit(solution)/shard_map/ppermute | solution.py:514
  209.5 8.3 %copy-start.10 = (bf16[8,64,1024]{2,1,0:T(8,128)(2,1)S(1)}, bf16[8,64,1024]{2,1,0:T(8,128)(2,1)}, u32[]{:S(2)}) copy-start(bf16[8,64,1024]{2,1,0:T(8,128)(2,1)} %get-tuple-element.69.own_ref) | copy-start | bytes 3145732
  214.6 0.8 copy-start.4
  215.4 8.5 %copy-start.11 = (bf16[2,128,1408]{2,1,0:T(8,128)(2,1)S(1)}, bf16[2,128,1408]{2,1,0:T(8,128)(2,1)}, u32[]{:S(2)}) copy-start(bf16[2,128,1408]{2,1,0:T(8,128)(2,1)} %get-tuple-element.77.refs_0_) | copy-start | bytes 2162692
  221.6 17.3 %copy-start.12 = (bf16[8,32,1024]{2,1,0:T(8,128)(2,1)S(1)}, bf16[8,32,1024]{2,1,0:T(8,128)(2,1)}, u32[]{:S(2)}) copy-start(bf16[8,32,1024]{2,1,0:T(8,128)(2,1)} %get-tuple-element.72.early_ref) | copy-start | bytes 1572868
  221.6 17.3 %collective-permute-start.10 = (bf16[8,32,1024]{2,1,0:T(8,128)(2,1)S(1)}, bf16[8,32,1024]{2,1,0:T(8,128)(2,1)S(1)}, u32[]{:S(2)}, u32[]{:S(2)}) collective-permute-start(bf16[8,32,1024]{2,1,0:T(8,128)(2,1)S(1)} %get-tuple-element.73), channel_id=1, source_target_pairs={{0,1},{1,0},{2,3},{3,2},{4,5},{5,4},{6,7},{7,6},{8,9},{9,8},{10,11... | collective-permute-start | bytes 1572872 | tf_op jit(solution)/shard_map/ppermute | solution.py:514
  225.8 7.9 %collective-permute-start.14 = (bf16[2,32,1408]{2,1,0:T(8,128)(2,1)S(1)}, bf16[2,32,1408]{2,1,0:T(8,128)(2,1)S(1)}, u32[]{:S(2)}, u32[]{:S(2)}) collective-permute-start(bf16[2,32,1408]{2,1,0:T(8,128)(2,1)S(1)} %get-tuple-element.80), channel_id=1, source_target_pairs={{0,2},{1,3},{2,0},{3,1},{4,6},{5,7},{6,4},{7,5},{8,10},{9,11},{10,... | collective-permute-start | bytes 540680 | tf_op jit(solution)/shard_map/ppermute | solution.py:514
  228.7 8.3 %collective-permute-start.15 = (bf16[2,32,1408]{2,1,0:T(8,128)(2,1)S(1)}, bf16[2,32,1408]{2,1,0:T(8,128)(2,1)S(1)}, u32[]{:S(2)}, u32[]{:S(2)}) collective-permute-start(bf16[2,32,1408]{2,1,0:T(8,128)(2,1)S(1)} %get-tuple-element.81), channel_id=1, source_target_pairs={{0,4},{1,5},{2,6},{3,7},{4,0},{5,1},{6,2},{7,3},{8,12},{9,13},{10,... | collective-permute-start | bytes 540680 | tf_op jit(solution)/shard_map/ppermute | solution.py:514
  230.3 8.6 %collective-permute-start.16 = (bf16[2,32,1408]{2,1,0:T(8,128)(2,1)S(1)}, bf16[2,32,1408]{2,1,0:T(8,128)(2,1)S(1)}, u32[]{:S(2)}, u32[]{:S(2)}) collective-permute-start(bf16[2,32,1408]{2,1,0:T(8,128)(2,1)S(1)} %get-tuple-element.82), channel_id=1, source_target_pairs={{0,6},{1,7},{2,4},{3,5},{4,2},{5,3},{6,0},{7,1},{8,14},{9,15},{10,... | collective-permute-start | bytes 540680 | tf_op jit(solution)/shard_map/ppermute | solution.py:514
  239.8 18.9 %copy-start.5 = (bf16[256,1024]{1,0:T(8,128)(2,1)S(1)}, bf16[256,1024]{1,0:T(8,128)(2,1)}, u32[]{:S(2)}) copy-start(bf16[256,1024]{1,0:T(8,128)(2,1)} %copy-done.4) | copy-start | bytes 1572868
  239.8 7.9 %collective-permute-start.17 = (bf16[2,32,2176]{2,1,0:T(8,128)(2,1)S(1)}, bf16[2,32,2176]{2,1,0:T(8,128)(2,1)S(1)}, u32[]{:S(2)}, u32[]{:S(2)}) collective-permute-start(bf16[2,32,2176]{2,1,0:T(8,128)(2,1)S(1)} %get-tuple-element.84), channel_id=1, source_target_pairs={{0,32},{8,40},{16,48},{24,56},{32,0},{40,8},{48,16},{56,24},{64,96... | collective-permute-start | bytes 835592 | tf_op jit(solution)/shard_map/ppermute | solution.py:514
  241.2 11.3 %collective-permute-start.18 = (bf16[2,32,2176]{2,1,0:T(8,128)(2,1)S(1)}, bf16[2,32,2176]{2,1,0:T(8,128)(2,1)S(1)}, u32[]{:S(2)}, u32[]{:S(2)}) collective-permute-start(bf16[2,32,2176]{2,1,0:T(8,128)(2,1)S(1)} %get-tuple-element.85), channel_id=1, source_target_pairs={{0,64},{8,72},{16,80},{24,88},{32,96},{40,104},{48,112},{56,120},{... | collective-permute-start | bytes 835592 | tf_op jit(solution)/shard_map/ppermute | solution.py:514
  243.8 11.1 %collective-permute-start.19 = (bf16[2,32,2176]{2,1,0:T(8,128)(2,1)S(1)}, bf16[2,32,2176]{2,1,0:T(8,128)(2,1)S(1)}, u32[]{:S(2)}, u32[]{:S(2)}) collective-permute-start(bf16[2,32,2176]{2,1,0:T(8,128)(2,1)S(1)} %get-tuple-element.86), channel_id=1, source_target_pairs={{0,96},{8,104},{16,112},{24,120},{32,64},{40,72},{48,80},{56,88},{... | collective-permute-start | bytes 835592 | tf_op jit(solution)/shard_map/ppermute | solution.py:514
  255.7 6.9 %collective-permute-start.20 = (bf16[4,32,640]{2,1,0:T(8,128)(2,1)S(1)}, bf16[4,32,640]{2,1,0:T(8,128)(2,1)S(1)}, u32[]{:S(2)}, u32[]{:S(2)}) collective-permute-start(bf16[4,32,640]{2,1,0:T(8,128)(2,1)S(1)} %get-tuple-element.88), channel_id=1, source_target_pairs={{0,16},{8,24},{16,0},{24,8},{32,48},{40,56},{48,32},{56,40},{64,80... | collective-permute-start | bytes 491528 | tf_op jit(solution)/shard_map/ppermute | solution.py:514

commit v9 on v8

--- a/solution.py
+++ b/solution.py
@@ -627,13 +627,13 @@
 
 
 def early_half(ids, parts):
-    narrow = pl.BlockSpec((2, 64, 512), lambda i, c: (i, 0, 0))
+    narrow = pl.BlockSpec((1, 64, 512), lambda i, c: (i, 0, 0))
     return prefetched(
         early_half_kernel, ids, parts,
-        [pl.BlockSpec((2, 128, 512), lambda i, c: (i, 0, 0))] * 4,
-        [pl.BlockSpec((2, 64, D), lambda i, c: (i, 0, 0)), narrow, narrow],
+        [pl.BlockSpec((1, 128, 512), lambda i, c: (i, 0, 0))] * 4,
+        [pl.BlockSpec((1, 64, D), lambda i, c: (i, 0, 0)), narrow, narrow],
         [pltpu.HBM((8, 64, D), BF)] + [jax.ShapeDtypeStruct((8, 64, 512), BF)] * 2,
-        "early_half", (4,),
+        "early_half", (8,),
     )
 
 
@@ -649,12 +649,12 @@
 
 
 def early_sums(ids, own, left, right, waits):
-    narrow = pl.BlockSpec((2, 64, 512), lambda i, c: (i, 0, 0))
+    narrow = pl.BlockSpec((1, 64, 512), lambda i, c: (i, 0, 0))
     keep, give = prefetched(
         early_z_kernel, ids, [own, left, right, *map(pinned, waits)],
-        [pl.BlockSpec((2, 64, D), lambda i, c: (i, 0, 0)), narrow, narrow] + [unused] * len(waits),
-        [pl.BlockSpec((2, 32, D), lambda i, c: (i, 0, 0))] * 2,
-        [pltpu.HBM((8, 32, D), BF), jax.ShapeDtypeStruct((8, 32, D), BF)], "early_z", (4,),
+        [pl.BlockSpec((1, 64, D), lambda i, c: (i, 0, 0)), narrow, narrow] + [unused] * len(waits),
+        [pl.BlockSpec((1, 32, D), lambda i, c: (i, 0, 0))] * 2,
+        [pltpu.HBM((8, 32, D), BF), jax.ShapeDtypeStruct((8, 32, D), BF)], "early_z", (8,),
     )
     return keep, swap(give, "mode", 1)
 

time: 265 us -> 271 us (1.023)
  Pallas kernels: 90.1 us -> 93.6 us
    ppermute x21, waiting for transfers between devices: 73.7 us -> 77.8 us  [swap(): return lax.ppermute(values, axis, [(n, n ^ bits) for n in range(size)])]
    pallas_call x10, Pallas kernels: 43 us -> 46.5 us  [prefetched(): pl.pallas_call(kernel, grid_spec=pltpu.PrefetchScalarGridSpec(num_scalar_...]
  transfers between devices with their start and end apart: 27 -> 27, of which waited for: 17 -> 16; matrix products, arithmetic and copies ran while one was open for 1% -> 1% of each run, Pallas kernels for 21% -> 22%
where the time goes in v9:
time: 271 us; the launch traced here: 269 us
  waiting for transfers between devices  108 us (40%)
  Pallas kernels  93.6 us (35%)
  starting transfers between devices  59.4 us (22%)
  local copies, waits for them, and re-layouts  4.28 us (2%)
    ppermute x21, waiting for transfers between devices, swap(): return lax.ppermute(values, axis, [(n, n ^ bits) for n in range(size)])  77.8 us
    pallas_call x10, Pallas kernels, prefetched(): pl.pallas_call(kernel, grid_spec=pltpu.PrefetchScalarGridSpec(num_scalar_...  46.5 us
    all_to_all x6, starting transfers between devices, exchange(): return lax.all_to_all(values, axis, split_axis=0, concat_axis=0, tiled=True)  34.4 us
    all_to_all x6, waiting for transfers between devices, exchange(): return lax.all_to_all(values, axis, split_axis=0, concat_axis=0, tiled=True)  30.6 us
    ppermute x21, starting transfers between devices, swap(): return lax.ppermute(values, axis, [(n, n ^ bits) for n in range(size)])  25 us
    pallas_call x1, Pallas kernels, mode_attention(): pl.pallas_call(mode_kernel, grid=(4,), in_specs=[spec] + [unused] * len(a...  9.42 us
    pallas_call x1, Pallas kernels, middle(): pl.pallas_call(middle_kernel, grid=(5,), in_specs=[fixed((ROWS, D)), fixe...  8.07 us
    pallas_call x1, Pallas kernels, agent_backward(): pl.pallas_call(agent_backward_all_kernel, grid=(4,), in_specs=agent_specs...  7.15 us
  transfers between devices with their start and end apart: 27, of which 16 were waited for; matrix products, arithmetic and copies ran while one was open for 1% of the time, Pallas kernels for 22%

profile of v9, /device:TPU:0, one launch (start us, length us, event | category | flops | bytes accessed | tf_op | source)
XLA Modules:
  0.0 268.8 jit_solution(3055346070859665286)
XLA Ops:
  0.6 1.2 reshape.64.tokens_ref
  1.9 5.5 %enter.1 = (bf16[16,384,128]{2,1,0:T(8,128)(2,1)}, bf16[256,1024]{1,0:T(8,128)(2,1)}, bf16[128,1024]{1,0:T(8,128)(2,1)}, bf16[128,1024]{1,0:T(8,128)(2,1)S(1)}) custom-call(s32[7]{0:T(128)S(1)} %stack.40.ids_ref, bf16[256,1024]{1,0:T(8,128)(2,1)S(1)} %reshape.64.tokens_ref, bf16[8,1024,1024]{2,1,0:T(8,128)(2,1)} %weights_ref.7), custom_call_target="tpu_custom_call" | custom-call | flops 1610612736 | bytes 8388608 | tf_op jit(solution)/shard_map/enter/pallas_call | solution.py:178
  7.4 7.3 %all-to-all-start = ((bf16[16,384,128]{2,1,0:T(8,128)(2,1)}), bf16[16,384,128]{2,1,0:T(8,128)(2,1)S(1)}, u32[]{:S(2)}, u32[]{:S(2)}) async-start(bf16[16,384,128]{2,1,0:T(8,128)(2,1)} %get-tuple-element.53), calls=%async_computation | async-start | bytes 3145728 | tf_op jit(solution)/shard_map/all_to_all | solution.py:844
  15.2 1.2 collective-permute-done
  16.3 3.4 %collective-permute-start.1 = (bf16[256,1024]{1,0:T(8,128)(2,1)S(1)}, bf16[256,1024]{1,0:T(8,128)(2,1)}, u32[]{:S(2)}, u32[]{:S(2)}) collective-permute-start(bf16[256,1024]{1,0:T(8,128)(2,1)S(1)} %constant_dynamic-update-slice_fusion), channel_id=1, source_target_pairs={{0,16},{8,24},{16,0},{24,8},{32,48},{40,56},{48,32},{56,40},{64,80... | collective-permute-start | bytes 1572872 | tf_op jit(solution)/shard_map/ppermute | solution.py:514
  19.8 18.5 %all-to-all-done.query_ref.keys_ref.values_ref.q.k.v = bf16[16,384,128]{2,1,0:T(8,128)(2,1)S(1)} async-done(((bf16[16,384,128]{2,1,0:T(8,128)(2,1)}), bf16[16,384,128]{2,1,0:T(8,128)(2,1)S(1)}, u32[]{:S(2)}, u32[]{:S(2)}) %all-to-all-start) | async-done | bytes 1572896 | tf_op jit(solution)/shard_map/all_to_all | solution.py:844
  38.3 4.8 %agent_forward.1 = (bf16[16,128,128]{2,1,0:T(8,128)(2,1)}, f32[4,4,256,128]{3,2,1,0:T(8,128)}) custom-call(bf16[16,384,128]{2,1,0:T(8,128)(2,1)S(1)} %all-to-all-done.query_ref.keys_ref.values_ref.q.k.v, bf16[16,384,128]{2,1,0:T(8,128)(2,1)S(1)} %all-to-all-done.query_ref.keys_ref.values_ref.q.k.v, ...), custom_call_target="tpu_custom_call" | custom-call | flops 3000000000 | bytes 4194304 | tf_op jit(solution)/shard_map/agent_forward/pallas_call | solution.py:228
  43.1 4.4 %all-to-all-start.1 = ((bf16[16,128,128]{2,1,0:T(8,128)(2,1)}), bf16[16,128,128]{2,1,0:T(8,128)(2,1)S(1)}, u32[]{:S(2)}, u32[]{:S(2)}) async-start(bf16[16,128,128]{2,1,0:T(8,128)(2,1)} %get-tuple-element.55), calls=%async_computation.1 | async-start | bytes 1048576 | tf_op jit(solution)/shard_map/all_to_all | solution.py:844
  47.6 2.1 pad_maximum_fusion.rest_0_.refs_0_
  49.8 10.1 %all-to-all-done.1 = bf16[16,128,128]{2,1,0:T(8,128)(2,1)S(1)} async-done(((bf16[16,128,128]{2,1,0:T(8,128)(2,1)}), bf16[16,128,128]{2,1,0:T(8,128)(2,1)S(1)}, u32[]{:S(2)}, u32[]{:S(2)}) %all-to-all-start.1) | async-done | bytes 524320 | tf_op jit(solution)/shard_map/all_to_all | solution.py:844
  59.8 8.1 %middle.1 = (bf16[8,4,256,128]{3,2,1,0:T(8,128)(2,1)}, bf16[256,1024]{1,0:T(8,128)(2,1)}, bf16[8,256,128]{2,1,0:T(8,128)(2,1)}, bf16[256,1024]{1,0:T(8,128)(2,1)}) custom-call(bf16[256,1024]{1,0:T(8,128)(2,1)S(1)} %copy-done.3, bf16[8,256,128]{2,1,0:T(8,128)(2,1)S(1)} %bitcast.25, bf16[256,1024]{1,0:T(8,128)(2,1)S(1)} %reshape.67.cotangent_ref, ...), custom_call_target="tpu_custom_call" | custom-call | flops 2684354560 | bytes 13631488 | tf_op jit(solution)/shard_map/middle/pallas_call | solution.py:339
  67.9 5.5 %all-to-all-start.2 = ((bf16[8,1024,128]{2,1,0:T(8,128)(2,1)}), bf16[8,1024,128]{2,1,0:T(8,128)(2,1)S(1)}, u32[]{:S(2)}, u32[]{:S(2)}) async-start(bf16[8,1024,128]{2,1,0:T(8,128)(2,1)} %bitcast.28), calls=%async_computation.2 | async-start | bytes 4194304 | tf_op jit(solution)/shard_map/all_to_all | solution.py:844
  74.3 24.4 %collective-permute-done.3.rest_1_.refs_3_ = bf16[2,256,1024]{2,1,0:T(8,128)(2,1)S(1)} collective-permute-done((bf16[2,256,1024]{2,1,0:T(8,128)(2,1)}, bf16[2,256,1024]{2,1,0:T(8,128)(2,1)S(1)}, u32[]{:S(2)}, u32[]{:S(2)}) %collective-permute-start.3) | collective-permute-done | bytes 1048608 | tf_op jit(solution)/shard_map/ppermute | solution.py:514
  98.8 1.0 copy-done.13
  99.8 9.4 %mode_attention.1 = bf16[8,4,256,128]{3,2,1,0:T(8,128)(2,1)} custom-call(bf16[8,4,256,128]{3,2,1,0:T(8,128)(2,1)S(1)} %bitcast.27, bf16[2,256,1024]{2,1,0:T(8,128)(2,1)} %collective-permute-done.2.rest_0_.refs_1_, bf16[2,256,1024]{2,1,0:T(8,128)(2,1)} %copy-done.13), custom_call_target="tpu_custom_call" | custom-call | flops 8000000000 | bytes 4194304 | tf_op jit(solution)/shard_map/mode_attention/pallas_call | solution.py:394
  109.2 5.4 %all-to-all-start.3 = ((bf16[8,1024,128]{2,1,0:T(8,128)(2,1)}), bf16[8,1024,128]{2,1,0:T(8,128)(2,1)S(1)}, u32[]{:S(2)}, u32[]{:S(2)}) async-start(bf16[8,1024,128]{2,1,0:T(8,128)(2,1)} %bitcast.29), calls=%async_computation.3 | async-start | bytes 4194304 | tf_op jit(solution)/shard_map/all_to_all | solution.py:844
  115.3 23.7 %collective-permute-done.4.rest_0_.refs_2_ = bf16[2,256,1024]{2,1,0:T(8,128)(2,1)} collective-permute-done((bf16[2,256,1024]{2,1,0:T(8,128)(2,1)}, bf16[2,256,1024]{2,1,0:T(8,128)(2,1)}, u32[]{:S(2)}, u32[]{:S(2)}) %collective-permute-start.4) | collective-permute-done | bytes 1048608 | tf_op jit(solution)/shard_map/ppermute | solution.py:514
  139.4 7.9 %early_first.1.rest_0_ = bf16[8,256,1024]{2,1,0:T(8,128)(2,1)} custom-call(s32[7]{0:T(128)S(1)} %constant_dynamic-update-slice_fusion.2.ids_ref, bf16[8,256,128]{2,1,0:T(8,128)(2,1)} %get-tuple-element.61.hidden_ref, bf16[8,4,256,128]{3,2,1,0:T(8,128)(2,1)S(1)} %bitcast.19, bf16[8,4,256,128]{3,2,1,0:T(8,128)(2,1)S(1)} %bitcast.20, ...), custom_call_target="tpu_custom_call" | custom-call | flops 1000000000 | bytes 5242880 | tf_op jit(solution)/shard_map/early_first/pallas_call | solution.py:522
  147.3 7.1 %turn.1 = (bf16[16,128,128]{2,1,0:T(8,128)(2,1)}, bf16[256,1024]{1,0:T(8,128)(2,1)}) custom-call(bf16[8,4,256,128]{3,2,1,0:T(8,128)(2,1)S(1)} %bitcast.21, bf16[256,1024]{1,0:T(8,128)(2,1)S(1)} %copy-done.2, bf16[256,1024]{1,0:T(8,128)(2,1)S(1)} %copy-done.9, bf16[8,1024,1024]{2,1,0:T(8,128)(2,1)} %weights_ref.7, bf16[8,256,1024]{2,1,0:T(8,128)(2,1)} %early_first.1.rest_0_), custom_call_target="tpu_custom_call" | custom-call | flops 2147483648 | bytes 12582912 | tf_op jit(solution)/shard_map/turn/pallas_call | solution.py:441
  154.4 4.8 %all-to-all-start.4 = ((bf16[16,128,128]{2,1,0:T(8,128)(2,1)}), bf16[16,128,128]{2,1,0:T(8,128)(2,1)S(1)}, u32[]{:S(2)}, u32[]{:S(2)}) async-start(bf16[16,128,128]{2,1,0:T(8,128)(2,1)} %get-tuple-element.62), calls=%async_computation.4 | async-start | bytes 1048576 | tf_op jit(solution)/shard_map/all_to_all | solution.py:844
  159.3 8.8 %early_add.1 = (bf16[8,128,512]{2,1,0:T(8,128)(2,1)}, bf16[8,128,512]{2,1,0:T(8,128)(2,1)}, bf16[8,128,512]{2,1,0:T(8,128)(2,1)}, bf16[8,128,512]{2,1,0:T(8,128)(2,1)}) custom-call(s32[7]{0:T(128)S(1)} %stack.40.ids_ref, bf16[8,256,128]{2,1,0:T(8,128)(2,1)} %get-tuple-element.61.hidden_ref, bf16[8,4,256,128]{3,2,1,0:T(8,128)(2,1)S(1)} %bitcast.22, ...), custom_call_target="tpu_custom_call" | custom-call | flops 1000000000 | bytes 5242880 | tf_op jit(solution)/shard_map/early_add/pallas_call | solution.py:522
  168.1 1.2 collective-permute-start.6
  169.3 2.1 collective-permute-start.7
  171.6 7.1 %agent_backward.1.refs_4_.refs_5_ = bf16[16,3,128,128]{3,2,1,0:T(8,128)(2,1)} custom-call(bf16[16,384,128]{2,1,0:T(8,128)(2,1)} %copy-done.6, bf16[16,384,128]{2,1,0:T(8,128)(2,1)} %copy-done.6, bf16[16,384,128]{2,1,0:T(8,128)(2,1)} %copy-done.6, bf16[16,128,128]{2,1,0:T(8,128)(2,1)S(1)} %all-to-all-done.4.g, f32[4,4,256,128]{3,2,1,0:T(8,128)} %get-tuple-element.63.table_ref), custom_call_target="tpu_custom_call" | custom-call | flops 6000000000 | bytes 6291456 | tf_op jit(solution)/shard_map/agent_backward/pallas_call | solution.py:283
  178.8 7.1 %all-to-all-start.5 = ((bf16[16,384,128]{2,1,0:T(8,128)(2,1)}), bf16[16,384,128]{2,1,0:T(8,128)(2,1)S(1)}, u32[]{:S(2)}, u32[]{:S(2)}) async-start(bf16[16,384,128]{2,1,0:T(8,128)(2,1)} %bitcast.16), calls=%async_computation.5 | async-start | bytes 3145728 | tf_op jit(solution)/shard_map/all_to_all | solution.py:844
  185.9 11.0 %late_products.1 = (bf16[2,256,1408]{2,1,0:T(8,128)(2,1)S(1)}, bf16[256,1408]{1,0:T(8,128)(2,1)S(1)}, bf16[256,1408]{1,0:T(8,128)(2,1)S(1)}) custom-call(s32[7]{0:T(128)S(1)} %stack.40.ids_ref, bf16[2,256,1024]{2,1,0:T(8,128)(2,1)} %pad_maximum_fusion.rest_0_.refs_0_, bf16[2,256,1024]{2,1,0:T(8,128)(2,1)} %collective-permute-done.2.rest_0_.refs_1_, ...), custom_call_target="tpu_custom_call" | custom-call | flops 1000000000 | bytes 5242880 | tf_op jit(solution)/shard_map/late_products/pallas_call | solution.py:522
  197.5 6.4 %early_half.1 = (bf16[8,64,1024]{2,1,0:T(8,128)(2,1)}, bf16[8,64,512]{2,1,0:T(8,128)(2,1)}, bf16[8,64,512]{2,1,0:T(8,128)(2,1)}) custom-call(s32[7]{0:T(128)S(1)} %stack.40.ids_ref, bf16[8,128,512]{2,1,0:T(8,128)(2,1)S(1)} %copy-done.7, bf16[8,128,512]{2,1,0:T(8,128)(2,1)} %collective-permute-done.6.left_in, bf16[8,128,512]{2,1,0:T(8,128)(2,1)S(1)} %copy-done.8, ...), custom_call_target="tpu_custom_call" | custom-call | flops 1000000000 | bytes 5242880 | tf_op jit(solution)/shard_map/early_half/pallas_call | solution.py:522
  203.9 1.2 collective-permute-start.8
  205.1 2.2 late_add.1
  208.2 1.3 all-to-all-done.5
  209.5 5.1 %leave.1.rest_0_ = bf16[256,1024]{1,0:T(8,128)(2,1)S(1)} custom-call(bf16[16,3,128,128]{3,2,1,0:T(8,128)(2,1)S(1)} %bitcast.24, bf16[256,1024]{1,0:T(8,128)(2,1)S(1)} %copy-done.3, bf16[256,1024]{1,0:T(8,128)(2,1)S(1)} %copy-done, bf16[8,1024,1024]{2,1,0:T(8,128)(2,1)} %weights_ref.7), custom_call_target="tpu_custom_call" | custom-call | flops 1610612736 | bytes 9437184 | tf_op jit(solution)/shard_map/leave/pallas_call | solution.py:490
  215.4 4.3 %collective-permute-done.8.left_ref = bf16[8,64,512]{2,1,0:T(8,128)(2,1)} collective-permute-done((bf16[8,64,512]{2,1,0:T(8,128)(2,1)}, bf16[8,64,512]{2,1,0:T(8,128)(2,1)}, u32[]{:S(2)}, u32[]{:S(2)}) %collective-permute-start.8) | collective-permute-done | bytes 524320 | tf_op jit(solution)/shard_map/ppermute | solution.py:514
  219.7 5.5 %early_z.1 = (bf16[8,32,1024]{2,1,0:T(8,128)(2,1)}, bf16[8,32,1024]{2,1,0:T(8,128)(2,1)S(1)}) custom-call(s32[7]{0:T(128)S(1)} %stack.40.ids_ref, bf16[8,64,1024]{2,1,0:T(8,128)(2,1)S(1)} %copy-done.10, bf16[8,64,512]{2,1,0:T(8,128)(2,1)} %collective-permute-done.8.left_ref, bf16[8,64,512]{2,1,0:T(8,128)(2,1)} %collective-permute-done.9.right_ref, ...), custom_call_target="tpu_custom_call" | custom-call | flops 1000000000 | bytes 5242880 | tf_op jit(solution)/shard_map/early_z/pallas_call | solution.py:522
  226.1 1.9 late_y.1
  228.0 1.6 collective-permute-start.14
  229.6 1.8 collective-permute-start.15
  231.3 1.4 collective-permute-start.16
  232.8 2.8 %collective-permute-done.14.rest_1_ = bf16[2,32,1408]{2,1,0:T(8,128)(2,1)S(1)} collective-permute-done((bf16[2,32,1408]{2,1,0:T(8,128)(2,1)S(1)}, bf16[2,32,1408]{2,1,0:T(8,128)(2,1)S(1)}, u32[]{:S(2)}, u32[]{:S(2)}) %collective-permute-start.14) | collective-permute-done | bytes 180256 | tf_op jit(solution)/shard_map/ppermute | solution.py:514
  235.5 3.5 %collective-permute-done.15.rest_2_ = bf16[2,32,1408]{2,1,0:T(8,128)(2,1)S(1)} collective-permute-done((bf16[2,32,1408]{2,1,0:T(8,128)(2,1)S(1)}, bf16[2,32,1408]{2,1,0:T(8,128)(2,1)S(1)}, u32[]{:S(2)}, u32[]{:S(2)}) %collective-permute-start.15) | collective-permute-done | bytes 180256 | tf_op jit(solution)/shard_map/ppermute | solution.py:514
  239.0 2.3 collective-permute-done.16.rest_3_
  242.2 1.2 collective-permute-start.17
  243.4 2.7 collective-permute-start.18
  247.0 4.9 %collective-permute-done.17.refs_1_ = bf16[2,32,2176]{2,1,0:T(8,128)(2,1)S(1)} collective-permute-done((bf16[2,32,2176]{2,1,0:T(8,128)(2,1)S(1)}, bf16[2,32,2176]{2,1,0:T(8,128)(2,1)S(1)}, u32[]{:S(2)}, u32[]{:S(2)}) %collective-permute-start.17) | collective-permute-done | bytes 278560 | tf_op jit(solution)/shard_map/ppermute | solution.py:514
  251.8 5.5 %collective-permute-done.18.refs_2_ = bf16[2,32,2176]{2,1,0:T(8,128)(2,1)S(1)} collective-permute-done((bf16[2,32,2176]{2,1,0:T(8,128)(2,1)S(1)}, bf16[2,32,2176]{2,1,0:T(8,128)(2,1)S(1)}, u32[]{:S(2)}, u32[]{:S(2)}) %collective-permute-start.18) | collective-permute-done | bytes 278560 | tf_op jit(solution)/shard_map/ppermute | solution.py:514
  257.4 2.6 collective-permute-done.19.refs_3_
  260.6 3.2 %collective-permute-start.20 = (bf16[4,32,640]{2,1,0:T(8,128)(2,1)S(1)}, bf16[4,32,640]{2,1,0:T(8,128)(2,1)S(1)}, u32[]{:S(2)}, u32[]{:S(2)}) collective-permute-start(bf16[4,32,640]{2,1,0:T(8,128)(2,1)S(1)} %get-tuple-element.88), channel_id=1, source_target_pairs={{0,16},{8,24},{16,0},{24,8},{32,48},{40,56},{48,32},{56,40},{64,80... | collective-permute-start | bytes 491528 | tf_op jit(solution)/shard_map/ppermute | solution.py:514
  264.8 2.7 %collective-permute-done.20.arrived_ref = bf16[4,32,640]{2,1,0:T(8,128)(2,1)S(1)} collective-permute-done((bf16[4,32,640]{2,1,0:T(8,128)(2,1)S(1)}, bf16[4,32,640]{2,1,0:T(8,128)(2,1)S(1)}, u32[]{:S(2)}, u32[]{:S(2)}) %collective-permute-start.20) | collective-permute-done | bytes 163872 | tf_op jit(solution)/shard_map/ppermute | solution.py:514
  267.5 1.3 last.1
  (67 shorter events, 9.6 us)
Async XLA Ops:
  7.4 7.7 %copy-start.15 = (bf16[128,1024]{1,0:T(8,128)(2,1)S(1)}, bf16[128,1024]{1,0:T(8,128)(2,1)}, u32[]{:S(2)}) copy-start(bf16[128,1024]{1,0:T(8,128)(2,1)} %get-tuple-element.56) | copy-start | bytes 786436
  7.4 7.7 %copy-start.16 = (s32[128]{0:T(128)S(1)}, s32[128]{0:T(128)}, u32[]{:S(2)}) copy-start(s32[128]{0:T(128)} %param.9) | copy-start | bytes 1540
  7.4 30.9 %all-to-all-start = ((bf16[16,384,128]{2,1,0:T(8,128)(2,1)}), bf16[16,384,128]{2,1,0:T(8,128)(2,1)S(1)}, u32[]{:S(2)}, u32[]{:S(2)}) async-start(bf16[16,384,128]{2,1,0:T(8,128)(2,1)} %get-tuple-element.53), calls=%async_computation | async-start | bytes 3145728 | tf_op jit(solution)/shard_map/all_to_all | solution.py:844
  14.7 1.6 collective-permute-start
  16.3 31.1 %copy-start.14 = (bf16[8,8,4,1024]{3,2,1,0:T(4,128)(2,1)S(1)}, bf16[8,8,4,1024]{3,2,1,0:T(4,128)(2,1)}, u32[]{:S(2)}) copy-start(bf16[8,8,4,1024]{3,2,1,0:T(4,128)(2,1)} %param.7) | copy-start | bytes 1572868
  16.3 31.3 %collective-permute-start.1 = (bf16[256,1024]{1,0:T(8,128)(2,1)S(1)}, bf16[256,1024]{1,0:T(8,128)(2,1)}, u32[]{:S(2)}, u32[]{:S(2)}) collective-permute-start(bf16[256,1024]{1,0:T(8,128)(2,1)S(1)} %constant_dynamic-update-slice_fusion), channel_id=1, source_target_pairs={{0,16},{8,24},{16,0},{24,8},{32,48},{40,56},{48,32},{56,40},{64,80... | collective-permute-start | bytes 1572872 | tf_op jit(solution)/shard_map/ppermute | solution.py:514
  38.3 4.8 %copy-start.6 = (bf16[16,384,128]{2,1,0:T(8,128)(2,1)}, bf16[16,384,128]{2,1,0:T(8,128)(2,1)S(1)}, u32[]{:S(2)}) copy-start(bf16[16,384,128]{2,1,0:T(8,128)(2,1)S(1)} %all-to-all-done.query_ref.keys_ref.values_ref.q.k.v) | copy-start | bytes 4718596
  43.1 16.7 %copy-start.3 = (bf16[256,1024]{1,0:T(8,128)(2,1)S(1)}, bf16[256,1024]{1,0:T(8,128)(2,1)}, u32[]{:S(2)}) copy-start(bf16[256,1024]{1,0:T(8,128)(2,1)} %get-tuple-element.54.tokens_ref) | copy-start | bytes 1572868
  43.1 16.7 %all-to-all-start.1 = ((bf16[16,128,128]{2,1,0:T(8,128)(2,1)}), bf16[16,128,128]{2,1,0:T(8,128)(2,1)S(1)}, u32[]{:S(2)}, u32[]{:S(2)}) async-start(bf16[16,128,128]{2,1,0:T(8,128)(2,1)} %get-tuple-element.55), calls=%async_computation.1 | async-start | bytes 1048576 | tf_op jit(solution)/shard_map/all_to_all | solution.py:844
  59.8 8.1 %copy-start.1 = (bf16[16,128,128]{2,1,0:T(8,128)(2,1)}, bf16[16,128,128]{2,1,0:T(8,128)(2,1)S(1)}, u32[]{:S(2)}) copy-start(bf16[16,128,128]{2,1,0:T(8,128)(2,1)S(1)} %all-to-all-done.1) | copy-start | bytes 1572868
  67.9 31.9 %all-to-all-start.2 = ((bf16[8,1024,128]{2,1,0:T(8,128)(2,1)}), bf16[8,1024,128]{2,1,0:T(8,128)(2,1)S(1)}, u32[]{:S(2)}, u32[]{:S(2)}) async-start(bf16[8,1024,128]{2,1,0:T(8,128)(2,1)} %bitcast.28), calls=%async_computation.2 | async-start | bytes 4194304 | tf_op jit(solution)/shard_map/all_to_all | solution.py:844
  73.4 25.4 %collective-permute-start.3 = (bf16[2,256,1024]{2,1,0:T(8,128)(2,1)}, bf16[2,256,1024]{2,1,0:T(8,128)(2,1)S(1)}, u32[]{:S(2)}, u32[]{:S(2)}) collective-permute-start(bf16[2,256,1024]{2,1,0:T(8,128)(2,1)} %pad_maximum_fusion.rest_0_.refs_0_), channel_id=1, source_target_pairs={{0,96},{8,104},{16,112},{24,120},{32,64},{40,72},{48,80},{56,88},{... | collective-permute-start | bytes 3145736 | tf_op jit(solution)/shard_map/ppermute | solution.py:514
  74.2 25.6 %collective-permute-start.2 = (bf16[2,256,1024]{2,1,0:T(8,128)(2,1)}, bf16[2,256,1024]{2,1,0:T(8,128)(2,1)}, u32[]{:S(2)}, u32[]{:S(2)}) collective-permute-start(bf16[2,256,1024]{2,1,0:T(8,128)(2,1)} %pad_maximum_fusion.rest_0_.refs_0_), channel_id=1, source_target_pairs={{0,32},{8,40},{16,48},{24,56},{32,0},{40,8},{48,16},{56,24},{64,96... | collective-permute-start | bytes 3145736 | tf_op jit(solution)/shard_map/ppermute | solution.py:514
  98.8 1.0 copy-start.13
  109.2 30.2 %all-to-all-start.3 = ((bf16[8,1024,128]{2,1,0:T(8,128)(2,1)}), bf16[8,1024,128]{2,1,0:T(8,128)(2,1)S(1)}, u32[]{:S(2)}, u32[]{:S(2)}) async-start(bf16[8,1024,128]{2,1,0:T(8,128)(2,1)} %bitcast.29), calls=%async_computation.3 | async-start | bytes 4194304 | tf_op jit(solution)/shard_map/all_to_all | solution.py:844
  114.6 24.3 %collective-permute-start.4 = (bf16[2,256,1024]{2,1,0:T(8,128)(2,1)}, bf16[2,256,1024]{2,1,0:T(8,128)(2,1)}, u32[]{:S(2)}, u32[]{:S(2)}) collective-permute-start(bf16[2,256,1024]{2,1,0:T(8,128)(2,1)} %pad_maximum_fusion.rest_0_.refs_0_), channel_id=1, source_target_pairs={{0,64},{8,72},{16,80},{24,88},{32,96},{40,104},{48,112},{56,120},{... | collective-permute-start | bytes 3145736 | tf_op jit(solution)/shard_map/ppermute | solution.py:514
  139.4 7.9 %copy-start.2 = (bf16[256,1024]{1,0:T(8,128)(2,1)S(1)}, bf16[256,1024]{1,0:T(8,128)(2,1)}, u32[]{:S(2)}) copy-start(bf16[256,1024]{1,0:T(8,128)(2,1)} %get-tuple-element.59.last_ref.cotangent_ref) | copy-start | bytes 1572868
  139.4 7.9 %copy-start.9 = (bf16[256,1024]{1,0:T(8,128)(2,1)S(1)}, bf16[256,1024]{1,0:T(8,128)(2,1)}, u32[]{:S(2)}) copy-start(bf16[256,1024]{1,0:T(8,128)(2,1)} %get-tuple-element.60.after_ref) | copy-start | bytes 1572868
  147.3 11.9 %collective-permute-start.5 = (bf16[8,256,1024]{2,1,0:T(8,128)(2,1)}, bf16[8,256,1024]{2,1,0:T(8,128)(2,1)}, u32[]{:S(2)}, u32[]{:S(2)}) collective-permute-start(bf16[8,256,1024]{2,1,0:T(8,128)(2,1)} %early_first.1.rest_0_), channel_id=1, source_target_pairs={{0,8},{8,0},{16,24},{24,16},{32,40},{40,32},{48,56},{56,48},{64,72... | collective-permute-start | bytes 12582920 | tf_op jit(solution)/shard_map/ppermute | solution.py:514
  154.4 17.2 %all-to-all-start.4 = ((bf16[16,128,128]{2,1,0:T(8,128)(2,1)}), bf16[16,128,128]{2,1,0:T(8,128)(2,1)S(1)}, u32[]{:S(2)}, u32[]{:S(2)}) async-start(bf16[16,128,128]{2,1,0:T(8,128)(2,1)} %get-tuple-element.62), calls=%async_computation.4 | async-start | bytes 1048576 | tf_op jit(solution)/shard_map/all_to_all | solution.py:844
  168.1 29.4 %collective-permute-start.6 = (bf16[8,128,512]{2,1,0:T(8,128)(2,1)}, bf16[8,128,512]{2,1,0:T(8,128)(2,1)}, u32[]{:S(2)}, u32[]{:S(2)}) collective-permute-start(bf16[8,128,512]{2,1,0:T(8,128)(2,1)} %get-tuple-element.66), channel_id=1, source_target_pairs={{0,2},{1,3},{2,0},{3,1},{4,6},{5,7},{6,4},{7,5},{8,10},{9,11},{10,... | collective-permute-start | bytes 3145736 | tf_op jit(solution)/shard_map/ppermute | solution.py:514
  169.3 28.2 %collective-permute-start.7 = (bf16[8,128,512]{2,1,0:T(8,128)(2,1)}, bf16[8,128,512]{2,1,0:T(8,128)(2,1)}, u32[]{:S(2)}, u32[]{:S(2)}) collective-permute-start(bf16[8,128,512]{2,1,0:T(8,128)(2,1)} %get-tuple-element.68), channel_id=1, source_target_pairs={{0,6},{1,7},{2,4},{3,5},{4,2},{5,3},{6,0},{7,1},{8,14},{9,15},{10,... | collective-permute-start | bytes 3145736 | tf_op jit(solution)/shard_map/ppermute | solution.py:514
  178.8 7.1 %copy-start = (bf16[256,1024]{1,0:T(8,128)(2,1)S(1)}, bf16[256,1024]{1,0:T(8,128)(2,1)}, u32[]{:S(2)}) copy-start(bf16[256,1024]{1,0:T(8,128)(2,1)} %get-tuple-element.64.grad_after_ref.rest_1_.refs_7_) | copy-start | bytes 1572868
  178.8 30.7 %all-to-all-start.5 = ((bf16[16,384,128]{2,1,0:T(8,128)(2,1)}), bf16[16,384,128]{2,1,0:T(8,128)(2,1)S(1)}, u32[]{:S(2)}, u32[]{:S(2)}) async-start(bf16[16,384,128]{2,1,0:T(8,128)(2,1)} %bitcast.16), calls=%async_computation.5 | async-start | bytes 3145728 | tf_op jit(solution)/shard_map/all_to_all | solution.py:844
  185.9 11.6 %copy-start.7 = (bf16[8,128,512]{2,1,0:T(8,128)(2,1)S(1)}, bf16[8,128,512]{2,1,0:T(8,128)(2,1)}, u32[]{:S(2)}) copy-start(bf16[8,128,512]{2,1,0:T(8,128)(2,1)} %get-tuple-element.65.left_ref) | copy-start | bytes 3145732
  185.9 11.6 %copy-start.8 = (bf16[8,128,512]{2,1,0:T(8,128)(2,1)S(1)}, bf16[8,128,512]{2,1,0:T(8,128)(2,1)}, u32[]{:S(2)}) copy-start(bf16[8,128,512]{2,1,0:T(8,128)(2,1)} %get-tuple-element.67.right_ref) | copy-start | bytes 3145732
  196.9 8.2 %collective-permute-start.11 = (bf16[256,1408]{1,0:T(8,128)(2,1)S(1)}, bf16[256,1408]{1,0:T(8,128)(2,1)S(1)}, u32[]{:S(2)}, u32[]{:S(2)}) collective-permute-start(bf16[256,1408]{1,0:T(8,128)(2,1)S(1)} %get-tuple-element.75), channel_id=1, source_target_pairs={{0,8},{8,0},{16,24},{24,16},{32,40},{40,32},{48,56},{56,48},{64,72... | collective-permute-start | bytes 2162696 | tf_op jit(solution)/shard_map/ppermute | solution.py:514
  197.4 7.7 %collective-permute-start.12 = (bf16[256,1408]{1,0:T(8,128)(2,1)S(1)}, bf16[256,1408]{1,0:T(8,128)(2,1)S(1)}, u32[]{:S(2)}, u32[]{:S(2)}) collective-permute-start(bf16[256,1408]{1,0:T(8,128)(2,1)S(1)} %get-tuple-element.76), channel_id=1, source_target_pairs={{0,8},{8,0},{16,24},{24,16},{32,40},{40,32},{48,56},{56,48},{64,72... | collective-permute-start | bytes 2162696 | tf_op jit(solution)/shard_map/ppermute | solution.py:514
  203.9 15.8 %collective-permute-start.8 = (bf16[8,64,512]{2,1,0:T(8,128)(2,1)}, bf16[8,64,512]{2,1,0:T(8,128)(2,1)}, u32[]{:S(2)}, u32[]{:S(2)}) collective-permute-start(bf16[8,64,512]{2,1,0:T(8,128)(2,1)} %get-tuple-element.70), channel_id=1, source_target_pairs={{0,6},{1,7},{2,4},{3,5},{4,2},{5,3},{6,0},{7,1},{8,14},{9,15},{10,... | collective-permute-start | bytes 1572872 | tf_op jit(solution)/shard_map/ppermute | solution.py:514
  205.1 14.6 %collective-permute-start.9 = (bf16[8,64,512]{2,1,0:T(8,128)(2,1)}, bf16[8,64,512]{2,1,0:T(8,128)(2,1)}, u32[]{:S(2)}, u32[]{:S(2)}) collective-permute-start(bf16[8,64,512]{2,1,0:T(8,128)(2,1)} %get-tuple-element.71), channel_id=1, source_target_pairs={{0,2},{1,3},{2,0},{3,1},{4,6},{5,7},{6,4},{7,5},{8,10},{9,11},{10,... | collective-permute-start | bytes 1572872 | tf_op jit(solution)/shard_map/ppermute | solution.py:514
  207.4 18.7 %collective-permute-start.13 = (bf16[2,128,1408]{2,1,0:T(8,128)(2,1)}, bf16[2,128,1408]{2,1,0:T(8,128)(2,1)}, u32[]{:S(2)}, u32[]{:S(2)}) collective-permute-start(bf16[2,128,1408]{2,1,0:T(8,128)(2,1)} %get-tuple-element.78), channel_id=1, source_target_pairs={{0,1},{1,0},{2,3},{3,2},{4,5},{5,4},{6,7},{7,6},{8,9},{9,8},{10,11... | collective-permute-start | bytes 2162696 | tf_op jit(solution)/shard_map/ppermute | solution.py:514
  209.5 10.2 %copy-start.10 = (bf16[8,64,1024]{2,1,0:T(8,128)(2,1)S(1)}, bf16[8,64,1024]{2,1,0:T(8,128)(2,1)}, u32[]{:S(2)}) copy-start(bf16[8,64,1024]{2,1,0:T(8,128)(2,1)} %get-tuple-element.69.own_ref) | copy-start | bytes 3145732
  214.6 0.8 copy-start.4
  215.4 10.7 %copy-start.11 = (bf16[2,128,1408]{2,1,0:T(8,128)(2,1)S(1)}, bf16[2,128,1408]{2,1,0:T(8,128)(2,1)}, u32[]{:S(2)}) copy-start(bf16[2,128,1408]{2,1,0:T(8,128)(2,1)} %get-tuple-element.77.refs_0_) | copy-start | bytes 2162692
  225.2 16.1 %copy-start.12 = (bf16[8,32,1024]{2,1,0:T(8,128)(2,1)S(1)}, bf16[8,32,1024]{2,1,0:T(8,128)(2,1)}, u32[]{:S(2)}) copy-start(bf16[8,32,1024]{2,1,0:T(8,128)(2,1)} %get-tuple-element.72.early_ref) | copy-start | bytes 1572868
  225.2 16.1 %collective-permute-start.10 = (bf16[8,32,1024]{2,1,0:T(8,128)(2,1)S(1)}, bf16[8,32,1024]{2,1,0:T(8,128)(2,1)S(1)}, u32[]{:S(2)}, u32[]{:S(2)}) collective-permute-start(bf16[8,32,1024]{2,1,0:T(8,128)(2,1)S(1)} %get-tuple-element.73), channel_id=1, source_target_pairs={{0,1},{1,0},{2,3},{3,2},{4,5},{5,4},{6,7},{7,6},{8,9},{9,8},{10,11... | collective-permute-start | bytes 1572872 | tf_op jit(solution)/shard_map/ppermute | solution.py:514
  228.0 7.6 %collective-permute-start.14 = (bf16[2,32,1408]{2,1,0:T(8,128)(2,1)S(1)}, bf16[2,32,1408]{2,1,0:T(8,128)(2,1)S(1)}, u32[]{:S(2)}, u32[]{:S(2)}) collective-permute-start(bf16[2,32,1408]{2,1,0:T(8,128)(2,1)S(1)} %get-tuple-element.80), channel_id=1, source_target_pairs={{0,2},{1,3},{2,0},{3,1},{4,6},{5,7},{6,4},{7,5},{8,10},{9,11},{10,... | collective-permute-start | bytes 540680 | tf_op jit(solution)/shard_map/ppermute | solution.py:514
  229.6 9.4 %collective-permute-start.15 = (bf16[2,32,1408]{2,1,0:T(8,128)(2,1)S(1)}, bf16[2,32,1408]{2,1,0:T(8,128)(2,1)S(1)}, u32[]{:S(2)}, u32[]{:S(2)}) collective-permute-start(bf16[2,32,1408]{2,1,0:T(8,128)(2,1)S(1)} %get-tuple-element.81), channel_id=1, source_target_pairs={{0,4},{1,5},{2,6},{3,7},{4,0},{5,1},{6,2},{7,3},{8,12},{9,13},{10,... | collective-permute-start | bytes 540680 | tf_op jit(solution)/shard_map/ppermute | solution.py:514
  231.3 10.0 %collective-permute-start.16 = (bf16[2,32,1408]{2,1,0:T(8,128)(2,1)S(1)}, bf16[2,32,1408]{2,1,0:T(8,128)(2,1)S(1)}, u32[]{:S(2)}, u32[]{:S(2)}) collective-permute-start(bf16[2,32,1408]{2,1,0:T(8,128)(2,1)S(1)} %get-tuple-element.82), channel_id=1, source_target_pairs={{0,6},{1,7},{2,4},{3,5},{4,2},{5,3},{6,0},{7,1},{8,14},{9,15},{10,... | collective-permute-start | bytes 540680 | tf_op jit(solution)/shard_map/ppermute | solution.py:514
  242.2 21.7 %copy-start.5 = (bf16[256,1024]{1,0:T(8,128)(2,1)S(1)}, bf16[256,1024]{1,0:T(8,128)(2,1)}, u32[]{:S(2)}) copy-start(bf16[256,1024]{1,0:T(8,128)(2,1)} %copy-done.4) | copy-start | bytes 1572868
  242.2 9.7 %collective-permute-start.17 = (bf16[2,32,2176]{2,1,0:T(8,128)(2,1)S(1)}, bf16[2,32,2176]{2,1,0:T(8,128)(2,1)S(1)}, u32[]{:S(2)}, u32[]{:S(2)}) collective-permute-start(bf16[2,32,2176]{2,1,0:T(8,128)(2,1)S(1)} %get-tuple-element.84), channel_id=1, source_target_pairs={{0,32},{8,40},{16,48},{24,56},{32,0},{40,8},{48,16},{56,24},{64,96... | collective-permute-start | bytes 835592 | tf_op jit(solution)/shard_map/ppermute | solution.py:514
  243.4 14.0 %collective-permute-start.18 = (bf16[2,32,2176]{2,1,0:T(8,128)(2,1)S(1)}, bf16[2,32,2176]{2,1,0:T(8,128)(2,1)S(1)}, u32[]{:S(2)}, u32[]{:S(2)}) collective-permute-start(bf16[2,32,2176]{2,1,0:T(8,128)(2,1)S(1)} %get-tuple-element.85), channel_id=1, source_target_pairs={{0,64},{8,72},{16,80},{24,88},{32,96},{40,104},{48,112},{56,120},{... | collective-permute-start | bytes 835592 | tf_op jit(solution)/shard_map/ppermute | solution.py:514
  246.1 13.9 %collective-permute-start.19 = (bf16[2,32,2176]{2,1,0:T(8,128)(2,1)S(1)}, bf16[2,32,2176]{2,1,0:T(8,128)(2,1)S(1)}, u32[]{:S(2)}, u32[]{:S(2)}) collective-permute-start(bf16[2,32,2176]{2,1,0:T(8,128)(2,1)S(1)} %get-tuple-element.86), channel_id=1, source_target_pairs={{0,96},{8,104},{16,112},{24,120},{32,64},{40,72},{48,80},{56,88},{... | collective-permute-start | bytes 835592 | tf_op jit(solution)/shard_map/ppermute | solution.py:514
  260.6 6.9 %collective-permute-start.20 = (bf16[4,32,640]{2,1,0:T(8,128)(2,1)S(1)}, bf16[4,32,640]{2,1,0:T(8,128)(2,1)S(1)}, u32[]{:S(2)}, u32[]{:S(2)}) collective-permute-start(bf16[4,32,640]{2,1,0:T(8,128)(2,1)S(1)} %get-tuple-element.88), channel_id=1, source_target_pairs={{0,16},{8,24},{16,0},{24,8},{32,48},{40,56},{48,32},{56,40},{64,80... | collective-permute-start | bytes 491528 | tf_op jit(solution)/shard_map/ppermute | solution.py:514
